TPU v7x, 512 devices: a whole 4x4x16 slice. The times are simulated.
512 devices in a mesh: replica: 8 (over z_hi, x), section: 8 (over y, core), tensor: 8 (over z_lo).
Axes of the slice: x: 4, y: 4, z: 16 (z_hi: 2, z_lo: 8; z = z_hi * 8 + z_lo), core: 2. Of those that a mesh axis runs over, the one named last changes fastest.
Arguments:
- activations: bfloat16 [8, 8, 512, 4096], P('replica', 'section', None, 'tensor'), may hold values from -6 to 6
- key_grads: bfloat16 [8, 8, 512, 512], P('replica', 'section', None, 'tensor'), may hold values from -6 to 6
- weight: bfloat16 [8, 8, 512, 4096], P('replica', 'section', 'tensor'), may hold values from -0.09375 to 0.09375
- first_moment: float32 [8, 8, 512, 4096], P('replica', 'section', 'tensor'), may hold values from -10 to 10
- second_moment: float32 [8, 8, 512, 4096], P('replica', 'section', 'tensor'), may hold values from 0.5 to 10
- probe_matrix: float32 [128, 8], replicated, may hold values from -6 to 6
- failed_replica: int32 [8, 8], replicated, may hold values from 0 to 7
- resend_spans: int32 [8, 8], replicated, may hold values from 0 to 31, as said below
Outputs:
- key_out: bfloat16 [8, 8, 512, 512], P('replica', 'section', None, 'tensor')
- input_grads: bfloat16 [8, 8, 512, 4096], P('replica', 'section', None, 'tensor')
- update: float32 [8, 8, 512, 4096], P('replica', 'section', 'tensor')
- checksums: float32 [8, 8, 2, 512, 256], P('replica', 'section', None, 'tensor')
- weight_checksums: float32 [8, 8, 512, 256], P('replica', 'section', 'tensor')
Inputs may be any that keep to these rules, and one draw needn't show every extreme that they name: `resend_spans`: each row holds 8 distinct span numbers.
All inputs are finite; a program needn't handle non-finite values.
Results may differ from a plain program's by a relative error of at most 0.014.
Values may be sent and summed in bfloat16 or wider, within the bound.
No kernel may reach another device: no remote copies, remote signals or barrier semaphores. Data moves between devices by JAX's collectives and lax.ppermute only.
A program may use at most 64 MiB of HBM per device.

v0:
```python
import jax
import jax.numpy as jnp
from jax import lax
from jax.sharding import PartitionSpec as P


def from_behind(block, axis, distance):
    devices = range(lax.axis_size(axis))
    route = [((i - distance) % len(devices), i) for i in devices]
    return lax.ppermute(block, axis, route)


def shards(
    activations,
    key_grads,
    weight,
    first_moment,
    second_moment,
    probe_matrix,
    failed_replica,
    resend_spans,
):
    copies = lax.axis_size("replica")
    my_replica = lax.axis_index("replica")
    my_section = lax.axis_index("section")
    my_tensor = lax.axis_index("tensor")
    failed = failed_replica[my_section, my_tensor]
    my_spans = resend_spans[my_section]
    own_weight = weight[0, 0]
    own_first = first_moment[0, 0]
    own_second = second_moment[0, 0]
    rows_here, full_width = own_weight.shape
    nchunk = full_width // 128
    onehot_rows = my_spans[:, None] == jnp.arange(nchunk, dtype=jnp.int32)[None, :]
    listed = jnp.any(onehot_rows, axis=0)
    columns = jnp.repeat(listed, 128)[None, :]
    primary = jnp.bitwise_xor(failed, copies // 2)
    second = jnp.bitwise_xor(failed, 1)
    chosen = jnp.where(columns, my_replica == second, my_replica == primary)
    fresh_weight = lax.psum(
        jnp.where(chosen, own_weight.astype(jnp.float32), 0.0).astype(jnp.bfloat16), "replica"
    )
    fresh_first, fresh_second = (
        lax.psum(jnp.where(chosen, own_first, 0.0).astype(jnp.bfloat16), "replica").astype(
            jnp.float32
        ),
        lax.psum(jnp.where(chosen, own_second, 0.0).astype(jnp.bfloat16), "replica").astype(
            jnp.float32
        ),
    )
    is_failed = my_replica == failed
    restored_weight = jnp.where(is_failed, fresh_weight, own_weight)
    restored_first = jnp.where(is_failed, fresh_first, own_first)
    restored_second = jnp.where(is_failed, fresh_second, own_second)
    incoming = from_behind(activations[0, 0], "section", 1)
    grads_here = key_grads[0, 0]
    own_slice = incoming.astype(jnp.float32)
    gathered = lax.all_gather(incoming, "tensor", axis=1, tiled=True)
    widened = gathered.astype(jnp.float32)
    inverse_rms = 1.0 / jnp.sqrt(
        jnp.sum(widened * widened, axis=1, keepdims=True) / full_width + 1e-05
    )
    normed = (widened * inverse_rms).astype(jnp.bfloat16)
    key_out = lax.dot_general(
        normed, restored_weight, (((1,), (1,)), ((), ())), preferred_element_type=jnp.float32
    ).astype(jnp.bfloat16)
    local_grads = lax.dot_general(
        grads_here, normed, (((0,), (0,)), ((), ())), preferred_element_type=jnp.float32
    )
    flipped = lax.psum_scatter(
        lax.dot_general(
            restored_weight,
            grads_here,
            (((0,), (1,)), ((), ())),
            preferred_element_type=jnp.float32,
        ).astype(jnp.bfloat16),
        "tensor",
        scatter_dimension=0,
        tiled=True,
    ).astype(jnp.float32)
    feature = flipped.T
    product = lax.psum(jnp.sum(feature * own_slice, axis=1), "tensor")
    product = product[:, None]
    mean_grad = lax.psum(local_grads.astype(jnp.bfloat16), "replica").astype(jnp.float32) / copies
    moment_one = 0.9 * restored_first + 0.1 * mean_grad
    moment_two = 0.95 * restored_second + 0.05 * (mean_grad * mean_grad)
    update = moment_one / (jnp.sqrt(moment_two) + 1e-08)
    input_grad = (
        inverse_rms * feature
        - inverse_rms * inverse_rms * inverse_rms * own_slice * product / full_width
    )
    outgoing = from_behind(input_grad.astype(jnp.bfloat16), "section", -1)

    def checksum(source):
        shaped = source.reshape(rows_here, nchunk, 128)
        mixed = jnp.einsum("jnc,cp->jnp", shaped, probe_matrix, precision=lax.Precision.HIGHEST)
        return mixed.reshape(rows_here, nchunk * probe_matrix.shape[1])

    checksums = jnp.stack([checksum(restored_first), checksum(restored_second)])
    weight_checksums = checksum(restored_weight.astype(jnp.float32))
    return (
        key_out[None, None],
        outgoing[None, None],
        update[None, None],
        checksums[None, None],
        weight_checksums[None, None],
    )


def solution(mesh):
    placed = (
        P("replica", "section", None, "tensor"),
        P("replica", "section", None, "tensor"),
        P("replica", "section", "tensor", None),
        P("replica", "section", "tensor", None),
        P("replica", "section", "tensor", None),
        P(),
        P(),
        P(),
    )
    return jax.shard_map(
        shards,
        mesh=mesh,
        in_specs=placed,
        out_specs=(
            P("replica", "section", None, "tensor"),
            P("replica", "section", None, "tensor"),
            P("replica", "section", "tensor", None),
            P("replica", "section", None, "tensor", None),
            P("replica", "section", "tensor", None),
        ),
        check_vma=False,
    )
```

profile of v0, /device:TPU:1, one launch (start us, length us, event | category | flops | bytes accessed | tf_op | source)
XLA Modules:
  0.0 515.9 jit_solution(841594404893438666)
XLA Ops:
  7.2 0.0 copy-start
  7.2 0.0 all-gather.2.cloned.1.call-start
  7.2 1.3 copy.22
  8.5 2.7 collective-permute-start
  11.2 6.1 %collective-permute-done = bf16[512,512]{0,1:T(8,128)(2,1)S(1)} collective-permute-done((bf16[512,512]{0,1:T(8,128)(2,1)S(1)}, bf16[512,512]{0,1:T(8,128)(2,1)S(1)}, u32[]{:S(2)}, u32[]{:S(2)}) %collective-permute-start) | collective-permute-done | bytes 524320 | tf_op jit(solution)/shard_map/ppermute | solution.py:10
  17.3 0.8 copy-done.1
  18.1 0.0 all-gather.2.cloned.1.call-update
  18.2 0.0 all-reduce.3.cloned.1.call-start
  18.2 1.3 dynamic_slice.6
  20.8 0.7 dynamic-slice_bitcast_fusion
  21.5 0.1 fusion.37
  21.6 0.1 broadcast_bitcast_fusion
  21.7 1.9 select_convert_fusion
  23.6 2.7 fusion.25
  26.3 101.4 %all-gather.2.cloned.1.call-done = bf16[512,4096]{0,1:T(8,128)(2,1)} async-done(((bf16[512,512]{0,1:T(8,128)(2,1)}), bf16[512,4096]{0,1:T(8,128)(2,1)}) %all-gather.2.cloned.1.call-update) | async-done | bytes 4194320 | tf_op jit(solution)/shard_map/all_gather | solution.py:58
  127.7 3.3 fusion
  131.0 0.0 copy-done
  131.0 0.1 copy-done.3
  131.1 2.2 fusion.2
  133.3 0.0 all-reduce.3.cloned.1.call-update
  133.4 0.0 reduce-scatter.2.cloned.1.call-start
  134.1 228.6 %all-reduce.3.cloned.1.call-done = (bf16[64,4096]{1,0:T(8,128)(2,1)}, bf16[64,4096]{1,0:T(8,128)(2,1)}, bf16[64,4096]{1,0:T(8,128)(2,1)}, bf16[64,4096]{1,0:T(8,128)(2,1)}) async-done(((bf16[64,4096]{1,0:T(8,128)(2,1)}, bf16[64,4096]{1,0:T(8,128)(2,1)}, bf16[64,4096]{1,0:T(8,128)(2,1)}, bf16[64,4096]{1,0:T(8,128)(2,1)}), (bf16[64,4096]{1,0:T(8,128)(2,1)}, bf16[64,4096]{1,0:T(8,128)(2,1)}, ...) | async-done | bytes 2097168 | tf_op jit(solution)/shard_map/psum | solution.py:40
  362.6 0.0 copy-done.6
  362.7 0.1 bitcast_select_fusion.4
  362.7 3.3 convolution_convert_fusion
  366.0 0.0 reduce-scatter.2.cloned.1.call-update
  366.0 0.1 copy.31
  366.1 1.1 copy-done.4
  367.2 0.3 copy-done.5
  367.5 3.1 fusion.27
  370.6 0.2 copy.29
  370.8 0.2 copy.30
  371.0 4.2 fusion.35
  375.2 4.2 fusion.33
  379.4 91.7 %reduce-scatter.2.cloned.1.call-done = bf16[512,512]{1,0:T(8,128)(2,1)} async-done(((bf16[4096,512]{1,0:T(8,128)(2,1)}), bf16[512,512]{1,0:T(8,128)(2,1)}) %reduce-scatter.2.cloned.1.call-update) | async-done | bytes 524304 | tf_op jit(solution)/shard_map/reduce_scatter | solution.py:70
  471.0 1.2 fusion.16
  472.3 22.5 %psum.36 = f32[512]{0:T(512)S(1)} all-reduce(f32[512]{0:T(512)S(1)} %fusion.16), channel_id=1, replica_groups=mesh['replica'=8,'section'=8,'tensor'=8] {'tensor'}, use_global_device_ids=true, to_apply=%region_5.6 | all-reduce | flops 512 | bytes 4096 | tf_op jit(solution)/shard_map/psum | solution.py:82
  494.8 1.3 fusion.15
  496.1 4.3 collective-permute-start.1
  500.4 2.1 fusion.31
  502.5 0.2 copy.25
  502.7 0.7 copy.28
  503.4 0.2 copy.23
  503.6 0.2 copy.24
  503.8 0.8 copy.27
  504.5 3.8 fusion.9
  508.3 0.1 collective-permute-done.1
  508.4 1.0 copy.26
  (12 shorter events, 0.1 us)
Async XLA Ops:
  7.2 123.8 %copy-start = (bf16[1,1,512,64]{2,3,1,0:T(8,128)(2,1)S(1)}, bf16[1,1,512,64]{2,3,1,0:T(8,128)(2,1)}, u32[]{:S(2)}) copy-start(bf16[1,1,512,64]{2,3,1,0:T(8,128)(2,1)} %param.9) | copy-start | bytes 196612
  7.2 120.5 %all-gather.2.cloned.1.call-start = ((), (), s32[]{:S(2)}) async-start(), calls=%async_computation.1 | async-start | bytes 4718592 | tf_op jit(solution)/shard_map/all_gather | solution.py:58
  8.5 8.8 %collective-permute-start = (bf16[512,512]{0,1:T(8,128)(2,1)S(1)}, bf16[512,512]{0,1:T(8,128)(2,1)S(1)}, u32[]{:S(2)}, u32[]{:S(2)}) collective-permute-start(bf16[512,512]{0,1:T(8,128)(2,1)S(1)} %bitcast.75), channel_id=1, source_target_pairs={{56,0},{0,8},{8,16},{16,24},{24,32},{32,40},{40,48},{48,56},{57,1}... | collective-permute-start | bytes 1572872 | tf_op jit(solution)/shard_map/ppermute | solution.py:10
  17.3 0.8 copy-start.1
  18.2 344.5 %all-reduce.3.cloned.1.call-start = ((), (), s32[]{:S(2)}) async-start(), calls=%async_computation.3 | async-start | bytes 4194304 | tf_op jit(solution)/shard_map/psum | solution.py:40
  127.7 3.4 copy-start.3
  131.1 231.5 %copy-start.6 = (bf16[1,1,64,4096]{3,2,1,0:T(8,128)(2,1)S(1)}, bf16[1,1,64,4096]{3,2,1,0:T(8,128)(2,1)}, u32[]{:S(2)}) copy-start(bf16[1,1,64,4096]{3,2,1,0:T(8,128)(2,1)} %param.10) | copy-start | bytes 1572868
  133.4 337.7 %reduce-scatter.2.cloned.1.call-start = ((), (), s32[]{:S(2)}) async-start(), calls=%async_computation.2 | async-start | bytes 4718592 | tf_op jit(solution)/shard_map/reduce_scatter | solution.py:70
  366.0 1.2 copy-start.4
  366.0 1.5 copy-start.5
  367.5 3.5 copy-start.7
  370.6 100.4 %copy-start.2 = (bf16[512,512]{0,1:T(8,128)(2,1)S(1)}, bf16[512,512]{0,1:T(8,128)(2,1)}, u32[]{:S(2)}) copy-start(bf16[512,512]{0,1:T(8,128)(2,1)} %copy-done.1) | copy-start | bytes 1572868
  496.1 12.3 %collective-permute-start.1 = (bf16[512,512]{0,1:T(8,128)(2,1)S(1)}, bf16[512,512]{0,1:T(8,128)(2,1)S(1)}, u32[]{:S(2)}, u32[]{:S(2)}) collective-permute-start(bf16[512,512]{0,1:T(8,128)(2,1)S(1)} %fusion.15), channel_id=1, source_target_pairs={{8,0},{16,8},{24,16},{32,24},{40,32},{48,40},{56,48},{0,56},{9,1},... | collective-permute-start | bytes 1572872 | tf_op jit(solution)/shard_map/ppermute | solution.py:10
Sparse Core Ops, SparseCore 0:
  18.3 109.3 all-gather.1
  133.5 229.1 all-reduce.2
  366.1 104.8 reduce-scatter.1
where the time goes:
time: 516 us
  waiting for transfers between devices  428 us (83%)
  blocking collectives  22.5 us (4%)
  matrix products  19.7 us (4%)
  between operations  15.8 us (3%)
  other arithmetic  13.8 us (3%)
  local copies, waits for them, and re-layouts  9.15 us (2%)
  starting transfers between devices  7.16 us (1%)
    psum x1, waiting for transfers between devices, shards(): lax.psum(jnp.where(chosen, own_weight.astype(jnp.float32), 0.0).astype(jn...  229 us
    all_gather x1, waiting for transfers between devices, shards(): gathered = lax.all_gather(incoming, 'tensor', axis=1, tiled=True)  101 us
    reduce_scatter x1, waiting for transfers between devices, shards(): lax.psum_scatter(lax.dot_general(restored_weight, grads_here, (((0,), (1,...  91.7 us
    psum x1, blocking collectives, shards(): product = lax.psum(jnp.sum(feature * own_slice, axis=1), 'tensor')  22.5 us
    dot_general x3, matrix products, checksum(): jnp.einsum('jnc,cp->jnp', shaped, probe_matrix, precision=lax.Precision.H...  10.5 us
  transfers between devices with their start and end apart: 5, of which 5 were waited for; matrix products, arithmetic and copies ran while one was open for 5% of the time, Pallas kernels for 0%

commit v1 on v0

v1 whole, which is shorter than its diff:
```python
import jax
import jax.numpy as jnp
from jax import lax
from jax.sharding import PartitionSpec as P

SHORT = jnp.bfloat16
WIDE = jnp.float32
PLANE = 4


def from_behind(block, axis, distance):
    n = lax.axis_size(axis)
    return lax.ppermute(block, axis, [((i - distance) % n, i) for i in range(n)])


def swap(block, axis, bit):
    return lax.ppermute(block, axis, [(i, i ^ bit) for i in range(lax.axis_size(axis))])


def exchange_x(block):
    groups = [[0, 1, 2, 3], [4, 5, 6, 7]]
    return lax.all_to_all(block, "replica", 0, 0, axis_index_groups=groups, tiled=True)


def two_halves(value):
    high = value.astype(SHORT)
    return high, (value - high.astype(WIDE)).astype(SHORT)


def gather_tensor(block):
    held = block[None]
    for bit in (4, 2, 1):
        held = jnp.concatenate([held, swap(held, "tensor", bit)], axis=0)
    order = (0, 4, 2, 6, 1, 5, 3, 7)
    held = jnp.stack([held[order.index(i)] for i in range(8)])
    mine = lax.axis_index("tensor")
    for bit in (4, 2, 1):
        shape = (8 // (2 * bit), 2, bit) + block.shape
        split = held.reshape(shape)
        held = jnp.where((mine & bit) != 0, split[:, ::-1], split).reshape(held.shape)
    return held


def adam(first, second, grad):
    one = 0.9 * first + 0.1 * grad
    two = 0.95 * second + 0.05 * (grad * grad)
    return one / (jnp.sqrt(two) + 1e-08)


def shards(activations, key_grads, weight, first_moment, second_moment, probe_matrix, failed_replica, resend_spans):
    copies = lax.axis_size("replica")
    my_replica = lax.axis_index("replica")
    my_section = lax.axis_index("section")
    my_tensor = lax.axis_index("tensor")
    failed = failed_replica[my_section, my_tensor]
    my_spans = resend_spans[my_section]
    own_weight = weight[0, 0]
    own_first = first_moment[0, 0]
    own_second = second_moment[0, 0]
    rows, width = own_weight.shape
    nchunk = width // 128
    listed = jnp.any(my_spans[:, None] == jnp.arange(nchunk, dtype=jnp.int32)[None, :], axis=0)
    columns = jnp.repeat(listed, 128)[None, :]
    primary = jnp.bitwise_xor(failed, PLANE)
    second = jnp.bitwise_xor(failed, 1)
    chosen = jnp.where(columns, my_replica == second, my_replica == primary)
    is_failed = my_replica == failed
    part = rows // PLANE

    local = activations[0, 0]
    tokens, cols = local.shape
    incoming = from_behind(local, "section", 1)
    squares = jnp.sum(jnp.square(local.astype(WIDE)), axis=1)
    high, low = two_halves(squares)
    extra = jnp.concatenate([high[None], low[None], jnp.zeros((6, tokens), SHORT)], axis=0)
    kg_rows = jnp.concatenate([key_grads[0, 0].T, extra], axis=0)
    kg_rows = gather_tensor(kg_rows)
    kg_all = kg_rows[:, :rows].reshape(8 * rows, tokens)
    total = jnp.sum(kg_rows[:, rows].astype(WIDE) + kg_rows[:, rows + 1].astype(WIDE), axis=0)
    total = from_behind(total.reshape(-1, 128), "section", 1).reshape(tokens)
    inverse_rms = 1.0 / jnp.sqrt(total / width + 1e-05)

    masked = [jnp.where(chosen, a.astype(SHORT), 0).reshape(PLANE, 1, part, width) for a in (own_weight, own_first, own_second)]
    spread = exchange_x(jnp.concatenate(masked, axis=1))
    spread = jnp.sum(spread.astype(WIDE), axis=0).astype(SHORT)
    fresh_weight = spread[0] + swap(spread[0], "replica", PLANE)
    fresh_moments = spread[1:] + swap(spread[1:], "replica", PLANE)
    groups = [[0, 1, 2, 3], [4, 5, 6, 7]]
    fresh_weight = lax.all_gather(fresh_weight, "replica", axis=0, tiled=True, axis_index_groups=groups)
    restored_weight = jnp.where(is_failed, fresh_weight, own_weight)

    x = incoming.astype(WIDE)
    normed = (x * inverse_rms[:, None]).astype(SHORT)
    grad = lax.dot_general(kg_all, normed, (((1,), (0,)), ((), ())), preferred_element_type=WIDE).astype(SHORT)
    grad = grad.reshape(8, PLANE, part, cols).transpose(1, 0, 2, 3)
    grad = jnp.sum(exchange_x(grad).astype(WIDE), axis=0).astype(SHORT)

    sent = jnp.concatenate([restored_weight.reshape(rows, 8, cols).transpose(1, 0, 2), grad], axis=1)
    got = lax.all_to_all(sent, "tensor", 0, 0, tiled=True)
    weight_cols = got[:, :rows].reshape(8 * rows, cols)
    grad_rows = got[:, rows:].transpose(1, 0, 2).reshape(part, width)
    mean_rows = (grad_rows.astype(WIDE) + swap(grad_rows, "replica", PLANE).astype(WIDE)) / copies

    keys = lax.dot_general(weight_cols, normed, (((1,), (1,)), ((), ())), preferred_element_type=WIDE).astype(SHORT)
    feature = lax.dot_general(kg_all, weight_cols, (((0,), (0,)), ((), ())), preferred_element_type=WIDE)
    high, low = two_halves(jnp.sum(feature * x, axis=1))
    extra = jnp.concatenate([high[None], low[None], jnp.zeros((6, tokens), SHORT)], axis=0)
    sent = jnp.concatenate([keys.reshape(8, rows, tokens), jnp.broadcast_to(extra[None], (8, 8, tokens))], axis=1)
    got = jnp.sum(lax.all_to_all(sent, "tensor", 0, 0, tiled=True).astype(WIDE), axis=0)
    key_out = got[:rows].T.astype(SHORT)
    product = (got[rows] + got[rows + 1])[:, None]
    scale = inverse_rms[:, None]
    input_grad = scale * feature - scale * scale * scale * x * product / width
    outgoing = from_behind(input_grad.astype(SHORT), "section", -1)

    def checksum(source):
        shaped = source.reshape(-1, nchunk, 128)
        mixed = jnp.einsum("jnc,cp->jnp", shaped, probe_matrix, precision=lax.Precision.HIGHEST)
        return mixed.reshape(-1, nchunk * probe_matrix.shape[1])

    fresh = fresh_moments.astype(WIDE)
    fresh_update = adam(fresh[0], fresh[1], mean_rows).astype(SHORT)
    fresh_sums = checksum(fresh.reshape(2 * part, width)).astype(SHORT).reshape(2, width)
    shared = jnp.concatenate([mean_rows.astype(SHORT), fresh_update, fresh_sums], axis=0)
    shared = exchange_x(jnp.broadcast_to(shared[None], (PLANE,) + shared.shape))
    mean_grad = shared[:, :part].reshape(rows, width).astype(WIDE)
    fresh_update = shared[:, part : 2 * part].reshape(rows, width).astype(WIDE)
    fresh_sums = shared[:, 2 * part :].reshape(PLANE, 2, part, -1).transpose(1, 0, 2, 3).reshape(2, rows, -1).astype(WIDE)
    update = jnp.where(is_failed, fresh_update, adam(own_first, own_second, mean_grad))
    own_sums = jnp.stack([checksum(own_first), checksum(own_second)])
    checksums = jnp.where(is_failed, fresh_sums, own_sums)
    weight_checksums = checksum(restored_weight.astype(WIDE))
    return (key_out[None, None], outgoing[None, None], update[None, None], checksums[None, None], weight_checksums[None, None])


def solution(mesh):
    by_rows = P("replica", "section", "tensor", None)
    by_features = P("replica", "section", None, "tensor")
    return jax.shard_map(
        shards,
        mesh=mesh,
        in_specs=(by_features, by_features, by_rows, by_rows, by_rows, P(), P(), P()),
        out_specs=(by_features, by_features, by_rows, P("replica", "section", None, "tensor", None), by_rows),
        check_vma=False,
    )
```

time: 516 us -> 262 us (0.51)
  waiting for transfers between devices: 428 us -> 63.8 us
  starting transfers between devices: 7.16 us -> 126 us
  local copies, waits for them, and re-layouts: 9.15 us -> 22 us
  between operations: 15.8 us -> 3.09 us
  blocking collectives: 22.5 us -> 10.4 us
    psum x1 -> x0, waiting for transfers between devices: 229 us -> none  [shards(): lax.psum(jnp.where(chosen, own_weight.astype(jnp.float32), 0.0).astype(jn...]
    all_gather x1 -> x0, waiting for transfers between devices: 101 us -> none  [shards(): gathered = lax.all_gather(incoming, 'tensor', axis=1, tiled=True)]
    reduce_scatter x1 -> x0, waiting for transfers between devices: 91.7 us -> none  [shards(): lax.psum_scatter(lax.dot_general(restored_weight, grads_here, (((0,), (1,...]
    ppermute x2 -> x9, starting transfers between devices: 7.03 us -> 68.5 us  [the longest x6 54.5 us: swap(): lax.ppermute(block, axis, [(i, i ^ bit) for i in range(lax.axis_size(axis...]
    all_to_all x0 -> x5, starting transfers between devices: none -> 57.6 us  [the longest x1 28.8 us: shards(): lax.all_to_all(sent, 'tensor', 0, 0, tiled=True).astype(WIDE)]
    all_to_all x0 -> x5, waiting for transfers between devices: none -> 41.1 us  [the longest x1 15 us: shards(): lax.all_to_all(sent, 'tensor', 0, 0, tiled=True).astype(WIDE)]
    psum x1 -> x0, blocking collectives: 22.5 us -> none  [shards(): product = lax.psum(jnp.sum(feature * own_slice, axis=1), 'tensor')]
    ppermute x2 -> x9, waiting for transfers between devices: 6.21 us -> 22.6 us  [the longest x6 15.4 us: swap(): lax.ppermute(block, axis, [(i, i ^ bit) for i in range(lax.axis_size(axis...]
  transfers between devices with their start and end apart: 5 -> 14, of which waited for: 5 -> 10; matrix products, arithmetic and copies ran while one was open for 5% -> 18% of each run, Pallas kernels for 0% -> 0%
where the time goes in v1:
time: 262 us; the launch traced here: 260 us
  starting transfers between devices  126 us (48%)
  waiting for transfers between devices  63.8 us (24%)
  local copies, waits for them, and re-layouts  22 us (8%)
  matrix products  19.2 us (7%)
  other arithmetic  16 us (6%)
  blocking collectives  10.4 us (4%)
  between operations  3.09 us (1%)
    ppermute x6, starting transfers between devices, swap(): lax.ppermute(block, axis, [(i, i ^ bit) for i in range(lax.axis_size(axis...  54.5 us
    all_to_all x1, starting transfers between devices, shards(): lax.all_to_all(sent, 'tensor', 0, 0, tiled=True).astype(WIDE)  28.8 us
    all_to_all x1, starting transfers between devices, shards(): got = lax.all_to_all(sent, 'tensor', 0, 0, tiled=True)  17.5 us
    ppermute x6, waiting for transfers between devices, swap(): lax.ppermute(block, axis, [(i, i ^ bit) for i in range(lax.axis_size(axis...  15.4 us
    all_to_all x1, waiting for transfers between devices, shards(): lax.all_to_all(sent, 'tensor', 0, 0, tiled=True).astype(WIDE)  15 us
    all_to_all x3, waiting for transfers between devices, exchange_x(): lax.all_to_all(block, 'replica', 0, 0, axis_index_groups=groups, tiled=True)  14.2 us
    ppermute x3, starting transfers between devices, from_behind(): lax.ppermute(block, axis, [((i - distance) % n, i) for i in range(n)])  13.9 us
    dot_general x4, matrix products, checksum(): jnp.einsum('jnc,cp->jnp', shaped, probe_matrix, precision=lax.Precision.H...  13.3 us
  transfers between devices with their start and end apart: 14, of which 10 were waited for; matrix products, arithmetic and copies ran while one was open for 18% of the time, Pallas kernels for 0%

profile of v1, /device:TPU:1, one launch (start us, length us, event | category | flops | bytes accessed | tf_op | source)
XLA Modules:
  0.0 260.4 jit_solution(2329345307319917588)
XLA Ops:
  0.7 1.3 copy.52
  2.2 9.8 %collective-permute-start.1 = (bf16[1,72,512]{2,1,0:T(8,128)(2,1)S(1)}, bf16[1,72,512]{2,1,0:T(8,128)(2,1)S(1)}, u32[]{:S(2)}, u32[]{:S(2)}) collective-permute-start(bf16[1,72,512]{2,1,0:T(8,128)(2,1)S(1)} %maximum_bitcast_fusion), channel_id=1, source_target_pairs={{0,4},{1,5},{2,6},{3,7},{4,0},{5,1},{6,2},{7,3},{8,12},{9,13},{10,... | collective-permute-start | bytes 221192 | tf_op jit(solution)/shard_map/ppermute | solution.py:17
  12.0 1.3 dynamic_slice.6
  15.7 5.5 %collective-permute-start.2 = (bf16[2,72,512]{2,1,0:T(8,128)(2,1)S(1)}, bf16[2,72,512]{2,1,0:T(8,128)(2,1)S(1)}, u32[]{:S(2)}, u32[]{:S(2)}) collective-permute-start(bf16[2,72,512]{2,1,0:T(8,128)(2,1)S(1)} %pad_maximum_fusion.5), channel_id=1, source_target_pairs={{0,2},{1,3},{2,0},{3,1},{4,6},{5,7},{6,4},{7,5},{8,10},{9,11},{10,... | collective-permute-start | bytes 442376 | tf_op jit(solution)/shard_map/ppermute | solution.py:17
  21.3 2.4 collective-permute-done.2
  24.5 7.3 %collective-permute-start.3 = (bf16[4,72,512]{2,1,0:T(8,128)(2,1)}, bf16[4,72,512]{2,1,0:T(8,128)(2,1)}, u32[]{:S(2)}, u32[]{:S(2)}) collective-permute-start(bf16[4,72,512]{2,1,0:T(8,128)(2,1)} %pad_maximum_fusion.4), channel_id=1, source_target_pairs={{0,1},{1,0},{2,3},{3,2},{4,5},{5,4},{6,7},{7,6},{8,9},{9,8},{10,11... | collective-permute-start | bytes 884744 | tf_op jit(solution)/shard_map/ppermute | solution.py:17
  31.8 1.3 pad_maximum_fusion
  33.1 4.3 %all-to-all-start = ((bf16[4,3,16,4096]{3,2,1,0:T(8,128)(2,1)}), bf16[4,3,16,4096]{3,2,1,0:T(8,128)(2,1)}, u32[]{:S(2)}, u32[]{:S(2)}) async-start(bf16[4,3,16,4096]{3,2,1,0:T(8,128)(2,1)} %pad_maximum_fusion), calls=%async_computation | async-start | bytes 3145728 | tf_op jit(solution)/shard_map/all_to_all | solution.py:22
  37.4 2.0 collective-permute-start.4
  40.3 0.9 slice_dynamic-update-slice_fusion.3
  43.4 1.8 collective-permute-start.5
  46.0 1.5 convolution_convert_fusion.1
  48.3 9.1 %all-to-all-done = bf16[4,3,16,4096]{3,2,1,0:T(8,128)(2,1)} async-done(((bf16[4,3,16,4096]{3,2,1,0:T(8,128)(2,1)}), bf16[4,3,16,4096]{3,2,1,0:T(8,128)(2,1)}, u32[]{:S(2)}, u32[]{:S(2)}) %all-to-all-start) | async-done | bytes 1572896 | tf_op jit(solution)/shard_map/all_to_all | solution.py:22
  57.5 3.5 %all-to-all-start.1 = ((bf16[4,8,16,512]{3,2,1,0:T(8,128)(2,1)}), bf16[4,8,16,512]{3,2,1,0:T(8,128)(2,1)S(1)}, u32[]{:S(2)}, u32[]{:S(2)}) async-start(bf16[4,8,16,512]{3,2,1,0:T(8,128)(2,1)} %bitcast.116), calls=%async_computation.1 | async-start | bytes 1048576 | tf_op jit(solution)/shard_map/all_to_all | solution.py:22
  60.9 1.7 reduce_sum.64
  63.3 14.8 %collective-permute-start = (bf16[16,4096]{1,0:T(8,128)(2,1)}, bf16[16,4096]{1,0:T(8,128)(2,1)}, u32[]{:S(2)}, u32[]{:S(2)}) collective-permute-start(bf16[16,4096]{1,0:T(8,128)(2,1)} %slice_bitcast_fusion.1), channel_id=1, source_target_pairs={{0,256},{64,320},{128,384},{192,448},{256,0},{320,64},{384,128},{4... | collective-permute-start | bytes 393224 | tf_op jit(solution)/shard_map/ppermute | solution.py:17
  79.5 1.4 collective-permute-done
  81.0 0.9 fusion.30
  81.9 10.4 %all_gather.3 = bf16[64,4096]{1,0:T(8,128)(2,1)S(1)} all-gather(bf16[16,4096]{1,0:T(8,128)(2,1)S(1)} %fusion.30), channel_id=1, replica_groups={{0,64,128,192},{256,320,384,448},{1,65,129,193},{257,321,385,449},{2,66..., dimensions={0}, use_global_device_ids=true | all-gather | bytes 655360 | tf_op jit(solution)/shard_map/all_gather | solution.py:89
  94.1 17.5 %all-to-all-start.2 = ((bf16[8,80,512]{2,1,0:T(8,128)(2,1)}), bf16[8,80,512]{2,1,0:T(8,128)(2,1)}, u32[]{:S(2)}, u32[]{:S(2)}) async-start(bf16[8,80,512]{2,1,0:T(8,128)(2,1)} %pad_maximum_fusion.1), calls=%async_computation.2 | async-start | bytes 1310720 | tf_op jit(solution)/shard_map/all_to_all | solution.py:99
  112.0 4.2 %fusion.24 = f32[64,32,8]{1,2,0:T(8,128)S(1)} fusion(f32[64,32,128]{2,1,0:T(8,128)S(1)} %bitcast.122, f32[128,8]{0,1:T(8,128)S(1)} %copy-done), kind=kOutput, calls=%fused_computation.70 | convolution fusion | flops 25165824 | bytes 1118208 | tf_op jit(solution)/shard_map/jnc,cp->jnp/dot_general | solution.py:118
  116.9 8.8 %collective-permute-start.8 = (bf16[2,16,4096]{2,1,0:T(8,128)(2,1)}, bf16[2,16,4096]{2,1,0:T(8,128)(2,1)}, u32[]{:S(2)}, u32[]{:S(2)}) collective-permute-start(bf16[2,16,4096]{2,1,0:T(8,128)(2,1)} %slice.102), channel_id=1, source_target_pairs={{0,256},{64,320},{128,384},{192,448},{256,0},{320,64},{384,128},{4... | collective-permute-start | bytes 786440 | tf_op jit(solution)/shard_map/ppermute | solution.py:17
  125.7 4.2 %fusion.26 = f32[64,32,8]{1,2,0:T(8,128)S(1)} fusion(f32[64,32,128]{2,1,0:T(8,128)S(1)} %bitcast.121, f32[128,8]{0,1:T(8,128)S(1)} %copy-done), kind=kOutput, calls=%fused_computation.72 | convolution fusion | flops 25165824 | bytes 1118208 | tf_op jit(solution)/shard_map/jnc,cp->jnp/dot_general | solution.py:118
  130.6 1.6 copy.60
  133.1 1.3 multiply_multiply_fusion
  134.4 0.9 copy.69
  136.2 1.0 fusion.33
  137.2 11.9 %all-to-all-done.2 = bf16[8,80,512]{2,1,0:T(8,128)(2,1)} async-done(((bf16[8,80,512]{2,1,0:T(8,128)(2,1)}), bf16[8,80,512]{2,1,0:T(8,128)(2,1)}, u32[]{:S(2)}, u32[]{:S(2)}) %all-to-all-start.2) | async-done | bytes 655392 | tf_op jit(solution)/shard_map/all_to_all | solution.py:99
  149.2 0.9 slice_bitcast_fusion
  150.1 8.4 %collective-permute-start.7 = (bf16[16,4096]{1,0:T(8,128)(2,1)S(1)}, bf16[16,4096]{1,0:T(8,128)(2,1)S(1)}, u32[]{:S(2)}, u32[]{:S(2)}) collective-permute-start(bf16[16,4096]{1,0:T(8,128)(2,1)S(1)} %bitcast.150), channel_id=1, source_target_pairs={{0,256},{64,320},{128,384},{192,448},{256,0},{320,64},{384,128},{4... | collective-permute-start | bytes 393224 | tf_op jit(solution)/shard_map/ppermute | solution.py:17
  158.5 1.1 convolution_convert_fusion.2
  160.0 10.7 %collective-permute-done.7 = bf16[16,4096]{1,0:T(8,128)(2,1)S(1)} collective-permute-done((bf16[16,4096]{1,0:T(8,128)(2,1)S(1)}, bf16[16,4096]{1,0:T(8,128)(2,1)S(1)}, u32[]{:S(2)}, u32[]{:S(2)}) %collective-permute-start.7) | collective-permute-done | bytes 131104 | tf_op jit(solution)/shard_map/ppermute | solution.py:17
  171.0 1.2 broadcast_in_dim.71
  172.2 3.5 %all-to-all-start.4 = ((bf16[4,34,4096]{2,1,0:T(8,128)(2,1)}), bf16[4,34,4096]{2,1,0:T(8,128)(2,1)S(1)}, u32[]{:S(2)}, u32[]{:S(2)}) async-start(bf16[4,34,4096]{2,1,0:T(8,128)(2,1)} %broadcast_in_dim.71), calls=%async_computation.4 | async-start | bytes 2621440 | tf_op jit(solution)/shard_map/all_to_all | solution.py:22
  175.7 2.8 %fusion.2 = (f32[512]{0:T(512)S(1)}, f32[512,512]{0,1:T(8,128)}) fusion(bf16[512,512]{0,1:T(8,128)(2,1)} %collective-permute-done.4, bf16[8,80,512]{2,1,0:T(8,128)(2,1)} %all-to-all-done.2, bf16[8,72,512]{2,1,0:T(8,128)(2,1)} %bitcast.129), kind=kOutput, calls=%fused_computation.13 | convolution fusion | flops 269221376 | bytes 2623488 | tf_op jit(solution)/shard_map/dot_general | solution.py:105
  178.6 1.1 slice.97
  179.7 1.5 convolution_convert_fusion
  182.1 5.1 %all-to-all-done.4 = bf16[4,34,4096]{2,1,0:T(8,128)(2,1)S(1)} async-done(((bf16[4,34,4096]{2,1,0:T(8,128)(2,1)}), bf16[4,34,4096]{2,1,0:T(8,128)(2,1)S(1)}, u32[]{:S(2)}, u32[]{:S(2)}) %all-to-all-start.4) | async-done | bytes 1114144 | tf_op jit(solution)/shard_map/all_to_all | solution.py:22
  187.1 28.8 %all-to-all-start.3 = ((bf16[8,72,512]{2,1,0:T(8,128)(2,1)}), bf16[8,72,512]{2,1,0:T(8,128)(2,1)}, u32[]{:S(2)}, u32[]{:S(2)}) async-start(bf16[8,72,512]{2,1,0:T(8,128)(2,1)} %pad_maximum_fusion.2), calls=%async_computation.3 | async-start | bytes 1179648 | tf_op jit(solution)/shard_map/all_to_all | solution.py:109
  215.9 3.9 %fusion.22 = f32[64,32,8]{1,2,0:T(8,128)} fusion(bf16[64,32,128]{2,1,0:T(8,128)(2,1)} %bitcast.132, f32[128,8]{0,1:T(8,128)S(1)} %copy-done), kind=kOutput, calls=%fused_computation.68 | convolution fusion | flops 25165824 | bytes 593920 | tf_op jit(solution)/shard_map/jnc,cp->jnp/dot_general | solution.py:118
  219.8 1.1 copy.61
  221.8 1.5 convert_select_fusion
  223.4 15.0 %all-to-all-done.3 = bf16[8,72,512]{2,1,0:T(8,128)(2,1)} async-done(((bf16[8,72,512]{2,1,0:T(8,128)(2,1)}), bf16[8,72,512]{2,1,0:T(8,128)(2,1)}, u32[]{:S(2)}, u32[]{:S(2)}) %all-to-all-start.3) | async-done | bytes 589856 | tf_op jit(solution)/shard_map/all_to_all | solution.py:109
  238.4 1.2 convert_reduce_fusion
  239.6 1.6 fusion.6
  241.2 10.1 %collective-permute-start.6 = (bf16[512,512]{0,1:T(8,128)(2,1)S(1)}, bf16[512,512]{0,1:T(8,128)(2,1)S(1)}, u32[]{:S(2)}, u32[]{:S(2)}) collective-permute-start(bf16[512,512]{0,1:T(8,128)(2,1)S(1)} %fusion.6), channel_id=1, source_target_pairs={{8,0},{16,8},{24,16},{32,24},{40,32},{48,40},{56,48},{0,56},{9,1},... | collective-permute-start | bytes 1572872 | tf_op jit(solution)/shard_map/ppermute | solution.py:13
  252.9 6.5 %collective-permute-done.6 = bf16[512,512]{0,1:T(8,128)(2,1)S(1)} collective-permute-done((bf16[512,512]{0,1:T(8,128)(2,1)S(1)}, bf16[512,512]{0,1:T(8,128)(2,1)S(1)}, u32[]{:S(2)}, u32[]{:S(2)}) %collective-permute-start.6) | collective-permute-done | bytes 524320 | tf_op jit(solution)/shard_map/ppermute | solution.py:13
  259.4 1.0 copy.62
  (87 shorter events, 17.7 us)
Async XLA Ops:
  0.6 111.3 %copy-start = (f32[128,8]{0,1:T(8,128)S(1)}, f32[128,8]{0,1:T(8,128)}, u32[]{:S(2)}) copy-start(f32[128,8]{0,1:T(8,128)} %param.13) | copy-start | bytes 12292
  0.6 1.6 copy-start.6
  0.7 14.8 %copy-start.1 = (f32[1,1,64,4096]{3,2,1,0:T(8,128)S(1)}, f32[1,1,64,4096]{3,2,1,0:T(8,128)}, u32[]{:S(2)}) copy-start(f32[1,1,64,4096]{3,2,1,0:T(8,128)} %param.11) | copy-start | bytes 3145732
  2.0 13.5 %copy-start.2 = (f32[1,1,64,4096]{3,2,1,0:T(8,128)S(1)}, f32[1,1,64,4096]{3,2,1,0:T(8,128)}, u32[]{:S(2)}) copy-start(f32[1,1,64,4096]{3,2,1,0:T(8,128)} %param.12) | copy-start | bytes 3145732
  2.2 13.4 %collective-permute-start.1 = (bf16[1,72,512]{2,1,0:T(8,128)(2,1)S(1)}, bf16[1,72,512]{2,1,0:T(8,128)(2,1)S(1)}, u32[]{:S(2)}, u32[]{:S(2)}) collective-permute-start(bf16[1,72,512]{2,1,0:T(8,128)(2,1)S(1)} %maximum_bitcast_fusion), channel_id=1, source_target_pairs={{0,4},{1,5},{2,6},{3,7},{4,0},{5,1},{6,2},{7,3},{8,12},{9,13},{10,... | collective-permute-start | bytes 221192 | tf_op jit(solution)/shard_map/ppermute | solution.py:17
  15.6 5.7 %copy-start.4 = (bf16[1,1,64,4096]{3,2,1,0:T(8,128)(2,1)S(1)}, bf16[1,1,64,4096]{3,2,1,0:T(8,128)(2,1)}, u32[]{:S(2)}) copy-start(bf16[1,1,64,4096]{3,2,1,0:T(8,128)(2,1)} %param.10) | copy-start | bytes 1572868
  15.7 8.1 %collective-permute-start.2 = (bf16[2,72,512]{2,1,0:T(8,128)(2,1)S(1)}, bf16[2,72,512]{2,1,0:T(8,128)(2,1)S(1)}, u32[]{:S(2)}, u32[]{:S(2)}) collective-permute-start(bf16[2,72,512]{2,1,0:T(8,128)(2,1)S(1)} %pad_maximum_fusion.5), channel_id=1, source_target_pairs={{0,2},{1,3},{2,0},{3,1},{4,6},{5,7},{6,4},{7,5},{8,10},{9,11},{10,... | collective-permute-start | bytes 442376 | tf_op jit(solution)/shard_map/ppermute | solution.py:17
  24.5 14.9 %collective-permute-start.3 = (bf16[4,72,512]{2,1,0:T(8,128)(2,1)}, bf16[4,72,512]{2,1,0:T(8,128)(2,1)}, u32[]{:S(2)}, u32[]{:S(2)}) collective-permute-start(bf16[4,72,512]{2,1,0:T(8,128)(2,1)} %pad_maximum_fusion.4), channel_id=1, source_target_pairs={{0,1},{1,0},{2,3},{3,2},{4,5},{5,4},{6,7},{7,6},{8,9},{9,8},{10,11... | collective-permute-start | bytes 884744 | tf_op jit(solution)/shard_map/ppermute | solution.py:17
  33.1 24.4 %all-to-all-start = ((bf16[4,3,16,4096]{3,2,1,0:T(8,128)(2,1)}), bf16[4,3,16,4096]{3,2,1,0:T(8,128)(2,1)}, u32[]{:S(2)}, u32[]{:S(2)}) async-start(bf16[4,3,16,4096]{3,2,1,0:T(8,128)(2,1)} %pad_maximum_fusion), calls=%async_computation | async-start | bytes 3145728 | tf_op jit(solution)/shard_map/all_to_all | solution.py:22
  37.4 8.6 %collective-permute-start.4 = (bf16[512,512]{0,1:T(8,128)(2,1)S(1)}, bf16[512,512]{0,1:T(8,128)(2,1)}, u32[]{:S(2)}, u32[]{:S(2)}) collective-permute-start(bf16[512,512]{0,1:T(8,128)(2,1)S(1)} %bitcast.131), channel_id=1, source_target_pairs={{56,0},{0,8},{8,16},{16,24},{24,32},{32,40},{40,48},{48,56},{57,1}... | collective-permute-start | bytes 1572872 | tf_op jit(solution)/shard_map/ppermute | solution.py:13
  43.4 4.1 %copy-start.3 = (bf16[4,2,1,72,512]{4,3,1,0,2:T(8,128)(2,1)}, bf16[4,2,1,72,512]{4,3,1,0,2:T(8,128)(2,1)S(1)}, u32[]{:S(2)}) copy-start(bf16[4,2,1,72,512]{4,3,1,0,2:T(8,128)(2,1)S(1)} %reverse_select_fusion) | copy-start | bytes 1769476
  43.4 2.5 collective-permute-start.5
  46.0 2.4 copy-start.10
  57.5 21.3 %all-to-all-start.1 = ((bf16[4,8,16,512]{3,2,1,0:T(8,128)(2,1)}), bf16[4,8,16,512]{3,2,1,0:T(8,128)(2,1)S(1)}, u32[]{:S(2)}, u32[]{:S(2)}) async-start(bf16[4,8,16,512]{3,2,1,0:T(8,128)(2,1)} %bitcast.116), calls=%async_computation.1 | async-start | bytes 1048576 | tf_op jit(solution)/shard_map/all_to_all | solution.py:22
  63.3 17.7 %collective-permute-start = (bf16[16,4096]{1,0:T(8,128)(2,1)}, bf16[16,4096]{1,0:T(8,128)(2,1)}, u32[]{:S(2)}, u32[]{:S(2)}) collective-permute-start(bf16[16,4096]{1,0:T(8,128)(2,1)} %slice_bitcast_fusion.1), channel_id=1, source_target_pairs={{0,256},{64,320},{128,384},{192,448},{256,0},{320,64},{384,128},{4... | collective-permute-start | bytes 393224 | tf_op jit(solution)/shard_map/ppermute | solution.py:17
  92.3 0.9 copy-start.5
  94.1 55.1 %all-to-all-start.2 = ((bf16[8,80,512]{2,1,0:T(8,128)(2,1)}), bf16[8,80,512]{2,1,0:T(8,128)(2,1)}, u32[]{:S(2)}, u32[]{:S(2)}) async-start(bf16[8,80,512]{2,1,0:T(8,128)(2,1)} %pad_maximum_fusion.1), calls=%async_computation.2 | async-start | bytes 1310720 | tf_op jit(solution)/shard_map/all_to_all | solution.py:99
  116.9 19.3 %collective-permute-start.8 = (bf16[2,16,4096]{2,1,0:T(8,128)(2,1)}, bf16[2,16,4096]{2,1,0:T(8,128)(2,1)}, u32[]{:S(2)}, u32[]{:S(2)}) collective-permute-start(bf16[2,16,4096]{2,1,0:T(8,128)(2,1)} %slice.102), channel_id=1, source_target_pairs={{0,256},{64,320},{128,384},{192,448},{256,0},{320,64},{384,128},{4... | collective-permute-start | bytes 786440 | tf_op jit(solution)/shard_map/ppermute | solution.py:17
  150.1 20.6 %collective-permute-start.7 = (bf16[16,4096]{1,0:T(8,128)(2,1)S(1)}, bf16[16,4096]{1,0:T(8,128)(2,1)S(1)}, u32[]{:S(2)}, u32[]{:S(2)}) collective-permute-start(bf16[16,4096]{1,0:T(8,128)(2,1)S(1)} %bitcast.150), channel_id=1, source_target_pairs={{0,256},{64,320},{128,384},{192,448},{256,0},{320,64},{384,128},{4... | collective-permute-start | bytes 393224 | tf_op jit(solution)/shard_map/ppermute | solution.py:17
  172.2 15.0 %all-to-all-start.4 = ((bf16[4,34,4096]{2,1,0:T(8,128)(2,1)}), bf16[4,34,4096]{2,1,0:T(8,128)(2,1)S(1)}, u32[]{:S(2)}, u32[]{:S(2)}) async-start(bf16[4,34,4096]{2,1,0:T(8,128)(2,1)} %broadcast_in_dim.71), calls=%async_computation.4 | async-start | bytes 2621440 | tf_op jit(solution)/shard_map/all_to_all | solution.py:22
  187.1 51.2 %all-to-all-start.3 = ((bf16[8,72,512]{2,1,0:T(8,128)(2,1)}), bf16[8,72,512]{2,1,0:T(8,128)(2,1)}, u32[]{:S(2)}, u32[]{:S(2)}) async-start(bf16[8,72,512]{2,1,0:T(8,128)(2,1)} %pad_maximum_fusion.2), calls=%async_computation.3 | async-start | bytes 1179648 | tf_op jit(solution)/shard_map/all_to_all | solution.py:109
  221.8 17.7 %copy-start.9 = (f32[512]{0:T(512)S(1)}, f32[512]{0:T(512)}, u32[]{:S(2)}) copy-start(f32[512]{0:T(512)} %multiply_multiply_fusion) | copy-start | bytes 6148
  239.6 12.0 %copy-start.7 = (f32[1,1,1,64,256]{4,3,2,1,0:T(8,128)S(1)}, f32[1,1,1,64,256]{4,3,2,1,0:T(8,128)}, u32[]{:S(2)}) copy-start(f32[1,1,1,64,256]{4,3,2,1,0:T(8,128)} %copy.60) | copy-start | bytes 196612
  239.6 12.0 %copy-start.8 = (f32[1,1,1,64,256]{4,3,2,1,0:T(8,128)S(1)}, f32[1,1,1,64,256]{4,3,2,1,0:T(8,128)}, u32[]{:S(2)}) copy-start(f32[1,1,1,64,256]{4,3,2,1,0:T(8,128)} %copy.59) | copy-start | bytes 196612
  241.2 18.2 %collective-permute-start.6 = (bf16[512,512]{0,1:T(8,128)(2,1)S(1)}, bf16[512,512]{0,1:T(8,128)(2,1)S(1)}, u32[]{:S(2)}, u32[]{:S(2)}) collective-permute-start(bf16[512,512]{0,1:T(8,128)(2,1)S(1)} %fusion.6), channel_id=1, source_target_pairs={{8,0},{16,8},{24,16},{32,24},{40,32},{48,40},{56,48},{0,56},{9,1},... | collective-permute-start | bytes 1572872 | tf_op jit(solution)/shard_map/ppermute | solution.py:13

commit v2 on v1

--- a/solution.py
+++ b/solution.py
@@ -27,18 +27,31 @@
     return high, (value - high.astype(WIDE)).astype(SHORT)
 
 
-def gather_tensor(block):
-    held = block[None]
-    for bit in (4, 2, 1):
-        held = jnp.concatenate([held, swap(held, "tensor", bit)], axis=0)
-    order = (0, 4, 2, 6, 1, 5, 3, 7)
-    held = jnp.stack([held[order.index(i)] for i in range(8)])
-    mine = lax.axis_index("tensor")
-    for bit in (4, 2, 1):
-        shape = (8 // (2 * bit), 2, bit) + block.shape
-        split = held.reshape(shape)
+def in_order(held, mine, bits):
+    for bit in bits:
+        split = held.reshape((held.shape[0] // (2 * bit), 2, bit) + held.shape[1:])
         held = jnp.where((mine & bit) != 0, split[:, ::-1], split).reshape(held.shape)
     return held
+
+
+def doubled(held, mine, axis):
+    bit = 4 >> axis
+    came = swap(held, "tensor", bit)
+    high = (mine & bit) != 0
+    return jnp.stack([jnp.where(high, came, held), jnp.where(high, held, came)], axis=axis)
+
+
+def gather_x(block):
+    held = jnp.stack([block] + [swap(block, "replica", bit) for bit in (1, 2, 3)])
+    return in_order(held, lax.axis_index("replica") & 3, (2, 1))
+
+
+def broadcast_x(block):
+    return exchange_x(jnp.broadcast_to(block[None], (PLANE,) + block.shape))
+
+
+def tied(value, *after):
+    return lax.optimization_barrier((value,) + after)[0]
 
 
 def adam(first, second, grad):
@@ -67,31 +80,45 @@
     is_failed = my_replica == failed
     part = rows // PLANE
 
+    def masked(block):
+        return jnp.where(chosen, block.astype(SHORT), 0).reshape(PLANE, 1, part, width)
+
+    def summed(parts):
+        return jnp.sum(parts.astype(WIDE), axis=0).astype(SHORT)
+
+    mask_weight = masked(own_weight)
+    spread_weight = summed(exchange_x(mask_weight))[0]
+    mask_moments = jnp.concatenate([masked(own_first), masked(own_second)], axis=1)
+
     local = activations[0, 0]
     tokens, cols = local.shape
-    incoming = from_behind(local, "section", 1)
     squares = jnp.sum(jnp.square(local.astype(WIDE)), axis=1)
     high, low = two_halves(squares)
     extra = jnp.concatenate([high[None], low[None], jnp.zeros((6, tokens), SHORT)], axis=0)
-    kg_rows = jnp.concatenate([key_grads[0, 0].T, extra], axis=0)
-    kg_rows = gather_tensor(kg_rows)
+    held = jnp.concatenate([key_grads[0, 0].T, extra], axis=0)
+    held = tied(held, mask_weight)
+    incoming = from_behind(tied(local, held), "section", 1)
+    held = doubled(doubled(held, my_tensor, 0), my_tensor, 1)
+    held, spread_weight = lax.optimization_barrier((held, spread_weight))
+    fresh_weight = spread_weight + swap(spread_weight, "replica", PLANE)
+    spread_moments = summed(exchange_x(tied(mask_moments, spread_weight)))
+    held = doubled(held, my_tensor, 2)
+    held, fresh_weight = lax.optimization_barrier((held, fresh_weight))
+    kg_rows = held.reshape((8,) + held.shape[3:])
     kg_all = kg_rows[:, :rows].reshape(8 * rows, tokens)
     total = jnp.sum(kg_rows[:, rows].astype(WIDE) + kg_rows[:, rows + 1].astype(WIDE), axis=0)
     total = from_behind(total.reshape(-1, 128), "section", 1).reshape(tokens)
     inverse_rms = 1.0 / jnp.sqrt(total / width + 1e-05)
 
-    masked = [jnp.where(chosen, a.astype(SHORT), 0).reshape(PLANE, 1, part, width) for a in (own_weight, own_first, own_second)]
-    spread = exchange_x(jnp.concatenate(masked, axis=1))
-    spread = jnp.sum(spread.astype(WIDE), axis=0).astype(SHORT)
-    fresh_weight = spread[0] + swap(spread[0], "replica", PLANE)
-    fresh_moments = spread[1:] + swap(spread[1:], "replica", PLANE)
-    groups = [[0, 1, 2, 3], [4, 5, 6, 7]]
-    fresh_weight = lax.all_gather(fresh_weight, "replica", axis=0, tiled=True, axis_index_groups=groups)
+    spread_moments = tied(spread_moments, fresh_weight)
+    fresh_moments = spread_moments + swap(spread_moments, "replica", PLANE)
+    fresh_weight = broadcast_x(tied(fresh_weight, spread_moments)).reshape(rows, width)
     restored_weight = jnp.where(is_failed, fresh_weight, own_weight)
 
     x = incoming.astype(WIDE)
     normed = (x * inverse_rms[:, None]).astype(SHORT)
     grad = lax.dot_general(kg_all, normed, (((1,), (0,)), ((), ())), preferred_element_type=WIDE).astype(SHORT)
+    grad = tied(grad, restored_weight, fresh_moments)
     grad = grad.reshape(8, PLANE, part, cols).transpose(1, 0, 2, 3)
     grad = jnp.sum(exchange_x(grad).astype(WIDE), axis=0).astype(SHORT)
 
@@ -122,7 +149,7 @@
     fresh_update = adam(fresh[0], fresh[1], mean_rows).astype(SHORT)
     fresh_sums = checksum(fresh.reshape(2 * part, width)).astype(SHORT).reshape(2, width)
     shared = jnp.concatenate([mean_rows.astype(SHORT), fresh_update, fresh_sums], axis=0)
-    shared = exchange_x(jnp.broadcast_to(shared[None], (PLANE,) + shared.shape))
+    shared = gather_x(shared)
     mean_grad = shared[:, :part].reshape(rows, width).astype(WIDE)
     fresh_update = shared[:, part : 2 * part].reshape(rows, width).astype(WIDE)
     fresh_sums = shared[:, 2 * part :].reshape(PLANE, 2, part, -1).transpose(1, 0, 2, 3).reshape(2, rows, -1).astype(WIDE)

time: 262 us -> 255 us (0.973)
  blocking collectives: 10.4 us -> 0 us
  other arithmetic: 16 us -> 26.1 us
  local copies, waits for them, and re-layouts: 22 us -> 16.3 us
  waiting for transfers between devices: 63.8 us -> 68.4 us
  starting transfers between devices: 126 us -> 122 us
    all_gather x1 -> x0, blocking collectives: 10.4 us -> none  [shards(): lax.all_gather(fresh_weight, 'replica', axis=0, tiled=True, axis_index_gr...]
    ppermute x6 -> x9, waiting for transfers between devices: 15.4 us -> 23.8 us  [swap(): lax.ppermute(block, axis, [(i, i ^ bit) for i in range(lax.axis_size(axis...]
    all_to_all x1, starting transfers between devices: 17.5 us -> 10.3 us  [shards(): got = lax.all_to_all(sent, 'tensor', 0, 0, tiled=True)]
    all_to_all x1, starting transfers between devices: 28.8 us -> 23.2 us  [shards(): lax.all_to_all(sent, 'tensor', 0, 0, tiled=True).astype(WIDE)]
    all_to_all x1, waiting for transfers between devices: 11.9 us -> 7.16 us  [shards(): got = lax.all_to_all(sent, 'tensor', 0, 0, tiled=True)]
    all_to_all x3 -> x4, starting transfers between devices: 11.3 us -> 16 us  [exchange_x(): lax.all_to_all(block, 'replica', 0, 0, axis_index_groups=groups, tiled=True)]
    all_to_all x1, waiting for transfers between devices: 15 us -> 19 us  [shards(): lax.all_to_all(sent, 'tensor', 0, 0, tiled=True).astype(WIDE)]
    another operation x0 -> x9, other arithmetic: none -> 3.54 us  [the longest x6 2.08 us: doubled(): jnp.stack([jnp.where(high, came, held), jnp.where(high, held, came)], axi...]
  transfers between devices with their start and end apart: 14 -> 18, of which waited for: 10 -> 9; matrix products, arithmetic and copies ran while one was open for 18% -> 17% of each run, Pallas kernels for 0% -> 0%
where the time goes in v2:
time: 255 us; the launch traced here: 254 us
  starting transfers between devices  122 us (48%)
  waiting for transfers between devices  68.4 us (27%)
  other arithmetic  26.1 us (10%)
  matrix products  18.3 us (7%)
  local copies, waits for them, and re-layouts  16.3 us (6%)
  between operations  3.19 us (1%)
    ppermute x9, starting transfers between devices, swap(): lax.ppermute(block, axis, [(i, i ^ bit) for i in range(lax.axis_size(axis...  55.8 us
    ppermute x9, waiting for transfers between devices, swap(): lax.ppermute(block, axis, [(i, i ^ bit) for i in range(lax.axis_size(axis...  23.8 us
    all_to_all x1, starting transfers between devices, shards(): lax.all_to_all(sent, 'tensor', 0, 0, tiled=True).astype(WIDE)  23.2 us
    all_to_all x1, waiting for transfers between devices, shards(): lax.all_to_all(sent, 'tensor', 0, 0, tiled=True).astype(WIDE)  19 us
    ppermute x3, starting transfers between devices, from_behind(): lax.ppermute(block, axis, [((i - distance) % n, i) for i in range(n)])  16.3 us
    all_to_all x4, starting transfers between devices, exchange_x(): lax.all_to_all(block, 'replica', 0, 0, axis_index_groups=groups, tiled=True)  16 us
    all_to_all x4, waiting for transfers between devices, exchange_x(): lax.all_to_all(block, 'replica', 0, 0, axis_index_groups=groups, tiled=True)  12 us
    dot_general x4, matrix products, checksum(): jnp.einsum('jnc,cp->jnp', shaped, probe_matrix, precision=lax.Precision.H...  11.6 us
  transfers between devices with their start and end apart: 18, of which 9 were waited for; matrix products, arithmetic and copies ran while one was open for 17% of the time, Pallas kernels for 0%

profile of v2, /device:TPU:1, one launch (start us, length us, event | category | flops | bytes accessed | tf_op | source)
XLA Modules:
  0.0 254.0 jit_solution(562311196835675456)
XLA Ops:
  0.7 1.3 copy.58
  2.2 1.4 dynamic_slice.6
  6.8 1.2 broadcast_select_fusion.1
  8.0 9.6 %collective-permute-start = (bf16[72,512]{1,0:T(8,128)(2,1)S(1)}, bf16[72,512]{1,0:T(8,128)(2,1)S(1)}, u32[]{:S(2)}, u32[]{:S(2)}) collective-permute-start(bf16[72,512]{1,0:T(8,128)(2,1)S(1)} %pad_maximum_fusion.8), channel_id=1, source_target_pairs={{0,4},{1,5},{2,6},{3,7},{4,0},{5,1},{6,2},{7,3},{8,12},{9,13},{10,... | collective-permute-start | bytes 221192 | tf_op jit(solution)/shard_map/ppermute | solution.py:17
  17.7 1.7 collective-permute-done
  19.4 7.4 %collective-permute-start.1 = (bf16[2,72,512]{2,1,0:T(8,128)(2,1)S(1)}, bf16[2,72,512]{2,1,0:T(8,128)(2,1)}, u32[]{:S(2)}, u32[]{:S(2)}) collective-permute-start(bf16[2,72,512]{2,1,0:T(8,128)(2,1)S(1)} %pad_maximum_fusion.7), channel_id=1, source_target_pairs={{0,2},{1,3},{2,0},{3,1},{4,6},{5,7},{6,4},{7,5},{8,10},{9,11},{10,... | collective-permute-start | bytes 442376 | tf_op jit(solution)/shard_map/ppermute | solution.py:17
  26.9 4.2 %all-to-all-start = ((bf16[4,1,16,4096]{3,2,1,0:T(8,128)(2,1)}), bf16[4,1,16,4096]{3,2,1,0:T(8,128)(2,1)}, u32[]{:S(2)}, u32[]{:S(2)}) async-start(bf16[4,1,16,4096]{3,2,1,0:T(8,128)(2,1)} %get-tuple-element.66), calls=%async_computation | async-start | bytes 1048576 | tf_op jit(solution)/shard_map/all_to_all | solution.py:22
  32.1 6.9 %all-to-all-done = bf16[4,1,16,4096]{3,2,1,0:T(8,128)(2,1)} async-done(((bf16[4,1,16,4096]{3,2,1,0:T(8,128)(2,1)}), bf16[4,1,16,4096]{3,2,1,0:T(8,128)(2,1)}, u32[]{:S(2)}, u32[]{:S(2)}) %all-to-all-start) | async-done | bytes 524320 | tf_op jit(solution)/shard_map/all_to_all | solution.py:22
  39.0 1.8 reduce_sum.78
  40.8 13.8 %collective-permute-start.3 = (bf16[16,4096]{1,0:T(8,128)(2,1)}, bf16[16,4096]{1,0:T(8,128)(2,1)}, u32[]{:S(2)}, u32[]{:S(2)}) collective-permute-start(bf16[16,4096]{1,0:T(8,128)(2,1)} %reduce_sum.78), channel_id=1, source_target_pairs={{0,256},{64,320},{128,384},{192,448},{256,0},{320,64},{384,128},{4... | collective-permute-start | bytes 393224 | tf_op jit(solution)/shard_map/ppermute | solution.py:17
  54.6 1.9 collective-permute-start.2
  56.5 2.3 pad_maximum_fusion.1
  58.8 4.2 %all-to-all-start.1 = ((bf16[4,2,16,4096]{3,2,1,0:T(8,128)(2,1)}), bf16[4,2,16,4096]{3,2,1,0:T(8,128)(2,1)}, u32[]{:S(2)}, u32[]{:S(2)}) async-start(bf16[4,2,16,4096]{3,2,1,0:T(8,128)(2,1)} %pad_maximum_fusion.1), calls=%async_computation.1 | async-start | bytes 2097152 | tf_op jit(solution)/shard_map/all_to_all | solution.py:22
  63.1 3.8 %collective-permute-start.4 = (bf16[512,512]{0,1:T(8,128)(2,1)S(1)}, bf16[512,512]{0,1:T(8,128)(2,1)}, u32[]{:S(2)}, u32[]{:S(2)}) collective-permute-start(bf16[512,512]{0,1:T(8,128)(2,1)S(1)} %bitcast.153), channel_id=1, source_target_pairs={{56,0},{0,8},{8,16},{16,24},{24,32},{32,40},{40,48},{48,56},{57,1}... | collective-permute-start | bytes 1572872 | tf_op jit(solution)/shard_map/ppermute | solution.py:13
  66.9 1.7 add.73
  68.6 4.0 %collective-permute-done.2 = bf16[2,2,72,512]{3,2,0,1:T(8,128)(2,1)} collective-permute-done((bf16[2,2,72,512]{3,2,0,1:T(8,128)(2,1)S(1)}, bf16[2,2,72,512]{3,2,0,1:T(8,128)(2,1)}, u32[]{:S(2)}, u32[]{:S(2)}) %collective-permute-start.2) | collective-permute-done | bytes 294944 | tf_op jit(solution)/shard_map/ppermute | solution.py:17
  73.8 2.3 collective-permute-start.5
  77.5 1.5 reduce_sum.79
  79.0 6.3 %collective-permute-start.6 = (bf16[2,16,4096]{2,1,0:T(8,128)(2,1)S(1)}, bf16[2,16,4096]{2,1,0:T(8,128)(2,1)}, u32[]{:S(2)}, u32[]{:S(2)}) collective-permute-start(bf16[2,16,4096]{2,1,0:T(8,128)(2,1)S(1)} %reduce_sum.79), channel_id=1, source_target_pairs={{0,256},{64,320},{128,384},{192,448},{256,0},{320,64},{384,128},{4... | collective-permute-start | bytes 786440 | tf_op jit(solution)/shard_map/ppermute | solution.py:17
  85.3 2.5 convolution_convert_fusion.1
  88.7 3.5 %all-to-all-start.2 = ((bf16[4,16,4096]{2,1,0:T(8,128)(2,1)}), bf16[4,16,4096]{2,1,0:T(8,128)(2,1)S(1)}, u32[]{:S(2)}, u32[]{:S(2)}) async-start(bf16[4,16,4096]{2,1,0:T(8,128)(2,1)} %broadcast_in_dim.64), calls=%async_computation.2 | async-start | bytes 1048576 | tf_op jit(solution)/shard_map/all_to_all | solution.py:22
  92.2 16.5 %collective-permute-done.6 = bf16[2,16,4096]{2,1,0:T(8,128)(2,1)} collective-permute-done((bf16[2,16,4096]{2,1,0:T(8,128)(2,1)S(1)}, bf16[2,16,4096]{2,1,0:T(8,128)(2,1)}, u32[]{:S(2)}, u32[]{:S(2)}) %collective-permute-start.6) | collective-permute-done | bytes 262176 | tf_op jit(solution)/shard_map/ppermute | solution.py:17
  108.7 1.9 fusion.35
  111.4 4.1 %all-to-all-start.3 = ((bf16[4,8,16,512]{3,2,1,0:T(8,128)(2,1)}), bf16[4,8,16,512]{3,2,1,0:T(8,128)(2,1)}, u32[]{:S(2)}, u32[]{:S(2)}) async-start(bf16[4,8,16,512]{3,2,1,0:T(8,128)(2,1)} %bitcast.154), calls=%async_computation.3 | async-start | bytes 1048576 | tf_op jit(solution)/shard_map/all_to_all | solution.py:22
  116.5 1.4 fusion.8
  117.9 5.1 %all-to-all-done.3 = bf16[4,8,16,512]{3,2,1,0:T(8,128)(2,1)} async-done(((bf16[4,8,16,512]{3,2,1,0:T(8,128)(2,1)}), bf16[4,8,16,512]{3,2,1,0:T(8,128)(2,1)}, u32[]{:S(2)}, u32[]{:S(2)}) %all-to-all-start.3) | async-done | bytes 524320 | tf_op jit(solution)/shard_map/all_to_all | solution.py:22
  123.0 1.1 reduce_sum.81
  124.1 1.9 pad_maximum_fusion.2
  126.1 10.3 %all-to-all-start.4 = ((bf16[8,80,512]{2,1,0:T(8,128)(2,1)}), bf16[8,80,512]{2,1,0:T(8,128)(2,1)}, u32[]{:S(2)}, u32[]{:S(2)}) async-start(bf16[8,80,512]{2,1,0:T(8,128)(2,1)} %pad_maximum_fusion.2), calls=%async_computation.4 | async-start | bytes 1310720 | tf_op jit(solution)/shard_map/all_to_all | solution.py:126
  137.5 4.2 %fusion.26 = f32[64,32,8]{1,2,0:T(8,128)S(1)} fusion(f32[64,32,128]{2,1,0:T(8,128)S(1)} %bitcast.145, f32[128,8]{0,1:T(8,128)S(1)} %copy-done), kind=kOutput, calls=%fused_computation.70 | convolution fusion | flops 25165824 | bytes 1118208 | tf_op jit(solution)/shard_map/jnc,cp->jnp/dot_general | solution.py:145
  142.7 4.2 %fusion.28 = f32[64,32,8]{1,2,0:T(8,128)S(1)} fusion(f32[64,32,128]{2,1,0:T(8,128)S(1)} %bitcast.146, f32[128,8]{0,1:T(8,128)S(1)} %copy-done), kind=kOutput, calls=%fused_computation.72 | convolution fusion | flops 25165824 | bytes 1118208 | tf_op jit(solution)/shard_map/jnc,cp->jnp/dot_general | solution.py:145
  150.3 2.1 fusion.24
  153.4 7.2 %all-to-all-done.4 = bf16[8,80,512]{2,1,0:T(8,128)(2,1)} async-done(((bf16[8,80,512]{2,1,0:T(8,128)(2,1)}), bf16[8,80,512]{2,1,0:T(8,128)(2,1)}, u32[]{:S(2)}, u32[]{:S(2)}) %all-to-all-start.4) | async-done | bytes 655392 | tf_op jit(solution)/shard_map/all_to_all | solution.py:126
  161.5 7.7 %collective-permute-start.8 = (bf16[16,4096]{1,0:T(8,128)(2,1)S(1)}, bf16[16,4096]{1,0:T(8,128)(2,1)S(1)}, u32[]{:S(2)}, u32[]{:S(2)}) collective-permute-start(bf16[16,4096]{1,0:T(8,128)(2,1)S(1)} %bitcast.171), channel_id=1, source_target_pairs={{0,256},{64,320},{128,384},{192,448},{256,0},{320,64},{384,128},{4... | collective-permute-start | bytes 393224 | tf_op jit(solution)/shard_map/ppermute | solution.py:17
  170.3 1.5 convolution_convert_fusion
  171.8 2.7 %fusion.3 = (f32[512]{0:T(512)S(1)}, f32[512,512]{0,1:T(8,128)}) fusion(bf16[512,512]{0,1:T(8,128)(2,1)} %collective-permute-done.4, bf16[8,80,512]{2,1,0:T(8,128)(2,1)} %all-to-all-done.4, bf16[8,72,512]{2,1,0:T(8,128)(2,1)S(1)} %bitcast.151), kind=kOutput, calls=%fused_computation.16 | convolution fusion | flops 269221376 | bytes 2623488 | tf_op jit(solution)/shard_map/dot_general | solution.py:132
  174.5 1.5 collective-permute-done.8
  176.3 2.3 collective-permute-start.10
  178.6 3.0 %collective-permute-start.9 = (bf16[34,4096]{1,0:T(8,128)(2,1)S(1)}, bf16[34,4096]{1,0:T(8,128)(2,1)S(1)}, u32[]{:S(2)}, u32[]{:S(2)}) collective-permute-start(bf16[34,4096]{1,0:T(8,128)(2,1)S(1)} %get-tuple-element.59), channel_id=1, source_target_pairs={{0,64},{64,0},{128,192},{192,128},{256,320},{320,256},{384,448},{4... | collective-permute-start | bytes 835592 | tf_op jit(solution)/shard_map/ppermute | solution.py:17
  181.6 3.7 %collective-permute-start.11 = (bf16[34,4096]{1,0:T(8,128)(2,1)S(1)}, bf16[34,4096]{1,0:T(8,128)(2,1)}, u32[]{:S(2)}, u32[]{:S(2)}) collective-permute-start(bf16[34,4096]{1,0:T(8,128)(2,1)S(1)} %get-tuple-element.59), channel_id=1, source_target_pairs={{0,192},{64,128},{128,64},{192,0},{256,448},{320,384},{384,320},{4... | collective-permute-start | bytes 835592 | tf_op jit(solution)/shard_map/ppermute | solution.py:17
  186.3 23.2 %all-to-all-start.5 = ((bf16[8,72,512]{2,1,0:T(8,128)(2,1)}), bf16[8,72,512]{2,1,0:T(8,128)(2,1)}, u32[]{:S(2)}, u32[]{:S(2)}) async-start(bf16[8,72,512]{2,1,0:T(8,128)(2,1)} %pad_maximum_fusion.4), calls=%async_computation.5 | async-start | bytes 1179648 | tf_op jit(solution)/shard_map/all_to_all | solution.py:136
  209.5 1.2 pad_maximum_fusion
  211.4 1.5 convert_select_fusion
  212.9 19.0 %all-to-all-done.5 = bf16[8,72,512]{2,1,0:T(8,128)(2,1)} async-done(((bf16[8,72,512]{2,1,0:T(8,128)(2,1)}), bf16[8,72,512]{2,1,0:T(8,128)(2,1)}, u32[]{:S(2)}, u32[]{:S(2)}) %all-to-all-start.5) | async-done | bytes 589856 | tf_op jit(solution)/shard_map/all_to_all | solution.py:136
  231.9 1.2 convert_reduce_fusion
  233.1 1.6 fusion.7
  234.8 10.1 %collective-permute-start.7 = (bf16[512,512]{0,1:T(8,128)(2,1)S(1)}, bf16[512,512]{0,1:T(8,128)(2,1)S(1)}, u32[]{:S(2)}, u32[]{:S(2)}) collective-permute-start(bf16[512,512]{0,1:T(8,128)(2,1)S(1)} %fusion.7), channel_id=1, source_target_pairs={{8,0},{16,8},{24,16},{32,24},{40,32},{48,40},{56,48},{0,56},{9,1},... | collective-permute-start | bytes 1572872 | tf_op jit(solution)/shard_map/ppermute | solution.py:13
  246.4 6.5 %collective-permute-done.7 = bf16[512,512]{0,1:T(8,128)(2,1)S(1)} collective-permute-done((bf16[512,512]{0,1:T(8,128)(2,1)S(1)}, bf16[512,512]{0,1:T(8,128)(2,1)S(1)}, u32[]{:S(2)}, u32[]{:S(2)}) %collective-permute-start.7) | collective-permute-done | bytes 524320 | tf_op jit(solution)/shard_map/ppermute | solution.py:13
  (101 shorter events, 20.6 us)
Async XLA Ops:
  0.6 136.8 %copy-start = (f32[128,8]{0,1:T(8,128)S(1)}, f32[128,8]{0,1:T(8,128)}, u32[]{:S(2)}) copy-start(f32[128,8]{0,1:T(8,128)} %param.13) | copy-start | bytes 12292
  0.6 5.1 %copy-start.1 = (f32[1,1,64,4096]{3,2,1,0:T(8,128)S(1)}, f32[1,1,64,4096]{3,2,1,0:T(8,128)}, u32[]{:S(2)}) copy-start(f32[1,1,64,4096]{3,2,1,0:T(8,128)} %param.11) | copy-start | bytes 3145732
  2.0 3.8 %copy-start.2 = (f32[1,1,64,4096]{3,2,1,0:T(8,128)S(1)}, f32[1,1,64,4096]{3,2,1,0:T(8,128)}, u32[]{:S(2)}) copy-start(f32[1,1,64,4096]{3,2,1,0:T(8,128)} %param.12) | copy-start | bytes 3145732
  5.8 0.8 copy-start.13
  5.8 1.1 copy-start.3
  8.0 11.4 %collective-permute-start = (bf16[72,512]{1,0:T(8,128)(2,1)S(1)}, bf16[72,512]{1,0:T(8,128)(2,1)S(1)}, u32[]{:S(2)}, u32[]{:S(2)}) collective-permute-start(bf16[72,512]{1,0:T(8,128)(2,1)S(1)} %pad_maximum_fusion.8), channel_id=1, source_target_pairs={{0,4},{1,5},{2,6},{3,7},{4,0},{5,1},{6,2},{7,3},{8,12},{9,13},{10,... | collective-permute-start | bytes 221192 | tf_op jit(solution)/shard_map/ppermute | solution.py:17
  19.4 11.6 %collective-permute-start.1 = (bf16[2,72,512]{2,1,0:T(8,128)(2,1)S(1)}, bf16[2,72,512]{2,1,0:T(8,128)(2,1)}, u32[]{:S(2)}, u32[]{:S(2)}) collective-permute-start(bf16[2,72,512]{2,1,0:T(8,128)(2,1)S(1)} %pad_maximum_fusion.7), channel_id=1, source_target_pairs={{0,2},{1,3},{2,0},{3,1},{4,6},{5,7},{6,4},{7,5},{8,10},{9,11},{10,... | collective-permute-start | bytes 442376 | tf_op jit(solution)/shard_map/ppermute | solution.py:17
  26.9 12.1 %all-to-all-start = ((bf16[4,1,16,4096]{3,2,1,0:T(8,128)(2,1)}), bf16[4,1,16,4096]{3,2,1,0:T(8,128)(2,1)}, u32[]{:S(2)}, u32[]{:S(2)}) async-start(bf16[4,1,16,4096]{3,2,1,0:T(8,128)(2,1)} %get-tuple-element.66), calls=%async_computation | async-start | bytes 1048576 | tf_op jit(solution)/shard_map/all_to_all | solution.py:22
  40.8 26.1 %collective-permute-start.3 = (bf16[16,4096]{1,0:T(8,128)(2,1)}, bf16[16,4096]{1,0:T(8,128)(2,1)}, u32[]{:S(2)}, u32[]{:S(2)}) collective-permute-start(bf16[16,4096]{1,0:T(8,128)(2,1)} %reduce_sum.78), channel_id=1, source_target_pairs={{0,256},{64,320},{128,384},{192,448},{256,0},{320,64},{384,128},{4... | collective-permute-start | bytes 393224 | tf_op jit(solution)/shard_map/ppermute | solution.py:17
  54.6 18.0 %collective-permute-start.2 = (bf16[2,2,72,512]{3,2,0,1:T(8,128)(2,1)S(1)}, bf16[2,2,72,512]{3,2,0,1:T(8,128)(2,1)}, u32[]{:S(2)}, u32[]{:S(2)}) collective-permute-start(bf16[2,2,72,512]{3,2,0,1:T(8,128)(2,1)S(1)} %pad_maximum_fusion.6), channel_id=1, source_target_pairs={{0,1},{1,0},{2,3},{3,2},{4,5},{5,4},{6,7},{7,6},{8,9},{9,8},{10,11... | collective-permute-start | bytes 884744 | tf_op jit(solution)/shard_map/ppermute | solution.py:17
  58.8 18.7 %all-to-all-start.1 = ((bf16[4,2,16,4096]{3,2,1,0:T(8,128)(2,1)}), bf16[4,2,16,4096]{3,2,1,0:T(8,128)(2,1)}, u32[]{:S(2)}, u32[]{:S(2)}) async-start(bf16[4,2,16,4096]{3,2,1,0:T(8,128)(2,1)} %pad_maximum_fusion.1), calls=%async_computation.1 | async-start | bytes 2097152 | tf_op jit(solution)/shard_map/all_to_all | solution.py:22
  63.1 22.3 %collective-permute-start.4 = (bf16[512,512]{0,1:T(8,128)(2,1)S(1)}, bf16[512,512]{0,1:T(8,128)(2,1)}, u32[]{:S(2)}, u32[]{:S(2)}) collective-permute-start(bf16[512,512]{0,1:T(8,128)(2,1)S(1)} %bitcast.153), channel_id=1, source_target_pairs={{56,0},{0,8},{8,16},{16,24},{24,32},{32,40},{40,48},{48,56},{57,1}... | collective-permute-start | bytes 1572872 | tf_op jit(solution)/shard_map/ppermute | solution.py:13
  73.7 2.4 copy-start.4
  73.8 3.2 %collective-permute-start.5 = (f32[4,128]{1,0:T(4,128)S(1)}, f32[4,128]{1,0:T(4,128)S(1)}, u32[]{:S(2)}, u32[]{:S(2)}) collective-permute-start(f32[4,128]{1,0:T(4,128)S(1)} %bitcast.181), channel_id=1, source_target_pairs={{56,0},{0,8},{8,16},{16,24},{24,32},{32,40},{40,48},{48,56},{57,1}... | collective-permute-start | bytes 6152 | tf_op jit(solution)/shard_map/ppermute | solution.py:13
  76.9 0.6 copy-start.14
  77.5 10.3 %copy-start.9 = (bf16[16,4096]{1,0:T(8,128)(2,1)S(1)}, bf16[16,4096]{1,0:T(8,128)(2,1)}, u32[]{:S(2)}) copy-start(bf16[16,4096]{1,0:T(8,128)(2,1)} %add.73) | copy-start | bytes 393220
  79.0 29.7 %collective-permute-start.6 = (bf16[2,16,4096]{2,1,0:T(8,128)(2,1)S(1)}, bf16[2,16,4096]{2,1,0:T(8,128)(2,1)}, u32[]{:S(2)}, u32[]{:S(2)}) collective-permute-start(bf16[2,16,4096]{2,1,0:T(8,128)(2,1)S(1)} %reduce_sum.79), channel_id=1, source_target_pairs={{0,256},{64,320},{128,384},{192,448},{256,0},{320,64},{384,128},{4... | collective-permute-start | bytes 786440 | tf_op jit(solution)/shard_map/ppermute | solution.py:17
  88.7 22.7 %all-to-all-start.2 = ((bf16[4,16,4096]{2,1,0:T(8,128)(2,1)}), bf16[4,16,4096]{2,1,0:T(8,128)(2,1)S(1)}, u32[]{:S(2)}, u32[]{:S(2)}) async-start(bf16[4,16,4096]{2,1,0:T(8,128)(2,1)} %broadcast_in_dim.64), calls=%async_computation.2 | async-start | bytes 1048576 | tf_op jit(solution)/shard_map/all_to_all | solution.py:22
  92.1 18.4 %copy-start.10 = (bf16[512,512]{1,0:T(8,128)(2,1)S(1)}, bf16[512,512]{1,0:T(8,128)(2,1)}, u32[]{:S(2)}) copy-start(bf16[512,512]{1,0:T(8,128)(2,1)} %convolution_convert_fusion.1) | copy-start | bytes 1572868
  111.4 11.6 %all-to-all-start.3 = ((bf16[4,8,16,512]{3,2,1,0:T(8,128)(2,1)}), bf16[4,8,16,512]{3,2,1,0:T(8,128)(2,1)}, u32[]{:S(2)}, u32[]{:S(2)}) async-start(bf16[4,8,16,512]{3,2,1,0:T(8,128)(2,1)} %bitcast.154), calls=%async_computation.3 | async-start | bytes 1048576 | tf_op jit(solution)/shard_map/all_to_all | solution.py:22
  126.1 34.5 %all-to-all-start.4 = ((bf16[8,80,512]{2,1,0:T(8,128)(2,1)}), bf16[8,80,512]{2,1,0:T(8,128)(2,1)}, u32[]{:S(2)}, u32[]{:S(2)}) async-start(bf16[8,80,512]{2,1,0:T(8,128)(2,1)} %pad_maximum_fusion.2), calls=%async_computation.4 | async-start | bytes 1310720 | tf_op jit(solution)/shard_map/all_to_all | solution.py:126
  142.7 5.8 %copy-start.8 = (bf16[2,16,4096]{2,1,0:T(8,128)(2,1)S(1)}, bf16[2,16,4096]{2,1,0:T(8,128)(2,1)}, u32[]{:S(2)}) copy-start(bf16[2,16,4096]{2,1,0:T(8,128)(2,1)} %get-tuple-element.51) | copy-start | bytes 786436
  147.1 3.1 %copy-start.7 = (bf16[8,8,32,128]{3,2,1,0:T(8,128)(2,1)S(1)}, bf16[8,8,32,128]{3,2,1,0:T(8,128)(2,1)}, u32[]{:S(2)}) copy-start(bf16[8,8,32,128]{3,2,1,0:T(8,128)(2,1)} %copy.80) | copy-start | bytes 1572868
  161.5 10.3 %copy-start.5 = (bf16[2,2,2,72,512]{4,3,2,1,0:T(8,128)(2,1)S(1)}, bf16[2,2,2,72,512]{4,3,2,1,0:T(8,128)(2,1)}, u32[]{:S(2)}) copy-start(bf16[2,2,2,72,512]{4,3,2,1,0:T(8,128)(2,1)} %copy-done.4) | copy-start | bytes 1769476
  161.5 14.6 %collective-permute-start.8 = (bf16[16,4096]{1,0:T(8,128)(2,1)S(1)}, bf16[16,4096]{1,0:T(8,128)(2,1)S(1)}, u32[]{:S(2)}, u32[]{:S(2)}) collective-permute-start(bf16[16,4096]{1,0:T(8,128)(2,1)S(1)} %bitcast.171), channel_id=1, source_target_pairs={{0,256},{64,320},{128,384},{192,448},{256,0},{320,64},{384,128},{4... | collective-permute-start | bytes 393224 | tf_op jit(solution)/shard_map/ppermute | solution.py:17
  171.8 4.3 %copy-start.6 = (f32[2,16,4096]{2,1,0:T(8,128)S(1)}, f32[2,16,4096]{2,1,0:T(8,128)}, u32[]{:S(2)}) copy-start(f32[2,16,4096]{2,1,0:T(8,128)} %get-tuple-element.50) | copy-start | bytes 1572868
  176.3 33.1 %collective-permute-start.10 = (bf16[34,4096]{1,0:T(8,128)(2,1)S(1)}, bf16[34,4096]{1,0:T(8,128)(2,1)S(1)}, u32[]{:S(2)}, u32[]{:S(2)}) collective-permute-start(bf16[34,4096]{1,0:T(8,128)(2,1)S(1)} %get-tuple-element.59), channel_id=1, source_target_pairs={{0,128},{64,192},{128,0},{192,64},{256,384},{320,448},{384,256},{4... | collective-permute-start | bytes 835592 | tf_op jit(solution)/shard_map/ppermute | solution.py:17
  178.6 30.8 %collective-permute-start.9 = (bf16[34,4096]{1,0:T(8,128)(2,1)S(1)}, bf16[34,4096]{1,0:T(8,128)(2,1)S(1)}, u32[]{:S(2)}, u32[]{:S(2)}) collective-permute-start(bf16[34,4096]{1,0:T(8,128)(2,1)S(1)} %get-tuple-element.59), channel_id=1, source_target_pairs={{0,64},{64,0},{128,192},{192,128},{256,320},{320,256},{384,448},{4... | collective-permute-start | bytes 835592 | tf_op jit(solution)/shard_map/ppermute | solution.py:17
  181.6 27.9 %collective-permute-start.11 = (bf16[34,4096]{1,0:T(8,128)(2,1)S(1)}, bf16[34,4096]{1,0:T(8,128)(2,1)}, u32[]{:S(2)}, u32[]{:S(2)}) collective-permute-start(bf16[34,4096]{1,0:T(8,128)(2,1)S(1)} %get-tuple-element.59), channel_id=1, source_target_pairs={{0,192},{64,128},{128,64},{192,0},{256,448},{320,384},{384,320},{4... | collective-permute-start | bytes 835592 | tf_op jit(solution)/shard_map/ppermute | solution.py:17
  186.3 45.7 %all-to-all-start.5 = ((bf16[8,72,512]{2,1,0:T(8,128)(2,1)}), bf16[8,72,512]{2,1,0:T(8,128)(2,1)}, u32[]{:S(2)}, u32[]{:S(2)}) async-start(bf16[8,72,512]{2,1,0:T(8,128)(2,1)} %pad_maximum_fusion.4), calls=%async_computation.5 | async-start | bytes 1179648 | tf_op jit(solution)/shard_map/all_to_all | solution.py:136
  233.1 12.0 %copy-start.11 = (f32[1,1,1,64,256]{4,3,2,1,0:T(8,128)S(1)}, f32[1,1,1,64,256]{4,3,2,1,0:T(8,128)}, u32[]{:S(2)}) copy-start(f32[1,1,1,64,256]{4,3,2,1,0:T(8,128)} %copy.69) | copy-start | bytes 196612
  233.1 12.0 %copy-start.12 = (f32[1,1,1,64,256]{4,3,2,1,0:T(8,128)S(1)}, f32[1,1,1,64,256]{4,3,2,1,0:T(8,128)}, u32[]{:S(2)}) copy-start(f32[1,1,1,64,256]{4,3,2,1,0:T(8,128)} %copy.68) | copy-start | bytes 196612
  234.8 18.2 %collective-permute-start.7 = (bf16[512,512]{0,1:T(8,128)(2,1)S(1)}, bf16[512,512]{0,1:T(8,128)(2,1)S(1)}, u32[]{:S(2)}, u32[]{:S(2)}) collective-permute-start(bf16[512,512]{0,1:T(8,128)(2,1)S(1)} %fusion.7), channel_id=1, source_target_pairs={{8,0},{16,8},{24,16},{32,24},{40,32},{48,40},{56,48},{0,56},{9,1},... | collective-permute-start | bytes 1572872 | tf_op jit(solution)/shard_map/ppermute | solution.py:13

commit v3 on v2

--- a/solution.py
+++ b/solution.py
@@ -1,11 +1,14 @@
 import jax
 import jax.numpy as jnp
 from jax import lax
+from jax.experimental import pallas as pl
+from jax.experimental.pallas import tpu as pltpu
 from jax.sharding import PartitionSpec as P
 
 SHORT = jnp.bfloat16
 WIDE = jnp.float32
 PLANE = 4
+SPAN = 128
 
 
 def from_behind(block, axis, distance):
@@ -52,6 +55,83 @@
 
 def tied(value, *after):
     return lax.optimization_barrier((value,) + after)[0]
+
+
+def listed_bits(spans_ref, section):
+    bits = jnp.int32(0)
+    for j in range(spans_ref.shape[1]):
+        bits = bits | lax.shift_left(jnp.int32(1), spans_ref[section, j])
+    return bits
+
+
+def pack_kernel(place_ref, spans_ref, weight_ref, primary_ref, second_ref):
+    bits = listed_bits(spans_ref, place_ref[0])
+    ahead = [jnp.int32(0), jnp.int32(0)]
+    for n in range(weight_ref.shape[1] // SPAN):
+        bit = lax.shift_right_logical(bits, n) & 1
+        block = weight_ref[:, n * SPAN : (n + 1) * SPAN]
+
+        def put(out_ref, slot, block=block):
+            out_ref[:, pl.ds(pl.multiple_of(slot * SPAN, SPAN), SPAN)] = block
+
+        pl.when(bit == 0)(lambda: put(primary_ref, ahead[0]))
+        pl.when(bit == 1)(lambda: put(second_ref, ahead[1]))
+        ahead = [ahead[0] + 1 - bit, ahead[1] + bit]
+
+
+def pack(place, spans, weight, count):
+    rows, width = weight.shape
+    return pl.pallas_call(
+        pack_kernel,
+        out_shape=(
+            jax.ShapeDtypeStruct((rows, width - count * SPAN), weight.dtype),
+            jax.ShapeDtypeStruct((rows, count * SPAN), weight.dtype),
+        ),
+        in_specs=[pl.BlockSpec(memory_space=pltpu.SMEM)] * 2 + [pl.BlockSpec(memory_space=pltpu.VMEM)],
+        out_specs=(pl.BlockSpec(memory_space=pltpu.VMEM),) * 2,
+        name="pack",
+    )(place, spans, weight)
+
+
+def assemble_kernel(place_ref, spans_ref, own_ref, primary_ref, second_ref, grads_ref, sent_ref, restored_ref):
+    bits = listed_bits(spans_ref, place_ref[0])
+    here = place_ref[1] == 1
+    rows = own_ref.shape[0]
+    apart = sent_ref.shape[2] // SPAN
+    last = (primary_ref.shape[1] // SPAN - 1, second_ref.shape[1] // SPAN - 1)
+    ahead = [jnp.int32(0), jnp.int32(0)]
+    for n in range(own_ref.shape[1] // SPAN):
+        bit = lax.shift_right_logical(bits, n) & 1
+
+        def taken(ref, slot, top):
+            return ref[:, pl.ds(pl.multiple_of(jnp.minimum(slot, top) * SPAN, SPAN), SPAN)]
+
+        fresh = jnp.where(bit == 1, taken(second_ref, ahead[1], last[1]), taken(primary_ref, ahead[0], last[0]))
+        block = jnp.where(here, fresh, own_ref[:, n * SPAN : (n + 1) * SPAN])
+        restored_ref[:, n * SPAN : (n + 1) * SPAN] = block
+        inside = (n % apart) * SPAN
+        sent_ref[n // apart, :rows, inside : inside + SPAN] = block
+        ahead = [ahead[0] + 1 - bit, ahead[1] + bit]
+    for t in range(sent_ref.shape[0]):
+        total = grads_ref[0, t].astype(WIDE)
+        for x in range(1, PLANE):
+            total = total + grads_ref[x, t].astype(WIDE)
+        sent_ref[t, rows:, :] = total.astype(SHORT)
+
+
+def assemble(place, spans, own, primary, second, grads):
+    rows, width = own.shape
+    _, groups, part, cols = grads.shape
+    return pl.pallas_call(
+        assemble_kernel,
+        out_shape=(
+            jax.ShapeDtypeStruct((groups, rows + part, cols), SHORT),
+            jax.ShapeDtypeStruct((rows, width), SHORT),
+        ),
+        in_specs=[pl.BlockSpec(memory_space=pltpu.SMEM)] * 2 + [pl.BlockSpec(memory_space=pltpu.VMEM)] * 4,
+        out_specs=(pl.BlockSpec(memory_space=pltpu.VMEM),) * 2,
+        name="assemble",
+    )(place, spans, own, primary, second, grads)
 
 
 def adam(first, second, grad):
@@ -80,49 +160,40 @@
     is_failed = my_replica == failed
     part = rows // PLANE
 
+    local = activations[0, 0]
+    tokens, cols = local.shape
+    incoming = from_behind(local, "section", 1)
+    x = incoming.astype(WIDE)
+
+    place = jnp.stack([my_section, is_failed.astype(jnp.int32)])
+    to_primary, to_second = pack(place, resend_spans, own_weight, my_spans.shape[0])
+    from_primary = swap(to_primary, "replica", PLANE)
+    from_second = swap(to_second, "replica", 1)
+
     def masked(block):
         return jnp.where(chosen, block.astype(SHORT), 0).reshape(PLANE, 1, part, width)
 
-    def summed(parts):
-        return jnp.sum(parts.astype(WIDE), axis=0).astype(SHORT)
-
-    mask_weight = masked(own_weight)
-    spread_weight = summed(exchange_x(mask_weight))[0]
-    mask_moments = jnp.concatenate([masked(own_first), masked(own_second)], axis=1)
-
-    local = activations[0, 0]
-    tokens, cols = local.shape
-    squares = jnp.sum(jnp.square(local.astype(WIDE)), axis=1)
-    high, low = two_halves(squares)
-    extra = jnp.concatenate([high[None], low[None], jnp.zeros((6, tokens), SHORT)], axis=0)
-    held = jnp.concatenate([key_grads[0, 0].T, extra], axis=0)
-    held = tied(held, mask_weight)
-    incoming = from_behind(tied(local, held), "section", 1)
+    served = exchange_x(jnp.concatenate([masked(own_first), masked(own_second)], axis=1))
+    served = jnp.sum(served.astype(WIDE), axis=0).astype(SHORT)
+
+    squares = jnp.sum(x * x, axis=1).reshape(1, -1, 128)
+    squares = lax.all_to_all(jnp.broadcast_to(squares, (8,) + squares.shape[1:]), "tensor", 0, 0, tiled=True)
+    held = tied(key_grads[0, 0].T, to_primary)
     held = doubled(doubled(held, my_tensor, 0), my_tensor, 1)
-    held, spread_weight = lax.optimization_barrier((held, spread_weight))
-    fresh_weight = spread_weight + swap(spread_weight, "replica", PLANE)
-    spread_moments = summed(exchange_x(tied(mask_moments, spread_weight)))
+    held, from_primary, from_second, squares, served = lax.optimization_barrier(
+        (held, from_primary, from_second, squares, served)
+    )
+    fresh_moments = served + swap(served, "replica", PLANE)
     held = doubled(held, my_tensor, 2)
-    held, fresh_weight = lax.optimization_barrier((held, fresh_weight))
-    kg_rows = held.reshape((8,) + held.shape[3:])
-    kg_all = kg_rows[:, :rows].reshape(8 * rows, tokens)
-    total = jnp.sum(kg_rows[:, rows].astype(WIDE) + kg_rows[:, rows + 1].astype(WIDE), axis=0)
-    total = from_behind(total.reshape(-1, 128), "section", 1).reshape(tokens)
-    inverse_rms = 1.0 / jnp.sqrt(total / width + 1e-05)
-
-    spread_moments = tied(spread_moments, fresh_weight)
-    fresh_moments = spread_moments + swap(spread_moments, "replica", PLANE)
-    fresh_weight = broadcast_x(tied(fresh_weight, spread_moments)).reshape(rows, width)
-    restored_weight = jnp.where(is_failed, fresh_weight, own_weight)
-
-    x = incoming.astype(WIDE)
+    kg_all = held.reshape(8 * rows, tokens)
+    inverse_rms = 1.0 / jnp.sqrt(jnp.sum(squares, axis=0).reshape(tokens) / width + 1e-05)
+
     normed = (x * inverse_rms[:, None]).astype(SHORT)
     grad = lax.dot_general(kg_all, normed, (((1,), (0,)), ((), ())), preferred_element_type=WIDE).astype(SHORT)
-    grad = tied(grad, restored_weight, fresh_moments)
     grad = grad.reshape(8, PLANE, part, cols).transpose(1, 0, 2, 3)
-    grad = jnp.sum(exchange_x(grad).astype(WIDE), axis=0).astype(SHORT)
-
-    sent = jnp.concatenate([restored_weight.reshape(rows, 8, cols).transpose(1, 0, 2), grad], axis=1)
+    grad, fresh_moments = lax.optimization_barrier((exchange_x(grad), fresh_moments))
+
+    sent, restored_weight = assemble(place, resend_spans, own_weight, from_primary, from_second, grad)
     got = lax.all_to_all(sent, "tensor", 0, 0, tiled=True)
     weight_cols = got[:, :rows].reshape(8 * rows, cols)
     grad_rows = got[:, rows:].transpose(1, 0, 2).reshape(part, width)
@@ -148,8 +219,7 @@
     fresh = fresh_moments.astype(WIDE)
     fresh_update = adam(fresh[0], fresh[1], mean_rows).astype(SHORT)
     fresh_sums = checksum(fresh.reshape(2 * part, width)).astype(SHORT).reshape(2, width)
-    shared = jnp.concatenate([mean_rows.astype(SHORT), fresh_update, fresh_sums], axis=0)
-    shared = gather_x(shared)
+    shared = gather_x(jnp.concatenate([mean_rows.astype(SHORT), fresh_update, fresh_sums], axis=0))
     mean_grad = shared[:, :part].reshape(rows, width).astype(WIDE)
     fresh_update = shared[:, part : 2 * part].reshape(rows, width).astype(WIDE)
     fresh_sums = shared[:, 2 * part :].reshape(PLANE, 2, part, -1).transpose(1, 0, 2, 3).reshape(2, rows, -1).astype(WIDE)

time: 255 us -> 254 us (level)
  other arithmetic: 26.1 us -> 14.3 us
  waiting for transfers between devices: 68.4 us -> 78.6 us
  starting transfers between devices: 122 us -> 113 us
  local copies, waits for them, and re-layouts: 16.3 us -> 21.5 us
  Pallas kernels: 0 us -> 4.95 us
    ppermute x9 -> x10, waiting for transfers between devices: 23.8 us -> 39.2 us  [swap(): lax.ppermute(block, axis, [(i, i ^ bit) for i in range(lax.axis_size(axis...]
    all_to_all x0 -> x1, waiting for transfers between devices: none -> 14.5 us  [shards(): lax.all_to_all(jnp.broadcast_to(squares, (8,) + squares.shape[1:]), 'tens...]
    all_to_all x4 -> x2, waiting for transfers between devices: 12 us -> 0.01 us  [exchange_x(): lax.all_to_all(block, 'replica', 0, 0, axis_index_groups=groups, tiled=True)]
    all_to_all x4 -> x2, starting transfers between devices: 16 us -> 8.06 us  [exchange_x(): lax.all_to_all(block, 'replica', 0, 0, axis_index_groups=groups, tiled=True)]
    all_to_all x1, waiting for transfers between devices: 7.16 us -> 0.01 us  [shards(): got = lax.all_to_all(sent, 'tensor', 0, 0, tiled=True)]
    all_to_all x0 -> x1, starting transfers between devices: none -> 5.89 us  [shards(): lax.all_to_all(jnp.broadcast_to(squares, (8,) + squares.shape[1:]), 'tens...]
    all_to_all x1, starting transfers between devices: 23.2 us -> 17.9 us  [shards(): lax.all_to_all(sent, 'tensor', 0, 0, tiled=True).astype(WIDE)]
    pallas_call x0 -> x2, Pallas kernels: none -> 4.95 us  [the longest x1 2.72 us: assemble(): pl.pallas_call(assemble_kernel, out_shape=(jax.ShapeDtypeStruct((groups,...]
  transfers between devices with their start and end apart: 18 -> 17, of which waited for: 9 -> 7; matrix products, arithmetic and copies ran while one was open for 17% -> 17% of each run, Pallas kernels for 0% -> 0%
where the time goes in v3:
time: 254 us; the launch traced here: 252 us
  starting transfers between devices  113 us (44%)
  waiting for transfers between devices  78.6 us (31%)
  local copies, waits for them, and re-layouts  21.5 us (8%)
  matrix products  16.8 us (7%)
  other arithmetic  14.3 us (6%)
  Pallas kernels  4.95 us (2%)
  between operations  3.09 us (1%)
    ppermute x10, starting transfers between devices, swap(): lax.ppermute(block, axis, [(i, i ^ bit) for i in range(lax.axis_size(axis...  57.2 us
    ppermute x10, waiting for transfers between devices, swap(): lax.ppermute(block, axis, [(i, i ^ bit) for i in range(lax.axis_size(axis...  39.2 us
    all_to_all x1, starting transfers between devices, shards(): lax.all_to_all(sent, 'tensor', 0, 0, tiled=True).astype(WIDE)  17.9 us
    all_to_all x1, waiting for transfers between devices, shards(): lax.all_to_all(sent, 'tensor', 0, 0, tiled=True).astype(WIDE)  17.9 us
    all_to_all x1, waiting for transfers between devices, shards(): lax.all_to_all(jnp.broadcast_to(squares, (8,) + squares.shape[1:]), 'tens...  14.5 us
    dot_general x4, matrix products, checksum(): jnp.einsum('jnc,cp->jnp', shaped, probe_matrix, precision=lax.Precision.H...  14.4 us
    ppermute x2, starting transfers between devices, from_behind(): lax.ppermute(block, axis, [((i - distance) % n, i) for i in range(n)])  12.5 us
    all_to_all x1, starting transfers between devices, shards(): got = lax.all_to_all(sent, 'tensor', 0, 0, tiled=True)  11.7 us
  transfers between devices with their start and end apart: 17, of which 7 were waited for; matrix products, arithmetic and copies ran while one was open for 17% of the time, Pallas kernels for 0%

profile of v3, /device:TPU:1, one launch (start us, length us, event | category | flops | bytes accessed | tf_op | source)
XLA Modules:
  0.0 252.5 jit_solution(5428199463457307801)
XLA Ops:
  0.7 1.4 dynamic_slice.6
  3.2 2.2 pack.1
  5.5 9.6 %collective-permute-start = (bf16[64,512]{1,0:T(8,128)(2,1)}, bf16[64,512]{1,0:T(8,128)(2,1)S(1)}, u32[]{:S(2)}, u32[]{:S(2)}) collective-permute-start(bf16[64,512]{1,0:T(8,128)(2,1)} %bitcast.155), channel_id=1, source_target_pairs={{0,4},{1,5},{2,6},{3,7},{4,0},{5,1},{6,2},{7,3},{8,12},{9,13},{10,... | collective-permute-start | bytes 196616 | tf_op jit(solution)/shard_map/ppermute | solution.py:20
  17.3 1.3 convert_element_type.158
  18.7 1.1 pad_maximum_fusion.1
  19.8 4.1 %all-to-all-start.1 = ((bf16[4,2,16,4096]{3,2,1,0:T(8,128)(2,1)}), bf16[4,2,16,4096]{3,2,1,0:T(8,128)(2,1)S(1)}, u32[]{:S(2)}, u32[]{:S(2)}) async-start(bf16[4,2,16,4096]{3,2,1,0:T(8,128)(2,1)} %pad_maximum_fusion.1), calls=%async_computation.1 | async-start | bytes 2097152 | tf_op jit(solution)/shard_map/all_to_all | solution.py:25
  24.2 2.4 collective-permute-start.4
  26.6 4.9 %collective-permute-start.1 = (bf16[2,64,512]{2,1,0:T(8,128)(2,1)S(1)}, bf16[2,64,512]{2,1,0:T(8,128)(2,1)}, u32[]{:S(2)}, u32[]{:S(2)}) collective-permute-start(bf16[2,64,512]{2,1,0:T(8,128)(2,1)S(1)} %pad_maximum_fusion.6), channel_id=1, source_target_pairs={{0,2},{1,3},{2,0},{3,1},{4,6},{5,7},{6,4},{7,5},{8,10},{9,11},{10,... | collective-permute-start | bytes 393224 | tf_op jit(solution)/shard_map/ppermute | solution.py:20
  31.6 8.8 %collective-permute-start.2 = (bf16[64,3072]{1,0:T(8,128)(2,1)}, bf16[64,3072]{1,0:T(8,128)(2,1)}, u32[]{:S(2)}, u32[]{:S(2)}) collective-permute-start(bf16[64,3072]{1,0:T(8,128)(2,1)} %get-tuple-element.17), channel_id=1, source_target_pairs={{0,256},{64,320},{128,384},{192,448},{256,0},{320,64},{384,128},{4... | collective-permute-start | bytes 1179656 | tf_op jit(solution)/shard_map/ppermute | solution.py:20
  40.4 3.7 %collective-permute-start.3 = (bf16[64,1024]{1,0:T(8,128)(2,1)}, bf16[64,1024]{1,0:T(8,128)(2,1)}, u32[]{:S(2)}, u32[]{:S(2)}) collective-permute-start(bf16[64,1024]{1,0:T(8,128)(2,1)} %get-tuple-element.19), channel_id=1, source_target_pairs={{0,64},{64,0},{128,192},{192,128},{256,320},{320,256},{384,448},{4... | collective-permute-start | bytes 393224 | tf_op jit(solution)/shard_map/ppermute | solution.py:20
  44.1 0.9 select_bitcast_fusion.3
  45.8 5.9 %all-to-all-start = ((f32[8,4,128]{2,1,0:T(4,128)}), f32[8,4,128]{2,1,0:T(4,128)S(1)}, u32[]{:S(2)}, u32[]{:S(2)}) async-start(f32[8,4,128]{2,1,0:T(4,128)} %broadcast_in_dim.58), calls=%async_computation | async-start | bytes 32768 | tf_op jit(solution)/shard_map/all_to_all | solution.py:180
  52.0 13.0 %collective-permute-done.2.primary_ref = bf16[64,3072]{1,0:T(8,128)(2,1)} collective-permute-done((bf16[64,3072]{1,0:T(8,128)(2,1)}, bf16[64,3072]{1,0:T(8,128)(2,1)}, u32[]{:S(2)}, u32[]{:S(2)}) %collective-permute-start.2) | collective-permute-done | bytes 393248 | tf_op jit(solution)/shard_map/ppermute | solution.py:20
  65.0 14.5 %all-to-all-done = f32[8,4,128]{2,1,0:T(4,128)S(1)} async-done(((f32[8,4,128]{2,1,0:T(4,128)}), f32[8,4,128]{2,1,0:T(4,128)S(1)}, u32[]{:S(2)}, u32[]{:S(2)}) %all-to-all-start) | async-done | bytes 16416 | tf_op jit(solution)/shard_map/all_to_all | solution.py:180
  79.4 2.4 collective-permute-start.5
  81.9 6.5 %collective-permute-done.5 = bf16[2,2,64,512]{3,2,1,0:T(8,128)(2,1)S(1)} collective-permute-done((bf16[2,2,64,512]{3,2,1,0:T(8,128)(2,1)S(1)}, bf16[2,2,64,512]{3,2,1,0:T(8,128)(2,1)S(1)}, u32[]{:S(2)}, u32[]{:S(2)}) %collective-permute-start.5) | collective-permute-done | bytes 262176 | tf_op jit(solution)/shard_map/ppermute | solution.py:20
  89.8 3.9 %all-to-all-start.2 = ((bf16[4,8,16,512]{3,2,1,0:T(8,128)(2,1)}), bf16[4,8,16,512]{3,2,1,0:T(8,128)(2,1)S(1)}, u32[]{:S(2)}, u32[]{:S(2)}) async-start(bf16[4,8,16,512]{3,2,1,0:T(8,128)(2,1)} %bitcast.120), calls=%async_computation.2 | async-start | bytes 1048576 | tf_op jit(solution)/shard_map/all_to_all | solution.py:25
  93.8 6.8 %collective-permute-start.6 = (bf16[2,16,4096]{2,1,0:T(8,128)(2,1)S(1)}, bf16[2,16,4096]{2,1,0:T(8,128)(2,1)S(1)}, u32[]{:S(2)}, u32[]{:S(2)}) collective-permute-start(bf16[2,16,4096]{2,1,0:T(8,128)(2,1)S(1)} %reduce_sum.51), channel_id=1, source_target_pairs={{0,256},{64,320},{128,384},{192,448},{256,0},{320,64},{384,128},{4... | collective-permute-start | bytes 786440 | tf_op jit(solution)/shard_map/ppermute | solution.py:20
  100.6 18.2 %collective-permute-done.6 = bf16[2,16,4096]{2,1,0:T(8,128)(2,1)S(1)} collective-permute-done((bf16[2,16,4096]{2,1,0:T(8,128)(2,1)S(1)}, bf16[2,16,4096]{2,1,0:T(8,128)(2,1)S(1)}, u32[]{:S(2)}, u32[]{:S(2)}) %collective-permute-start.6) | collective-permute-done | bytes 262176 | tf_op jit(solution)/shard_map/ppermute | solution.py:20
  119.7 2.7 %assemble.1 = (bf16[8,80,512]{2,1,0:T(8,128)(2,1)}, bf16[64,4096]{1,0:T(8,128)(2,1)}) custom-call(s32[2]{0:T(128)} %pad_add_fusion.place_ref, s32[8,8]{1,0:T(8,128)} %spans_ref.3, bf16[64,4096]{1,0:T(8,128)(2,1)} %bitcast.134, bf16[64,3072]{1,0:T(8,128)(2,1)} %collective-permute-done.2.primary_ref, bf16[64,1024]{1,0:T(8,128)(2,1)} %collective-permute-done.3.second_ref, ...), custom_call_target="tpu_custom_call" | custom-call | tf_op jit(solution)/shard_map/assemble/pallas_call | solution.py:125
  122.4 11.7 %all-to-all-start.3 = ((bf16[8,80,512]{2,1,0:T(8,128)(2,1)}), bf16[8,80,512]{2,1,0:T(8,128)(2,1)S(1)}, u32[]{:S(2)}, u32[]{:S(2)}) async-start(bf16[8,80,512]{2,1,0:T(8,128)(2,1)} %get-tuple-element.26), calls=%async_computation.3 | async-start | bytes 1310720 | tf_op jit(solution)/shard_map/all_to_all | solution.py:197
  134.3 4.9 %fusion.24 = f32[64,32,8]{1,2,0:T(8,128)} fusion(f32[64,32,128]{2,1,0:T(8,128)S(1)} %bitcast.127, f32[128,8]{0,1:T(8,128)S(1)} %copy-done), kind=kOutput, calls=%fused_computation.60 | convolution fusion | flops 25165824 | bytes 1118208 | tf_op jit(solution)/shard_map/jnc,cp->jnp/dot_general | solution.py:216
  139.2 1.7 copy.64
  140.9 1.6 copy.66
  142.7 4.9 %fusion.26 = f32[64,32,8]{1,2,0:T(8,128)} fusion(f32[64,32,128]{2,1,0:T(8,128)S(1)} %bitcast.128, f32[128,8]{0,1:T(8,128)S(1)} %copy-done), kind=kOutput, calls=%fused_computation.62 | convolution fusion | flops 25165824 | bytes 1118208 | tf_op jit(solution)/shard_map/jnc,cp->jnp/dot_general | solution.py:216
  147.6 1.7 copy.63
  149.3 1.6 copy.65
  151.6 1.1 copy.74
  152.7 2.9 %fusion.22 = f32[64,32,8]{1,2,0:T(8,128)} fusion(bf16[64,32,128]{2,1,0:T(8,128)(2,1)S(1)} %bitcast.137, f32[128,8]{0,1:T(8,128)S(1)} %copy-done), kind=kOutput, calls=%fused_computation.58 | convolution fusion | flops 25165824 | bytes 593920 | tf_op jit(solution)/shard_map/jnc,cp->jnp/dot_general | solution.py:216
  155.6 1.7 copy.67
  157.3 1.6 copy.69
  159.8 1.8 convolution_convert_fusion.2
  161.6 1.0 copy.61
  163.5 11.3 %collective-permute-start.8 = (bf16[16,4096]{1,0:T(8,128)(2,1)S(1)}, bf16[16,4096]{1,0:T(8,128)(2,1)S(1)}, u32[]{:S(2)}, u32[]{:S(2)}) collective-permute-start(bf16[16,4096]{1,0:T(8,128)(2,1)S(1)} %bitcast.153), channel_id=1, source_target_pairs={{0,256},{64,320},{128,384},{192,448},{256,0},{320,64},{384,128},{4... | collective-permute-start | bytes 393224 | tf_op jit(solution)/shard_map/ppermute | solution.py:20
  174.9 1.5 fusion.4
  176.9 1.5 collective-permute-done.8
  179.4 4.9 %collective-permute-start.10 = (bf16[34,4096]{1,0:T(8,128)(2,1)}, bf16[34,4096]{1,0:T(8,128)(2,1)}, u32[]{:S(2)}, u32[]{:S(2)}) collective-permute-start(bf16[34,4096]{1,0:T(8,128)(2,1)} %get-tuple-element.59), channel_id=1, source_target_pairs={{0,128},{64,192},{128,0},{192,64},{256,384},{320,448},{384,256},{4... | collective-permute-start | bytes 835592 | tf_op jit(solution)/shard_map/ppermute | solution.py:20
  184.2 2.2 collective-permute-start.9
  186.4 2.5 %collective-permute-start.11 = (bf16[34,4096]{1,0:T(8,128)(2,1)}, bf16[34,4096]{1,0:T(8,128)(2,1)}, u32[]{:S(2)}, u32[]{:S(2)}) collective-permute-start(bf16[34,4096]{1,0:T(8,128)(2,1)} %get-tuple-element.59), channel_id=1, source_target_pairs={{0,192},{64,128},{128,64},{192,0},{256,448},{320,384},{384,320},{4... | collective-permute-start | bytes 835592 | tf_op jit(solution)/shard_map/ppermute | solution.py:20
  190.0 17.9 %all-to-all-start.4 = ((bf16[8,72,512]{2,1,0:T(8,128)(2,1)}), bf16[8,72,512]{2,1,0:T(8,128)(2,1)S(1)}, u32[]{:S(2)}, u32[]{:S(2)}) async-start(bf16[8,72,512]{2,1,0:T(8,128)(2,1)} %pad_maximum_fusion.2), calls=%async_computation.4 | async-start | bytes 1179648 | tf_op jit(solution)/shard_map/all_to_all | solution.py:207
  207.9 1.4 pad_maximum_fusion
  210.8 1.5 convert_select_fusion
  212.4 17.9 %all-to-all-done.4 = bf16[8,72,512]{2,1,0:T(8,128)(2,1)S(1)} async-done(((bf16[8,72,512]{2,1,0:T(8,128)(2,1)}), bf16[8,72,512]{2,1,0:T(8,128)(2,1)S(1)}, u32[]{:S(2)}, u32[]{:S(2)}) %all-to-all-start.4) | async-done | bytes 589856 | tf_op jit(solution)/shard_map/all_to_all | solution.py:207
  230.4 1.5 fusion.8
  231.9 10.1 %collective-permute-start.7 = (bf16[512,512]{0,1:T(8,128)(2,1)S(1)}, bf16[512,512]{0,1:T(8,128)(2,1)S(1)}, u32[]{:S(2)}, u32[]{:S(2)}) collective-permute-start(bf16[512,512]{0,1:T(8,128)(2,1)S(1)} %fusion.8), channel_id=1, source_target_pairs={{8,0},{16,8},{24,16},{32,24},{40,32},{48,40},{56,48},{0,56},{9,1},... | collective-permute-start | bytes 1572872 | tf_op jit(solution)/shard_map/ppermute | solution.py:16
  242.0 1.0 slice_convert_fusion.1
  244.4 7.0 %collective-permute-done.7 = bf16[512,512]{0,1:T(8,128)(2,1)S(1)} collective-permute-done((bf16[512,512]{0,1:T(8,128)(2,1)S(1)}, bf16[512,512]{0,1:T(8,128)(2,1)S(1)}, u32[]{:S(2)}, u32[]{:S(2)}) %collective-permute-start.7) | collective-permute-done | bytes 524320 | tf_op jit(solution)/shard_map/ppermute | solution.py:16
  251.5 1.0 copy.68
  (88 shorter events, 13.6 us)
Async XLA Ops:
  0.6 133.6 %copy-start = (f32[128,8]{0,1:T(8,128)S(1)}, f32[128,8]{0,1:T(8,128)}, u32[]{:S(2)}) copy-start(f32[128,8]{0,1:T(8,128)} %param.13) | copy-start | bytes 12292
  0.6 17.9 %copy-start.2 = (f32[1,1,64,4096]{3,2,1,0:T(8,128)S(1)}, f32[1,1,64,4096]{3,2,1,0:T(8,128)}, u32[]{:S(2)}) copy-start(f32[1,1,64,4096]{3,2,1,0:T(8,128)} %param.12) | copy-start | bytes 3145732
  5.5 21.1 %collective-permute-start = (bf16[64,512]{1,0:T(8,128)(2,1)}, bf16[64,512]{1,0:T(8,128)(2,1)S(1)}, u32[]{:S(2)}, u32[]{:S(2)}) collective-permute-start(bf16[64,512]{1,0:T(8,128)(2,1)} %bitcast.155), channel_id=1, source_target_pairs={{0,4},{1,5},{2,6},{3,7},{4,0},{5,1},{6,2},{7,3},{8,12},{9,13},{10,... | collective-permute-start | bytes 196616 | tf_op jit(solution)/shard_map/ppermute | solution.py:20
  19.8 4.2 %copy-start.8 = (bf16[1,1,512,512]{3,2,1,0:T(8,128)(2,1)S(1)}, bf16[1,1,512,512]{3,2,1,0:T(8,128)(2,1)}, u32[]{:S(2)}) copy-start(bf16[1,1,512,512]{3,2,1,0:T(8,128)(2,1)} %param.8) | copy-start | bytes 1572868
  19.8 6.8 %copy-start.12 = (bf16[1,1,512,64]{2,3,1,0:T(8,128)(2,1)S(1)}, bf16[1,1,512,64]{2,3,1,0:T(8,128)(2,1)}, u32[]{:S(2)}) copy-start(bf16[1,1,512,64]{2,3,1,0:T(8,128)(2,1)} %param.9) | copy-start | bytes 196612
  19.8 25.4 %all-to-all-start.1 = ((bf16[4,2,16,4096]{3,2,1,0:T(8,128)(2,1)}), bf16[4,2,16,4096]{3,2,1,0:T(8,128)(2,1)S(1)}, u32[]{:S(2)}, u32[]{:S(2)}) async-start(bf16[4,2,16,4096]{3,2,1,0:T(8,128)(2,1)} %pad_maximum_fusion.1), calls=%async_computation.1 | async-start | bytes 2097152 | tf_op jit(solution)/shard_map/all_to_all | solution.py:25
  24.2 20.9 %collective-permute-start.4 = (bf16[512,512]{0,1:T(8,128)(2,1)S(1)}, bf16[512,512]{0,1:T(8,128)(2,1)S(1)}, u32[]{:S(2)}, u32[]{:S(2)}) collective-permute-start(bf16[512,512]{0,1:T(8,128)(2,1)S(1)} %bitcast.147), channel_id=1, source_target_pairs={{56,0},{0,8},{8,16},{16,24},{24,32},{32,40},{40,48},{48,56},{57,1}... | collective-permute-start | bytes 1572872 | tf_op jit(solution)/shard_map/ppermute | solution.py:16
  26.6 17.4 %collective-permute-start.1 = (bf16[2,64,512]{2,1,0:T(8,128)(2,1)S(1)}, bf16[2,64,512]{2,1,0:T(8,128)(2,1)}, u32[]{:S(2)}, u32[]{:S(2)}) collective-permute-start(bf16[2,64,512]{2,1,0:T(8,128)(2,1)S(1)} %pad_maximum_fusion.6), channel_id=1, source_target_pairs={{0,2},{1,3},{2,0},{3,1},{4,6},{5,7},{6,4},{7,5},{8,10},{9,11},{10,... | collective-permute-start | bytes 393224 | tf_op jit(solution)/shard_map/ppermute | solution.py:20
  31.6 33.4 %collective-permute-start.2 = (bf16[64,3072]{1,0:T(8,128)(2,1)}, bf16[64,3072]{1,0:T(8,128)(2,1)}, u32[]{:S(2)}, u32[]{:S(2)}) collective-permute-start(bf16[64,3072]{1,0:T(8,128)(2,1)} %get-tuple-element.17), channel_id=1, source_target_pairs={{0,256},{64,320},{128,384},{192,448},{256,0},{320,64},{384,128},{4... | collective-permute-start | bytes 1179656 | tf_op jit(solution)/shard_map/ppermute | solution.py:20
  40.4 11.5 %collective-permute-start.3 = (bf16[64,1024]{1,0:T(8,128)(2,1)}, bf16[64,1024]{1,0:T(8,128)(2,1)}, u32[]{:S(2)}, u32[]{:S(2)}) collective-permute-start(bf16[64,1024]{1,0:T(8,128)(2,1)} %get-tuple-element.19), channel_id=1, source_target_pairs={{0,64},{64,0},{128,192},{192,128},{256,320},{320,256},{384,448},{4... | collective-permute-start | bytes 393224 | tf_op jit(solution)/shard_map/ppermute | solution.py:20
  45.8 33.6 %all-to-all-start = ((f32[8,4,128]{2,1,0:T(4,128)}), f32[8,4,128]{2,1,0:T(4,128)S(1)}, u32[]{:S(2)}, u32[]{:S(2)}) async-start(f32[8,4,128]{2,1,0:T(4,128)} %broadcast_in_dim.58), calls=%async_computation | async-start | bytes 32768 | tf_op jit(solution)/shard_map/all_to_all | solution.py:180
  79.4 9.0 %collective-permute-start.5 = (bf16[2,2,64,512]{3,2,1,0:T(8,128)(2,1)S(1)}, bf16[2,2,64,512]{3,2,1,0:T(8,128)(2,1)S(1)}, u32[]{:S(2)}, u32[]{:S(2)}) collective-permute-start(bf16[2,2,64,512]{3,2,1,0:T(8,128)(2,1)S(1)} %pad_maximum_fusion.5), channel_id=1, source_target_pairs={{0,1},{1,0},{2,3},{3,2},{4,5},{5,4},{6,7},{7,6},{8,9},{9,8},{10,11... | collective-permute-start | bytes 786440 | tf_op jit(solution)/shard_map/ppermute | solution.py:20
  88.5 1.3 copy-start.6
  89.8 29.0 %all-to-all-start.2 = ((bf16[4,8,16,512]{3,2,1,0:T(8,128)(2,1)}), bf16[4,8,16,512]{3,2,1,0:T(8,128)(2,1)S(1)}, u32[]{:S(2)}, u32[]{:S(2)}) async-start(bf16[4,8,16,512]{3,2,1,0:T(8,128)(2,1)} %bitcast.120), calls=%async_computation.2 | async-start | bytes 1048576 | tf_op jit(solution)/shard_map/all_to_all | solution.py:25
  93.8 25.0 %collective-permute-start.6 = (bf16[2,16,4096]{2,1,0:T(8,128)(2,1)S(1)}, bf16[2,16,4096]{2,1,0:T(8,128)(2,1)S(1)}, u32[]{:S(2)}, u32[]{:S(2)}) collective-permute-start(bf16[2,16,4096]{2,1,0:T(8,128)(2,1)S(1)} %reduce_sum.51), channel_id=1, source_target_pairs={{0,256},{64,320},{128,384},{192,448},{256,0},{320,64},{384,128},{4... | collective-permute-start | bytes 786440 | tf_op jit(solution)/shard_map/ppermute | solution.py:20
  118.9 0.8 copy-start.5
  122.4 41.1 %all-to-all-start.3 = ((bf16[8,80,512]{2,1,0:T(8,128)(2,1)}), bf16[8,80,512]{2,1,0:T(8,128)(2,1)S(1)}, u32[]{:S(2)}, u32[]{:S(2)}) async-start(bf16[8,80,512]{2,1,0:T(8,128)(2,1)} %get-tuple-element.26), calls=%async_computation.3 | async-start | bytes 1310720 | tf_op jit(solution)/shard_map/all_to_all | solution.py:197
  134.3 8.2 %copy-start.1 = (f32[1,1,64,4096]{3,2,1,0:T(8,128)S(1)}, f32[1,1,64,4096]{3,2,1,0:T(8,128)}, u32[]{:S(2)}) copy-start(f32[1,1,64,4096]{3,2,1,0:T(8,128)} %param.11) | copy-start | bytes 3145732
  163.5 11.4 %copy-start.7 = (bf16[2,2,2,64,512]{4,3,2,1,0:T(8,128)(2,1)S(1)}, bf16[2,2,2,64,512]{4,3,2,1,0:T(8,128)(2,1)}, u32[]{:S(2)}) copy-start(bf16[2,2,2,64,512]{4,3,2,1,0:T(8,128)(2,1)} %copy-done.6) | copy-start | bytes 1572868
  163.5 14.9 %collective-permute-start.8 = (bf16[16,4096]{1,0:T(8,128)(2,1)S(1)}, bf16[16,4096]{1,0:T(8,128)(2,1)S(1)}, u32[]{:S(2)}, u32[]{:S(2)}) collective-permute-start(bf16[16,4096]{1,0:T(8,128)(2,1)S(1)} %bitcast.153), channel_id=1, source_target_pairs={{0,256},{64,320},{128,384},{192,448},{256,0},{320,64},{384,128},{4... | collective-permute-start | bytes 393224 | tf_op jit(solution)/shard_map/ppermute | solution.py:20
  176.4 2.0 copy-start.4
  176.4 2.2 copy-start.11
  176.9 12.1 %copy-start.13 = (bf16[8]{0:T(256)(128)(2,1)S(1)}, bf16[8]{0:T(256)(128)(2,1)}, u32[]{:S(2)}) copy-start(bf16[8]{0:T(256)(128)(2,1)} %pad.13.clone) | copy-start | bytes 52
  179.4 28.5 %collective-permute-start.10 = (bf16[34,4096]{1,0:T(8,128)(2,1)}, bf16[34,4096]{1,0:T(8,128)(2,1)}, u32[]{:S(2)}, u32[]{:S(2)}) collective-permute-start(bf16[34,4096]{1,0:T(8,128)(2,1)} %get-tuple-element.59), channel_id=1, source_target_pairs={{0,128},{64,192},{128,0},{192,64},{256,384},{320,448},{384,256},{4... | collective-permute-start | bytes 835592 | tf_op jit(solution)/shard_map/ppermute | solution.py:20
  184.2 23.6 %collective-permute-start.9 = (bf16[34,4096]{1,0:T(8,128)(2,1)}, bf16[34,4096]{1,0:T(8,128)(2,1)}, u32[]{:S(2)}, u32[]{:S(2)}) collective-permute-start(bf16[34,4096]{1,0:T(8,128)(2,1)} %get-tuple-element.59), channel_id=1, source_target_pairs={{0,64},{64,0},{128,192},{192,128},{256,320},{320,256},{384,448},{4... | collective-permute-start | bytes 835592 | tf_op jit(solution)/shard_map/ppermute | solution.py:20
  186.4 21.4 %collective-permute-start.11 = (bf16[34,4096]{1,0:T(8,128)(2,1)}, bf16[34,4096]{1,0:T(8,128)(2,1)}, u32[]{:S(2)}, u32[]{:S(2)}) collective-permute-start(bf16[34,4096]{1,0:T(8,128)(2,1)} %get-tuple-element.59), channel_id=1, source_target_pairs={{0,192},{64,128},{128,64},{192,0},{256,448},{320,384},{384,320},{4... | collective-permute-start | bytes 835592 | tf_op jit(solution)/shard_map/ppermute | solution.py:20
  190.0 40.3 %all-to-all-start.4 = ((bf16[8,72,512]{2,1,0:T(8,128)(2,1)}), bf16[8,72,512]{2,1,0:T(8,128)(2,1)S(1)}, u32[]{:S(2)}, u32[]{:S(2)}) async-start(bf16[8,72,512]{2,1,0:T(8,128)(2,1)} %pad_maximum_fusion.2), calls=%async_computation.4 | async-start | bytes 1179648 | tf_op jit(solution)/shard_map/all_to_all | solution.py:207
  209.8 1.1 copy-start.3
  230.3 12.8 %copy-start.9 = (f32[1,1,1,64,256]{4,3,2,1,0:T(8,128)S(1)}, f32[1,1,1,64,256]{4,3,2,1,0:T(8,128)}, u32[]{:S(2)}) copy-start(f32[1,1,1,64,256]{4,3,2,1,0:T(8,128)} %copy.66) | copy-start | bytes 196612
  230.4 12.8 %copy-start.10 = (f32[1,1,1,64,256]{4,3,2,1,0:T(8,128)S(1)}, f32[1,1,1,64,256]{4,3,2,1,0:T(8,128)}, u32[]{:S(2)}) copy-start(f32[1,1,1,64,256]{4,3,2,1,0:T(8,128)} %copy.65) | copy-start | bytes 196612
  231.9 19.6 %collective-permute-start.7 = (bf16[512,512]{0,1:T(8,128)(2,1)S(1)}, bf16[512,512]{0,1:T(8,128)(2,1)S(1)}, u32[]{:S(2)}, u32[]{:S(2)}) collective-permute-start(bf16[512,512]{0,1:T(8,128)(2,1)S(1)} %fusion.8), channel_id=1, source_target_pairs={{8,0},{16,8},{24,16},{32,24},{40,32},{48,40},{56,48},{0,56},{9,1},... | collective-permute-start | bytes 1572872 | tf_op jit(solution)/shard_map/ppermute | solution.py:16

commit v4 on v2

--- a/solution.py
+++ b/solution.py
@@ -1,11 +1,14 @@
 import jax
 import jax.numpy as jnp
 from jax import lax
+from jax.experimental import pallas as pl
+from jax.experimental.pallas import tpu as pltpu
 from jax.sharding import PartitionSpec as P
 
 SHORT = jnp.bfloat16
 WIDE = jnp.float32
 PLANE = 4
+SPAN = 128
 
 
 def from_behind(block, axis, distance):
@@ -52,6 +55,71 @@
 
 def tied(value, *after):
     return lax.optimization_barrier((value,) + after)[0]
+
+
+def serve_kernel(failed_ref, spans_ref, weight_ref, first_ref, second_ref, out_ref):
+    section = lax.axis_index("section")
+    me = lax.axis_index("replica")
+    failed = failed_ref[section, lax.axis_index("tensor")]
+    is_primary = (failed ^ PLANE) == me
+    is_second = (failed ^ 1) == me
+    part = out_ref.shape[2]
+    for n in range(weight_ref.shape[1] // SPAN):
+        listed = spans_ref[section, 0] == n
+        for j in range(1, spans_ref.shape[1]):
+            listed = listed | (spans_ref[section, j] == n)
+        take = (listed & is_second) | (jnp.logical_not(listed) & is_primary)
+        here = pl.ds(n * SPAN, SPAN)
+        for k, ref in enumerate((weight_ref, first_ref, second_ref)):
+            for x in range(PLANE):
+                block = ref[x * part : (x + 1) * part, here].astype(SHORT)
+                out_ref[x, k, :, here] = jnp.where(take, block, jnp.zeros_like(block))
+
+
+def serve(failed, spans, weight, first, second):
+    rows, width = weight.shape
+    return pl.pallas_call(
+        serve_kernel,
+        out_shape=jax.ShapeDtypeStruct((PLANE, 3, rows // PLANE, width), SHORT),
+        in_specs=[pl.BlockSpec(memory_space=pltpu.SMEM)] * 2 + [pl.BlockSpec(memory_space=pltpu.VMEM)] * 3,
+        out_specs=pl.BlockSpec(memory_space=pltpu.VMEM),
+        name="serve",
+    )(failed, spans, weight, first, second)
+
+
+def assemble_kernel(failed_ref, own_ref, fresh0_ref, fresh1_ref, fresh2_ref, fresh3_ref, grads_ref, sent_ref, restored_ref):
+    me = lax.axis_index("replica")
+    here = failed_ref[lax.axis_index("section"), lax.axis_index("tensor")] == me
+    rows = own_ref.shape[0]
+    groups, _, cols = sent_ref.shape
+    part = fresh0_ref.shape[0]
+    for k, fresh_ref in enumerate((fresh0_ref, fresh1_ref, fresh2_ref, fresh3_ref)):
+        at = pl.ds(pl.multiple_of(((me & 3) ^ k) * part, part), part)
+        for t in range(groups):
+            span = pl.ds(t * cols, cols)
+            block = jnp.where(here, fresh_ref[:, span], own_ref[at, span])
+            restored_ref[at, span] = block
+            sent_ref[t, at, :] = block
+    for t in range(groups):
+        total = grads_ref[0, t].astype(WIDE)
+        for x in range(1, PLANE):
+            total = total + grads_ref[x, t].astype(WIDE)
+        sent_ref[t, rows:, :] = total.astype(SHORT)
+
+
+def assemble(failed, own, fresh, grads):
+    rows, width = own.shape
+    _, groups, part, cols = grads.shape
+    return pl.pallas_call(
+        assemble_kernel,
+        out_shape=(
+            jax.ShapeDtypeStruct((groups, rows + part, cols), SHORT),
+            jax.ShapeDtypeStruct((rows, width), SHORT),
+        ),
+        in_specs=[pl.BlockSpec(memory_space=pltpu.SMEM)] + [pl.BlockSpec(memory_space=pltpu.VMEM)] * 6,
+        out_specs=(pl.BlockSpec(memory_space=pltpu.VMEM),) * 2,
+        name="assemble",
+    )(failed, own, *fresh, grads)
 
 
 def adam(first, second, grad):
@@ -80,49 +148,34 @@
     is_failed = my_replica == failed
     part = rows // PLANE
 
-    def masked(block):
-        return jnp.where(chosen, block.astype(SHORT), 0).reshape(PLANE, 1, part, width)
-
-    def summed(parts):
-        return jnp.sum(parts.astype(WIDE), axis=0).astype(SHORT)
-
-    mask_weight = masked(own_weight)
-    spread_weight = summed(exchange_x(mask_weight))[0]
-    mask_moments = jnp.concatenate([masked(own_first), masked(own_second)], axis=1)
-
     local = activations[0, 0]
     tokens, cols = local.shape
-    squares = jnp.sum(jnp.square(local.astype(WIDE)), axis=1)
-    high, low = two_halves(squares)
-    extra = jnp.concatenate([high[None], low[None], jnp.zeros((6, tokens), SHORT)], axis=0)
-    held = jnp.concatenate([key_grads[0, 0].T, extra], axis=0)
-    held = tied(held, mask_weight)
-    incoming = from_behind(tied(local, held), "section", 1)
+    incoming = from_behind(local, "section", 1)
+    x = incoming.astype(WIDE)
+
+    mask = serve(failed_replica, resend_spans, own_weight, own_first, own_second)
+    served = jnp.sum(exchange_x(mask).astype(WIDE), axis=0).astype(SHORT)
+
+    squares = jnp.sum(x * x, axis=1).reshape(1, -1, 128)
+    squares = lax.all_to_all(jnp.broadcast_to(squares, (8,) + squares.shape[1:]), "tensor", 0, 0, tiled=True)
+    held = tied(key_grads[0, 0].T, mask)
     held = doubled(doubled(held, my_tensor, 0), my_tensor, 1)
-    held, spread_weight = lax.optimization_barrier((held, spread_weight))
-    fresh_weight = spread_weight + swap(spread_weight, "replica", PLANE)
-    spread_moments = summed(exchange_x(tied(mask_moments, spread_weight)))
+    held, served = lax.optimization_barrier((held, served))
+    fresh_weight = served[0] + swap(served[0], "replica", PLANE)
     held = doubled(held, my_tensor, 2)
-    held, fresh_weight = lax.optimization_barrier((held, fresh_weight))
-    kg_rows = held.reshape((8,) + held.shape[3:])
-    kg_all = kg_rows[:, :rows].reshape(8 * rows, tokens)
-    total = jnp.sum(kg_rows[:, rows].astype(WIDE) + kg_rows[:, rows + 1].astype(WIDE), axis=0)
-    total = from_behind(total.reshape(-1, 128), "section", 1).reshape(tokens)
-    inverse_rms = 1.0 / jnp.sqrt(total / width + 1e-05)
-
-    spread_moments = tied(spread_moments, fresh_weight)
-    fresh_moments = spread_moments + swap(spread_moments, "replica", PLANE)
-    fresh_weight = broadcast_x(tied(fresh_weight, spread_moments)).reshape(rows, width)
-    restored_weight = jnp.where(is_failed, fresh_weight, own_weight)
-
-    x = incoming.astype(WIDE)
+    held, fresh_weight, squares = lax.optimization_barrier((held, fresh_weight, squares))
+    served_moments = tied(served[1:], fresh_weight)
+    fresh_moments = served_moments + swap(served_moments, "replica", PLANE)
+    kg_all = held.reshape(8 * rows, tokens)
+    inverse_rms = 1.0 / jnp.sqrt(jnp.sum(squares, axis=0).reshape(tokens) / width + 1e-05)
+    fresh_weight = [fresh_weight] + [swap(fresh_weight, "replica", bit) for bit in (1, 2, 3)]
+
     normed = (x * inverse_rms[:, None]).astype(SHORT)
     grad = lax.dot_general(kg_all, normed, (((1,), (0,)), ((), ())), preferred_element_type=WIDE).astype(SHORT)
-    grad = tied(grad, restored_weight, fresh_moments)
     grad = grad.reshape(8, PLANE, part, cols).transpose(1, 0, 2, 3)
-    grad = jnp.sum(exchange_x(grad).astype(WIDE), axis=0).astype(SHORT)
-
-    sent = jnp.concatenate([restored_weight.reshape(rows, 8, cols).transpose(1, 0, 2), grad], axis=1)
+    grad, fresh_moments = lax.optimization_barrier((exchange_x(grad), fresh_moments))
+
+    sent, restored_weight = assemble(failed_replica, own_weight, fresh_weight, grad)
     got = lax.all_to_all(sent, "tensor", 0, 0, tiled=True)
     weight_cols = got[:, :rows].reshape(8 * rows, cols)
     grad_rows = got[:, rows:].transpose(1, 0, 2).reshape(part, width)
@@ -130,15 +183,15 @@
 
     keys = lax.dot_general(weight_cols, normed, (((1,), (1,)), ((), ())), preferred_element_type=WIDE).astype(SHORT)
     feature = lax.dot_general(kg_all, weight_cols, (((0,), (0,)), ((), ())), preferred_element_type=WIDE)
-    high, low = two_halves(jnp.sum(feature * x, axis=1))
-    extra = jnp.concatenate([high[None], low[None], jnp.zeros((6, tokens), SHORT)], axis=0)
-    sent = jnp.concatenate([keys.reshape(8, rows, tokens), jnp.broadcast_to(extra[None], (8, 8, tokens))], axis=1)
-    got = jnp.sum(lax.all_to_all(sent, "tensor", 0, 0, tiled=True).astype(WIDE), axis=0)
-    key_out = got[:rows].T.astype(SHORT)
-    product = (got[rows] + got[rows + 1])[:, None]
+    product = jnp.sum(feature * x, axis=1).reshape(-1, 128)
+    for bit in (1, 2, 4):
+        product = product + swap(product, "tensor", bit)
+    product = product.reshape(tokens, 1)
     scale = inverse_rms[:, None]
     input_grad = scale * feature - scale * scale * scale * x * product / width
     outgoing = from_behind(input_grad.astype(SHORT), "section", -1)
+    got = lax.all_to_all(keys.reshape(8, rows, tokens), "tensor", 0, 0, tiled=True)
+    key_out = jnp.sum(got.astype(WIDE), axis=0).T.astype(SHORT)
 
     def checksum(source):
         shaped = source.reshape(-1, nchunk, 128)
@@ -148,8 +201,7 @@
     fresh = fresh_moments.astype(WIDE)
     fresh_update = adam(fresh[0], fresh[1], mean_rows).astype(SHORT)
     fresh_sums = checksum(fresh.reshape(2 * part, width)).astype(SHORT).reshape(2, width)
-    shared = jnp.concatenate([mean_rows.astype(SHORT), fresh_update, fresh_sums], axis=0)
-    shared = gather_x(shared)
+    shared = gather_x(jnp.concatenate([mean_rows.astype(SHORT), fresh_update, fresh_sums], axis=0))
     mean_grad = shared[:, :part].reshape(rows, width).astype(WIDE)
     fresh_update = shared[:, part : 2 * part].reshape(rows, width).astype(WIDE)
     fresh_sums = shared[:, 2 * part :].reshape(PLANE, 2, part, -1).transpose(1, 0, 2, 3).reshape(2, rows, -1).astype(WIDE)

time: 255 us -> 212 us (0.83)
  waiting for transfers between devices: 68.4 us -> 20.9 us
  starting transfers between devices: 122 us -> 142 us
  other arithmetic: 26.1 us -> 7.73 us
  Pallas kernels: 0 us -> 5.97 us
    ppermute x9 -> x15, starting transfers between devices: 55.8 us -> 86.5 us  [swap(): lax.ppermute(block, axis, [(i, i ^ bit) for i in range(lax.axis_size(axis...]
    all_to_all x1 -> x2, waiting for transfers between devices: 19 us -> 0.36 us  [the longest x1 0.36 us: shards(): lax.all_to_all(jnp.broadcast_to(squares, (8,) + squares.shape[1:]), 'tens...]
    all_to_all x1 -> x2, starting transfers between devices: 23.2 us -> 11.1 us  [the longest x1 6.38 us: shards(): lax.all_to_all(keys.reshape(8, rows, tokens), 'tensor', 0, 0, tiled=True)]
    all_to_all x4 -> x2, waiting for transfers between devices: 12 us -> 0.01 us  [exchange_x(): lax.all_to_all(block, 'replica', 0, 0, axis_index_groups=groups, tiled=True)]
    all_to_all x1, starting transfers between devices: 10.3 us -> 22.2 us  [shards(): got = lax.all_to_all(sent, 'tensor', 0, 0, tiled=True)]
    ppermute x9 -> x15, waiting for transfers between devices: 23.8 us -> 13.6 us  [swap(): lax.ppermute(block, axis, [(i, i ^ bit) for i in range(lax.axis_size(axis...]
    all_to_all x4 -> x2, starting transfers between devices: 16 us -> 9.19 us  [exchange_x(): lax.all_to_all(block, 'replica', 0, 0, axis_index_groups=groups, tiled=True)]
    all_to_all x1, waiting for transfers between devices: 7.16 us -> 1.02 us  [shards(): got = lax.all_to_all(sent, 'tensor', 0, 0, tiled=True)]
  transfers between devices with their start and end apart: 18 -> 22, of which waited for: 9 -> 9; matrix products, arithmetic and copies ran while one was open for 17% -> 17% of each run, Pallas kernels for 0% -> 0%
where the time goes in v4:
time: 212 us; the launch traced here: 211 us
  starting transfers between devices  142 us (67%)
  waiting for transfers between devices  20.9 us (10%)
  matrix products  16.9 us (8%)
  local copies, waits for them, and re-layouts  15.5 us (7%)
  other arithmetic  7.73 us (4%)
  Pallas kernels  5.97 us (3%)
    ppermute x15, starting transfers between devices, swap(): lax.ppermute(block, axis, [(i, i ^ bit) for i in range(lax.axis_size(axis...  86.5 us
    all_to_all x1, starting transfers between devices, shards(): got = lax.all_to_all(sent, 'tensor', 0, 0, tiled=True)  22.2 us
    dot_general x4, matrix products, checksum(): jnp.einsum('jnc,cp->jnp', shaped, probe_matrix, precision=lax.Precision.H...  13.7 us
    ppermute x15, waiting for transfers between devices, swap(): lax.ppermute(block, axis, [(i, i ^ bit) for i in range(lax.axis_size(axis...  13.6 us
    ppermute x2, starting transfers between devices, from_behind(): lax.ppermute(block, axis, [((i - distance) % n, i) for i in range(n)])  13.2 us
    all_to_all x2, starting transfers between devices, exchange_x(): lax.all_to_all(block, 'replica', 0, 0, axis_index_groups=groups, tiled=True)  9.19 us
    all_to_all x1, starting transfers between devices, shards(): lax.all_to_all(keys.reshape(8, rows, tokens), 'tensor', 0, 0, tiled=True)  6.38 us
    unnamed x32, local copies, waits for them, and re-layouts  6.35 us
  transfers between devices with their start and end apart: 22, of which 9 were waited for; matrix products, arithmetic and copies ran while one was open for 17% of the time, Pallas kernels for 0%

profile of v4, /device:TPU:1, one launch (start us, length us, event | category | flops | bytes accessed | tf_op | source)
XLA Modules:
  0.0 210.9 jit_solution(16452447150779610014)
XLA Ops:
  0.6 3.4 %serve.1 = bf16[4,3,16,4096]{3,2,1,0:T(8,128)(2,1)} custom-call(s32[8,8]{1,0:T(8,128)} %failed_ref.3, s32[8,8]{1,0:T(8,128)} %spans_ref.1, bf16[64,4096]{1,0:T(8,128)(2,1)} %bitcast.141, f32[64,4096]{1,0:T(8,128)} %bitcast.122, f32[64,4096]{1,0:T(8,128)} %bitcast.124), custom_call_target="tpu_custom_call" | custom-call | tf_op jit(solution)/shard_map/serve/pallas_call | solution.py:81
  4.1 5.0 %all-to-all-start = ((bf16[4,3,16,4096]{3,2,1,0:T(8,128)(2,1)}), bf16[4,3,16,4096]{3,2,1,0:T(8,128)(2,1)S(1)}, u32[]{:S(2)}, u32[]{:S(2)}) async-start(bf16[4,3,16,4096]{3,2,1,0:T(8,128)(2,1)} %serve.1), calls=%async_computation | async-start | bytes 3145728 | tf_op jit(solution)/shard_map/all_to_all | solution.py:25
  9.0 8.8 %collective-permute-start = (bf16[64,512]{1,0:T(8,128)(2,1)S(1)}, bf16[64,512]{1,0:T(8,128)(2,1)S(1)}, u32[]{:S(2)}, u32[]{:S(2)}) collective-permute-start(bf16[64,512]{1,0:T(8,128)(2,1)S(1)} %bitcast.157), channel_id=1, source_target_pairs={{0,4},{1,5},{2,6},{3,7},{4,0},{5,1},{6,2},{7,3},{8,12},{9,13},{10,... | collective-permute-start | bytes 196616 | tf_op jit(solution)/shard_map/ppermute | solution.py:20
  17.9 1.6 collective-permute-done
  19.5 7.0 %collective-permute-start.1 = (bf16[2,64,512]{2,1,0:T(8,128)(2,1)S(1)}, bf16[2,64,512]{2,1,0:T(8,128)(2,1)S(1)}, u32[]{:S(2)}, u32[]{:S(2)}) collective-permute-start(bf16[2,64,512]{2,1,0:T(8,128)(2,1)S(1)} %pad_maximum_fusion.4), channel_id=1, source_target_pairs={{0,2},{1,3},{2,0},{3,1},{4,6},{5,7},{6,4},{7,5},{8,10},{9,11},{10,... | collective-permute-start | bytes 393224 | tf_op jit(solution)/shard_map/ppermute | solution.py:20
  26.5 1.0 copy.32
  27.6 2.6 %collective-permute-start.4 = (bf16[512,512]{0,1:T(8,128)(2,1)}, bf16[512,512]{0,1:T(8,128)(2,1)S(1)}, u32[]{:S(2)}, u32[]{:S(2)}) collective-permute-start(bf16[512,512]{0,1:T(8,128)(2,1)} %bitcast.14), channel_id=1, source_target_pairs={{56,0},{0,8},{8,16},{16,24},{24,32},{32,40},{40,48},{48,56},{57,1}... | collective-permute-start | bytes 1572872 | tf_op jit(solution)/shard_map/ppermute | solution.py:16
  30.6 18.0 %collective-permute-start.3 = (bf16[16,4096]{1,0:T(8,128)(2,1)S(1)}, bf16[16,4096]{1,0:T(8,128)(2,1)S(1)}, u32[]{:S(2)}, u32[]{:S(2)}) collective-permute-start(bf16[16,4096]{1,0:T(8,128)(2,1)S(1)} %slice_bitcast_fusion.1), channel_id=1, source_target_pairs={{0,256},{64,320},{128,384},{192,448},{256,0},{320,64},{384,128},{4... | collective-permute-start | bytes 393224 | tf_op jit(solution)/shard_map/ppermute | solution.py:20
  49.3 4.8 %all-to-all-start.1 = ((f32[8,4,128]{2,1,0:T(4,128)}), f32[8,4,128]{2,1,0:T(4,128)S(1)}, u32[]{:S(2)}, u32[]{:S(2)}) async-start(f32[8,4,128]{2,1,0:T(4,128)} %broadcast_in_dim.18), calls=%async_computation.1 | async-start | bytes 32768 | tf_op jit(solution)/shard_map/all_to_all | solution.py:160
  54.1 3.4 %collective-permute-start.2 = (bf16[2,2,64,512]{3,2,1,0:T(8,128)(2,1)S(1)}, bf16[2,2,64,512]{3,2,1,0:T(8,128)(2,1)S(1)}, u32[]{:S(2)}, u32[]{:S(2)}) collective-permute-start(bf16[2,2,64,512]{3,2,1,0:T(8,128)(2,1)S(1)} %pad_maximum_fusion.3), channel_id=1, source_target_pairs={{0,1},{1,0},{2,3},{3,2},{4,5},{5,4},{6,7},{7,6},{8,9},{9,8},{10,11... | collective-permute-start | bytes 786440 | tf_op jit(solution)/shard_map/ppermute | solution.py:20
  57.5 5.5 %collective-permute-done.2 = bf16[2,2,64,512]{3,2,1,0:T(8,128)(2,1)S(1)} collective-permute-done((bf16[2,2,64,512]{3,2,1,0:T(8,128)(2,1)S(1)}, bf16[2,2,64,512]{3,2,1,0:T(8,128)(2,1)S(1)}, u32[]{:S(2)}, u32[]{:S(2)}) %collective-permute-start.2) | collective-permute-done | bytes 262176 | tf_op jit(solution)/shard_map/ppermute | solution.py:20
  64.8 4.2 %all-to-all-start.2 = ((bf16[4,8,16,512]{3,2,1,0:T(8,128)(2,1)}), bf16[4,8,16,512]{3,2,1,0:T(8,128)(2,1)S(1)}, u32[]{:S(2)}, u32[]{:S(2)}) async-start(bf16[4,8,16,512]{3,2,1,0:T(8,128)(2,1)} %bitcast.121), calls=%async_computation.2 | async-start | bytes 1048576 | tf_op jit(solution)/shard_map/all_to_all | solution.py:25
  69.0 6.5 %collective-permute-start.8 = (bf16[2,16,4096]{2,1,0:T(8,128)(2,1)S(1)}, bf16[2,16,4096]{2,1,0:T(8,128)(2,1)S(1)}, u32[]{:S(2)}, u32[]{:S(2)}) collective-permute-start(bf16[2,16,4096]{2,1,0:T(8,128)(2,1)S(1)} %slice.29), channel_id=1, source_target_pairs={{0,256},{64,320},{128,384},{192,448},{256,0},{320,64},{384,128},{4... | collective-permute-start | bytes 786440 | tf_op jit(solution)/shard_map/ppermute | solution.py:20
  75.5 4.6 %collective-permute-start.7 = (bf16[16,4096]{1,0:T(8,128)(2,1)S(1)}, bf16[16,4096]{1,0:T(8,128)(2,1)S(1)}, u32[]{:S(2)}, u32[]{:S(2)}) collective-permute-start(bf16[16,4096]{1,0:T(8,128)(2,1)S(1)} %fusion.28.fresh0_ref), channel_id=1, source_target_pairs={{0,192},{64,128},{128,64},{192,0},{256,448},{320,384},{384,320},{4... | collective-permute-start | bytes 393224 | tf_op jit(solution)/shard_map/ppermute | solution.py:20
  80.1 2.5 %collective-permute-start.6 = (bf16[16,4096]{1,0:T(8,128)(2,1)S(1)}, bf16[16,4096]{1,0:T(8,128)(2,1)S(1)}, u32[]{:S(2)}, u32[]{:S(2)}) collective-permute-start(bf16[16,4096]{1,0:T(8,128)(2,1)S(1)} %fusion.28.fresh0_ref), channel_id=1, source_target_pairs={{0,128},{64,192},{128,0},{192,64},{256,384},{320,448},{384,256},{4... | collective-permute-start | bytes 393224 | tf_op jit(solution)/shard_map/ppermute | solution.py:20
  82.6 1.9 collective-permute-start.5
  84.5 4.3 %collective-permute-done.8 = bf16[2,16,4096]{2,1,0:T(8,128)(2,1)S(1)} collective-permute-done((bf16[2,16,4096]{2,1,0:T(8,128)(2,1)S(1)}, bf16[2,16,4096]{2,1,0:T(8,128)(2,1)S(1)}, u32[]{:S(2)}, u32[]{:S(2)}) %collective-permute-start.8) | collective-permute-done | bytes 262176 | tf_op jit(solution)/shard_map/ppermute | solution.py:20
  89.8 2.6 %assemble.1 = (bf16[8,80,512]{2,1,0:T(8,128)(2,1)}, bf16[64,4096]{1,0:T(8,128)(2,1)}) custom-call(s32[8,8]{1,0:T(8,128)} %failed_ref.3, bf16[64,4096]{1,0:T(8,128)(2,1)} %bitcast.142, bf16[16,4096]{1,0:T(8,128)(2,1)} %copy-done.5, bf16[16,4096]{1,0:T(8,128)(2,1)} %collective-permute-done.5.fresh1_ref, bf16[16,4096]{1,0:T(8,128)(2,1)} %copy-done.10, ...), custom_call_target="tpu_custom_call" | custom-call | tf_op jit(solution)/shard_map/assemble/pallas_call | solution.py:113
  92.4 22.2 %all-to-all-start.3 = ((bf16[8,80,512]{2,1,0:T(8,128)(2,1)}), bf16[8,80,512]{2,1,0:T(8,128)(2,1)}, u32[]{:S(2)}, u32[]{:S(2)}) async-start(bf16[8,80,512]{2,1,0:T(8,128)(2,1)} %get-tuple-element.24), calls=%async_computation.3 | async-start | bytes 1310720 | tf_op jit(solution)/shard_map/all_to_all | solution.py:179
  114.5 1.3 dynamic_slice.3
  116.7 4.9 %fusion.23 = f32[64,32,8]{1,2,0:T(8,128)} fusion(f32[64,32,128]{2,1,0:T(8,128)S(1)} %bitcast.130, f32[128,8]{0,1:T(8,128)S(1)} %copy-done), kind=kOutput, calls=%fused_computation.52 | convolution fusion | flops 25165824 | bytes 1118208 | tf_op jit(solution)/shard_map/jnc,cp->jnp/dot_general | solution.py:198
  121.6 1.1 copy.38
  123.5 4.9 %fusion.25 = f32[64,32,8]{1,2,0:T(8,128)} fusion(f32[64,32,128]{2,1,0:T(8,128)S(1)} %bitcast.131, f32[128,8]{0,1:T(8,128)S(1)} %copy-done), kind=kOutput, calls=%fused_computation.54 | convolution fusion | flops 25165824 | bytes 1118208 | tf_op jit(solution)/shard_map/jnc,cp->jnp/dot_general | solution.py:198
  128.4 1.1 copy.37
  130.2 1.1 copy.48
  131.4 2.8 %fusion.21 = f32[64,32,8]{1,2,0:T(8,128)} fusion(bf16[64,32,128]{2,1,0:T(8,128)(2,1)S(1)} %bitcast.136, f32[128,8]{0,1:T(8,128)S(1)} %copy-done), kind=kOutput, calls=%fused_computation.50 | convolution fusion | flops 25165824 | bytes 593920 | tf_op jit(solution)/shard_map/jnc,cp->jnp/dot_general | solution.py:198
  134.2 1.1 copy.41
  136.9 1.1 convolution_convert_fusion.2
  138.5 1.0 all-to-all-done.3
  139.5 1.1 slice.37
  140.6 1.5 fusion.8
  142.0 9.8 %collective-permute-start.9 = (f32[4,128]{1,0:T(4,128)S(1)}, f32[4,128]{1,0:T(4,128)S(1)}, u32[]{:S(2)}, u32[]{:S(2)}) collective-permute-start(f32[4,128]{1,0:T(4,128)S(1)} %bitcast.160), channel_id=1, source_target_pairs={{0,1},{1,0},{2,3},{3,2},{4,5},{5,4},{6,7},{7,6},{8,9},{9,8},{10,11... | collective-permute-start | bytes 6152 | tf_op jit(solution)/shard_map/ppermute | solution.py:20
  151.9 0.9 slice_bitcast_fusion
  152.8 5.3 %collective-permute-start.13 = (bf16[16,4096]{1,0:T(8,128)(2,1)S(1)}, bf16[16,4096]{1,0:T(8,128)(2,1)S(1)}, u32[]{:S(2)}, u32[]{:S(2)}) collective-permute-start(bf16[16,4096]{1,0:T(8,128)(2,1)S(1)} %bitcast.152), channel_id=1, source_target_pairs={{0,256},{64,320},{128,384},{192,448},{256,0},{320,64},{384,128},{4... | collective-permute-start | bytes 393224 | tf_op jit(solution)/shard_map/ppermute | solution.py:20
  158.2 1.9 collective-permute-start.10
  160.1 1.3 convolution_convert_fusion
  161.4 6.4 %all-to-all-start.4 = ((bf16[8,64,512]{2,1,0:T(8,128)(2,1)}), bf16[8,64,512]{2,1,0:T(8,128)(2,1)S(1)}, u32[]{:S(2)}, u32[]{:S(2)}) async-start(bf16[8,64,512]{2,1,0:T(8,128)(2,1)} %bitcast.147), calls=%async_computation.4 | async-start | bytes 1048576 | tf_op jit(solution)/shard_map/all_to_all | solution.py:193
  167.8 7.6 %collective-permute-start.11 = (f32[4,128]{1,0:T(4,128)S(1)}, f32[4,128]{1,0:T(4,128)S(1)}, u32[]{:S(2)}, u32[]{:S(2)}) collective-permute-start(f32[4,128]{1,0:T(4,128)S(1)} %fusion.38), channel_id=1, source_target_pairs={{0,4},{1,5},{2,6},{3,7},{4,0},{5,1},{6,2},{7,3},{8,12},{9,13},{10,... | collective-permute-start | bytes 6152 | tf_op jit(solution)/shard_map/ppermute | solution.py:20
  175.8 1.2 fusion.20
  177.1 4.5 %collective-permute-start.15 = (bf16[34,4096]{1,0:T(8,128)(2,1)S(1)}, bf16[34,4096]{1,0:T(8,128)(2,1)S(1)}, u32[]{:S(2)}, u32[]{:S(2)}) collective-permute-start(bf16[34,4096]{1,0:T(8,128)(2,1)S(1)} %get-tuple-element.47), channel_id=1, source_target_pairs={{0,128},{64,192},{128,0},{192,64},{256,384},{320,448},{384,256},{4... | collective-permute-start | bytes 835592 | tf_op jit(solution)/shard_map/ppermute | solution.py:20
  181.6 2.2 %collective-permute-start.14 = (bf16[34,4096]{1,0:T(8,128)(2,1)S(1)}, bf16[34,4096]{1,0:T(8,128)(2,1)S(1)}, u32[]{:S(2)}, u32[]{:S(2)}) collective-permute-start(bf16[34,4096]{1,0:T(8,128)(2,1)S(1)} %get-tuple-element.47), channel_id=1, source_target_pairs={{0,64},{64,0},{128,192},{192,128},{256,320},{320,256},{384,448},{4... | collective-permute-start | bytes 835592 | tf_op jit(solution)/shard_map/ppermute | solution.py:20
  183.8 2.5 %collective-permute-start.16 = (bf16[34,4096]{1,0:T(8,128)(2,1)S(1)}, bf16[34,4096]{1,0:T(8,128)(2,1)S(1)}, u32[]{:S(2)}, u32[]{:S(2)}) collective-permute-start(bf16[34,4096]{1,0:T(8,128)(2,1)S(1)} %get-tuple-element.47), channel_id=1, source_target_pairs={{0,192},{64,128},{128,64},{192,0},{256,448},{320,384},{384,320},{4... | collective-permute-start | bytes 835592 | tf_op jit(solution)/shard_map/ppermute | solution.py:20
  186.3 1.0 collective-permute-done.11
  187.3 1.0 fusion.7
  188.4 10.6 %collective-permute-start.12 = (bf16[512,512]{0,1:T(8,128)(2,1)}, bf16[512,512]{0,1:T(8,128)(2,1)}, u32[]{:S(2)}, u32[]{:S(2)}) collective-permute-start(bf16[512,512]{0,1:T(8,128)(2,1)} %fusion.7), channel_id=1, source_target_pairs={{8,0},{16,8},{24,16},{32,24},{40,32},{48,40},{56,48},{0,56},{9,1},... | collective-permute-start | bytes 1572872 | tf_op jit(solution)/shard_map/ppermute | solution.py:16
  199.9 1.5 convert_select_fusion
  202.3 5.9 %collective-permute-done.12 = bf16[512,512]{0,1:T(8,128)(2,1)} collective-permute-done((bf16[512,512]{0,1:T(8,128)(2,1)}, bf16[512,512]{0,1:T(8,128)(2,1)}, u32[]{:S(2)}, u32[]{:S(2)}) %collective-permute-start.12) | collective-permute-done | bytes 524320 | tf_op jit(solution)/shard_map/ppermute | solution.py:16
  208.2 2.0 copy.42
  (82 shorter events, 10.8 us)
Async XLA Ops:
  0.6 116.0 %copy-start = (f32[128,8]{0,1:T(8,128)S(1)}, f32[128,8]{0,1:T(8,128)}, u32[]{:S(2)}) copy-start(f32[128,8]{0,1:T(8,128)} %param.13) | copy-start | bytes 12292
  4.1 5.0 %copy-start.11 = (bf16[1,1,512,64]{2,3,1,0:T(8,128)(2,1)S(1)}, bf16[1,1,512,64]{2,3,1,0:T(8,128)(2,1)}, u32[]{:S(2)}) copy-start(bf16[1,1,512,64]{2,3,1,0:T(8,128)(2,1)} %param.9) | copy-start | bytes 196612
  4.1 22.5 %copy-start.6 = (bf16[1,1,512,512]{3,2,1,0:T(8,128)(2,1)S(1)}, bf16[1,1,512,512]{3,2,1,0:T(8,128)(2,1)}, u32[]{:S(2)}) copy-start(bf16[1,1,512,512]{3,2,1,0:T(8,128)(2,1)} %param.8) | copy-start | bytes 1572868
  4.1 26.2 %all-to-all-start = ((bf16[4,3,16,4096]{3,2,1,0:T(8,128)(2,1)}), bf16[4,3,16,4096]{3,2,1,0:T(8,128)(2,1)S(1)}, u32[]{:S(2)}, u32[]{:S(2)}) async-start(bf16[4,3,16,4096]{3,2,1,0:T(8,128)(2,1)} %serve.1), calls=%async_computation | async-start | bytes 3145728 | tf_op jit(solution)/shard_map/all_to_all | solution.py:25
  9.0 10.5 %collective-permute-start = (bf16[64,512]{1,0:T(8,128)(2,1)S(1)}, bf16[64,512]{1,0:T(8,128)(2,1)S(1)}, u32[]{:S(2)}, u32[]{:S(2)}) collective-permute-start(bf16[64,512]{1,0:T(8,128)(2,1)S(1)} %bitcast.157), channel_id=1, source_target_pairs={{0,4},{1,5},{2,6},{3,7},{4,0},{5,1},{6,2},{7,3},{8,12},{9,13},{10,... | collective-permute-start | bytes 196616 | tf_op jit(solution)/shard_map/ppermute | solution.py:20
  19.5 10.6 %collective-permute-start.1 = (bf16[2,64,512]{2,1,0:T(8,128)(2,1)S(1)}, bf16[2,64,512]{2,1,0:T(8,128)(2,1)S(1)}, u32[]{:S(2)}, u32[]{:S(2)}) collective-permute-start(bf16[2,64,512]{2,1,0:T(8,128)(2,1)S(1)} %pad_maximum_fusion.4), channel_id=1, source_target_pairs={{0,2},{1,3},{2,0},{3,1},{4,6},{5,7},{6,4},{7,5},{8,10},{9,11},{10,... | collective-permute-start | bytes 393224 | tf_op jit(solution)/shard_map/ppermute | solution.py:20
  27.6 21.0 %collective-permute-start.4 = (bf16[512,512]{0,1:T(8,128)(2,1)}, bf16[512,512]{0,1:T(8,128)(2,1)S(1)}, u32[]{:S(2)}, u32[]{:S(2)}) collective-permute-start(bf16[512,512]{0,1:T(8,128)(2,1)} %bitcast.14), channel_id=1, source_target_pairs={{56,0},{0,8},{8,16},{16,24},{24,32},{32,40},{40,48},{48,56},{57,1}... | collective-permute-start | bytes 1572872 | tf_op jit(solution)/shard_map/ppermute | solution.py:16
  30.6 26.9 %collective-permute-start.3 = (bf16[16,4096]{1,0:T(8,128)(2,1)S(1)}, bf16[16,4096]{1,0:T(8,128)(2,1)S(1)}, u32[]{:S(2)}, u32[]{:S(2)}) collective-permute-start(bf16[16,4096]{1,0:T(8,128)(2,1)S(1)} %slice_bitcast_fusion.1), channel_id=1, source_target_pairs={{0,256},{64,320},{128,384},{192,448},{256,0},{320,64},{384,128},{4... | collective-permute-start | bytes 393224 | tf_op jit(solution)/shard_map/ppermute | solution.py:20
  49.3 14.1 %all-to-all-start.1 = ((f32[8,4,128]{2,1,0:T(4,128)}), f32[8,4,128]{2,1,0:T(4,128)S(1)}, u32[]{:S(2)}, u32[]{:S(2)}) async-start(f32[8,4,128]{2,1,0:T(4,128)} %broadcast_in_dim.18), calls=%async_computation.1 | async-start | bytes 32768 | tf_op jit(solution)/shard_map/all_to_all | solution.py:160
  54.1 8.9 %collective-permute-start.2 = (bf16[2,2,64,512]{3,2,1,0:T(8,128)(2,1)S(1)}, bf16[2,2,64,512]{3,2,1,0:T(8,128)(2,1)S(1)}, u32[]{:S(2)}, u32[]{:S(2)}) collective-permute-start(bf16[2,2,64,512]{3,2,1,0:T(8,128)(2,1)S(1)} %pad_maximum_fusion.3), channel_id=1, source_target_pairs={{0,1},{1,0},{2,3},{3,2},{4,5},{5,4},{6,7},{7,6},{8,9},{9,8},{10,11... | collective-permute-start | bytes 786440 | tf_op jit(solution)/shard_map/ppermute | solution.py:20
  57.5 25.1 %copy-start.5 = (bf16[16,4096]{1,0:T(8,128)(2,1)}, bf16[16,4096]{1,0:T(8,128)(2,1)S(1)}, u32[]{:S(2)}) copy-start(bf16[16,4096]{1,0:T(8,128)(2,1)S(1)} %fusion.28.fresh0_ref) | copy-start | bytes 393220
  64.8 24.1 %all-to-all-start.2 = ((bf16[4,8,16,512]{3,2,1,0:T(8,128)(2,1)}), bf16[4,8,16,512]{3,2,1,0:T(8,128)(2,1)S(1)}, u32[]{:S(2)}, u32[]{:S(2)}) async-start(bf16[4,8,16,512]{3,2,1,0:T(8,128)(2,1)} %bitcast.121), calls=%async_computation.2 | async-start | bytes 1048576 | tf_op jit(solution)/shard_map/all_to_all | solution.py:25
  69.0 19.8 %collective-permute-start.8 = (bf16[2,16,4096]{2,1,0:T(8,128)(2,1)S(1)}, bf16[2,16,4096]{2,1,0:T(8,128)(2,1)S(1)}, u32[]{:S(2)}, u32[]{:S(2)}) collective-permute-start(bf16[2,16,4096]{2,1,0:T(8,128)(2,1)S(1)} %slice.29), channel_id=1, source_target_pairs={{0,256},{64,320},{128,384},{192,448},{256,0},{320,64},{384,128},{4... | collective-permute-start | bytes 786440 | tf_op jit(solution)/shard_map/ppermute | solution.py:20
  75.5 13.4 %collective-permute-start.7 = (bf16[16,4096]{1,0:T(8,128)(2,1)S(1)}, bf16[16,4096]{1,0:T(8,128)(2,1)S(1)}, u32[]{:S(2)}, u32[]{:S(2)}) collective-permute-start(bf16[16,4096]{1,0:T(8,128)(2,1)S(1)} %fusion.28.fresh0_ref), channel_id=1, source_target_pairs={{0,192},{64,128},{128,64},{192,0},{256,448},{320,384},{384,320},{4... | collective-permute-start | bytes 393224 | tf_op jit(solution)/shard_map/ppermute | solution.py:20
  80.1 8.8 %collective-permute-start.6 = (bf16[16,4096]{1,0:T(8,128)(2,1)S(1)}, bf16[16,4096]{1,0:T(8,128)(2,1)S(1)}, u32[]{:S(2)}, u32[]{:S(2)}) collective-permute-start(bf16[16,4096]{1,0:T(8,128)(2,1)S(1)} %fusion.28.fresh0_ref), channel_id=1, source_target_pairs={{0,128},{64,192},{128,0},{192,64},{256,384},{320,448},{384,256},{4... | collective-permute-start | bytes 393224 | tf_op jit(solution)/shard_map/ppermute | solution.py:20
  82.6 7.1 %collective-permute-start.5 = (bf16[16,4096]{1,0:T(8,128)(2,1)S(1)}, bf16[16,4096]{1,0:T(8,128)(2,1)}, u32[]{:S(2)}, u32[]{:S(2)}) collective-permute-start(bf16[16,4096]{1,0:T(8,128)(2,1)S(1)} %fusion.28.fresh0_ref), channel_id=1, source_target_pairs={{0,64},{64,0},{128,192},{192,128},{256,320},{320,256},{384,448},{4... | collective-permute-start | bytes 393224 | tf_op jit(solution)/shard_map/ppermute | solution.py:20
  88.9 27.6 %copy-start.2 = (f32[1,1,64,4096]{3,2,1,0:T(8,128)S(1)}, f32[1,1,64,4096]{3,2,1,0:T(8,128)}, u32[]{:S(2)}) copy-start(f32[1,1,64,4096]{3,2,1,0:T(8,128)} %param.12) | copy-start | bytes 3145732
  88.9 0.8 copy-start.4
  88.9 0.8 copy-start.9
  89.0 0.8 copy-start.10
  92.4 47.1 %all-to-all-start.3 = ((bf16[8,80,512]{2,1,0:T(8,128)(2,1)}), bf16[8,80,512]{2,1,0:T(8,128)(2,1)}, u32[]{:S(2)}, u32[]{:S(2)}) async-start(bf16[8,80,512]{2,1,0:T(8,128)(2,1)} %get-tuple-element.24), calls=%async_computation.3 | async-start | bytes 1310720 | tf_op jit(solution)/shard_map/all_to_all | solution.py:179
  116.7 6.7 %copy-start.1 = (f32[1,1,64,4096]{3,2,1,0:T(8,128)S(1)}, f32[1,1,64,4096]{3,2,1,0:T(8,128)}, u32[]{:S(2)}) copy-start(f32[1,1,64,4096]{3,2,1,0:T(8,128)} %param.11) | copy-start | bytes 3145732
  142.0 16.1 %collective-permute-start.9 = (f32[4,128]{1,0:T(4,128)S(1)}, f32[4,128]{1,0:T(4,128)S(1)}, u32[]{:S(2)}, u32[]{:S(2)}) collective-permute-start(f32[4,128]{1,0:T(4,128)S(1)} %bitcast.160), channel_id=1, source_target_pairs={{0,1},{1,0},{2,3},{3,2},{4,5},{5,4},{6,7},{7,6},{8,9},{9,8},{10,11... | collective-permute-start | bytes 6152 | tf_op jit(solution)/shard_map/ppermute | solution.py:20
  152.8 23.0 %collective-permute-start.13 = (bf16[16,4096]{1,0:T(8,128)(2,1)S(1)}, bf16[16,4096]{1,0:T(8,128)(2,1)S(1)}, u32[]{:S(2)}, u32[]{:S(2)}) collective-permute-start(bf16[16,4096]{1,0:T(8,128)(2,1)S(1)} %bitcast.152), channel_id=1, source_target_pairs={{0,256},{64,320},{128,384},{192,448},{256,0},{320,64},{384,128},{4... | collective-permute-start | bytes 393224 | tf_op jit(solution)/shard_map/ppermute | solution.py:20
  158.2 9.6 %collective-permute-start.10 = (f32[4,128]{1,0:T(4,128)S(1)}, f32[4,128]{1,0:T(4,128)S(1)}, u32[]{:S(2)}, u32[]{:S(2)}) collective-permute-start(f32[4,128]{1,0:T(4,128)S(1)} %bitcast_add_fusion), channel_id=1, source_target_pairs={{0,2},{1,3},{2,0},{3,1},{4,6},{5,7},{6,4},{7,5},{8,10},{9,11},{10,... | collective-permute-start | bytes 6152 | tf_op jit(solution)/shard_map/ppermute | solution.py:20
  161.4 48.9 %all-to-all-start.4 = ((bf16[8,64,512]{2,1,0:T(8,128)(2,1)}), bf16[8,64,512]{2,1,0:T(8,128)(2,1)S(1)}, u32[]{:S(2)}, u32[]{:S(2)}) async-start(bf16[8,64,512]{2,1,0:T(8,128)(2,1)} %bitcast.147), calls=%async_computation.4 | async-start | bytes 1048576 | tf_op jit(solution)/shard_map/all_to_all | solution.py:193
  167.8 19.6 %copy-start.3 = (f32[512,512]{0,1:T(8,128)S(1)}, f32[512,512]{0,1:T(8,128)}, u32[]{:S(2)}) copy-start(f32[512,512]{0,1:T(8,128)} %get-tuple-element.55) | copy-start | bytes 3145732
  167.8 19.5 %collective-permute-start.11 = (f32[4,128]{1,0:T(4,128)S(1)}, f32[4,128]{1,0:T(4,128)S(1)}, u32[]{:S(2)}, u32[]{:S(2)}) collective-permute-start(f32[4,128]{1,0:T(4,128)S(1)} %fusion.38), channel_id=1, source_target_pairs={{0,4},{1,5},{2,6},{3,7},{4,0},{5,1},{6,2},{7,3},{8,12},{9,13},{10,... | collective-permute-start | bytes 6152 | tf_op jit(solution)/shard_map/ppermute | solution.py:20
  177.1 21.8 %collective-permute-start.15 = (bf16[34,4096]{1,0:T(8,128)(2,1)S(1)}, bf16[34,4096]{1,0:T(8,128)(2,1)S(1)}, u32[]{:S(2)}, u32[]{:S(2)}) collective-permute-start(bf16[34,4096]{1,0:T(8,128)(2,1)S(1)} %get-tuple-element.47), channel_id=1, source_target_pairs={{0,128},{64,192},{128,0},{192,64},{256,384},{320,448},{384,256},{4... | collective-permute-start | bytes 835592 | tf_op jit(solution)/shard_map/ppermute | solution.py:20
  181.6 17.4 %collective-permute-start.14 = (bf16[34,4096]{1,0:T(8,128)(2,1)S(1)}, bf16[34,4096]{1,0:T(8,128)(2,1)S(1)}, u32[]{:S(2)}, u32[]{:S(2)}) collective-permute-start(bf16[34,4096]{1,0:T(8,128)(2,1)S(1)} %get-tuple-element.47), channel_id=1, source_target_pairs={{0,64},{64,0},{128,192},{192,128},{256,320},{320,256},{384,448},{4... | collective-permute-start | bytes 835592 | tf_op jit(solution)/shard_map/ppermute | solution.py:20
  183.8 15.2 %collective-permute-start.16 = (bf16[34,4096]{1,0:T(8,128)(2,1)S(1)}, bf16[34,4096]{1,0:T(8,128)(2,1)S(1)}, u32[]{:S(2)}, u32[]{:S(2)}) collective-permute-start(bf16[34,4096]{1,0:T(8,128)(2,1)S(1)} %get-tuple-element.47), channel_id=1, source_target_pairs={{0,192},{64,128},{128,64},{192,0},{256,448},{320,384},{384,320},{4... | collective-permute-start | bytes 835592 | tf_op jit(solution)/shard_map/ppermute | solution.py:20
  188.4 19.8 %collective-permute-start.12 = (bf16[512,512]{0,1:T(8,128)(2,1)}, bf16[512,512]{0,1:T(8,128)(2,1)}, u32[]{:S(2)}, u32[]{:S(2)}) collective-permute-start(bf16[512,512]{0,1:T(8,128)(2,1)} %fusion.7), channel_id=1, source_target_pairs={{8,0},{16,8},{24,16},{32,24},{40,32},{48,40},{56,48},{0,56},{9,1},... | collective-permute-start | bytes 1572872 | tf_op jit(solution)/shard_map/ppermute | solution.py:16
  199.9 1.7 copy-start.7
  199.9 1.7 copy-start.8

commit v5 on v4

--- a/solution.py
+++ b/solution.py
@@ -57,32 +57,38 @@
     return lax.optimization_barrier((value,) + after)[0]
 
 
-def serve_kernel(failed_ref, spans_ref, weight_ref, first_ref, second_ref, out_ref):
+def serve_kernel(failed_ref, spans_ref, weight_ref, first_ref, second_ref, weight_out_ref, moments_out_ref):
     section = lax.axis_index("section")
     me = lax.axis_index("replica")
     failed = failed_ref[section, lax.axis_index("tensor")]
     is_primary = (failed ^ PLANE) == me
     is_second = (failed ^ 1) == me
-    part = out_ref.shape[2]
+    part = weight_out_ref.shape[1]
     for n in range(weight_ref.shape[1] // SPAN):
         listed = spans_ref[section, 0] == n
         for j in range(1, spans_ref.shape[1]):
             listed = listed | (spans_ref[section, j] == n)
         take = (listed & is_second) | (jnp.logical_not(listed) & is_primary)
         here = pl.ds(n * SPAN, SPAN)
-        for k, ref in enumerate((weight_ref, first_ref, second_ref)):
-            for x in range(PLANE):
-                block = ref[x * part : (x + 1) * part, here].astype(SHORT)
-                out_ref[x, k, :, here] = jnp.where(take, block, jnp.zeros_like(block))
+        for x in range(PLANE):
+            at = pl.ds(x * part, part)
+            block = weight_ref[at, here]
+            weight_out_ref[x, :, here] = jnp.where(take, block, jnp.zeros_like(block))
+            for k, ref in enumerate((first_ref, second_ref)):
+                block = ref[at, here].astype(SHORT)
+                moments_out_ref[x, k, :, here] = jnp.where(take, block, jnp.zeros_like(block))
 
 
 def serve(failed, spans, weight, first, second):
     rows, width = weight.shape
     return pl.pallas_call(
         serve_kernel,
-        out_shape=jax.ShapeDtypeStruct((PLANE, 3, rows // PLANE, width), SHORT),
+        out_shape=(
+            jax.ShapeDtypeStruct((PLANE, rows // PLANE, width), SHORT),
+            jax.ShapeDtypeStruct((PLANE, 2, rows // PLANE, width), SHORT),
+        ),
         in_specs=[pl.BlockSpec(memory_space=pltpu.SMEM)] * 2 + [pl.BlockSpec(memory_space=pltpu.VMEM)] * 3,
-        out_specs=pl.BlockSpec(memory_space=pltpu.VMEM),
+        out_specs=(pl.BlockSpec(memory_space=pltpu.VMEM),) * 2,
         name="serve",
     )(failed, spans, weight, first, second)
 
@@ -153,22 +159,26 @@
     incoming = from_behind(local, "section", 1)
     x = incoming.astype(WIDE)
 
-    mask = serve(failed_replica, resend_spans, own_weight, own_first, own_second)
-    served = jnp.sum(exchange_x(mask).astype(WIDE), axis=0).astype(SHORT)
+    def summed(parts):
+        return jnp.sum(parts.astype(WIDE), axis=0).astype(SHORT)
+
+    mask_weight, mask_moments = serve(failed_replica, resend_spans, own_weight, own_first, own_second)
+    served_weight = summed(exchange_x(mask_weight))
+    served_moments = summed(exchange_x(tied(mask_moments, served_weight)))
 
     squares = jnp.sum(x * x, axis=1).reshape(1, -1, 128)
     squares = lax.all_to_all(jnp.broadcast_to(squares, (8,) + squares.shape[1:]), "tensor", 0, 0, tiled=True)
-    held = tied(key_grads[0, 0].T, mask)
-    held = doubled(doubled(held, my_tensor, 0), my_tensor, 1)
-    held, served = lax.optimization_barrier((held, served))
-    fresh_weight = served[0] + swap(served[0], "replica", PLANE)
+    held = doubled(tied(key_grads[0, 0].T, mask_weight), my_tensor, 0)
+    held, served_weight = lax.optimization_barrier((held, served_weight))
+    fresh_weight = served_weight + swap(served_weight, "replica", PLANE)
+    held = doubled(held, my_tensor, 1)
+    held, fresh_weight, served_moments = lax.optimization_barrier((held, fresh_weight, served_moments))
+    fresh_moments = served_moments + swap(served_moments, "replica", PLANE)
+    fresh_weight = [fresh_weight] + [swap(fresh_weight, "replica", bit) for bit in (1, 2, 3)]
     held = doubled(held, my_tensor, 2)
     held, fresh_weight, squares = lax.optimization_barrier((held, fresh_weight, squares))
-    served_moments = tied(served[1:], fresh_weight)
-    fresh_moments = served_moments + swap(served_moments, "replica", PLANE)
     kg_all = held.reshape(8 * rows, tokens)
     inverse_rms = 1.0 / jnp.sqrt(jnp.sum(squares, axis=0).reshape(tokens) / width + 1e-05)
-    fresh_weight = [fresh_weight] + [swap(fresh_weight, "replica", bit) for bit in (1, 2, 3)]
 
     normed = (x * inverse_rms[:, None]).astype(SHORT)
     grad = lax.dot_general(kg_all, normed, (((1,), (0,)), ((), ())), preferred_element_type=WIDE).astype(SHORT)

time: 212 us -> 228 us (1.075)
  waiting for transfers between devices: 20.9 us -> 30.8 us
  local copies, waits for them, and re-layouts: 15.5 us -> 20.5 us
    ppermute x15, starting transfers between devices: 86.5 us -> 72.7 us  [swap(): lax.ppermute(block, axis, [(i, i ^ bit) for i in range(lax.axis_size(axis...]
    ppermute x15, waiting for transfers between devices: 13.6 us -> 25.7 us  [swap(): lax.ppermute(block, axis, [(i, i ^ bit) for i in range(lax.axis_size(axis...]
    all_to_all x1, starting transfers between devices: 22.2 us -> 27.7 us  [shards(): got = lax.all_to_all(sent, 'tensor', 0, 0, tiled=True)]
    all_to_all x2 -> x3, starting transfers between devices: 9.19 us -> 13.1 us  [exchange_x(): lax.all_to_all(block, 'replica', 0, 0, axis_index_groups=groups, tiled=True)]
    unnamed x32 -> x40, local copies, waits for them, and re-layouts: 6.35 us -> 7.3 us
  transfers between devices with their start and end apart: 22 -> 23, of which waited for: 9 -> 6; matrix products, arithmetic and copies ran while one was open for 17% -> 18% of each run, Pallas kernels for 0% -> 0%
where the time goes in v5:
time: 228 us; the launch traced here: 226 us
  starting transfers between devices  142 us (62%)
  waiting for transfers between devices  30.8 us (14%)
  local copies, waits for them, and re-layouts  20.5 us (9%)
  matrix products  17.5 us (8%)
  other arithmetic  7.76 us (3%)
  Pallas kernels  5.97 us (3%)
    ppermute x15, starting transfers between devices, swap(): lax.ppermute(block, axis, [(i, i ^ bit) for i in range(lax.axis_size(axis...  72.7 us
    all_to_all x1, starting transfers between devices, shards(): got = lax.all_to_all(sent, 'tensor', 0, 0, tiled=True)  27.7 us
    ppermute x15, waiting for transfers between devices, swap(): lax.ppermute(block, axis, [(i, i ^ bit) for i in range(lax.axis_size(axis...  25.7 us
    ppermute x2, starting transfers between devices, from_behind(): lax.ppermute(block, axis, [((i - distance) % n, i) for i in range(n)])  14.9 us
    dot_general x4, matrix products, checksum(): jnp.einsum('jnc,cp->jnp', shaped, probe_matrix, precision=lax.Precision.H...  14.3 us
    all_to_all x3, starting transfers between devices, exchange_x(): lax.all_to_all(block, 'replica', 0, 0, axis_index_groups=groups, tiled=True)  13.1 us
    unnamed x40, local copies, waits for them, and re-layouts  7.3 us
    all_to_all x1, starting transfers between devices, shards(): lax.all_to_all(jnp.broadcast_to(squares, (8,) + squares.shape[1:]), 'tens...  6.7 us
  transfers between devices with their start and end apart: 23, of which 6 were waited for; matrix products, arithmetic and copies ran while one was open for 18% of the time, Pallas kernels for 0%

profile of v5, /device:TPU:1, one launch (start us, length us, event | category | flops | bytes accessed | tf_op | source)
XLA Modules:
  0.0 226.1 jit_solution(10204677487491371604)
XLA Ops:
  0.7 3.4 %serve.1 = (bf16[4,16,4096]{2,1,0:T(8,128)(2,1)}, bf16[4,2,16,4096]{3,2,1,0:T(8,128)(2,1)}) custom-call(s32[8,8]{1,0:T(8,128)} %failed_ref.3, s32[8,8]{1,0:T(8,128)} %spans_ref.1, bf16[64,4096]{1,0:T(8,128)(2,1)} %bitcast.131, f32[64,4096]{1,0:T(8,128)} %bitcast.118, f32[64,4096]{1,0:T(8,128)} %bitcast.120), custom_call_target="tpu_custom_call" | custom-call | tf_op jit(solution)/shard_map/serve/pallas_call | solution.py:84
  4.1 4.8 %all-to-all-start = ((bf16[4,16,4096]{2,1,0:T(8,128)(2,1)}), bf16[4,16,4096]{2,1,0:T(8,128)(2,1)S(1)}, u32[]{:S(2)}, u32[]{:S(2)}) async-start(bf16[4,16,4096]{2,1,0:T(8,128)(2,1)} %get-tuple-element.24), calls=%async_computation | async-start | bytes 1048576 | tf_op jit(solution)/shard_map/all_to_all | solution.py:25
  8.9 8.8 %collective-permute-start = (bf16[64,512]{1,0:T(8,128)(2,1)S(1)}, bf16[64,512]{1,0:T(8,128)(2,1)S(1)}, u32[]{:S(2)}, u32[]{:S(2)}) collective-permute-start(bf16[64,512]{1,0:T(8,128)(2,1)S(1)} %bitcast.154), channel_id=1, source_target_pairs={{0,4},{1,5},{2,6},{3,7},{4,0},{5,1},{6,2},{7,3},{8,12},{9,13},{10,... | collective-permute-start | bytes 196616 | tf_op jit(solution)/shard_map/ppermute | solution.py:20
  17.8 4.4 %all-to-all-start.1 = ((bf16[4,2,16,4096]{3,2,1,0:T(8,128)(2,1)}), bf16[4,2,16,4096]{3,2,1,0:T(8,128)(2,1)S(1)}, u32[]{:S(2)}, u32[]{:S(2)}) async-start(bf16[4,2,16,4096]{3,2,1,0:T(8,128)(2,1)} %get-tuple-element.29), calls=%async_computation.1 | async-start | bytes 2097152 | tf_op jit(solution)/shard_map/all_to_all | solution.py:25
  22.3 15.6 %collective-permute-start.2 = (bf16[16,4096]{1,0:T(8,128)(2,1)S(1)}, bf16[16,4096]{1,0:T(8,128)(2,1)S(1)}, u32[]{:S(2)}, u32[]{:S(2)}) collective-permute-start(bf16[16,4096]{1,0:T(8,128)(2,1)S(1)} %reduce_sum.63), channel_id=1, source_target_pairs={{0,256},{64,320},{128,384},{192,448},{256,0},{320,64},{384,128},{4... | collective-permute-start | bytes 393224 | tf_op jit(solution)/shard_map/ppermute | solution.py:20
  37.9 1.9 collective-permute-start.1
  40.1 3.6 %collective-permute-start.7 = (bf16[512,512]{0,1:T(8,128)(2,1)S(1)}, bf16[512,512]{0,1:T(8,128)(2,1)S(1)}, u32[]{:S(2)}, u32[]{:S(2)}) collective-permute-start(bf16[512,512]{0,1:T(8,128)(2,1)S(1)} %bitcast.145), channel_id=1, source_target_pairs={{56,0},{0,8},{8,16},{16,24},{24,32},{32,40},{40,48},{48,56},{57,1}... | collective-permute-start | bytes 1572872 | tf_op jit(solution)/shard_map/ppermute | solution.py:16
  43.8 11.3 %collective-permute-done.1 = bf16[2,64,512]{2,1,0:T(8,128)(2,1)S(1)} collective-permute-done((bf16[2,64,512]{2,1,0:T(8,128)(2,1)S(1)}, bf16[2,64,512]{2,1,0:T(8,128)(2,1)S(1)}, u32[]{:S(2)}, u32[]{:S(2)}) %collective-permute-start.1) | collective-permute-done | bytes 131104 | tf_op jit(solution)/shard_map/ppermute | solution.py:20
  55.4 1.9 collective-permute-start.3
  58.1 6.7 %all-to-all-start.2 = ((f32[8,4,128]{2,1,0:T(4,128)}), f32[8,4,128]{2,1,0:T(4,128)S(1)}, u32[]{:S(2)}, u32[]{:S(2)}) async-start(f32[8,4,128]{2,1,0:T(4,128)} %broadcast_in_dim.18), calls=%async_computation.2 | async-start | bytes 32768 | tf_op jit(solution)/shard_map/all_to_all | solution.py:170
  64.8 4.5 %collective-permute-start.6 = (bf16[16,4096]{1,0:T(8,128)(2,1)S(1)}, bf16[16,4096]{1,0:T(8,128)(2,1)S(1)}, u32[]{:S(2)}, u32[]{:S(2)}) collective-permute-start(bf16[16,4096]{1,0:T(8,128)(2,1)S(1)} %add.65.fresh0_ref), channel_id=1, source_target_pairs={{0,192},{64,128},{128,64},{192,0},{256,448},{320,384},{384,320},{4... | collective-permute-start | bytes 393224 | tf_op jit(solution)/shard_map/ppermute | solution.py:20
  69.3 2.5 %collective-permute-start.5 = (bf16[16,4096]{1,0:T(8,128)(2,1)S(1)}, bf16[16,4096]{1,0:T(8,128)(2,1)S(1)}, u32[]{:S(2)}, u32[]{:S(2)}) collective-permute-start(bf16[16,4096]{1,0:T(8,128)(2,1)S(1)} %add.65.fresh0_ref), channel_id=1, source_target_pairs={{0,128},{64,192},{128,0},{192,64},{256,384},{320,448},{384,256},{4... | collective-permute-start | bytes 393224 | tf_op jit(solution)/shard_map/ppermute | solution.py:20
  71.8 2.0 collective-permute-start.4
  74.1 2.4 %collective-permute-done.5.fresh2_ref = bf16[16,4096]{1,0:T(8,128)(2,1)S(1)} collective-permute-done((bf16[16,4096]{1,0:T(8,128)(2,1)S(1)}, bf16[16,4096]{1,0:T(8,128)(2,1)S(1)}, u32[]{:S(2)}, u32[]{:S(2)}) %collective-permute-start.5) | collective-permute-done | bytes 131104 | tf_op jit(solution)/shard_map/ppermute | solution.py:20
  76.5 1.3 collective-permute-done.4.fresh1_ref
  79.2 3.9 %all-to-all-start.3 = ((bf16[4,8,16,512]{3,2,1,0:T(8,128)(2,1)}), bf16[4,8,16,512]{3,2,1,0:T(8,128)(2,1)S(1)}, u32[]{:S(2)}, u32[]{:S(2)}) async-start(bf16[4,8,16,512]{3,2,1,0:T(8,128)(2,1)} %bitcast.117), calls=%async_computation.3 | async-start | bytes 1048576 | tf_op jit(solution)/shard_map/all_to_all | solution.py:25
  83.0 5.4 %collective-permute-start.8 = (bf16[2,16,4096]{2,1,0:T(8,128)(2,1)S(1)}, bf16[2,16,4096]{2,1,0:T(8,128)(2,1)S(1)}, u32[]{:S(2)}, u32[]{:S(2)}) collective-permute-start(bf16[2,16,4096]{2,1,0:T(8,128)(2,1)S(1)} %reduce_sum.64), channel_id=1, source_target_pairs={{0,256},{64,320},{128,384},{192,448},{256,0},{320,64},{384,128},{4... | collective-permute-start | bytes 786440 | tf_op jit(solution)/shard_map/ppermute | solution.py:20
  88.5 10.7 %collective-permute-done.8 = bf16[2,16,4096]{2,1,0:T(8,128)(2,1)S(1)} collective-permute-done((bf16[2,16,4096]{2,1,0:T(8,128)(2,1)S(1)}, bf16[2,16,4096]{2,1,0:T(8,128)(2,1)S(1)}, u32[]{:S(2)}, u32[]{:S(2)}) %collective-permute-start.8) | collective-permute-done | bytes 262176 | tf_op jit(solution)/shard_map/ppermute | solution.py:20
  100.0 2.6 %assemble.1 = (bf16[8,80,512]{2,1,0:T(8,128)(2,1)}, bf16[64,4096]{1,0:T(8,128)(2,1)}) custom-call(s32[8,8]{1,0:T(8,128)} %failed_ref.3, bf16[64,4096]{1,0:T(8,128)(2,1)} %bitcast.132, bf16[16,4096]{1,0:T(8,128)(2,1)} %copy-done.7, bf16[16,4096]{1,0:T(8,128)(2,1)} %copy-done.13, bf16[16,4096]{1,0:T(8,128)(2,1)} %copy-done.12, bf16[16,4096]{1,0:T(8,128)(2,1)} %copy-done.11, ...), custom_call_target="tpu_custom_call" | custom-call | tf_op jit(solution)/shard_map/assemble/pallas_call | solution.py:119
  102.6 27.7 %all-to-all-start.4 = ((bf16[8,80,512]{2,1,0:T(8,128)(2,1)}), bf16[8,80,512]{2,1,0:T(8,128)(2,1)S(1)}, u32[]{:S(2)}, u32[]{:S(2)}) async-start(bf16[8,80,512]{2,1,0:T(8,128)(2,1)} %get-tuple-element.40), calls=%async_computation.4 | async-start | bytes 1310720 | tf_op jit(solution)/shard_map/all_to_all | solution.py:189
  130.3 1.3 dynamic_slice.3
  132.5 4.9 %fusion.23 = f32[64,32,8]{1,2,0:T(8,128)} fusion(f32[64,32,128]{2,1,0:T(8,128)S(1)} %bitcast.126, f32[128,8]{0,1:T(8,128)S(1)} %copy-done), kind=kOutput, calls=%fused_computation.51 | convolution fusion | flops 25165824 | bytes 1118208 | tf_op jit(solution)/shard_map/jnc,cp->jnp/dot_general | solution.py:208
  137.3 1.7 copy.36
  139.1 1.6 copy.38
  140.9 4.9 %fusion.25 = f32[64,32,8]{1,2,0:T(8,128)} fusion(f32[64,32,128]{2,1,0:T(8,128)S(1)} %bitcast.127, f32[128,8]{0,1:T(8,128)S(1)} %copy-done), kind=kOutput, calls=%fused_computation.53 | convolution fusion | flops 25165824 | bytes 1118208 | tf_op jit(solution)/shard_map/jnc,cp->jnp/dot_general | solution.py:208
  145.7 1.7 copy.35
  147.5 1.6 copy.37
  149.1 1.1 copy.46
  150.2 2.8 %fusion.21 = f32[64,32,8]{1,2,0:T(8,128)} fusion(bf16[64,32,128]{2,1,0:T(8,128)(2,1)S(1)} %bitcast.134, f32[128,8]{0,1:T(8,128)S(1)} %copy-done), kind=kOutput, calls=%fused_computation.49 | convolution fusion | flops 25165824 | bytes 593920 | tf_op jit(solution)/shard_map/jnc,cp->jnp/dot_general | solution.py:208
  153.1 1.7 copy.39
  154.8 1.6 copy.41
  157.3 1.8 convolution_convert_fusion.2
  162.0 1.5 fusion.8
  163.4 4.0 %collective-permute-start.9 = (f32[4,128]{1,0:T(4,128)S(1)}, f32[4,128]{1,0:T(4,128)S(1)}, u32[]{:S(2)}, u32[]{:S(2)}) collective-permute-start(f32[4,128]{1,0:T(4,128)S(1)} %bitcast.157), channel_id=1, source_target_pairs={{0,1},{1,0},{2,3},{3,2},{4,5},{5,4},{6,7},{7,6},{8,9},{9,8},{10,11... | collective-permute-start | bytes 6152 | tf_op jit(solution)/shard_map/ppermute | solution.py:20
  167.5 5.5 %collective-permute-start.13 = (bf16[16,4096]{1,0:T(8,128)(2,1)S(1)}, bf16[16,4096]{1,0:T(8,128)(2,1)S(1)}, u32[]{:S(2)}, u32[]{:S(2)}) collective-permute-start(bf16[16,4096]{1,0:T(8,128)(2,1)S(1)} %bitcast.149), channel_id=1, source_target_pairs={{0,256},{64,320},{128,384},{192,448},{256,0},{320,64},{384,128},{4... | collective-permute-start | bytes 393224 | tf_op jit(solution)/shard_map/ppermute | solution.py:20
  173.0 3.3 %collective-permute-start.10 = (f32[4,128]{1,0:T(4,128)S(1)}, f32[4,128]{1,0:T(4,128)S(1)}, u32[]{:S(2)}, u32[]{:S(2)}) collective-permute-start(f32[4,128]{1,0:T(4,128)S(1)} %bitcast_add_fusion), channel_id=1, source_target_pairs={{0,2},{1,3},{2,0},{3,1},{4,6},{5,7},{6,4},{7,5},{8,10},{9,11},{10,... | collective-permute-start | bytes 6152 | tf_op jit(solution)/shard_map/ppermute | solution.py:20
  176.3 1.3 convolution_convert_fusion
  177.6 6.5 %all-to-all-start.5 = ((bf16[8,64,512]{2,1,0:T(8,128)(2,1)}), bf16[8,64,512]{2,1,0:T(8,128)(2,1)S(1)}, u32[]{:S(2)}, u32[]{:S(2)}) async-start(bf16[8,64,512]{2,1,0:T(8,128)(2,1)} %bitcast.143), calls=%async_computation.5 | async-start | bytes 1048576 | tf_op jit(solution)/shard_map/all_to_all | solution.py:203
  184.1 7.6 %collective-permute-start.11 = (f32[4,128]{1,0:T(4,128)S(1)}, f32[4,128]{1,0:T(4,128)S(1)}, u32[]{:S(2)}, u32[]{:S(2)}) collective-permute-start(f32[4,128]{1,0:T(4,128)S(1)} %fusion.37), channel_id=1, source_target_pairs={{0,4},{1,5},{2,6},{3,7},{4,0},{5,1},{6,2},{7,3},{8,12},{9,13},{10,... | collective-permute-start | bytes 6152 | tf_op jit(solution)/shard_map/ppermute | solution.py:20
  191.7 1.2 fusion.20
  193.0 4.9 %collective-permute-start.15 = (bf16[34,4096]{1,0:T(8,128)(2,1)S(1)}, bf16[34,4096]{1,0:T(8,128)(2,1)S(1)}, u32[]{:S(2)}, u32[]{:S(2)}) collective-permute-start(bf16[34,4096]{1,0:T(8,128)(2,1)S(1)} %get-tuple-element.63), channel_id=1, source_target_pairs={{0,128},{64,192},{128,0},{192,64},{256,384},{320,448},{384,256},{4... | collective-permute-start | bytes 835592 | tf_op jit(solution)/shard_map/ppermute | solution.py:20
  197.9 2.2 collective-permute-start.14
  200.1 2.5 %collective-permute-start.16 = (bf16[34,4096]{1,0:T(8,128)(2,1)S(1)}, bf16[34,4096]{1,0:T(8,128)(2,1)S(1)}, u32[]{:S(2)}, u32[]{:S(2)}) collective-permute-start(bf16[34,4096]{1,0:T(8,128)(2,1)S(1)} %get-tuple-element.63), channel_id=1, source_target_pairs={{0,192},{64,128},{128,64},{192,0},{256,448},{320,384},{384,320},{4... | collective-permute-start | bytes 835592 | tf_op jit(solution)/shard_map/ppermute | solution.py:20
  202.7 1.0 fusion.7
  203.7 11.3 %collective-permute-start.12 = (bf16[512,512]{0,1:T(8,128)(2,1)}, bf16[512,512]{0,1:T(8,128)(2,1)}, u32[]{:S(2)}, u32[]{:S(2)}) collective-permute-start(bf16[512,512]{0,1:T(8,128)(2,1)} %fusion.7), channel_id=1, source_target_pairs={{8,0},{16,8},{24,16},{32,24},{40,32},{48,40},{56,48},{0,56},{9,1},... | collective-permute-start | bytes 1572872 | tf_op jit(solution)/shard_map/ppermute | solution.py:16
  216.0 1.5 convert_select_fusion
  218.4 4.9 %collective-permute-done.12 = bf16[512,512]{0,1:T(8,128)(2,1)} collective-permute-done((bf16[512,512]{0,1:T(8,128)(2,1)}, bf16[512,512]{0,1:T(8,128)(2,1)}, u32[]{:S(2)}, u32[]{:S(2)}) %collective-permute-start.12) | collective-permute-done | bytes 524320 | tf_op jit(solution)/shard_map/ppermute | solution.py:16
  223.3 2.0 copy.40
  (91 shorter events, 10.7 us)
Async XLA Ops:
  0.6 131.8 %copy-start = (f32[128,8]{0,1:T(8,128)S(1)}, f32[128,8]{0,1:T(8,128)}, u32[]{:S(2)}) copy-start(f32[128,8]{0,1:T(8,128)} %param.13) | copy-start | bytes 12292
  0.6 8.3 %copy-start.15 = (bf16[1,1,512,64]{2,3,1,0:T(8,128)(2,1)S(1)}, bf16[1,1,512,64]{2,3,1,0:T(8,128)(2,1)}, u32[]{:S(2)}) copy-start(bf16[1,1,512,64]{2,3,1,0:T(8,128)(2,1)} %param.9) | copy-start | bytes 196612
  4.1 13.7 %all-to-all-start = ((bf16[4,16,4096]{2,1,0:T(8,128)(2,1)}), bf16[4,16,4096]{2,1,0:T(8,128)(2,1)S(1)}, u32[]{:S(2)}, u32[]{:S(2)}) async-start(bf16[4,16,4096]{2,1,0:T(8,128)(2,1)} %get-tuple-element.24), calls=%async_computation | async-start | bytes 1048576 | tf_op jit(solution)/shard_map/all_to_all | solution.py:25
  8.9 13.3 %collective-permute-start = (bf16[64,512]{1,0:T(8,128)(2,1)S(1)}, bf16[64,512]{1,0:T(8,128)(2,1)S(1)}, u32[]{:S(2)}, u32[]{:S(2)}) collective-permute-start(bf16[64,512]{1,0:T(8,128)(2,1)S(1)} %bitcast.154), channel_id=1, source_target_pairs={{0,4},{1,5},{2,6},{3,7},{4,0},{5,1},{6,2},{7,3},{8,12},{9,13},{10,... | collective-permute-start | bytes 196616 | tf_op jit(solution)/shard_map/ppermute | solution.py:20
  17.8 22.0 %copy-start.8 = (bf16[1,1,512,512]{3,2,1,0:T(8,128)(2,1)S(1)}, bf16[1,1,512,512]{3,2,1,0:T(8,128)(2,1)}, u32[]{:S(2)}) copy-start(bf16[1,1,512,512]{3,2,1,0:T(8,128)(2,1)} %param.8) | copy-start | bytes 1572868
  17.8 37.3 %all-to-all-start.1 = ((bf16[4,2,16,4096]{3,2,1,0:T(8,128)(2,1)}), bf16[4,2,16,4096]{3,2,1,0:T(8,128)(2,1)S(1)}, u32[]{:S(2)}, u32[]{:S(2)}) async-start(bf16[4,2,16,4096]{3,2,1,0:T(8,128)(2,1)} %get-tuple-element.29), calls=%async_computation.1 | async-start | bytes 2097152 | tf_op jit(solution)/shard_map/all_to_all | solution.py:25
  22.3 21.4 %collective-permute-start.2 = (bf16[16,4096]{1,0:T(8,128)(2,1)S(1)}, bf16[16,4096]{1,0:T(8,128)(2,1)S(1)}, u32[]{:S(2)}, u32[]{:S(2)}) collective-permute-start(bf16[16,4096]{1,0:T(8,128)(2,1)S(1)} %reduce_sum.63), channel_id=1, source_target_pairs={{0,256},{64,320},{128,384},{192,448},{256,0},{320,64},{384,128},{4... | collective-permute-start | bytes 393224 | tf_op jit(solution)/shard_map/ppermute | solution.py:20
  37.9 17.1 %collective-permute-start.1 = (bf16[2,64,512]{2,1,0:T(8,128)(2,1)S(1)}, bf16[2,64,512]{2,1,0:T(8,128)(2,1)S(1)}, u32[]{:S(2)}, u32[]{:S(2)}) collective-permute-start(bf16[2,64,512]{2,1,0:T(8,128)(2,1)S(1)} %pad_maximum_fusion.4), channel_id=1, source_target_pairs={{0,2},{1,3},{2,0},{3,1},{4,6},{5,7},{6,4},{7,5},{8,10},{9,11},{10,... | collective-permute-start | bytes 393224 | tf_op jit(solution)/shard_map/ppermute | solution.py:20
  40.1 17.2 %collective-permute-start.7 = (bf16[512,512]{0,1:T(8,128)(2,1)S(1)}, bf16[512,512]{0,1:T(8,128)(2,1)S(1)}, u32[]{:S(2)}, u32[]{:S(2)}) collective-permute-start(bf16[512,512]{0,1:T(8,128)(2,1)S(1)} %bitcast.145), channel_id=1, source_target_pairs={{56,0},{0,8},{8,16},{16,24},{24,32},{32,40},{40,48},{48,56},{57,1}... | collective-permute-start | bytes 1572872 | tf_op jit(solution)/shard_map/ppermute | solution.py:16
  43.7 28.0 %copy-start.7 = (bf16[16,4096]{1,0:T(8,128)(2,1)}, bf16[16,4096]{1,0:T(8,128)(2,1)S(1)}, u32[]{:S(2)}) copy-start(bf16[16,4096]{1,0:T(8,128)(2,1)S(1)} %add.65.fresh0_ref) | copy-start | bytes 393220
  55.4 18.4 %collective-permute-start.3 = (bf16[2,2,64,512]{3,2,1,0:T(8,128)(2,1)S(1)}, bf16[2,2,64,512]{3,2,1,0:T(8,128)(2,1)S(1)}, u32[]{:S(2)}, u32[]{:S(2)}) collective-permute-start(bf16[2,2,64,512]{3,2,1,0:T(8,128)(2,1)S(1)} %pad_maximum_fusion.3), channel_id=1, source_target_pairs={{0,1},{1,0},{2,3},{3,2},{4,5},{5,4},{6,7},{7,6},{8,9},{9,8},{10,11... | collective-permute-start | bytes 786440 | tf_op jit(solution)/shard_map/ppermute | solution.py:20
  58.1 16.1 %all-to-all-start.2 = ((f32[8,4,128]{2,1,0:T(4,128)}), f32[8,4,128]{2,1,0:T(4,128)S(1)}, u32[]{:S(2)}, u32[]{:S(2)}) async-start(f32[8,4,128]{2,1,0:T(4,128)} %broadcast_in_dim.18), calls=%async_computation.2 | async-start | bytes 32768 | tf_op jit(solution)/shard_map/all_to_all | solution.py:170
  64.8 9.4 %collective-permute-start.6 = (bf16[16,4096]{1,0:T(8,128)(2,1)S(1)}, bf16[16,4096]{1,0:T(8,128)(2,1)S(1)}, u32[]{:S(2)}, u32[]{:S(2)}) collective-permute-start(bf16[16,4096]{1,0:T(8,128)(2,1)S(1)} %add.65.fresh0_ref), channel_id=1, source_target_pairs={{0,192},{64,128},{128,64},{192,0},{256,448},{320,384},{384,320},{4... | collective-permute-start | bytes 393224 | tf_op jit(solution)/shard_map/ppermute | solution.py:20
  69.3 7.2 %collective-permute-start.5 = (bf16[16,4096]{1,0:T(8,128)(2,1)S(1)}, bf16[16,4096]{1,0:T(8,128)(2,1)S(1)}, u32[]{:S(2)}, u32[]{:S(2)}) collective-permute-start(bf16[16,4096]{1,0:T(8,128)(2,1)S(1)} %add.65.fresh0_ref), channel_id=1, source_target_pairs={{0,128},{64,192},{128,0},{192,64},{256,384},{320,448},{384,256},{4... | collective-permute-start | bytes 393224 | tf_op jit(solution)/shard_map/ppermute | solution.py:20
  71.8 6.0 %collective-permute-start.4 = (bf16[16,4096]{1,0:T(8,128)(2,1)S(1)}, bf16[16,4096]{1,0:T(8,128)(2,1)S(1)}, u32[]{:S(2)}, u32[]{:S(2)}) collective-permute-start(bf16[16,4096]{1,0:T(8,128)(2,1)S(1)} %add.65.fresh0_ref), channel_id=1, source_target_pairs={{0,64},{64,0},{128,192},{192,128},{256,320},{320,256},{384,448},{4... | collective-permute-start | bytes 393224 | tf_op jit(solution)/shard_map/ppermute | solution.py:20
  73.9 5.3 %copy-start.5 = (bf16[2,2,2,64,512]{4,3,2,1,0:T(8,128)(2,1)}, bf16[2,2,2,64,512]{4,3,2,1,0:T(8,128)(2,1)S(1)}, u32[]{:S(2)}) copy-start(bf16[2,2,2,64,512]{4,3,2,1,0:T(8,128)(2,1)S(1)} %pad_maximum_fusion.1) | copy-start | bytes 1572868
  74.1 5.0 %copy-start.11 = (bf16[16,4096]{1,0:T(8,128)(2,1)}, bf16[16,4096]{1,0:T(8,128)(2,1)S(1)}, u32[]{:S(2)}) copy-start(bf16[16,4096]{1,0:T(8,128)(2,1)S(1)} %collective-permute-done.6.fresh3_ref) | copy-start | bytes 393220
  76.5 2.6 %copy-start.12 = (bf16[16,4096]{1,0:T(8,128)(2,1)}, bf16[16,4096]{1,0:T(8,128)(2,1)S(1)}, u32[]{:S(2)}) copy-start(bf16[16,4096]{1,0:T(8,128)(2,1)S(1)} %collective-permute-done.5.fresh2_ref) | copy-start | bytes 393220
  77.8 1.4 copy-start.13
  79.2 20.1 %all-to-all-start.3 = ((bf16[4,8,16,512]{3,2,1,0:T(8,128)(2,1)}), bf16[4,8,16,512]{3,2,1,0:T(8,128)(2,1)S(1)}, u32[]{:S(2)}, u32[]{:S(2)}) async-start(bf16[4,8,16,512]{3,2,1,0:T(8,128)(2,1)} %bitcast.117), calls=%async_computation.3 | async-start | bytes 1048576 | tf_op jit(solution)/shard_map/all_to_all | solution.py:25
  83.0 16.1 %collective-permute-start.8 = (bf16[2,16,4096]{2,1,0:T(8,128)(2,1)S(1)}, bf16[2,16,4096]{2,1,0:T(8,128)(2,1)S(1)}, u32[]{:S(2)}, u32[]{:S(2)}) collective-permute-start(bf16[2,16,4096]{2,1,0:T(8,128)(2,1)S(1)} %reduce_sum.64), channel_id=1, source_target_pairs={{0,256},{64,320},{128,384},{192,448},{256,0},{320,64},{384,128},{4... | collective-permute-start | bytes 786440 | tf_op jit(solution)/shard_map/ppermute | solution.py:20
  99.2 33.0 %copy-start.2 = (f32[1,1,64,4096]{3,2,1,0:T(8,128)S(1)}, f32[1,1,64,4096]{3,2,1,0:T(8,128)}, u32[]{:S(2)}) copy-start(f32[1,1,64,4096]{3,2,1,0:T(8,128)} %param.12) | copy-start | bytes 3145732
  99.2 0.8 copy-start.4
  102.6 58.4 %all-to-all-start.4 = ((bf16[8,80,512]{2,1,0:T(8,128)(2,1)}), bf16[8,80,512]{2,1,0:T(8,128)(2,1)S(1)}, u32[]{:S(2)}, u32[]{:S(2)}) async-start(bf16[8,80,512]{2,1,0:T(8,128)(2,1)} %get-tuple-element.40), calls=%async_computation.4 | async-start | bytes 1310720 | tf_op jit(solution)/shard_map/all_to_all | solution.py:189
  132.4 8.2 %copy-start.1 = (f32[1,1,64,4096]{3,2,1,0:T(8,128)S(1)}, f32[1,1,64,4096]{3,2,1,0:T(8,128)}, u32[]{:S(2)}) copy-start(f32[1,1,64,4096]{3,2,1,0:T(8,128)} %param.11) | copy-start | bytes 3145732
  160.9 1.0 copy-start.6
  163.4 9.6 %collective-permute-start.9 = (f32[4,128]{1,0:T(4,128)S(1)}, f32[4,128]{1,0:T(4,128)S(1)}, u32[]{:S(2)}, u32[]{:S(2)}) collective-permute-start(f32[4,128]{1,0:T(4,128)S(1)} %bitcast.157), channel_id=1, source_target_pairs={{0,1},{1,0},{2,3},{3,2},{4,5},{5,4},{6,7},{7,6},{8,9},{9,8},{10,11... | collective-permute-start | bytes 6152 | tf_op jit(solution)/shard_map/ppermute | solution.py:20
  167.5 24.2 %collective-permute-start.13 = (bf16[16,4096]{1,0:T(8,128)(2,1)S(1)}, bf16[16,4096]{1,0:T(8,128)(2,1)S(1)}, u32[]{:S(2)}, u32[]{:S(2)}) collective-permute-start(bf16[16,4096]{1,0:T(8,128)(2,1)S(1)} %bitcast.149), channel_id=1, source_target_pairs={{0,256},{64,320},{128,384},{192,448},{256,0},{320,64},{384,128},{4... | collective-permute-start | bytes 393224 | tf_op jit(solution)/shard_map/ppermute | solution.py:20
  173.0 11.1 %collective-permute-start.10 = (f32[4,128]{1,0:T(4,128)S(1)}, f32[4,128]{1,0:T(4,128)S(1)}, u32[]{:S(2)}, u32[]{:S(2)}) collective-permute-start(f32[4,128]{1,0:T(4,128)S(1)} %bitcast_add_fusion), channel_id=1, source_target_pairs={{0,2},{1,3},{2,0},{3,1},{4,6},{5,7},{6,4},{7,5},{8,10},{9,11},{10,... | collective-permute-start | bytes 6152 | tf_op jit(solution)/shard_map/ppermute | solution.py:20
  177.6 15.4 %copy-start.14 = (bf16[2,4096]{1,0:T(2,128)(2,1)S(1)}, bf16[2,4096]{1,0:T(2,128)(2,1)}, u32[]{:S(2)}) copy-start(bf16[2,4096]{1,0:T(2,128)(2,1)} %convert_element_type.105) | copy-start | bytes 49156
  177.6 47.8 %all-to-all-start.5 = ((bf16[8,64,512]{2,1,0:T(8,128)(2,1)}), bf16[8,64,512]{2,1,0:T(8,128)(2,1)S(1)}, u32[]{:S(2)}, u32[]{:S(2)}) async-start(bf16[8,64,512]{2,1,0:T(8,128)(2,1)} %bitcast.143), calls=%async_computation.5 | async-start | bytes 1048576 | tf_op jit(solution)/shard_map/all_to_all | solution.py:203
  184.1 18.6 %copy-start.3 = (f32[512,512]{0,1:T(8,128)S(1)}, f32[512,512]{0,1:T(8,128)}, u32[]{:S(2)}) copy-start(f32[512,512]{0,1:T(8,128)} %get-tuple-element.71) | copy-start | bytes 3145732
  184.1 18.5 %collective-permute-start.11 = (f32[4,128]{1,0:T(4,128)S(1)}, f32[4,128]{1,0:T(4,128)S(1)}, u32[]{:S(2)}, u32[]{:S(2)}) collective-permute-start(f32[4,128]{1,0:T(4,128)S(1)} %fusion.37), channel_id=1, source_target_pairs={{0,4},{1,5},{2,6},{3,7},{4,0},{5,1},{6,2},{7,3},{8,12},{9,13},{10,... | collective-permute-start | bytes 6152 | tf_op jit(solution)/shard_map/ppermute | solution.py:20
  193.0 22.0 %collective-permute-start.15 = (bf16[34,4096]{1,0:T(8,128)(2,1)S(1)}, bf16[34,4096]{1,0:T(8,128)(2,1)S(1)}, u32[]{:S(2)}, u32[]{:S(2)}) collective-permute-start(bf16[34,4096]{1,0:T(8,128)(2,1)S(1)} %get-tuple-element.63), channel_id=1, source_target_pairs={{0,128},{64,192},{128,0},{192,64},{256,384},{320,448},{384,256},{4... | collective-permute-start | bytes 835592 | tf_op jit(solution)/shard_map/ppermute | solution.py:20
  197.9 17.1 %collective-permute-start.14 = (bf16[34,4096]{1,0:T(8,128)(2,1)S(1)}, bf16[34,4096]{1,0:T(8,128)(2,1)S(1)}, u32[]{:S(2)}, u32[]{:S(2)}) collective-permute-start(bf16[34,4096]{1,0:T(8,128)(2,1)S(1)} %get-tuple-element.63), channel_id=1, source_target_pairs={{0,64},{64,0},{128,192},{192,128},{256,320},{320,256},{384,448},{4... | collective-permute-start | bytes 835592 | tf_op jit(solution)/shard_map/ppermute | solution.py:20
  200.1 14.9 %collective-permute-start.16 = (bf16[34,4096]{1,0:T(8,128)(2,1)S(1)}, bf16[34,4096]{1,0:T(8,128)(2,1)S(1)}, u32[]{:S(2)}, u32[]{:S(2)}) collective-permute-start(bf16[34,4096]{1,0:T(8,128)(2,1)S(1)} %get-tuple-element.63), channel_id=1, source_target_pairs={{0,192},{64,128},{128,64},{192,0},{256,448},{320,384},{384,320},{4... | collective-permute-start | bytes 835592 | tf_op jit(solution)/shard_map/ppermute | solution.py:20
  203.7 19.7 %collective-permute-start.12 = (bf16[512,512]{0,1:T(8,128)(2,1)}, bf16[512,512]{0,1:T(8,128)(2,1)}, u32[]{:S(2)}, u32[]{:S(2)}) collective-permute-start(bf16[512,512]{0,1:T(8,128)(2,1)} %fusion.7), channel_id=1, source_target_pairs={{8,0},{16,8},{24,16},{32,24},{40,32},{48,40},{56,48},{0,56},{9,1},... | collective-permute-start | bytes 1572872 | tf_op jit(solution)/shard_map/ppermute | solution.py:16
  216.0 1.7 copy-start.9
  216.0 1.7 copy-start.10

commit v6 on v4

--- a/solution.py
+++ b/solution.py
@@ -164,8 +164,6 @@
     fresh_weight = served[0] + swap(served[0], "replica", PLANE)
     held = doubled(held, my_tensor, 2)
     held, fresh_weight, squares = lax.optimization_barrier((held, fresh_weight, squares))
-    served_moments = tied(served[1:], fresh_weight)
-    fresh_moments = served_moments + swap(served_moments, "replica", PLANE)
     kg_all = held.reshape(8 * rows, tokens)
     inverse_rms = 1.0 / jnp.sqrt(jnp.sum(squares, axis=0).reshape(tokens) / width + 1e-05)
     fresh_weight = [fresh_weight] + [swap(fresh_weight, "replica", bit) for bit in (1, 2, 3)]
@@ -173,7 +171,7 @@
     normed = (x * inverse_rms[:, None]).astype(SHORT)
     grad = lax.dot_general(kg_all, normed, (((1,), (0,)), ((), ())), preferred_element_type=WIDE).astype(SHORT)
     grad = grad.reshape(8, PLANE, part, cols).transpose(1, 0, 2, 3)
-    grad, fresh_moments = lax.optimization_barrier((exchange_x(grad), fresh_moments))
+    grad = exchange_x(grad)
 
     sent, restored_weight = assemble(failed_replica, own_weight, fresh_weight, grad)
     got = lax.all_to_all(sent, "tensor", 0, 0, tiled=True)
@@ -184,7 +182,9 @@
     keys = lax.dot_general(weight_cols, normed, (((1,), (1,)), ((), ())), preferred_element_type=WIDE).astype(SHORT)
     feature = lax.dot_general(kg_all, weight_cols, (((0,), (0,)), ((), ())), preferred_element_type=WIDE)
     product = jnp.sum(feature * x, axis=1).reshape(-1, 128)
-    for bit in (1, 2, 4):
+    product = product + swap(product, "tensor", 1)
+    product, mean_rows = lax.optimization_barrier((product, mean_rows))
+    for bit in (2, 4):
         product = product + swap(product, "tensor", bit)
     product = product.reshape(tokens, 1)
     scale = inverse_rms[:, None]
@@ -198,10 +198,16 @@
         mixed = jnp.einsum("jnc,cp->jnp", shaped, probe_matrix, precision=lax.Precision.HIGHEST)
         return mixed.reshape(-1, nchunk * probe_matrix.shape[1])
 
-    fresh = fresh_moments.astype(WIDE)
-    fresh_update = adam(fresh[0], fresh[1], mean_rows).astype(SHORT)
-    fresh_sums = checksum(fresh.reshape(2 * part, width)).astype(SHORT).reshape(2, width)
-    shared = gather_x(jnp.concatenate([mean_rows.astype(SHORT), fresh_update, fresh_sums], axis=0))
+    served_moments = served[1:].astype(WIDE)
+    served_update = adam(served_moments[0], served_moments[1], mean_rows).astype(SHORT)
+    served_sums = checksum(served_moments.reshape(2 * part, width)).astype(SHORT).reshape(2, width)
+    mine = jnp.concatenate([served_update, served_sums], axis=0)
+    other = swap(mine, "replica", PLANE)
+    fresh_update = jnp.where(columns, mine[:part], other[:part])
+    fresh_sums = mine[part:] + other[part:]
+    shared = jnp.concatenate([mean_rows.astype(SHORT), fresh_update, fresh_sums], axis=0)
+    shared, key_out = lax.optimization_barrier((shared, key_out))
+    shared = gather_x(shared)
     mean_grad = shared[:, :part].reshape(rows, width).astype(WIDE)
     fresh_update = shared[:, part : 2 * part].reshape(rows, width).astype(WIDE)
     fresh_sums = shared[:, 2 * part :].reshape(PLANE, 2, part, -1).transpose(1, 0, 2, 3).reshape(2, rows, -1).astype(WIDE)

time: 212 us -> 231 us (1.090)
  waiting for transfers between devices: 20.9 us -> 41.5 us
  starting transfers between devices: 142 us -> 133 us
  other arithmetic: 7.73 us -> 12.1 us
    ppermute x15, waiting for transfers between devices: 13.6 us -> 31.8 us  [swap(): lax.ppermute(block, axis, [(i, i ^ bit) for i in range(lax.axis_size(axis...]
    all_to_all x1, starting transfers between devices: 22.2 us -> 8.42 us  [shards(): got = lax.all_to_all(sent, 'tensor', 0, 0, tiled=True)]
    ppermute x15, starting transfers between devices: 86.5 us -> 99.6 us  [swap(): lax.ppermute(block, axis, [(i, i ^ bit) for i in range(lax.axis_size(axis...]
    all_to_all x1, waiting for transfers between devices: 1.02 us -> 9.27 us  [shards(): got = lax.all_to_all(sent, 'tensor', 0, 0, tiled=True)]
    ppermute x2, starting transfers between devices: 13.2 us -> 5.23 us  [from_behind(): lax.ppermute(block, axis, [((i - distance) % n, i) for i in range(n)])]
    ppermute x2, waiting for transfers between devices: 5.86 us -> 0.01 us  [from_behind(): lax.ppermute(block, axis, [((i - distance) % n, i) for i in range(n)])]
    unnamed x32 -> x50, local copies, waits for them, and re-layouts: 6.35 us -> 7.22 us
  transfers between devices with their start and end apart: 22 -> 22, of which waited for: 9 -> 8; matrix products, arithmetic and copies ran while one was open for 17% -> 16% of each run, Pallas kernels for 0% -> 0%
where the time goes in v6:
time: 231 us; the launch traced here: 229 us
  starting transfers between devices  133 us (58%)
  waiting for transfers between devices  41.5 us (18%)
  matrix products  18.1 us (8%)
  local copies, waits for them, and re-layouts  16.8 us (7%)
  other arithmetic  12.1 us (5%)
  Pallas kernels  6 us (3%)
    ppermute x15, starting transfers between devices, swap(): lax.ppermute(block, axis, [(i, i ^ bit) for i in range(lax.axis_size(axis...  99.6 us
    ppermute x15, waiting for transfers between devices, swap(): lax.ppermute(block, axis, [(i, i ^ bit) for i in range(lax.axis_size(axis...  31.8 us
    dot_general x4, matrix products, checksum(): jnp.einsum('jnc,cp->jnp', shaped, probe_matrix, precision=lax.Precision.H...  14.9 us
    all_to_all x1, waiting for transfers between devices, shards(): got = lax.all_to_all(sent, 'tensor', 0, 0, tiled=True)  9.27 us
    all_to_all x2, starting transfers between devices, exchange_x(): lax.all_to_all(block, 'replica', 0, 0, axis_index_groups=groups, tiled=True)  9.19 us
    all_to_all x1, starting transfers between devices, shards(): got = lax.all_to_all(sent, 'tensor', 0, 0, tiled=True)  8.42 us
    unnamed x50, local copies, waits for them, and re-layouts  7.22 us
    all_to_all x1, starting transfers between devices, shards(): lax.all_to_all(keys.reshape(8, rows, tokens), 'tensor', 0, 0, tiled=True)  5.96 us
  transfers between devices with their start and end apart: 22, of which 8 were waited for; matrix products, arithmetic and copies ran while one was open for 16% of the time, Pallas kernels for 0%

profile of v6, /device:TPU:1, one launch (start us, length us, event | category | flops | bytes accessed | tf_op | source)
XLA Modules:
  0.0 229.5 jit_solution(17378498076584167375)
XLA Ops:
  0.6 3.4 %serve.1 = bf16[4,3,16,4096]{3,2,1,0:T(8,128)(2,1)} custom-call(s32[8,8]{1,0:T(8,128)} %failed_ref.3, s32[8,8]{1,0:T(8,128)} %spans_ref.1, bf16[64,4096]{1,0:T(8,128)(2,1)} %bitcast.140, f32[64,4096]{1,0:T(8,128)} %bitcast.122, f32[64,4096]{1,0:T(8,128)} %bitcast.124), custom_call_target="tpu_custom_call" | custom-call | tf_op jit(solution)/shard_map/serve/pallas_call | solution.py:81
  4.1 5.0 %all-to-all-start = ((bf16[4,3,16,4096]{3,2,1,0:T(8,128)(2,1)}), bf16[4,3,16,4096]{3,2,1,0:T(8,128)(2,1)S(1)}, u32[]{:S(2)}, u32[]{:S(2)}) async-start(bf16[4,3,16,4096]{3,2,1,0:T(8,128)(2,1)} %serve.1), calls=%async_computation | async-start | bytes 3145728 | tf_op jit(solution)/shard_map/all_to_all | solution.py:25
  9.0 8.8 %collective-permute-start = (bf16[64,512]{1,0:T(8,128)(2,1)S(1)}, bf16[64,512]{1,0:T(8,128)(2,1)S(1)}, u32[]{:S(2)}, u32[]{:S(2)}) collective-permute-start(bf16[64,512]{1,0:T(8,128)(2,1)S(1)} %bitcast.156), channel_id=1, source_target_pairs={{0,4},{1,5},{2,6},{3,7},{4,0},{5,1},{6,2},{7,3},{8,12},{9,13},{10,... | collective-permute-start | bytes 196616 | tf_op jit(solution)/shard_map/ppermute | solution.py:20
  17.9 1.6 collective-permute-done
  19.5 7.0 %collective-permute-start.1 = (bf16[2,64,512]{2,1,0:T(8,128)(2,1)S(1)}, bf16[2,64,512]{2,1,0:T(8,128)(2,1)S(1)}, u32[]{:S(2)}, u32[]{:S(2)}) collective-permute-start(bf16[2,64,512]{2,1,0:T(8,128)(2,1)S(1)} %pad_maximum_fusion.5), channel_id=1, source_target_pairs={{0,2},{1,3},{2,0},{3,1},{4,6},{5,7},{6,4},{7,5},{8,10},{9,11},{10,... | collective-permute-start | bytes 393224 | tf_op jit(solution)/shard_map/ppermute | solution.py:20
  26.8 2.6 %collective-permute-start.4 = (bf16[512,512]{0,1:T(8,128)(2,1)S(1)}, bf16[512,512]{0,1:T(8,128)(2,1)S(1)}, u32[]{:S(2)}, u32[]{:S(2)}) collective-permute-start(bf16[512,512]{0,1:T(8,128)(2,1)S(1)} %bitcast.150), channel_id=1, source_target_pairs={{56,0},{0,8},{8,16},{16,24},{24,32},{32,40},{40,48},{48,56},{57,1}... | collective-permute-start | bytes 1572872 | tf_op jit(solution)/shard_map/ppermute | solution.py:16
  29.8 18.7 %collective-permute-start.3 = (bf16[16,4096]{1,0:T(8,128)(2,1)S(1)}, bf16[16,4096]{1,0:T(8,128)(2,1)S(1)}, u32[]{:S(2)}, u32[]{:S(2)}) collective-permute-start(bf16[16,4096]{1,0:T(8,128)(2,1)S(1)} %slice_bitcast_fusion.1), channel_id=1, source_target_pairs={{0,256},{64,320},{128,384},{192,448},{256,0},{320,64},{384,128},{4... | collective-permute-start | bytes 393224 | tf_op jit(solution)/shard_map/ppermute | solution.py:20
  49.3 4.8 %all-to-all-start.1 = ((f32[8,4,128]{2,1,0:T(4,128)}), f32[8,4,128]{2,1,0:T(4,128)S(1)}, u32[]{:S(2)}, u32[]{:S(2)}) async-start(f32[8,4,128]{2,1,0:T(4,128)} %broadcast_in_dim.32), calls=%async_computation.1 | async-start | bytes 32768 | tf_op jit(solution)/shard_map/all_to_all | solution.py:160
  54.1 3.4 %collective-permute-start.2 = (bf16[2,2,64,512]{3,2,1,0:T(8,128)(2,1)S(1)}, bf16[2,2,64,512]{3,2,1,0:T(8,128)(2,1)S(1)}, u32[]{:S(2)}, u32[]{:S(2)}) collective-permute-start(bf16[2,2,64,512]{3,2,1,0:T(8,128)(2,1)S(1)} %pad_maximum_fusion.3), channel_id=1, source_target_pairs={{0,1},{1,0},{2,3},{3,2},{4,5},{5,4},{6,7},{7,6},{8,9},{9,8},{10,11... | collective-permute-start | bytes 786440 | tf_op jit(solution)/shard_map/ppermute | solution.py:20
  57.5 5.5 %collective-permute-done.2 = bf16[2,2,64,512]{3,2,1,0:T(8,128)(2,1)S(1)} collective-permute-done((bf16[2,2,64,512]{3,2,1,0:T(8,128)(2,1)S(1)}, bf16[2,2,64,512]{3,2,1,0:T(8,128)(2,1)S(1)}, u32[]{:S(2)}, u32[]{:S(2)}) %collective-permute-start.2) | collective-permute-done | bytes 262176 | tf_op jit(solution)/shard_map/ppermute | solution.py:20
  64.8 4.2 %all-to-all-start.2 = ((bf16[4,8,16,512]{3,2,1,0:T(8,128)(2,1)}), bf16[4,8,16,512]{3,2,1,0:T(8,128)(2,1)S(1)}, u32[]{:S(2)}, u32[]{:S(2)}) async-start(bf16[4,8,16,512]{3,2,1,0:T(8,128)(2,1)} %bitcast.121), calls=%async_computation.2 | async-start | bytes 1048576 | tf_op jit(solution)/shard_map/all_to_all | solution.py:25
  69.0 4.7 %collective-permute-start.7 = (bf16[16,4096]{1,0:T(8,128)(2,1)S(1)}, bf16[16,4096]{1,0:T(8,128)(2,1)S(1)}, u32[]{:S(2)}, u32[]{:S(2)}) collective-permute-start(bf16[16,4096]{1,0:T(8,128)(2,1)S(1)} %fusion.27.fresh0_ref), channel_id=1, source_target_pairs={{0,192},{64,128},{128,64},{192,0},{256,448},{320,384},{384,320},{4... | collective-permute-start | bytes 393224 | tf_op jit(solution)/shard_map/ppermute | solution.py:20
  73.7 2.5 %collective-permute-start.6 = (bf16[16,4096]{1,0:T(8,128)(2,1)S(1)}, bf16[16,4096]{1,0:T(8,128)(2,1)S(1)}, u32[]{:S(2)}, u32[]{:S(2)}) collective-permute-start(bf16[16,4096]{1,0:T(8,128)(2,1)S(1)} %fusion.27.fresh0_ref), channel_id=1, source_target_pairs={{0,128},{64,192},{128,0},{192,64},{256,384},{320,448},{384,256},{4... | collective-permute-start | bytes 393224 | tf_op jit(solution)/shard_map/ppermute | solution.py:20
  76.2 1.9 collective-permute-start.5
  78.2 3.6 %collective-permute-done.7.fresh3_ref = bf16[16,4096]{1,0:T(8,128)(2,1)S(1)} collective-permute-done((bf16[16,4096]{1,0:T(8,128)(2,1)S(1)}, bf16[16,4096]{1,0:T(8,128)(2,1)S(1)}, u32[]{:S(2)}, u32[]{:S(2)}) %collective-permute-start.7) | collective-permute-done | bytes 131104 | tf_op jit(solution)/shard_map/ppermute | solution.py:20
  81.8 1.8 collective-permute-done.5.fresh1_ref
  85.0 2.6 %assemble.1 = (bf16[8,80,512]{2,1,0:T(8,128)(2,1)}, bf16[64,4096]{1,0:T(8,128)(2,1)}) custom-call(s32[8,8]{1,0:T(8,128)} %failed_ref.3, bf16[64,4096]{1,0:T(8,128)(2,1)} %bitcast.141, bf16[16,4096]{1,0:T(8,128)(2,1)} %copy-done.11, bf16[16,4096]{1,0:T(8,128)(2,1)} %copy-done.18, bf16[16,4096]{1,0:T(8,128)(2,1)} %copy-done.17, bf16[16,4096]{1,0:T(8,128)(2,1)} %copy-done.16, ...), custom_call_target="tpu_custom_call" | custom-call | tf_op jit(solution)/shard_map/assemble/pallas_call | solution.py:113
  87.6 8.4 %all-to-all-start.3 = ((bf16[8,80,512]{2,1,0:T(8,128)(2,1)}), bf16[8,80,512]{2,1,0:T(8,128)(2,1)S(1)}, u32[]{:S(2)}, u32[]{:S(2)}) async-start(bf16[8,80,512]{2,1,0:T(8,128)(2,1)} %get-tuple-element.23), calls=%async_computation.3 | async-start | bytes 1310720 | tf_op jit(solution)/shard_map/all_to_all | solution.py:177
  96.0 1.2 copy.61
  97.5 1.2 copy.60
  99.6 6.1 %fusion.21 = f32[64,32,8]{1,2,0:T(8,128)} fusion(f32[64,32,128]{2,1,0:T(8,128)} %bitcast.131, f32[128,8]{0,1:T(8,128)S(1)} %copy-done), kind=kOutput, calls=%fused_computation.54 | convolution fusion | flops 25165824 | bytes 1118208 | tf_op jit(solution)/shard_map/jnc,cp->jnp/dot_general | solution.py:198
  106.6 1.8 convolution_convert_fusion.2
  110.8 9.3 %all-to-all-done.3 = bf16[8,80,512]{2,1,0:T(8,128)(2,1)S(1)} async-done(((bf16[8,80,512]{2,1,0:T(8,128)(2,1)}), bf16[8,80,512]{2,1,0:T(8,128)(2,1)S(1)}, u32[]{:S(2)}, u32[]{:S(2)}) %all-to-all-start.3) | async-done | bytes 655392 | tf_op jit(solution)/shard_map/all_to_all | solution.py:177
  120.1 4.7 %collective-permute-start.9 = (bf16[16,4096]{1,0:T(8,128)(2,1)S(1)}, bf16[16,4096]{1,0:T(8,128)(2,1)S(1)}, u32[]{:S(2)}, u32[]{:S(2)}) collective-permute-start(bf16[16,4096]{1,0:T(8,128)(2,1)S(1)} %bitcast.154), channel_id=1, source_target_pairs={{0,256},{64,320},{128,384},{192,448},{256,0},{320,64},{384,128},{4... | collective-permute-start | bytes 393224 | tf_op jit(solution)/shard_map/ppermute | solution.py:20
  124.9 1.5 fusion.4
  126.4 10.1 %collective-permute-start.8 = (f32[4,128]{1,0:T(4,128)S(1)}, f32[4,128]{1,0:T(4,128)S(1)}, u32[]{:S(2)}, u32[]{:S(2)}) collective-permute-start(f32[4,128]{1,0:T(4,128)S(1)} %bitcast.160), channel_id=1, source_target_pairs={{0,1},{1,0},{2,3},{3,2},{4,5},{5,4},{6,7},{7,6},{8,9},{9,8},{10,11... | collective-permute-start | bytes 6152 | tf_op jit(solution)/shard_map/ppermute | solution.py:20
  136.5 1.2 convolution_convert_fusion
  137.7 6.0 %all-to-all-start.4 = ((bf16[8,64,512]{2,1,0:T(8,128)(2,1)}), bf16[8,64,512]{2,1,0:T(8,128)(2,1)}, u32[]{:S(2)}, u32[]{:S(2)}) async-start(bf16[8,64,512]{2,1,0:T(8,128)(2,1)} %bitcast.149), calls=%async_computation.4 | async-start | bytes 1048576 | tf_op jit(solution)/shard_map/all_to_all | solution.py:193
  143.8 4.4 %collective-permute-start.11 = (f32[4,128]{1,0:T(4,128)S(1)}, f32[4,128]{1,0:T(4,128)S(1)}, u32[]{:S(2)}, u32[]{:S(2)}) collective-permute-start(f32[4,128]{1,0:T(4,128)S(1)} %bitcast_add_fusion), channel_id=1, source_target_pairs={{0,2},{1,3},{2,0},{3,1},{4,6},{5,7},{6,4},{7,5},{8,10},{9,11},{10,... | collective-permute-start | bytes 6152 | tf_op jit(solution)/shard_map/ppermute | solution.py:20
  148.4 6.7 %collective-permute-done.11 = f32[4,128]{1,0:T(4,128)S(1)} collective-permute-done((f32[4,128]{1,0:T(4,128)S(1)}, f32[4,128]{1,0:T(4,128)S(1)}, u32[]{:S(2)}, u32[]{:S(2)}) %collective-permute-start.11) | collective-permute-done | bytes 2080 | tf_op jit(solution)/shard_map/ppermute | solution.py:20
  155.0 14.9 %collective-permute-start.12 = (f32[4,128]{1,0:T(4,128)S(1)}, f32[4,128]{1,0:T(4,128)S(1)}, u32[]{:S(2)}, u32[]{:S(2)}) collective-permute-start(f32[4,128]{1,0:T(4,128)S(1)} %add.77), channel_id=1, source_target_pairs={{0,4},{1,5},{2,6},{3,7},{4,0},{5,1},{6,2},{7,3},{8,12},{9,13},{10,... | collective-permute-start | bytes 6152 | tf_op jit(solution)/shard_map/ppermute | solution.py:20
  169.9 9.4 %collective-permute-start.10 = (bf16[18,4096]{1,0:T(8,128)(2,1)S(1)}, bf16[18,4096]{1,0:T(8,128)(2,1)S(1)}, u32[]{:S(2)}, u32[]{:S(2)}) collective-permute-start(bf16[18,4096]{1,0:T(8,128)(2,1)S(1)} %pad_maximum_fusion.4), channel_id=1, source_target_pairs={{0,256},{64,320},{128,384},{192,448},{256,0},{320,64},{384,128},{4... | collective-permute-start | bytes 442376 | tf_op jit(solution)/shard_map/ppermute | solution.py:20
  179.4 1.0 fusion.8
  180.4 2.6 %collective-permute-start.13 = (bf16[512,512]{0,1:T(8,128)(2,1)}, bf16[512,512]{0,1:T(8,128)(2,1)}, u32[]{:S(2)}, u32[]{:S(2)}) collective-permute-start(bf16[512,512]{0,1:T(8,128)(2,1)} %fusion.8), channel_id=1, source_target_pairs={{8,0},{16,8},{24,16},{32,24},{40,32},{48,40},{56,48},{0,56},{9,1},... | collective-permute-start | bytes 1572872 | tf_op jit(solution)/shard_map/ppermute | solution.py:16
  183.1 12.6 %collective-permute-done.10 = bf16[18,4096]{1,0:T(8,128)(2,1)S(1)} collective-permute-done((bf16[18,4096]{1,0:T(8,128)(2,1)S(1)}, bf16[18,4096]{1,0:T(8,128)(2,1)S(1)}, u32[]{:S(2)}, u32[]{:S(2)}) %collective-permute-start.10) | collective-permute-done | bytes 147488 | tf_op jit(solution)/shard_map/ppermute | solution.py:20
  195.8 1.8 reduce_sum.55
  197.5 2.8 %collective-permute-start.16 = (bf16[34,4096]{1,0:T(8,128)(2,1)S(1)}, bf16[34,4096]{1,0:T(8,128)(2,1)}, u32[]{:S(2)}, u32[]{:S(2)}) collective-permute-start(bf16[34,4096]{1,0:T(8,128)(2,1)S(1)} %pad_maximum_fusion.2), channel_id=1, source_target_pairs={{0,192},{64,128},{128,64},{192,0},{256,448},{320,384},{384,320},{4... | collective-permute-start | bytes 835592 | tf_op jit(solution)/shard_map/ppermute | solution.py:20
  200.3 2.7 %collective-permute-start.15 = (bf16[34,4096]{1,0:T(8,128)(2,1)S(1)}, bf16[34,4096]{1,0:T(8,128)(2,1)}, u32[]{:S(2)}, u32[]{:S(2)}) collective-permute-start(bf16[34,4096]{1,0:T(8,128)(2,1)S(1)} %pad_maximum_fusion.2), channel_id=1, source_target_pairs={{0,128},{64,192},{128,0},{192,64},{256,384},{320,448},{384,256},{4... | collective-permute-start | bytes 835592 | tf_op jit(solution)/shard_map/ppermute | solution.py:20
  203.0 3.7 %collective-permute-start.14 = (bf16[34,4096]{1,0:T(8,128)(2,1)S(1)}, bf16[34,4096]{1,0:T(8,128)(2,1)}, u32[]{:S(2)}, u32[]{:S(2)}) collective-permute-start(bf16[34,4096]{1,0:T(8,128)(2,1)S(1)} %pad_maximum_fusion.2), channel_id=1, source_target_pairs={{0,64},{64,0},{128,192},{192,128},{256,320},{320,256},{384,448},{4... | collective-permute-start | bytes 835592 | tf_op jit(solution)/shard_map/ppermute | solution.py:20
  206.7 4.9 %fusion.23 = f32[64,32,8]{1,2,0:T(8,128)} fusion(f32[64,32,128]{2,1,0:T(8,128)S(1)} %bitcast.130, f32[128,8]{0,1:T(8,128)S(1)} %copy-done), kind=kOutput, calls=%fused_computation.56 | convolution fusion | flops 25165824 | bytes 1118208 | tf_op jit(solution)/shard_map/jnc,cp->jnp/dot_general | solution.py:198
  211.6 1.3 dynamic_slice.7
  213.5 1.1 copy.52
  214.7 1.1 copy.51
  216.6 2.1 fusion.19
  219.6 2.0 copy.56
  221.7 1.4 pad_maximum_fusion
  224.5 1.2 convert_multiply_fusion.5
  226.5 3.0 %convert_select_fusion = f32[1,1,64,4096]{3,2,1,0:T(8,128)} fusion(bf16[1,1,64,4096]{3,2,1,0:T(8,128)(2,1)} %bitcast.134, f32[1,1,64,4096]{3,2,1,0:T(8,128)} %bitcast.133, f32[1,1,64,4096]{3,2,1,0:T(8,128)S(1)} %copy-done.2, f32[1,1,64,4096]{3,2,1,0:T(8,128)S(1)} %bitcast.132, f32[1,1,64,4096]{3,2,1,0:T(8,128)S(1)} %copy-done.1, pred[]{:T(512)S(6)} %eq.22), kind=kLoop, calls=%fused_computation.21 | loop fusion | flops 2097152 | bytes 5767169 | tf_op jit(solution)/shard_map/jit(_where)/select_n | solution.py:214
  (105 shorter events, 13.6 us)
Async XLA Ops:
  0.6 98.9 %copy-start = (f32[128,8]{0,1:T(8,128)S(1)}, f32[128,8]{0,1:T(8,128)}, u32[]{:S(2)}) copy-start(f32[128,8]{0,1:T(8,128)} %param.13) | copy-start | bytes 12292
  4.1 5.0 %copy-start.19 = (bf16[1,1,512,64]{2,3,1,0:T(8,128)(2,1)S(1)}, bf16[1,1,512,64]{2,3,1,0:T(8,128)(2,1)}, u32[]{:S(2)}) copy-start(bf16[1,1,512,64]{2,3,1,0:T(8,128)(2,1)} %param.9) | copy-start | bytes 196612
  4.1 22.5 %copy-start.12 = (bf16[1,1,512,512]{3,2,1,0:T(8,128)(2,1)S(1)}, bf16[1,1,512,512]{3,2,1,0:T(8,128)(2,1)}, u32[]{:S(2)}) copy-start(bf16[1,1,512,512]{3,2,1,0:T(8,128)(2,1)} %param.8) | copy-start | bytes 1572868
  4.1 25.4 %all-to-all-start = ((bf16[4,3,16,4096]{3,2,1,0:T(8,128)(2,1)}), bf16[4,3,16,4096]{3,2,1,0:T(8,128)(2,1)S(1)}, u32[]{:S(2)}, u32[]{:S(2)}) async-start(bf16[4,3,16,4096]{3,2,1,0:T(8,128)(2,1)} %serve.1), calls=%async_computation | async-start | bytes 3145728 | tf_op jit(solution)/shard_map/all_to_all | solution.py:25
  9.0 10.5 %collective-permute-start = (bf16[64,512]{1,0:T(8,128)(2,1)S(1)}, bf16[64,512]{1,0:T(8,128)(2,1)S(1)}, u32[]{:S(2)}, u32[]{:S(2)}) collective-permute-start(bf16[64,512]{1,0:T(8,128)(2,1)S(1)} %bitcast.156), channel_id=1, source_target_pairs={{0,4},{1,5},{2,6},{3,7},{4,0},{5,1},{6,2},{7,3},{8,12},{9,13},{10,... | collective-permute-start | bytes 196616 | tf_op jit(solution)/shard_map/ppermute | solution.py:20
  19.5 9.8 %collective-permute-start.1 = (bf16[2,64,512]{2,1,0:T(8,128)(2,1)S(1)}, bf16[2,64,512]{2,1,0:T(8,128)(2,1)S(1)}, u32[]{:S(2)}, u32[]{:S(2)}) collective-permute-start(bf16[2,64,512]{2,1,0:T(8,128)(2,1)S(1)} %pad_maximum_fusion.5), channel_id=1, source_target_pairs={{0,2},{1,3},{2,0},{3,1},{4,6},{5,7},{6,4},{7,5},{8,10},{9,11},{10,... | collective-permute-start | bytes 393224 | tf_op jit(solution)/shard_map/ppermute | solution.py:20
  26.8 21.8 %collective-permute-start.4 = (bf16[512,512]{0,1:T(8,128)(2,1)S(1)}, bf16[512,512]{0,1:T(8,128)(2,1)S(1)}, u32[]{:S(2)}, u32[]{:S(2)}) collective-permute-start(bf16[512,512]{0,1:T(8,128)(2,1)S(1)} %bitcast.150), channel_id=1, source_target_pairs={{56,0},{0,8},{8,16},{16,24},{24,32},{32,40},{40,48},{48,56},{57,1}... | collective-permute-start | bytes 1572872 | tf_op jit(solution)/shard_map/ppermute | solution.py:16
  29.8 33.3 %copy-start.5 = (bf16[3,16,4096]{2,1,0:T(8,128)(2,1)}, bf16[3,16,4096]{2,1,0:T(8,128)(2,1)S(1)}, u32[]{:S(2)}) copy-start(bf16[3,16,4096]{2,1,0:T(8,128)(2,1)S(1)} %reduce_sum.51) | copy-start | bytes 1179652
  29.8 27.7 %collective-permute-start.3 = (bf16[16,4096]{1,0:T(8,128)(2,1)S(1)}, bf16[16,4096]{1,0:T(8,128)(2,1)S(1)}, u32[]{:S(2)}, u32[]{:S(2)}) collective-permute-start(bf16[16,4096]{1,0:T(8,128)(2,1)S(1)} %slice_bitcast_fusion.1), channel_id=1, source_target_pairs={{0,256},{64,320},{128,384},{192,448},{256,0},{320,64},{384,128},{4... | collective-permute-start | bytes 393224 | tf_op jit(solution)/shard_map/ppermute | solution.py:20
  49.3 14.1 %all-to-all-start.1 = ((f32[8,4,128]{2,1,0:T(4,128)}), f32[8,4,128]{2,1,0:T(4,128)S(1)}, u32[]{:S(2)}, u32[]{:S(2)}) async-start(f32[8,4,128]{2,1,0:T(4,128)} %broadcast_in_dim.32), calls=%async_computation.1 | async-start | bytes 32768 | tf_op jit(solution)/shard_map/all_to_all | solution.py:160
  54.1 8.9 %collective-permute-start.2 = (bf16[2,2,64,512]{3,2,1,0:T(8,128)(2,1)S(1)}, bf16[2,2,64,512]{3,2,1,0:T(8,128)(2,1)S(1)}, u32[]{:S(2)}, u32[]{:S(2)}) collective-permute-start(bf16[2,2,64,512]{3,2,1,0:T(8,128)(2,1)S(1)} %pad_maximum_fusion.3), channel_id=1, source_target_pairs={{0,1},{1,0},{2,3},{3,2},{4,5},{5,4},{6,7},{7,6},{8,9},{9,8},{10,11... | collective-permute-start | bytes 786440 | tf_op jit(solution)/shard_map/ppermute | solution.py:20
  57.5 18.7 %copy-start.11 = (bf16[16,4096]{1,0:T(8,128)(2,1)}, bf16[16,4096]{1,0:T(8,128)(2,1)S(1)}, u32[]{:S(2)}) copy-start(bf16[16,4096]{1,0:T(8,128)(2,1)S(1)} %fusion.27.fresh0_ref) | copy-start | bytes 393220
  63.1 1.7 copy-start.9
  64.8 18.8 %all-to-all-start.2 = ((bf16[4,8,16,512]{3,2,1,0:T(8,128)(2,1)}), bf16[4,8,16,512]{3,2,1,0:T(8,128)(2,1)S(1)}, u32[]{:S(2)}, u32[]{:S(2)}) async-start(bf16[4,8,16,512]{3,2,1,0:T(8,128)(2,1)} %bitcast.121), calls=%async_computation.2 | async-start | bytes 1048576 | tf_op jit(solution)/shard_map/all_to_all | solution.py:25
  69.0 27.0 %copy-start.2 = (f32[1,1,64,4096]{3,2,1,0:T(8,128)S(1)}, f32[1,1,64,4096]{3,2,1,0:T(8,128)}, u32[]{:S(2)}) copy-start(f32[1,1,64,4096]{3,2,1,0:T(8,128)} %param.12) | copy-start | bytes 3145732
  69.0 12.7 %collective-permute-start.7 = (bf16[16,4096]{1,0:T(8,128)(2,1)S(1)}, bf16[16,4096]{1,0:T(8,128)(2,1)S(1)}, u32[]{:S(2)}, u32[]{:S(2)}) collective-permute-start(bf16[16,4096]{1,0:T(8,128)(2,1)S(1)} %fusion.27.fresh0_ref), channel_id=1, source_target_pairs={{0,192},{64,128},{128,64},{192,0},{256,448},{320,384},{384,320},{4... | collective-permute-start | bytes 393224 | tf_op jit(solution)/shard_map/ppermute | solution.py:20
  73.7 8.0 %collective-permute-start.6 = (bf16[16,4096]{1,0:T(8,128)(2,1)S(1)}, bf16[16,4096]{1,0:T(8,128)(2,1)S(1)}, u32[]{:S(2)}, u32[]{:S(2)}) collective-permute-start(bf16[16,4096]{1,0:T(8,128)(2,1)S(1)} %fusion.27.fresh0_ref), channel_id=1, source_target_pairs={{0,128},{64,192},{128,0},{192,64},{256,384},{320,448},{384,256},{4... | collective-permute-start | bytes 393224 | tf_op jit(solution)/shard_map/ppermute | solution.py:20
  76.2 7.4 %collective-permute-start.5 = (bf16[16,4096]{1,0:T(8,128)(2,1)S(1)}, bf16[16,4096]{1,0:T(8,128)(2,1)S(1)}, u32[]{:S(2)}, u32[]{:S(2)}) collective-permute-start(bf16[16,4096]{1,0:T(8,128)(2,1)S(1)} %fusion.27.fresh0_ref), channel_id=1, source_target_pairs={{0,64},{64,0},{128,192},{192,128},{256,320},{320,256},{384,448},{4... | collective-permute-start | bytes 393224 | tf_op jit(solution)/shard_map/ppermute | solution.py:20
  81.8 1.8 copy-start.16
  81.8 1.8 copy-start.17
  83.6 0.7 copy-start.18
  84.2 0.8 copy-start.7
  87.6 32.5 %all-to-all-start.3 = ((bf16[8,80,512]{2,1,0:T(8,128)(2,1)}), bf16[8,80,512]{2,1,0:T(8,128)(2,1)S(1)}, u32[]{:S(2)}, u32[]{:S(2)}) async-start(bf16[8,80,512]{2,1,0:T(8,128)(2,1)} %get-tuple-element.23), calls=%async_computation.3 | async-start | bytes 1310720 | tf_op jit(solution)/shard_map/all_to_all | solution.py:177
  96.0 1.5 copy-start.1
  98.6 7.0 %copy-start.6 = (bf16[3,16,4096]{2,1,0:T(8,128)(2,1)S(1)}, bf16[3,16,4096]{2,1,0:T(8,128)(2,1)}, u32[]{:S(2)}) copy-start(bf16[3,16,4096]{2,1,0:T(8,128)(2,1)} %copy-done.5) | copy-start | bytes 1179652
  120.1 4.8 %copy-start.10 = (bf16[2,2,2,64,512]{4,3,2,1,0:T(8,128)(2,1)S(1)}, bf16[2,2,2,64,512]{4,3,2,1,0:T(8,128)(2,1)}, u32[]{:S(2)}) copy-start(bf16[2,2,2,64,512]{4,3,2,1,0:T(8,128)(2,1)} %copy-done.9) | copy-start | bytes 1572868
  120.1 23.6 %collective-permute-start.9 = (bf16[16,4096]{1,0:T(8,128)(2,1)S(1)}, bf16[16,4096]{1,0:T(8,128)(2,1)S(1)}, u32[]{:S(2)}, u32[]{:S(2)}) collective-permute-start(bf16[16,4096]{1,0:T(8,128)(2,1)S(1)} %bitcast.154), channel_id=1, source_target_pairs={{0,256},{64,320},{128,384},{192,448},{256,0},{320,64},{384,128},{4... | collective-permute-start | bytes 393224 | tf_op jit(solution)/shard_map/ppermute | solution.py:20
  126.4 21.8 %copy-start.8 = (f32[2,16,4096]{2,1,0:T(8,128)S(1)}, f32[2,16,4096]{2,1,0:T(8,128)}, u32[]{:S(2)}) copy-start(f32[2,16,4096]{2,1,0:T(8,128)} %get-tuple-element.53) | copy-start | bytes 1572868
  126.4 17.3 %collective-permute-start.8 = (f32[4,128]{1,0:T(4,128)S(1)}, f32[4,128]{1,0:T(4,128)S(1)}, u32[]{:S(2)}, u32[]{:S(2)}) collective-permute-start(f32[4,128]{1,0:T(4,128)S(1)} %bitcast.160), channel_id=1, source_target_pairs={{0,1},{1,0},{2,3},{3,2},{4,5},{5,4},{6,7},{7,6},{8,9},{9,8},{10,11... | collective-permute-start | bytes 6152 | tf_op jit(solution)/shard_map/ppermute | solution.py:20
  137.7 32.2 %copy-start.15 = (bf16[2,4096]{1,0:T(2,128)(2,1)S(1)}, bf16[2,4096]{1,0:T(2,128)(2,1)}, u32[]{:S(2)}) copy-start(bf16[2,4096]{1,0:T(2,128)(2,1)} %convert_element_type.100) | copy-start | bytes 49156
  137.7 41.7 %copy-start.20 = (f32[512]{0:T(512)S(1)}, f32[512]{0:T(512)}, u32[]{:S(2)}) copy-start(f32[512]{0:T(512)} %multiply_multiply_fusion) | copy-start | bytes 6148
  137.7 58.0 %all-to-all-start.4 = ((bf16[8,64,512]{2,1,0:T(8,128)(2,1)}), bf16[8,64,512]{2,1,0:T(8,128)(2,1)}, u32[]{:S(2)}, u32[]{:S(2)}) async-start(bf16[8,64,512]{2,1,0:T(8,128)(2,1)} %bitcast.149), calls=%async_computation.4 | async-start | bytes 1048576 | tf_op jit(solution)/shard_map/all_to_all | solution.py:193
  143.7 35.7 %copy-start.4 = (f32[512,512]{0,1:T(8,128)S(1)}, f32[512,512]{0,1:T(8,128)}, u32[]{:S(2)}) copy-start(f32[512,512]{0,1:T(8,128)} %get-tuple-element.62) | copy-start | bytes 3145732
  143.8 11.3 %collective-permute-start.11 = (f32[4,128]{1,0:T(4,128)S(1)}, f32[4,128]{1,0:T(4,128)S(1)}, u32[]{:S(2)}, u32[]{:S(2)}) collective-permute-start(f32[4,128]{1,0:T(4,128)S(1)} %bitcast_add_fusion), channel_id=1, source_target_pairs={{0,2},{1,3},{2,0},{3,1},{4,6},{5,7},{6,4},{7,5},{8,10},{9,11},{10,... | collective-permute-start | bytes 6152 | tf_op jit(solution)/shard_map/ppermute | solution.py:20
  155.0 24.3 %collective-permute-start.12 = (f32[4,128]{1,0:T(4,128)S(1)}, f32[4,128]{1,0:T(4,128)S(1)}, u32[]{:S(2)}, u32[]{:S(2)}) collective-permute-start(f32[4,128]{1,0:T(4,128)S(1)} %add.77), channel_id=1, source_target_pairs={{0,4},{1,5},{2,6},{3,7},{4,0},{5,1},{6,2},{7,3},{8,12},{9,13},{10,... | collective-permute-start | bytes 6152 | tf_op jit(solution)/shard_map/ppermute | solution.py:20
  169.9 25.7 %collective-permute-start.10 = (bf16[18,4096]{1,0:T(8,128)(2,1)S(1)}, bf16[18,4096]{1,0:T(8,128)(2,1)S(1)}, u32[]{:S(2)}, u32[]{:S(2)}) collective-permute-start(bf16[18,4096]{1,0:T(8,128)(2,1)S(1)} %pad_maximum_fusion.4), channel_id=1, source_target_pairs={{0,256},{64,320},{128,384},{192,448},{256,0},{320,64},{384,128},{4... | collective-permute-start | bytes 442376 | tf_op jit(solution)/shard_map/ppermute | solution.py:20
  180.4 26.3 %copy-start.3 = (f32[8,8,32,128]{3,2,1,0:T(8,128)S(1)}, f32[8,8,32,128]{3,2,1,0:T(8,128)}, u32[]{:S(2)}) copy-start(f32[8,8,32,128]{3,2,1,0:T(8,128)} %copy.60) | copy-start | bytes 3145732
  180.4 39.2 %collective-permute-start.13 = (bf16[512,512]{0,1:T(8,128)(2,1)}, bf16[512,512]{0,1:T(8,128)(2,1)}, u32[]{:S(2)}, u32[]{:S(2)}) collective-permute-start(bf16[512,512]{0,1:T(8,128)(2,1)} %fusion.8), channel_id=1, source_target_pairs={{8,0},{16,8},{24,16},{32,24},{40,32},{48,40},{56,48},{0,56},{9,1},... | collective-permute-start | bytes 1572872 | tf_op jit(solution)/shard_map/ppermute | solution.py:16
  197.5 24.2 %collective-permute-start.16 = (bf16[34,4096]{1,0:T(8,128)(2,1)S(1)}, bf16[34,4096]{1,0:T(8,128)(2,1)}, u32[]{:S(2)}, u32[]{:S(2)}) collective-permute-start(bf16[34,4096]{1,0:T(8,128)(2,1)S(1)} %pad_maximum_fusion.2), channel_id=1, source_target_pairs={{0,192},{64,128},{128,64},{192,0},{256,448},{320,384},{384,320},{4... | collective-permute-start | bytes 835592 | tf_op jit(solution)/shard_map/ppermute | solution.py:20
  200.3 21.4 %collective-permute-start.15 = (bf16[34,4096]{1,0:T(8,128)(2,1)S(1)}, bf16[34,4096]{1,0:T(8,128)(2,1)}, u32[]{:S(2)}, u32[]{:S(2)}) collective-permute-start(bf16[34,4096]{1,0:T(8,128)(2,1)S(1)} %pad_maximum_fusion.2), channel_id=1, source_target_pairs={{0,128},{64,192},{128,0},{192,64},{256,384},{320,448},{384,256},{4... | collective-permute-start | bytes 835592 | tf_op jit(solution)/shard_map/ppermute | solution.py:20
  203.0 18.7 %collective-permute-start.14 = (bf16[34,4096]{1,0:T(8,128)(2,1)S(1)}, bf16[34,4096]{1,0:T(8,128)(2,1)}, u32[]{:S(2)}, u32[]{:S(2)}) collective-permute-start(bf16[34,4096]{1,0:T(8,128)(2,1)S(1)} %pad_maximum_fusion.2), channel_id=1, source_target_pairs={{0,64},{64,0},{128,192},{192,128},{256,320},{320,256},{384,448},{4... | collective-permute-start | bytes 835592 | tf_op jit(solution)/shard_map/ppermute | solution.py:20
  211.6 5.0 %copy-start.13 = (bf16[64,4096]{1,0:T(8,128)(2,1)S(1)}, bf16[64,4096]{1,0:T(8,128)(2,1)}, u32[]{:S(2)}) copy-start(bf16[64,4096]{1,0:T(8,128)(2,1)} %get-tuple-element.28) | copy-start | bytes 1572868
  224.5 1.3 copy-start.14

commit v7 on v6

--- a/solution.py
+++ b/solution.py
@@ -87,10 +87,9 @@
     )(failed, spans, weight, first, second)
 
 
-def assemble_kernel(failed_ref, own_ref, fresh0_ref, fresh1_ref, fresh2_ref, fresh3_ref, grads_ref, sent_ref, restored_ref):
+def assemble_kernel(failed_ref, own_ref, fresh0_ref, fresh1_ref, fresh2_ref, fresh3_ref, sent_ref, restored_ref):
     me = lax.axis_index("replica")
     here = failed_ref[lax.axis_index("section"), lax.axis_index("tensor")] == me
-    rows = own_ref.shape[0]
     groups, _, cols = sent_ref.shape
     part = fresh0_ref.shape[0]
     for k, fresh_ref in enumerate((fresh0_ref, fresh1_ref, fresh2_ref, fresh3_ref)):
@@ -100,26 +99,21 @@
             block = jnp.where(here, fresh_ref[:, span], own_ref[at, span])
             restored_ref[at, span] = block
             sent_ref[t, at, :] = block
-    for t in range(groups):
-        total = grads_ref[0, t].astype(WIDE)
-        for x in range(1, PLANE):
-            total = total + grads_ref[x, t].astype(WIDE)
-        sent_ref[t, rows:, :] = total.astype(SHORT)
-
-
-def assemble(failed, own, fresh, grads):
+
+
+def assemble(failed, own, fresh):
     rows, width = own.shape
-    _, groups, part, cols = grads.shape
+    groups = 8
     return pl.pallas_call(
         assemble_kernel,
         out_shape=(
-            jax.ShapeDtypeStruct((groups, rows + part, cols), SHORT),
+            jax.ShapeDtypeStruct((groups, rows, width // groups), SHORT),
             jax.ShapeDtypeStruct((rows, width), SHORT),
         ),
-        in_specs=[pl.BlockSpec(memory_space=pltpu.SMEM)] + [pl.BlockSpec(memory_space=pltpu.VMEM)] * 6,
+        in_specs=[pl.BlockSpec(memory_space=pltpu.SMEM)] + [pl.BlockSpec(memory_space=pltpu.VMEM)] * 5,
         out_specs=(pl.BlockSpec(memory_space=pltpu.VMEM),) * 2,
         name="assemble",
-    )(failed, own, *fresh, grads)
+    )(failed, own, *fresh)
 
 
 def adam(first, second, grad):
@@ -161,30 +155,29 @@
     held = tied(key_grads[0, 0].T, mask)
     held = doubled(doubled(held, my_tensor, 0), my_tensor, 1)
     held, served = lax.optimization_barrier((held, served))
-    fresh_weight = served[0] + swap(served[0], "replica", PLANE)
     held = doubled(held, my_tensor, 2)
-    held, fresh_weight, squares = lax.optimization_barrier((held, fresh_weight, squares))
+    held, squares, served = lax.optimization_barrier((held, squares, served))
     kg_all = held.reshape(8 * rows, tokens)
     inverse_rms = 1.0 / jnp.sqrt(jnp.sum(squares, axis=0).reshape(tokens) / width + 1e-05)
+    fresh_weight = served[0] + swap(served[0], "replica", PLANE)
     fresh_weight = [fresh_weight] + [swap(fresh_weight, "replica", bit) for bit in (1, 2, 3)]
 
     normed = (x * inverse_rms[:, None]).astype(SHORT)
     grad = lax.dot_general(kg_all, normed, (((1,), (0,)), ((), ())), preferred_element_type=WIDE).astype(SHORT)
     grad = grad.reshape(8, PLANE, part, cols).transpose(1, 0, 2, 3)
-    grad = exchange_x(grad)
-
-    sent, restored_weight = assemble(failed_replica, own_weight, fresh_weight, grad)
-    got = lax.all_to_all(sent, "tensor", 0, 0, tiled=True)
-    weight_cols = got[:, :rows].reshape(8 * rows, cols)
-    grad_rows = got[:, rows:].transpose(1, 0, 2).reshape(part, width)
+    grad = jnp.sum(exchange_x(grad).astype(WIDE), axis=0).astype(SHORT)
+    grad_rows = lax.all_to_all(grad, "tensor", 0, 0, tiled=True)
+
+    sent, restored_weight = assemble(failed_replica, own_weight, fresh_weight)
+    sent, grad_rows = lax.optimization_barrier((sent, grad_rows))
+    weight_cols = lax.all_to_all(sent, "tensor", 0, 0, tiled=True).reshape(8 * rows, cols)
+    grad_rows = grad_rows.transpose(1, 0, 2).reshape(part, width)
     mean_rows = (grad_rows.astype(WIDE) + swap(grad_rows, "replica", PLANE).astype(WIDE)) / copies
 
     keys = lax.dot_general(weight_cols, normed, (((1,), (1,)), ((), ())), preferred_element_type=WIDE).astype(SHORT)
     feature = lax.dot_general(kg_all, weight_cols, (((0,), (0,)), ((), ())), preferred_element_type=WIDE)
     product = jnp.sum(feature * x, axis=1).reshape(-1, 128)
-    product = product + swap(product, "tensor", 1)
-    product, mean_rows = lax.optimization_barrier((product, mean_rows))
-    for bit in (2, 4):
+    for bit in (1, 2, 4):
         product = product + swap(product, "tensor", bit)
     product = product.reshape(tokens, 1)
     scale = inverse_rms[:, None]
@@ -206,8 +199,7 @@
     fresh_update = jnp.where(columns, mine[:part], other[:part])
     fresh_sums = mine[part:] + other[part:]
     shared = jnp.concatenate([mean_rows.astype(SHORT), fresh_update, fresh_sums], axis=0)
-    shared, key_out = lax.optimization_barrier((shared, key_out))
-    shared = gather_x(shared)
+    shared = gather_x(tied(shared, weight_cols))
     mean_grad = shared[:, :part].reshape(rows, width).astype(WIDE)
     fresh_update = shared[:, part : 2 * part].reshape(rows, width).astype(WIDE)
     fresh_sums = shared[:, 2 * part :].reshape(PLANE, 2, part, -1).transpose(1, 0, 2, 3).reshape(2, rows, -1).astype(WIDE)

time: 231 us -> 237 us (1.026)
  the two profiles are of different devices: /device:TPU:1 before, /device:TPU:18 now
where the time goes in v7:
time: 237 us; the launch traced here: 235 us
  starting transfers between devices  108 us (46%)
  waiting for transfers between devices  63.6 us (27%)
  other arithmetic  19.6 us (8%)
  local copies, waits for them, and re-layouts  18.3 us (8%)
  matrix products  17.8 us (8%)
  Pallas kernels  5.7 us (2%)
    ppermute x15, starting transfers between devices, swap(): lax.ppermute(block, axis, [(i, i ^ bit) for i in range(lax.axis_size(axis...  73.6 us
    all_to_all x1, waiting for transfers between devices, shards(): lax.all_to_all(sent, 'tensor', 0, 0, tiled=True).reshape(8 * rows, cols)  20.5 us
    all_to_all x1, waiting for transfers between devices, shards(): lax.all_to_all(keys.reshape(8, rows, tokens), 'tensor', 0, 0, tiled=True)  13.7 us
    dot_general x4, matrix products, checksum(): jnp.einsum('jnc,cp->jnp', shaped, probe_matrix, precision=lax.Precision.H...  12.5 us
    ppermute x15, waiting for transfers between devices, swap(): lax.ppermute(block, axis, [(i, i ^ bit) for i in range(lax.axis_size(axis...  11.6 us
    all_to_all x1, starting transfers between devices, shards(): lax.all_to_all(sent, 'tensor', 0, 0, tiled=True).reshape(8 * rows, cols)  9.81 us
    all_to_all x2, starting transfers between devices, exchange_x(): lax.all_to_all(block, 'replica', 0, 0, axis_index_groups=groups, tiled=True)  9.78 us
    unnamed x37, local copies, waits for them, and re-layouts  9.5 us
  transfers between devices with their start and end apart: 23, of which 11 were waited for; matrix products, arithmetic and copies ran while one was open for 20% of the time, Pallas kernels for 2%

profile of v7, /device:TPU:18, one launch (start us, length us, event | category | flops | bytes accessed | tf_op | source)
XLA Modules:
  0.0 235.0 jit_solution(2809009904862901182)
XLA Ops:
  0.6 2.1 copy.56
  2.7 3.4 %serve.1 = bf16[4,3,16,4096]{3,2,1,0:T(8,128)(2,1)} custom-call(s32[8,8]{1,0:T(8,128)} %failed_ref.3, s32[8,8]{1,0:T(8,128)} %spans_ref.1, bf16[64,4096]{1,0:T(8,128)(2,1)} %bitcast.140, f32[64,4096]{1,0:T(8,128)} %bitcast.124, f32[64,4096]{1,0:T(8,128)} %bitcast.126), custom_call_target="tpu_custom_call" | custom-call | tf_op jit(solution)/shard_map/serve/pallas_call | solution.py:81
  6.1 5.0 %all-to-all-start = ((bf16[4,3,16,4096]{3,2,1,0:T(8,128)(2,1)}), bf16[4,3,16,4096]{3,2,1,0:T(8,128)(2,1)}, u32[]{:S(2)}, u32[]{:S(2)}) async-start(bf16[4,3,16,4096]{3,2,1,0:T(8,128)(2,1)} %serve.1), calls=%async_computation | async-start | bytes 3145728 | tf_op jit(solution)/shard_map/all_to_all | solution.py:25
  11.1 9.2 %collective-permute-start = (bf16[64,512]{1,0:T(8,128)(2,1)S(1)}, bf16[64,512]{1,0:T(8,128)(2,1)S(1)}, u32[]{:S(2)}, u32[]{:S(2)}) collective-permute-start(bf16[64,512]{1,0:T(8,128)(2,1)S(1)} %bitcast.155), channel_id=1, source_target_pairs={{0,4},{1,5},{2,6},{3,7},{4,0},{5,1},{6,2},{7,3},{8,12},{9,13},{10,... | collective-permute-start | bytes 196616 | tf_op jit(solution)/shard_map/ppermute | solution.py:20
  20.7 4.2 %fusion.23 = f32[64,32,8]{1,2,0:T(8,128)S(1)} fusion(f32[64,32,128]{2,1,0:T(8,128)S(1)} %bitcast.133, f32[128,8]{0,1:T(8,128)S(1)} %copy-done), kind=kOutput, calls=%fused_computation.55 | convolution fusion | flops 25165824 | bytes 1118208 | tf_op jit(solution)/shard_map/jnc,cp->jnp/dot_general | solution.py:191
  24.9 4.2 %fusion.25 = f32[64,32,8]{1,2,0:T(8,128)S(1)} fusion(f32[64,32,128]{2,1,0:T(8,128)S(1)} %bitcast.132, f32[128,8]{0,1:T(8,128)S(1)} %copy-done), kind=kOutput, calls=%fused_computation.57 | convolution fusion | flops 25165824 | bytes 1118208 | tf_op jit(solution)/shard_map/jnc,cp->jnp/dot_general | solution.py:191
  29.7 5.2 %collective-permute-start.1 = (bf16[2,64,512]{2,1,0:T(8,128)(2,1)}, bf16[2,64,512]{2,1,0:T(8,128)(2,1)S(1)}, u32[]{:S(2)}, u32[]{:S(2)}) collective-permute-start(bf16[2,64,512]{2,1,0:T(8,128)(2,1)} %pad_maximum_fusion.5), channel_id=1, source_target_pairs={{0,2},{1,3},{2,0},{3,1},{4,6},{5,7},{6,4},{7,5},{8,10},{9,11},{10,... | collective-permute-start | bytes 393224 | tf_op jit(solution)/shard_map/ppermute | solution.py:20
  39.3 2.8 %collective-permute-done.1 = bf16[2,64,512]{2,1,0:T(8,128)(2,1)S(1)} collective-permute-done((bf16[2,64,512]{2,1,0:T(8,128)(2,1)}, bf16[2,64,512]{2,1,0:T(8,128)(2,1)S(1)}, u32[]{:S(2)}, u32[]{:S(2)}) %collective-permute-start.1) | collective-permute-done | bytes 131104 | tf_op jit(solution)/shard_map/ppermute | solution.py:20
  42.2 1.7 reduce_sum.63
  43.9 3.0 %collective-permute-start.2 = (bf16[2,2,64,512]{3,2,1,0:T(8,128)(2,1)S(1)}, bf16[2,2,64,512]{3,2,1,0:T(8,128)(2,1)S(1)}, u32[]{:S(2)}, u32[]{:S(2)}) collective-permute-start(bf16[2,2,64,512]{3,2,1,0:T(8,128)(2,1)S(1)} %pad_maximum_fusion.3), channel_id=1, source_target_pairs={{0,1},{1,0},{2,3},{3,2},{4,5},{5,4},{6,7},{7,6},{8,9},{9,8},{10,11... | collective-permute-start | bytes 786440 | tf_op jit(solution)/shard_map/ppermute | solution.py:20
  47.8 5.3 %all-to-all-start.1 = ((f32[8,4,128]{2,1,0:T(4,128)}), f32[8,4,128]{2,1,0:T(4,128)}, u32[]{:S(2)}, u32[]{:S(2)}) async-start(f32[8,4,128]{2,1,0:T(4,128)} %broadcast_in_dim.32), calls=%async_computation.1 | async-start | bytes 32768 | tf_op jit(solution)/shard_map/all_to_all | solution.py:154
  54.2 9.4 %all-to-all-done.1 = f32[8,4,128]{2,1,0:T(4,128)} async-done(((f32[8,4,128]{2,1,0:T(4,128)}), f32[8,4,128]{2,1,0:T(4,128)}, u32[]{:S(2)}, u32[]{:S(2)}) %all-to-all-start.1) | async-done | bytes 16416 | tf_op jit(solution)/shard_map/all_to_all | solution.py:154
  65.1 10.9 %collective-permute-start.4 = (bf16[16,4096]{1,0:T(8,128)(2,1)}, bf16[16,4096]{1,0:T(8,128)(2,1)}, u32[]{:S(2)}, u32[]{:S(2)}) collective-permute-start(bf16[16,4096]{1,0:T(8,128)(2,1)} %slice_bitcast_fusion), channel_id=1, source_target_pairs={{0,256},{64,320},{128,384},{192,448},{256,0},{320,64},{384,128},{4... | collective-permute-start | bytes 393224 | tf_op jit(solution)/shard_map/ppermute | solution.py:20
  77.3 4.8 %all-to-all-start.2 = ((bf16[4,8,16,512]{3,2,1,0:T(8,128)(2,1)}), bf16[4,8,16,512]{3,2,1,0:T(8,128)(2,1)}, u32[]{:S(2)}, u32[]{:S(2)}) async-start(bf16[4,8,16,512]{3,2,1,0:T(8,128)(2,1)} %bitcast.123), calls=%async_computation.2 | async-start | bytes 1048576 | tf_op jit(solution)/shard_map/all_to_all | solution.py:25
  82.9 5.9 %all-to-all-done.2 = bf16[4,8,16,512]{3,2,1,0:T(8,128)(2,1)} async-done(((bf16[4,8,16,512]{3,2,1,0:T(8,128)(2,1)}), bf16[4,8,16,512]{3,2,1,0:T(8,128)(2,1)}, u32[]{:S(2)}, u32[]{:S(2)}) %all-to-all-start.2) | async-done | bytes 524320 | tf_op jit(solution)/shard_map/all_to_all | solution.py:25
  88.8 1.8 reduce_sum.66
  90.6 4.0 %all-to-all-start.3 = ((bf16[8,16,512]{2,1,0:T(8,128)(2,1)}), bf16[8,16,512]{2,1,0:T(8,128)(2,1)}, u32[]{:S(2)}, u32[]{:S(2)}) async-start(bf16[8,16,512]{2,1,0:T(8,128)(2,1)} %reduce_sum.66), calls=%async_computation.3 | async-start | bytes 262144 | tf_op jit(solution)/shard_map/all_to_all | solution.py:169
  94.7 1.6 fusion.29.fresh0_ref
  96.2 1.9 collective-permute-start.7
  98.2 5.4 %collective-permute-start.6 = (bf16[16,4096]{1,0:T(8,128)(2,1)}, bf16[16,4096]{1,0:T(8,128)(2,1)}, u32[]{:S(2)}, u32[]{:S(2)}) collective-permute-start(bf16[16,4096]{1,0:T(8,128)(2,1)} %fusion.29.fresh0_ref), channel_id=1, source_target_pairs={{0,128},{64,192},{128,0},{192,64},{256,384},{320,448},{384,256},{4... | collective-permute-start | bytes 393224 | tf_op jit(solution)/shard_map/ppermute | solution.py:20
  103.6 2.5 %collective-permute-start.5 = (bf16[16,4096]{1,0:T(8,128)(2,1)}, bf16[16,4096]{1,0:T(8,128)(2,1)}, u32[]{:S(2)}, u32[]{:S(2)}) collective-permute-start(bf16[16,4096]{1,0:T(8,128)(2,1)} %fusion.29.fresh0_ref), channel_id=1, source_target_pairs={{0,64},{64,0},{128,192},{192,128},{256,320},{320,256},{384,448},{4... | collective-permute-start | bytes 393224 | tf_op jit(solution)/shard_map/ppermute | solution.py:20
  106.1 2.1 convolution_convert_fusion.2
  109.2 1.6 collective-permute-done.5.fresh1_ref
  110.8 2.3 assemble.1
  114.0 3.6 %collective-permute-start.12 = (bf16[16,4096]{1,0:T(8,128)(2,1)S(1)}, bf16[16,4096]{1,0:T(8,128)(2,1)S(1)}, u32[]{:S(2)}, u32[]{:S(2)}) collective-permute-start(bf16[16,4096]{1,0:T(8,128)(2,1)S(1)} %bitcast.153), channel_id=1, source_target_pairs={{0,256},{64,320},{128,384},{192,448},{256,0},{320,64},{384,128},{4... | collective-permute-start | bytes 393224 | tf_op jit(solution)/shard_map/ppermute | solution.py:20
  118.3 2.0 copy.74
  120.2 9.8 %all-to-all-start.4 = ((bf16[8,64,512]{2,1,0:T(8,128)(2,1)}), bf16[8,64,512]{2,1,0:T(8,128)(2,1)}, u32[]{:S(2)}, u32[]{:S(2)}) async-start(bf16[8,64,512]{2,1,0:T(8,128)(2,1)} %get-tuple-element.23), calls=%async_computation.4 | async-start | bytes 1048576 | tf_op jit(solution)/shard_map/all_to_all | solution.py:173
  134.0 10.0 %collective-permute-start.13 = (bf16[18,4096]{1,0:T(8,128)(2,1)}, bf16[18,4096]{1,0:T(8,128)(2,1)}, u32[]{:S(2)}, u32[]{:S(2)}) collective-permute-start(bf16[18,4096]{1,0:T(8,128)(2,1)} %pad_maximum_fusion.4), channel_id=1, source_target_pairs={{0,256},{64,320},{128,384},{192,448},{256,0},{320,64},{384,128},{4... | collective-permute-start | bytes 442376 | tf_op jit(solution)/shard_map/ppermute | solution.py:20
  144.0 2.1 fusion.21
  146.9 1.6 copy.68
  148.6 2.5 %collective-permute-done.13 = bf16[18,4096]{1,0:T(8,128)(2,1)} collective-permute-done((bf16[18,4096]{1,0:T(8,128)(2,1)}, bf16[18,4096]{1,0:T(8,128)(2,1)}, u32[]{:S(2)}, u32[]{:S(2)}) %collective-permute-start.13) | collective-permute-done | bytes 147488 | tf_op jit(solution)/shard_map/ppermute | solution.py:20
  151.1 1.6 slice_select_fusion
  152.6 20.5 %all-to-all-done.4 = bf16[8,64,512]{2,1,0:T(8,128)(2,1)} async-done(((bf16[8,64,512]{2,1,0:T(8,128)(2,1)}), bf16[8,64,512]{2,1,0:T(8,128)(2,1)}, u32[]{:S(2)}, u32[]{:S(2)}) %all-to-all-start.4) | async-done | bytes 524320 | tf_op jit(solution)/shard_map/all_to_all | solution.py:173
  173.2 2.5 %fusion.8 = (f32[512]{0:T(512)S(1)}, f32[512,512]{0,1:T(8,128)}) fusion(bf16[512,512]{0,1:T(8,128)(2,1)S(1)} %collective-permute-done.3, bf16[512,512]{1,0:T(8,128)(2,1)S(1)} %bitcast.139, bf16[512,512]{1,0:T(8,128)(2,1)} %bitcast.20), kind=kOutput, calls=%fused_computation.20 | convolution fusion | flops 269221376 | bytes 2623488 | tf_op jit(solution)/shard_map/dot_general | solution.py:178
  175.7 1.9 collective-permute-start.8
  178.5 2.7 %collective-permute-done.8 = f32[4,128]{1,0:T(4,128)S(1)} collective-permute-done((f32[4,128]{1,0:T(4,128)S(1)}, f32[4,128]{1,0:T(4,128)S(1)}, u32[]{:S(2)}, u32[]{:S(2)}) %collective-permute-start.8) | collective-permute-done | bytes 2080 | tf_op jit(solution)/shard_map/ppermute | solution.py:20
  181.2 6.0 %collective-permute-start.9 = (f32[4,128]{1,0:T(4,128)S(1)}, f32[4,128]{1,0:T(4,128)S(1)}, u32[]{:S(2)}, u32[]{:S(2)}) collective-permute-start(f32[4,128]{1,0:T(4,128)S(1)} %bitcast_add_fusion), channel_id=1, source_target_pairs={{0,2},{1,3},{2,0},{3,1},{4,6},{5,7},{6,4},{7,5},{8,10},{9,11},{10,... | collective-permute-start | bytes 6152 | tf_op jit(solution)/shard_map/ppermute | solution.py:20
  187.2 2.2 collective-permute-start.16
  189.5 4.1 %collective-permute-start.15 = (bf16[34,4096]{1,0:T(8,128)(2,1)S(1)}, bf16[34,4096]{1,0:T(8,128)(2,1)}, u32[]{:S(2)}, u32[]{:S(2)}) collective-permute-start(bf16[34,4096]{1,0:T(8,128)(2,1)S(1)} %pad_maximum_fusion.2), channel_id=1, source_target_pairs={{0,128},{64,192},{128,0},{192,64},{256,384},{320,448},{384,256},{4... | collective-permute-start | bytes 835592 | tf_op jit(solution)/shard_map/ppermute | solution.py:20
  193.6 3.7 %collective-permute-start.14 = (bf16[34,4096]{1,0:T(8,128)(2,1)S(1)}, bf16[34,4096]{1,0:T(8,128)(2,1)}, u32[]{:S(2)}, u32[]{:S(2)}) collective-permute-start(bf16[34,4096]{1,0:T(8,128)(2,1)S(1)} %pad_maximum_fusion.2), channel_id=1, source_target_pairs={{0,64},{64,0},{128,192},{192,128},{256,320},{320,256},{384,448},{4... | collective-permute-start | bytes 835592 | tf_op jit(solution)/shard_map/ppermute | solution.py:20
  197.3 4.0 %collective-permute-start.10 = (f32[4,128]{1,0:T(4,128)S(1)}, f32[4,128]{1,0:T(4,128)S(1)}, u32[]{:S(2)}, u32[]{:S(2)}) collective-permute-start(f32[4,128]{1,0:T(4,128)S(1)} %fusion.38), channel_id=1, source_target_pairs={{0,4},{1,5},{2,6},{3,7},{4,0},{5,1},{6,2},{7,3},{8,12},{9,13},{10,... | collective-permute-start | bytes 6152 | tf_op jit(solution)/shard_map/ppermute | solution.py:20
  201.3 2.3 convolution_convert_fusion
  203.6 5.6 %all-to-all-start.5 = ((bf16[8,64,512]{2,1,0:T(8,128)(2,1)}), bf16[8,64,512]{2,1,0:T(8,128)(2,1)S(1)}, u32[]{:S(2)}, u32[]{:S(2)}) async-start(bf16[8,64,512]{2,1,0:T(8,128)(2,1)} %bitcast.148), calls=%async_computation.5 | async-start | bytes 1048576 | tf_op jit(solution)/shard_map/all_to_all | solution.py:186
  209.2 2.3 fusion.7
  213.7 1.5 convert_select_fusion
  216.1 2.4 %collective-permute-done.11 = bf16[512,512]{0,1:T(8,128)(2,1)} collective-permute-done((bf16[512,512]{0,1:T(8,128)(2,1)}, bf16[512,512]{0,1:T(8,128)(2,1)}, u32[]{:S(2)}, u32[]{:S(2)}) %collective-permute-start.11) | collective-permute-done | bytes 524320 | tf_op jit(solution)/shard_map/ppermute | solution.py:16
  218.5 2.0 copy.67
  220.6 13.7 %all-to-all-done.5 = bf16[8,64,512]{2,1,0:T(8,128)(2,1)S(1)} async-done(((bf16[8,64,512]{2,1,0:T(8,128)(2,1)}), bf16[8,64,512]{2,1,0:T(8,128)(2,1)S(1)}, u32[]{:S(2)}, u32[]{:S(2)}) %all-to-all-start.5) | async-done | bytes 524320 | tf_op jit(solution)/shard_map/all_to_all | solution.py:186
  (93 shorter events, 22.3 us)
Async XLA Ops:
  0.6 20.1 %copy-start = (f32[128,8]{0,1:T(8,128)S(1)}, f32[128,8]{0,1:T(8,128)}, u32[]{:S(2)}) copy-start(f32[128,8]{0,1:T(8,128)} %param.13) | copy-start | bytes 12292
  2.7 44.3 %collective-permute-start.3 = (bf16[512,512]{0,1:T(8,128)(2,1)}, bf16[512,512]{0,1:T(8,128)(2,1)S(1)}, u32[]{:S(2)}, u32[]{:S(2)}) collective-permute-start(bf16[512,512]{0,1:T(8,128)(2,1)} %bitcast.13), channel_id=1, source_target_pairs={{56,0},{0,8},{8,16},{16,24},{24,32},{32,40},{40,48},{48,56},{57,1}... | collective-permute-start | bytes 1572872 | tf_op jit(solution)/shard_map/ppermute | solution.py:16
  6.1 5.0 %copy-start.13 = (bf16[1,1,512,64]{2,3,1,0:T(8,128)(2,1)S(1)}, bf16[1,1,512,64]{2,3,1,0:T(8,128)(2,1)}, u32[]{:S(2)}) copy-start(bf16[1,1,512,64]{2,3,1,0:T(8,128)(2,1)} %param.9) | copy-start | bytes 196612
  6.1 14.2 %copy-start.2 = (f32[1,1,64,4096]{3,2,1,0:T(8,128)S(1)}, f32[1,1,64,4096]{3,2,1,0:T(8,128)}, u32[]{:S(2)}) copy-start(f32[1,1,64,4096]{3,2,1,0:T(8,128)} %param.12) | copy-start | bytes 3145732
  6.1 36.1 %all-to-all-start = ((bf16[4,3,16,4096]{3,2,1,0:T(8,128)(2,1)}), bf16[4,3,16,4096]{3,2,1,0:T(8,128)(2,1)}, u32[]{:S(2)}, u32[]{:S(2)}) async-start(bf16[4,3,16,4096]{3,2,1,0:T(8,128)(2,1)} %serve.1), calls=%async_computation | async-start | bytes 3145728 | tf_op jit(solution)/shard_map/all_to_all | solution.py:25
  11.1 9.4 %copy-start.1 = (f32[1,1,64,4096]{3,2,1,0:T(8,128)S(1)}, f32[1,1,64,4096]{3,2,1,0:T(8,128)}, u32[]{:S(2)}) copy-start(f32[1,1,64,4096]{3,2,1,0:T(8,128)} %param.11) | copy-start | bytes 3145732
  11.1 18.0 %collective-permute-start = (bf16[64,512]{1,0:T(8,128)(2,1)S(1)}, bf16[64,512]{1,0:T(8,128)(2,1)S(1)}, u32[]{:S(2)}, u32[]{:S(2)}) collective-permute-start(bf16[64,512]{1,0:T(8,128)(2,1)S(1)} %bitcast.155), channel_id=1, source_target_pairs={{0,4},{1,5},{2,6},{3,7},{4,0},{5,1},{6,2},{7,3},{8,12},{9,13},{10,... | collective-permute-start | bytes 196616 | tf_op jit(solution)/shard_map/ppermute | solution.py:20
  29.7 12.4 %collective-permute-start.1 = (bf16[2,64,512]{2,1,0:T(8,128)(2,1)}, bf16[2,64,512]{2,1,0:T(8,128)(2,1)S(1)}, u32[]{:S(2)}, u32[]{:S(2)}) collective-permute-start(bf16[2,64,512]{2,1,0:T(8,128)(2,1)} %pad_maximum_fusion.5), channel_id=1, source_target_pairs={{0,2},{1,3},{2,0},{3,1},{4,6},{5,7},{6,4},{7,5},{8,10},{9,11},{10,... | collective-permute-start | bytes 393224 | tf_op jit(solution)/shard_map/ppermute | solution.py:20
  43.9 10.2 %collective-permute-start.2 = (bf16[2,2,64,512]{3,2,1,0:T(8,128)(2,1)S(1)}, bf16[2,2,64,512]{3,2,1,0:T(8,128)(2,1)S(1)}, u32[]{:S(2)}, u32[]{:S(2)}) collective-permute-start(bf16[2,2,64,512]{3,2,1,0:T(8,128)(2,1)S(1)} %pad_maximum_fusion.3), channel_id=1, source_target_pairs={{0,1},{1,0},{2,3},{3,2},{4,5},{5,4},{6,7},{7,6},{8,9},{9,8},{10,11... | collective-permute-start | bytes 786440 | tf_op jit(solution)/shard_map/ppermute | solution.py:20
  47.8 15.9 %all-to-all-start.1 = ((f32[8,4,128]{2,1,0:T(4,128)}), f32[8,4,128]{2,1,0:T(4,128)}, u32[]{:S(2)}, u32[]{:S(2)}) async-start(f32[8,4,128]{2,1,0:T(4,128)} %broadcast_in_dim.32), calls=%async_computation.1 | async-start | bytes 32768 | tf_op jit(solution)/shard_map/all_to_all | solution.py:154
  54.2 23.1 %copy-start.4 = (bf16[2,2,2,64,512]{4,3,2,1,0:T(8,128)(2,1)}, bf16[2,2,2,64,512]{4,3,2,1,0:T(8,128)(2,1)S(1)}, u32[]{:S(2)}) copy-start(bf16[2,2,2,64,512]{4,3,2,1,0:T(8,128)(2,1)S(1)} %pad_maximum_fusion.1) | copy-start | bytes 1572868
  65.1 29.6 %collective-permute-start.4 = (bf16[16,4096]{1,0:T(8,128)(2,1)}, bf16[16,4096]{1,0:T(8,128)(2,1)}, u32[]{:S(2)}, u32[]{:S(2)}) collective-permute-start(bf16[16,4096]{1,0:T(8,128)(2,1)} %slice_bitcast_fusion), channel_id=1, source_target_pairs={{0,256},{64,320},{128,384},{192,448},{256,0},{320,64},{384,128},{4... | collective-permute-start | bytes 393224 | tf_op jit(solution)/shard_map/ppermute | solution.py:20
  77.3 11.5 %all-to-all-start.2 = ((bf16[4,8,16,512]{3,2,1,0:T(8,128)(2,1)}), bf16[4,8,16,512]{3,2,1,0:T(8,128)(2,1)}, u32[]{:S(2)}, u32[]{:S(2)}) async-start(bf16[4,8,16,512]{3,2,1,0:T(8,128)(2,1)} %bitcast.123), calls=%async_computation.2 | async-start | bytes 1048576 | tf_op jit(solution)/shard_map/all_to_all | solution.py:25
  90.6 22.5 %all-to-all-start.3 = ((bf16[8,16,512]{2,1,0:T(8,128)(2,1)}), bf16[8,16,512]{2,1,0:T(8,128)(2,1)}, u32[]{:S(2)}, u32[]{:S(2)}) async-start(bf16[8,16,512]{2,1,0:T(8,128)(2,1)} %reduce_sum.66), calls=%async_computation.3 | async-start | bytes 262144 | tf_op jit(solution)/shard_map/all_to_all | solution.py:169
  96.2 13.0 %collective-permute-start.7 = (bf16[16,4096]{1,0:T(8,128)(2,1)}, bf16[16,4096]{1,0:T(8,128)(2,1)}, u32[]{:S(2)}, u32[]{:S(2)}) collective-permute-start(bf16[16,4096]{1,0:T(8,128)(2,1)} %fusion.29.fresh0_ref), channel_id=1, source_target_pairs={{0,192},{64,128},{128,64},{192,0},{256,448},{320,384},{384,320},{4... | collective-permute-start | bytes 393224 | tf_op jit(solution)/shard_map/ppermute | solution.py:20
  98.2 11.0 %collective-permute-start.6 = (bf16[16,4096]{1,0:T(8,128)(2,1)}, bf16[16,4096]{1,0:T(8,128)(2,1)}, u32[]{:S(2)}, u32[]{:S(2)}) collective-permute-start(bf16[16,4096]{1,0:T(8,128)(2,1)} %fusion.29.fresh0_ref), channel_id=1, source_target_pairs={{0,128},{64,192},{128,0},{192,64},{256,384},{320,448},{384,256},{4... | collective-permute-start | bytes 393224 | tf_op jit(solution)/shard_map/ppermute | solution.py:20
  103.6 7.2 %collective-permute-start.5 = (bf16[16,4096]{1,0:T(8,128)(2,1)}, bf16[16,4096]{1,0:T(8,128)(2,1)}, u32[]{:S(2)}, u32[]{:S(2)}) collective-permute-start(bf16[16,4096]{1,0:T(8,128)(2,1)} %fusion.29.fresh0_ref), channel_id=1, source_target_pairs={{0,64},{64,0},{128,192},{192,128},{256,320},{320,256},{384,448},{4... | collective-permute-start | bytes 393224 | tf_op jit(solution)/shard_map/ppermute | solution.py:20
  114.0 17.0 %collective-permute-start.12 = (bf16[16,4096]{1,0:T(8,128)(2,1)S(1)}, bf16[16,4096]{1,0:T(8,128)(2,1)S(1)}, u32[]{:S(2)}, u32[]{:S(2)}) collective-permute-start(bf16[16,4096]{1,0:T(8,128)(2,1)S(1)} %bitcast.153), channel_id=1, source_target_pairs={{0,256},{64,320},{128,384},{192,448},{256,0},{320,64},{384,128},{4... | collective-permute-start | bytes 393224 | tf_op jit(solution)/shard_map/ppermute | solution.py:20
  120.2 52.9 %all-to-all-start.4 = ((bf16[8,64,512]{2,1,0:T(8,128)(2,1)}), bf16[8,64,512]{2,1,0:T(8,128)(2,1)}, u32[]{:S(2)}, u32[]{:S(2)}) async-start(bf16[8,64,512]{2,1,0:T(8,128)(2,1)} %get-tuple-element.23), calls=%async_computation.4 | async-start | bytes 1048576 | tf_op jit(solution)/shard_map/all_to_all | solution.py:173
  130.0 14.0 %copy-start.3 = (bf16[8,8,32,128]{3,2,1,0:T(8,128)(2,1)S(1)}, bf16[8,8,32,128]{3,2,1,0:T(8,128)(2,1)}, u32[]{:S(2)}) copy-start(bf16[8,8,32,128]{3,2,1,0:T(8,128)(2,1)} %copy.74) | copy-start | bytes 1572868
  131.9 0.7 copy-start.6
  131.9 41.3 %copy-start.5 = (bf16[2,2,2,64,512]{4,3,2,1,0:T(8,128)(2,1)S(1)}, bf16[2,2,2,64,512]{4,3,2,1,0:T(8,128)(2,1)}, u32[]{:S(2)}) copy-start(bf16[2,2,2,64,512]{4,3,2,1,0:T(8,128)(2,1)} %copy-done.4) | copy-start | bytes 1572868
  134.0 17.1 %copy-start.7 = (bf16[16,4096]{1,0:T(8,128)(2,1)S(1)}, bf16[16,4096]{1,0:T(8,128)(2,1)}, u32[]{:S(2)}) copy-start(bf16[16,4096]{1,0:T(8,128)(2,1)} %copy-done.6) | copy-start | bytes 393220
  134.0 17.1 %collective-permute-start.13 = (bf16[18,4096]{1,0:T(8,128)(2,1)}, bf16[18,4096]{1,0:T(8,128)(2,1)}, u32[]{:S(2)}, u32[]{:S(2)}) collective-permute-start(bf16[18,4096]{1,0:T(8,128)(2,1)} %pad_maximum_fusion.4), channel_id=1, source_target_pairs={{0,256},{64,320},{128,384},{192,448},{256,0},{320,64},{384,128},{4... | collective-permute-start | bytes 442376 | tf_op jit(solution)/shard_map/ppermute | solution.py:20
  173.2 4.5 %copy-start.12 = (bf16[2,4096]{1,0:T(2,128)(2,1)S(1)}, bf16[2,4096]{1,0:T(2,128)(2,1)}, u32[]{:S(2)}) copy-start(bf16[2,4096]{1,0:T(2,128)(2,1)} %convert_element_type.105) | copy-start | bytes 49156
  173.2 14.0 %copy-start.8 = (bf16[16,4096]{1,0:T(8,128)(2,1)S(1)}, bf16[16,4096]{1,0:T(8,128)(2,1)}, u32[]{:S(2)}) copy-start(bf16[16,4096]{1,0:T(8,128)(2,1)} %slice_select_fusion) | copy-start | bytes 393220
  173.2 14.0 %copy-start.9 = (bf16[16,4096]{1,0:T(8,128)(2,1)S(1)}, bf16[16,4096]{1,0:T(8,128)(2,1)}, u32[]{:S(2)}) copy-start(bf16[16,4096]{1,0:T(8,128)(2,1)} %get-tuple-element.58) | copy-start | bytes 393220
  175.7 5.5 %collective-permute-start.8 = (f32[4,128]{1,0:T(4,128)S(1)}, f32[4,128]{1,0:T(4,128)S(1)}, u32[]{:S(2)}, u32[]{:S(2)}) collective-permute-start(f32[4,128]{1,0:T(4,128)S(1)} %bitcast.158), channel_id=1, source_target_pairs={{0,1},{1,0},{2,3},{3,2},{4,5},{5,4},{6,7},{7,6},{8,9},{9,8},{10,11... | collective-permute-start | bytes 6152 | tf_op jit(solution)/shard_map/ppermute | solution.py:20
  181.2 16.1 %collective-permute-start.9 = (f32[4,128]{1,0:T(4,128)S(1)}, f32[4,128]{1,0:T(4,128)S(1)}, u32[]{:S(2)}, u32[]{:S(2)}) collective-permute-start(f32[4,128]{1,0:T(4,128)S(1)} %bitcast_add_fusion), channel_id=1, source_target_pairs={{0,2},{1,3},{2,0},{3,1},{4,6},{5,7},{6,4},{7,5},{8,10},{9,11},{10,... | collective-permute-start | bytes 6152 | tf_op jit(solution)/shard_map/ppermute | solution.py:20
  187.2 24.3 %collective-permute-start.16 = (bf16[34,4096]{1,0:T(8,128)(2,1)S(1)}, bf16[34,4096]{1,0:T(8,128)(2,1)}, u32[]{:S(2)}, u32[]{:S(2)}) collective-permute-start(bf16[34,4096]{1,0:T(8,128)(2,1)S(1)} %pad_maximum_fusion.2), channel_id=1, source_target_pairs={{0,192},{64,128},{128,64},{192,0},{256,448},{320,384},{384,320},{4... | collective-permute-start | bytes 835592 | tf_op jit(solution)/shard_map/ppermute | solution.py:20
  189.5 22.1 %collective-permute-start.15 = (bf16[34,4096]{1,0:T(8,128)(2,1)S(1)}, bf16[34,4096]{1,0:T(8,128)(2,1)}, u32[]{:S(2)}, u32[]{:S(2)}) collective-permute-start(bf16[34,4096]{1,0:T(8,128)(2,1)S(1)} %pad_maximum_fusion.2), channel_id=1, source_target_pairs={{0,128},{64,192},{128,0},{192,64},{256,384},{320,448},{384,256},{4... | collective-permute-start | bytes 835592 | tf_op jit(solution)/shard_map/ppermute | solution.py:20
  193.6 18.0 %collective-permute-start.14 = (bf16[34,4096]{1,0:T(8,128)(2,1)S(1)}, bf16[34,4096]{1,0:T(8,128)(2,1)}, u32[]{:S(2)}, u32[]{:S(2)}) collective-permute-start(bf16[34,4096]{1,0:T(8,128)(2,1)S(1)} %pad_maximum_fusion.2), channel_id=1, source_target_pairs={{0,64},{64,0},{128,192},{192,128},{256,320},{320,256},{384,448},{4... | collective-permute-start | bytes 835592 | tf_op jit(solution)/shard_map/ppermute | solution.py:20
  197.3 12.0 %copy-start.14 = (f32[512]{0:T(512)S(1)}, f32[512]{0:T(512)}, u32[]{:S(2)}) copy-start(f32[512]{0:T(512)} %multiply_multiply_fusion) | copy-start | bytes 6148
  197.3 11.9 %collective-permute-start.10 = (f32[4,128]{1,0:T(4,128)S(1)}, f32[4,128]{1,0:T(4,128)S(1)}, u32[]{:S(2)}, u32[]{:S(2)}) collective-permute-start(f32[4,128]{1,0:T(4,128)S(1)} %fusion.38), channel_id=1, source_target_pairs={{0,4},{1,5},{2,6},{3,7},{4,0},{5,1},{6,2},{7,3},{8,12},{9,13},{10,... | collective-permute-start | bytes 6152 | tf_op jit(solution)/shard_map/ppermute | solution.py:20
  203.6 30.7 %all-to-all-start.5 = ((bf16[8,64,512]{2,1,0:T(8,128)(2,1)}), bf16[8,64,512]{2,1,0:T(8,128)(2,1)S(1)}, u32[]{:S(2)}, u32[]{:S(2)}) async-start(bf16[8,64,512]{2,1,0:T(8,128)(2,1)} %bitcast.148), calls=%async_computation.5 | async-start | bytes 1048576 | tf_op jit(solution)/shard_map/all_to_all | solution.py:186
  211.5 7.0 %collective-permute-start.11 = (bf16[512,512]{0,1:T(8,128)(2,1)}, bf16[512,512]{0,1:T(8,128)(2,1)}, u32[]{:S(2)}, u32[]{:S(2)}) collective-permute-start(bf16[512,512]{0,1:T(8,128)(2,1)} %fusion.7), channel_id=1, source_target_pairs={{8,0},{16,8},{24,16},{32,24},{40,32},{48,40},{56,48},{0,56},{9,1},... | collective-permute-start | bytes 1572872 | tf_op jit(solution)/shard_map/ppermute | solution.py:16
  213.7 1.7 copy-start.10
  213.7 1.7 copy-start.11

commit v8 on v4

--- a/solution.py
+++ b/solution.py
@@ -161,11 +161,10 @@
     held = tied(key_grads[0, 0].T, mask)
     held = doubled(doubled(held, my_tensor, 0), my_tensor, 1)
     held, served = lax.optimization_barrier((held, served))
+    held = doubled(held, my_tensor, 2)
+    held, squares, served = lax.optimization_barrier((held, squares, served))
     fresh_weight = served[0] + swap(served[0], "replica", PLANE)
-    held = doubled(held, my_tensor, 2)
-    held, fresh_weight, squares = lax.optimization_barrier((held, fresh_weight, squares))
-    served_moments = tied(served[1:], fresh_weight)
-    fresh_moments = served_moments + swap(served_moments, "replica", PLANE)
+    fresh_moments = served[1:] + swap(served[1:], "replica", PLANE)
     kg_all = held.reshape(8 * rows, tokens)
     inverse_rms = 1.0 / jnp.sqrt(jnp.sum(squares, axis=0).reshape(tokens) / width + 1e-05)
     fresh_weight = [fresh_weight] + [swap(fresh_weight, "replica", bit) for bit in (1, 2, 3)]
@@ -176,6 +175,7 @@
     grad, fresh_moments = lax.optimization_barrier((exchange_x(grad), fresh_moments))
 
     sent, restored_weight = assemble(failed_replica, own_weight, fresh_weight, grad)
+    own_first, own_second, restored_weight = lax.optimization_barrier((own_first, own_second, restored_weight))
     got = lax.all_to_all(sent, "tensor", 0, 0, tiled=True)
     weight_cols = got[:, :rows].reshape(8 * rows, cols)
     grad_rows = got[:, rows:].transpose(1, 0, 2).reshape(part, width)

time: 212 us -> 214 us (level)
  waiting for transfers between devices: 20.9 us -> 29.5 us
  starting transfers between devices: 142 us -> 136 us
  matrix products: 16.9 us -> 14.7 us
    all_to_all x1, waiting for transfers between devices: 0.36 us -> 9.23 us  [shards(): lax.all_to_all(jnp.broadcast_to(squares, (8,) + squares.shape[1:]), 'tens...]
    all_to_all x1, starting transfers between devices: 22.2 us -> 14 us  [shards(): got = lax.all_to_all(sent, 'tensor', 0, 0, tiled=True)]
    all_to_all x1, starting transfers between devices: 4.75 us -> 10.5 us  [shards(): lax.all_to_all(jnp.broadcast_to(squares, (8,) + squares.shape[1:]), 'tens...]
    ppermute x15, starting transfers between devices: 86.5 us -> 83.1 us  [swap(): lax.ppermute(block, axis, [(i, i ^ bit) for i in range(lax.axis_size(axis...]
    ppermute x2, waiting for transfers between devices: 5.86 us -> 3.15 us  [from_behind(): lax.ppermute(block, axis, [((i - distance) % n, i) for i in range(n)])]
    unnamed x32 -> x40, local copies, waits for them, and re-layouts: 6.35 us -> 5.99 us
  transfers between devices with their start and end apart: 22 -> 22, of which waited for: 9 -> 6; matrix products, arithmetic and copies ran while one was open for 17% -> 16% of each run, Pallas kernels for 0% -> 0%
where the time goes in v8:
time: 214 us; the launch traced here: 212 us
  starting transfers between devices  136 us (64%)
  waiting for transfers between devices  29.5 us (14%)
  local copies, waits for them, and re-layouts  15.6 us (7%)
  matrix products  14.7 us (7%)
  other arithmetic  8.32 us (4%)
  Pallas kernels  5.97 us (3%)
    ppermute x15, starting transfers between devices, swap(): lax.ppermute(block, axis, [(i, i ^ bit) for i in range(lax.axis_size(axis...  83.1 us
    ppermute x15, waiting for transfers between devices, swap(): lax.ppermute(block, axis, [(i, i ^ bit) for i in range(lax.axis_size(axis...  14.1 us
    all_to_all x1, starting transfers between devices, shards(): got = lax.all_to_all(sent, 'tensor', 0, 0, tiled=True)  14 us
    ppermute x2, starting transfers between devices, from_behind(): lax.ppermute(block, axis, [((i - distance) % n, i) for i in range(n)])  13.5 us
    dot_general x4, matrix products, checksum(): jnp.einsum('jnc,cp->jnp', shaped, probe_matrix, precision=lax.Precision.H...  11.6 us
    all_to_all x1, starting transfers between devices, shards(): lax.all_to_all(jnp.broadcast_to(squares, (8,) + squares.shape[1:]), 'tens...  10.5 us
    all_to_all x1, waiting for transfers between devices, shards(): lax.all_to_all(jnp.broadcast_to(squares, (8,) + squares.shape[1:]), 'tens...  9.23 us
    all_to_all x2, starting transfers between devices, exchange_x(): lax.all_to_all(block, 'replica', 0, 0, axis_index_groups=groups, tiled=True)  9.01 us
  transfers between devices with their start and end apart: 22, of which 6 were waited for; matrix products, arithmetic and copies ran while one was open for 16% of the time, Pallas kernels for 0%

profile of v8, /device:TPU:1, one launch (start us, length us, event | category | flops | bytes accessed | tf_op | source)
XLA Modules:
  0.0 212.4 jit_solution(17425237198665025740)
XLA Ops:
  0.6 3.4 %serve.1 = bf16[4,3,16,4096]{3,2,1,0:T(8,128)(2,1)} custom-call(s32[8,8]{1,0:T(8,128)} %failed_ref.3, s32[8,8]{1,0:T(8,128)} %spans_ref.1, bf16[64,4096]{1,0:T(8,128)(2,1)} %bitcast.151, f32[64,4096]{1,0:T(8,128)} %bitcast.134, f32[64,4096]{1,0:T(8,128)} %bitcast.137), custom_call_target="tpu_custom_call" | custom-call | tf_op jit(solution)/shard_map/serve/pallas_call | solution.py:81
  4.1 5.0 %all-to-all-start = ((bf16[4,3,16,4096]{3,2,1,0:T(8,128)(2,1)}), bf16[4,3,16,4096]{3,2,1,0:T(8,128)(2,1)S(1)}, u32[]{:S(2)}, u32[]{:S(2)}) async-start(bf16[4,3,16,4096]{3,2,1,0:T(8,128)(2,1)} %serve.1), calls=%async_computation | async-start | bytes 3145728 | tf_op jit(solution)/shard_map/all_to_all | solution.py:25
  9.0 8.8 %collective-permute-start = (bf16[64,512]{1,0:T(8,128)(2,1)S(1)}, bf16[64,512]{1,0:T(8,128)(2,1)S(1)}, u32[]{:S(2)}, u32[]{:S(2)}) collective-permute-start(bf16[64,512]{1,0:T(8,128)(2,1)S(1)} %bitcast.168), channel_id=1, source_target_pairs={{0,4},{1,5},{2,6},{3,7},{4,0},{5,1},{6,2},{7,3},{8,12},{9,13},{10,... | collective-permute-start | bytes 196616 | tf_op jit(solution)/shard_map/ppermute | solution.py:20
  17.9 1.6 collective-permute-done
  19.5 7.0 %collective-permute-start.1 = (bf16[2,64,512]{2,1,0:T(8,128)(2,1)S(1)}, bf16[2,64,512]{2,1,0:T(8,128)(2,1)S(1)}, u32[]{:S(2)}, u32[]{:S(2)}) collective-permute-start(bf16[2,64,512]{2,1,0:T(8,128)(2,1)S(1)} %pad_maximum_fusion.4), channel_id=1, source_target_pairs={{0,2},{1,3},{2,0},{3,1},{4,6},{5,7},{6,4},{7,5},{8,10},{9,11},{10,... | collective-permute-start | bytes 393224 | tf_op jit(solution)/shard_map/ppermute | solution.py:20
  26.8 2.6 %collective-permute-start.3 = (bf16[512,512]{0,1:T(8,128)(2,1)S(1)}, bf16[512,512]{0,1:T(8,128)(2,1)S(1)}, u32[]{:S(2)}, u32[]{:S(2)}) collective-permute-start(bf16[512,512]{0,1:T(8,128)(2,1)S(1)} %bitcast.160), channel_id=1, source_target_pairs={{56,0},{0,8},{8,16},{16,24},{24,32},{32,40},{40,48},{48,56},{57,1}... | collective-permute-start | bytes 1572872 | tf_op jit(solution)/shard_map/ppermute | solution.py:16
  29.8 5.9 %collective-permute-start.2 = (bf16[2,2,64,512]{3,2,1,0:T(8,128)(2,1)S(1)}, bf16[2,2,64,512]{3,2,1,0:T(8,128)(2,1)S(1)}, u32[]{:S(2)}, u32[]{:S(2)}) collective-permute-start(bf16[2,2,64,512]{3,2,1,0:T(8,128)(2,1)S(1)} %pad_maximum_fusion.3), channel_id=1, source_target_pairs={{0,1},{1,0},{2,3},{3,2},{4,5},{5,4},{6,7},{7,6},{8,9},{9,8},{10,11... | collective-permute-start | bytes 786440 | tf_op jit(solution)/shard_map/ppermute | solution.py:20
  36.5 10.5 %all-to-all-start.1 = ((f32[8,4,128]{2,1,0:T(4,128)}), f32[8,4,128]{2,1,0:T(4,128)S(1)}, u32[]{:S(2)}, u32[]{:S(2)}) async-start(f32[8,4,128]{2,1,0:T(4,128)} %broadcast_in_dim.20), calls=%async_computation.1 | async-start | bytes 32768 | tf_op jit(solution)/shard_map/all_to_all | solution.py:160
  47.1 9.2 %all-to-all-done.1 = f32[8,4,128]{2,1,0:T(4,128)S(1)} async-done(((f32[8,4,128]{2,1,0:T(4,128)}), f32[8,4,128]{2,1,0:T(4,128)S(1)}, u32[]{:S(2)}, u32[]{:S(2)}) %all-to-all-start.1) | async-done | bytes 16416 | tf_op jit(solution)/shard_map/all_to_all | solution.py:160
  56.4 9.2 %collective-permute-start.4 = (bf16[16,4096]{1,0:T(8,128)(2,1)S(1)}, bf16[16,4096]{1,0:T(8,128)(2,1)S(1)}, u32[]{:S(2)}, u32[]{:S(2)}) collective-permute-start(bf16[16,4096]{1,0:T(8,128)(2,1)S(1)} %slice_bitcast_fusion.1), channel_id=1, source_target_pairs={{0,256},{64,320},{128,384},{192,448},{256,0},{320,64},{384,128},{4... | collective-permute-start | bytes 393224 | tf_op jit(solution)/shard_map/ppermute | solution.py:20
  65.7 4.8 %collective-permute-start.8 = (bf16[2,16,4096]{2,1,0:T(8,128)(2,1)S(1)}, bf16[2,16,4096]{2,1,0:T(8,128)(2,1)S(1)}, u32[]{:S(2)}, u32[]{:S(2)}) collective-permute-start(bf16[2,16,4096]{2,1,0:T(8,128)(2,1)S(1)} %slice.30), channel_id=1, source_target_pairs={{0,256},{64,320},{128,384},{192,448},{256,0},{320,64},{384,128},{4... | collective-permute-start | bytes 786440 | tf_op jit(solution)/shard_map/ppermute | solution.py:20
  70.9 0.8 copy.76
  71.8 4.0 %all-to-all-start.2 = ((bf16[4,8,16,512]{3,2,1,0:T(8,128)(2,1)}), bf16[4,8,16,512]{3,2,1,0:T(8,128)(2,1)S(1)}, u32[]{:S(2)}, u32[]{:S(2)}) async-start(bf16[4,8,16,512]{3,2,1,0:T(8,128)(2,1)} %bitcast.133), calls=%async_computation.2 | async-start | bytes 1048576 | tf_op jit(solution)/shard_map/all_to_all | solution.py:25
  75.8 5.0 %collective-permute-done.4 = bf16[16,4096]{1,0:T(8,128)(2,1)S(1)} collective-permute-done((bf16[16,4096]{1,0:T(8,128)(2,1)S(1)}, bf16[16,4096]{1,0:T(8,128)(2,1)S(1)}, u32[]{:S(2)}, u32[]{:S(2)}) %collective-permute-start.4) | collective-permute-done | bytes 131104 | tf_op jit(solution)/shard_map/ppermute | solution.py:20
  80.8 3.9 %collective-permute-start.7 = (bf16[16,4096]{1,0:T(8,128)(2,1)S(1)}, bf16[16,4096]{1,0:T(8,128)(2,1)S(1)}, u32[]{:S(2)}, u32[]{:S(2)}) collective-permute-start(bf16[16,4096]{1,0:T(8,128)(2,1)S(1)} %fusion.32.fresh0_ref), channel_id=1, source_target_pairs={{0,192},{64,128},{128,64},{192,0},{256,448},{320,384},{384,320},{4... | collective-permute-start | bytes 393224 | tf_op jit(solution)/shard_map/ppermute | solution.py:20
  84.7 2.5 %collective-permute-start.6 = (bf16[16,4096]{1,0:T(8,128)(2,1)S(1)}, bf16[16,4096]{1,0:T(8,128)(2,1)S(1)}, u32[]{:S(2)}, u32[]{:S(2)}) collective-permute-start(bf16[16,4096]{1,0:T(8,128)(2,1)S(1)} %fusion.32.fresh0_ref), channel_id=1, source_target_pairs={{0,128},{64,192},{128,0},{192,64},{256,384},{320,448},{384,256},{4... | collective-permute-start | bytes 393224 | tf_op jit(solution)/shard_map/ppermute | solution.py:20
  87.2 2.6 %collective-permute-start.5 = (bf16[16,4096]{1,0:T(8,128)(2,1)S(1)}, bf16[16,4096]{1,0:T(8,128)(2,1)S(1)}, u32[]{:S(2)}, u32[]{:S(2)}) collective-permute-start(bf16[16,4096]{1,0:T(8,128)(2,1)S(1)} %fusion.32.fresh0_ref), channel_id=1, source_target_pairs={{0,64},{64,0},{128,192},{192,128},{256,320},{320,256},{384,448},{4... | collective-permute-start | bytes 393224 | tf_op jit(solution)/shard_map/ppermute | solution.py:20
  89.8 7.5 %collective-permute-done.8 = bf16[2,16,4096]{2,1,0:T(8,128)(2,1)S(1)} collective-permute-done((bf16[2,16,4096]{2,1,0:T(8,128)(2,1)S(1)}, bf16[2,16,4096]{2,1,0:T(8,128)(2,1)S(1)}, u32[]{:S(2)}, u32[]{:S(2)}) %collective-permute-start.8) | collective-permute-done | bytes 262176 | tf_op jit(solution)/shard_map/ppermute | solution.py:20
  98.8 2.6 %assemble.1 = (bf16[8,80,512]{2,1,0:T(8,128)(2,1)}, bf16[64,4096]{1,0:T(8,128)(2,1)}) custom-call(s32[8,8]{1,0:T(8,128)} %failed_ref.3, bf16[64,4096]{1,0:T(8,128)(2,1)} %bitcast.152, bf16[16,4096]{1,0:T(8,128)(2,1)} %copy-done.7, bf16[16,4096]{1,0:T(8,128)(2,1)} %copy-done.13, bf16[16,4096]{1,0:T(8,128)(2,1)} %copy-done.12, bf16[16,4096]{1,0:T(8,128)(2,1)} %copy-done.11, ...), custom_call_target="tpu_custom_call" | custom-call | tf_op jit(solution)/shard_map/assemble/pallas_call | solution.py:113
  101.4 14.0 %all-to-all-start.3 = ((bf16[8,80,512]{2,1,0:T(8,128)(2,1)}), bf16[8,80,512]{2,1,0:T(8,128)(2,1)S(1)}, u32[]{:S(2)}, u32[]{:S(2)}) async-start(bf16[8,80,512]{2,1,0:T(8,128)(2,1)} %get-tuple-element.25), calls=%async_computation.3 | async-start | bytes 1310720 | tf_op jit(solution)/shard_map/all_to_all | solution.py:179
  115.5 1.3 dynamic_slice.3
  117.5 2.1 %fusion.25 = f32[64,32,8]{1,2,0:T(8,128)S(1)} fusion(bf16[64,32,128]{2,1,0:T(8,128)(2,1)S(1)} %bitcast.146, f32[128,8]{0,1:T(8,128)S(1)} %copy-done), kind=kOutput, calls=%fused_computation.56 | convolution fusion | flops 25165824 | bytes 593920 | tf_op jit(solution)/shard_map/jnc,cp->jnp/dot_general | solution.py:198
  120.5 0.8 convert_element_type.83
  121.4 1.1 convolution_convert_fusion.2
  122.7 0.9 convert_element_type.86
  123.8 4.2 %fusion.27 = f32[64,32,8]{1,2,0:T(8,128)S(1)} fusion(f32[64,32,128]{2,1,0:T(8,128)S(1)} %bitcast.143, f32[128,8]{0,1:T(8,128)S(1)} %copy-done), kind=kOutput, calls=%fused_computation.58 | convolution fusion | flops 25165824 | bytes 1118208 | tf_op jit(solution)/shard_map/jnc,cp->jnp/dot_general | solution.py:198
  128.8 1.6 copy.58
  130.6 4.2 %fusion.29 = f32[64,32,8]{1,2,0:T(8,128)S(1)} fusion(f32[64,32,128]{2,1,0:T(8,128)S(1)} %bitcast.144, f32[128,8]{0,1:T(8,128)S(1)} %copy-done), kind=kOutput, calls=%fused_computation.60 | convolution fusion | flops 25165824 | bytes 1118208 | tf_op jit(solution)/shard_map/jnc,cp->jnp/dot_general | solution.py:198
  134.7 0.8 copy.55
  135.6 1.0 copy.57
  136.5 2.9 %all-to-all-done.3 = bf16[8,80,512]{2,1,0:T(8,128)(2,1)S(1)} async-done(((bf16[8,80,512]{2,1,0:T(8,128)(2,1)}), bf16[8,80,512]{2,1,0:T(8,128)(2,1)S(1)}, u32[]{:S(2)}, u32[]{:S(2)}) %all-to-all-start.3) | async-done | bytes 655392 | tf_op jit(solution)/shard_map/all_to_all | solution.py:179
  139.5 1.0 copy-done.6
  140.5 1.5 fusion.8
  142.0 10.0 %collective-permute-start.9 = (f32[4,128]{1,0:T(4,128)S(1)}, f32[4,128]{1,0:T(4,128)S(1)}, u32[]{:S(2)}, u32[]{:S(2)}) collective-permute-start(f32[4,128]{1,0:T(4,128)S(1)} %bitcast.171), channel_id=1, source_target_pairs={{0,1},{1,0},{2,3},{3,2},{4,5},{5,4},{6,7},{7,6},{8,9},{9,8},{10,11... | collective-permute-start | bytes 6152 | tf_op jit(solution)/shard_map/ppermute | solution.py:20
  152.0 8.9 %collective-permute-start.13 = (bf16[16,4096]{1,0:T(8,128)(2,1)S(1)}, bf16[16,4096]{1,0:T(8,128)(2,1)S(1)}, u32[]{:S(2)}, u32[]{:S(2)}) collective-permute-start(bf16[16,4096]{1,0:T(8,128)(2,1)S(1)} %bitcast.163), channel_id=1, source_target_pairs={{0,256},{64,320},{128,384},{192,448},{256,0},{320,64},{384,128},{4... | collective-permute-start | bytes 393224 | tf_op jit(solution)/shard_map/ppermute | solution.py:20
  161.0 1.9 collective-permute-start.10
  162.9 1.2 convolution_convert_fusion
  164.2 6.2 %all-to-all-start.4 = ((bf16[8,64,512]{2,1,0:T(8,128)(2,1)}), bf16[8,64,512]{2,1,0:T(8,128)(2,1)S(1)}, u32[]{:S(2)}, u32[]{:S(2)}) async-start(bf16[8,64,512]{2,1,0:T(8,128)(2,1)} %bitcast.158), calls=%async_computation.4 | async-start | bytes 1048576 | tf_op jit(solution)/shard_map/all_to_all | solution.py:193
  170.4 7.6 %collective-permute-start.11 = (f32[4,128]{1,0:T(4,128)S(1)}, f32[4,128]{1,0:T(4,128)S(1)}, u32[]{:S(2)}, u32[]{:S(2)}) collective-permute-start(f32[4,128]{1,0:T(4,128)S(1)} %fusion.42), channel_id=1, source_target_pairs={{0,4},{1,5},{2,6},{3,7},{4,0},{5,1},{6,2},{7,3},{8,12},{9,13},{10,... | collective-permute-start | bytes 6152 | tf_op jit(solution)/shard_map/ppermute | solution.py:20
  178.0 1.2 fusion.24
  179.3 2.1 collective-permute-start.15
  181.5 3.5 %collective-permute-start.14 = (bf16[34,4096]{1,0:T(8,128)(2,1)S(1)}, bf16[34,4096]{1,0:T(8,128)(2,1)S(1)}, u32[]{:S(2)}, u32[]{:S(2)}) collective-permute-start(bf16[34,4096]{1,0:T(8,128)(2,1)S(1)} %get-tuple-element.58), channel_id=1, source_target_pairs={{0,64},{64,0},{128,192},{192,128},{256,320},{320,256},{384,448},{4... | collective-permute-start | bytes 835592 | tf_op jit(solution)/shard_map/ppermute | solution.py:20
  185.0 4.3 %collective-permute-start.16 = (bf16[34,4096]{1,0:T(8,128)(2,1)S(1)}, bf16[34,4096]{1,0:T(8,128)(2,1)S(1)}, u32[]{:S(2)}, u32[]{:S(2)}) collective-permute-start(bf16[34,4096]{1,0:T(8,128)(2,1)S(1)} %get-tuple-element.58), channel_id=1, source_target_pairs={{0,192},{64,128},{128,64},{192,0},{256,448},{320,384},{384,320},{4... | collective-permute-start | bytes 835592 | tf_op jit(solution)/shard_map/ppermute | solution.py:20
  189.4 1.0 fusion.7
  190.4 10.9 %collective-permute-start.12 = (bf16[512,512]{0,1:T(8,128)(2,1)}, bf16[512,512]{0,1:T(8,128)(2,1)}, u32[]{:S(2)}, u32[]{:S(2)}) collective-permute-start(bf16[512,512]{0,1:T(8,128)(2,1)} %fusion.7), channel_id=1, source_target_pairs={{8,0},{16,8},{24,16},{32,24},{40,32},{48,40},{56,48},{0,56},{9,1},... | collective-permute-start | bytes 1572872 | tf_op jit(solution)/shard_map/ppermute | solution.py:16
  204.2 1.5 fusion.12
  206.5 3.1 %collective-permute-done.12 = bf16[512,512]{0,1:T(8,128)(2,1)} collective-permute-done((bf16[512,512]{0,1:T(8,128)(2,1)}, bf16[512,512]{0,1:T(8,128)(2,1)}, u32[]{:S(2)}, u32[]{:S(2)}) %collective-permute-start.12) | collective-permute-done | bytes 524320 | tf_op jit(solution)/shard_map/ppermute | solution.py:16
  209.7 2.0 copy.60
  (92 shorter events, 10.4 us)
Async XLA Ops:
  0.6 116.9 %copy-start = (f32[128,8]{0,1:T(8,128)S(1)}, f32[128,8]{0,1:T(8,128)}, u32[]{:S(2)}) copy-start(f32[128,8]{0,1:T(8,128)} %param.13) | copy-start | bytes 12292
  4.1 5.0 %copy-start.15 = (bf16[1,1,512,64]{2,3,1,0:T(8,128)(2,1)S(1)}, bf16[1,1,512,64]{2,3,1,0:T(8,128)(2,1)}, u32[]{:S(2)}) copy-start(bf16[1,1,512,64]{2,3,1,0:T(8,128)(2,1)} %param.9) | copy-start | bytes 196612
  4.1 22.5 %copy-start.8 = (bf16[1,1,512,512]{3,2,1,0:T(8,128)(2,1)S(1)}, bf16[1,1,512,512]{3,2,1,0:T(8,128)(2,1)}, u32[]{:S(2)}) copy-start(bf16[1,1,512,512]{3,2,1,0:T(8,128)(2,1)} %param.8) | copy-start | bytes 1572868
  4.1 25.4 %all-to-all-start = ((bf16[4,3,16,4096]{3,2,1,0:T(8,128)(2,1)}), bf16[4,3,16,4096]{3,2,1,0:T(8,128)(2,1)S(1)}, u32[]{:S(2)}, u32[]{:S(2)}) async-start(bf16[4,3,16,4096]{3,2,1,0:T(8,128)(2,1)} %serve.1), calls=%async_computation | async-start | bytes 3145728 | tf_op jit(solution)/shard_map/all_to_all | solution.py:25
  9.0 10.5 %collective-permute-start = (bf16[64,512]{1,0:T(8,128)(2,1)S(1)}, bf16[64,512]{1,0:T(8,128)(2,1)S(1)}, u32[]{:S(2)}, u32[]{:S(2)}) collective-permute-start(bf16[64,512]{1,0:T(8,128)(2,1)S(1)} %bitcast.168), channel_id=1, source_target_pairs={{0,4},{1,5},{2,6},{3,7},{4,0},{5,1},{6,2},{7,3},{8,12},{9,13},{10,... | collective-permute-start | bytes 196616 | tf_op jit(solution)/shard_map/ppermute | solution.py:20
  19.5 9.8 %collective-permute-start.1 = (bf16[2,64,512]{2,1,0:T(8,128)(2,1)S(1)}, bf16[2,64,512]{2,1,0:T(8,128)(2,1)S(1)}, u32[]{:S(2)}, u32[]{:S(2)}) collective-permute-start(bf16[2,64,512]{2,1,0:T(8,128)(2,1)S(1)} %pad_maximum_fusion.4), channel_id=1, source_target_pairs={{0,2},{1,3},{2,0},{3,1},{4,6},{5,7},{6,4},{7,5},{8,10},{9,11},{10,... | collective-permute-start | bytes 393224 | tf_op jit(solution)/shard_map/ppermute | solution.py:20
  26.8 8.9 %collective-permute-start.3 = (bf16[512,512]{0,1:T(8,128)(2,1)S(1)}, bf16[512,512]{0,1:T(8,128)(2,1)S(1)}, u32[]{:S(2)}, u32[]{:S(2)}) collective-permute-start(bf16[512,512]{0,1:T(8,128)(2,1)S(1)} %bitcast.160), channel_id=1, source_target_pairs={{56,0},{0,8},{8,16},{16,24},{24,32},{32,40},{40,48},{48,56},{57,1}... | collective-permute-start | bytes 1572872 | tf_op jit(solution)/shard_map/ppermute | solution.py:16
  29.8 17.2 %collective-permute-start.2 = (bf16[2,2,64,512]{3,2,1,0:T(8,128)(2,1)S(1)}, bf16[2,2,64,512]{3,2,1,0:T(8,128)(2,1)S(1)}, u32[]{:S(2)}, u32[]{:S(2)}) collective-permute-start(bf16[2,2,64,512]{3,2,1,0:T(8,128)(2,1)S(1)} %pad_maximum_fusion.3), channel_id=1, source_target_pairs={{0,1},{1,0},{2,3},{3,2},{4,5},{5,4},{6,7},{7,6},{8,9},{9,8},{10,11... | collective-permute-start | bytes 786440 | tf_op jit(solution)/shard_map/ppermute | solution.py:20
  36.5 19.9 %all-to-all-start.1 = ((f32[8,4,128]{2,1,0:T(4,128)}), f32[8,4,128]{2,1,0:T(4,128)S(1)}, u32[]{:S(2)}, u32[]{:S(2)}) async-start(f32[8,4,128]{2,1,0:T(4,128)} %broadcast_in_dim.20), calls=%async_computation.1 | async-start | bytes 32768 | tf_op jit(solution)/shard_map/all_to_all | solution.py:160
  47.1 24.6 %copy-start.5 = (bf16[2,2,2,64,512]{4,3,2,1,0:T(8,128)(2,1)}, bf16[2,2,2,64,512]{4,3,2,1,0:T(8,128)(2,1)S(1)}, u32[]{:S(2)}) copy-start(bf16[2,2,2,64,512]{4,3,2,1,0:T(8,128)(2,1)S(1)} %pad_maximum_fusion.1) | copy-start | bytes 1572868
  56.4 24.3 %collective-permute-start.4 = (bf16[16,4096]{1,0:T(8,128)(2,1)S(1)}, bf16[16,4096]{1,0:T(8,128)(2,1)S(1)}, u32[]{:S(2)}, u32[]{:S(2)}) collective-permute-start(bf16[16,4096]{1,0:T(8,128)(2,1)S(1)} %slice_bitcast_fusion.1), channel_id=1, source_target_pairs={{0,256},{64,320},{128,384},{192,448},{256,0},{320,64},{384,128},{4... | collective-permute-start | bytes 393224 | tf_op jit(solution)/shard_map/ppermute | solution.py:20
  65.7 31.6 %collective-permute-start.8 = (bf16[2,16,4096]{2,1,0:T(8,128)(2,1)S(1)}, bf16[2,16,4096]{2,1,0:T(8,128)(2,1)S(1)}, u32[]{:S(2)}, u32[]{:S(2)}) collective-permute-start(bf16[2,16,4096]{2,1,0:T(8,128)(2,1)S(1)} %slice.30), channel_id=1, source_target_pairs={{0,256},{64,320},{128,384},{192,448},{256,0},{320,64},{384,128},{4... | collective-permute-start | bytes 786440 | tf_op jit(solution)/shard_map/ppermute | solution.py:20
  71.8 25.6 %all-to-all-start.2 = ((bf16[4,8,16,512]{3,2,1,0:T(8,128)(2,1)}), bf16[4,8,16,512]{3,2,1,0:T(8,128)(2,1)S(1)}, u32[]{:S(2)}, u32[]{:S(2)}) async-start(bf16[4,8,16,512]{3,2,1,0:T(8,128)(2,1)} %bitcast.133), calls=%async_computation.2 | async-start | bytes 1048576 | tf_op jit(solution)/shard_map/all_to_all | solution.py:25
  80.8 16.6 %copy-start.7 = (bf16[16,4096]{1,0:T(8,128)(2,1)}, bf16[16,4096]{1,0:T(8,128)(2,1)S(1)}, u32[]{:S(2)}) copy-start(bf16[16,4096]{1,0:T(8,128)(2,1)S(1)} %fusion.32.fresh0_ref) | copy-start | bytes 393220
  80.8 16.6 %collective-permute-start.7 = (bf16[16,4096]{1,0:T(8,128)(2,1)S(1)}, bf16[16,4096]{1,0:T(8,128)(2,1)S(1)}, u32[]{:S(2)}, u32[]{:S(2)}) collective-permute-start(bf16[16,4096]{1,0:T(8,128)(2,1)S(1)} %fusion.32.fresh0_ref), channel_id=1, source_target_pairs={{0,192},{64,128},{128,64},{192,0},{256,448},{320,384},{384,320},{4... | collective-permute-start | bytes 393224 | tf_op jit(solution)/shard_map/ppermute | solution.py:20
  84.7 12.7 %collective-permute-start.6 = (bf16[16,4096]{1,0:T(8,128)(2,1)S(1)}, bf16[16,4096]{1,0:T(8,128)(2,1)S(1)}, u32[]{:S(2)}, u32[]{:S(2)}) collective-permute-start(bf16[16,4096]{1,0:T(8,128)(2,1)S(1)} %fusion.32.fresh0_ref), channel_id=1, source_target_pairs={{0,128},{64,192},{128,0},{192,64},{256,384},{320,448},{384,256},{4... | collective-permute-start | bytes 393224 | tf_op jit(solution)/shard_map/ppermute | solution.py:20
  87.2 10.2 %collective-permute-start.5 = (bf16[16,4096]{1,0:T(8,128)(2,1)S(1)}, bf16[16,4096]{1,0:T(8,128)(2,1)S(1)}, u32[]{:S(2)}, u32[]{:S(2)}) collective-permute-start(bf16[16,4096]{1,0:T(8,128)(2,1)S(1)} %fusion.32.fresh0_ref), channel_id=1, source_target_pairs={{0,64},{64,0},{128,192},{192,128},{256,320},{320,256},{384,448},{4... | collective-permute-start | bytes 393224 | tf_op jit(solution)/shard_map/ppermute | solution.py:20
  97.3 0.8 copy-start.4
  97.4 0.8 copy-start.11
  97.4 0.8 copy-start.12
  98.2 0.6 copy-start.13
  101.4 16.0 %copy-start.9 = (bf16[64,4096]{1,0:T(8,128)(2,1)S(1)}, bf16[64,4096]{1,0:T(8,128)(2,1)}, u32[]{:S(2)}) copy-start(bf16[64,4096]{1,0:T(8,128)(2,1)} %get-tuple-element.30) | copy-start | bytes 1572868
  101.4 38.1 %all-to-all-start.3 = ((bf16[8,80,512]{2,1,0:T(8,128)(2,1)}), bf16[8,80,512]{2,1,0:T(8,128)(2,1)S(1)}, u32[]{:S(2)}, u32[]{:S(2)}) async-start(bf16[8,80,512]{2,1,0:T(8,128)(2,1)} %get-tuple-element.25), calls=%async_computation.3 | async-start | bytes 1310720 | tf_op jit(solution)/shard_map/all_to_all | solution.py:179
  119.8 3.8 %copy-start.2 = (f32[1,1,64,4096]{3,2,1,0:T(8,128)S(1)}, f32[1,1,64,4096]{3,2,1,0:T(8,128)}, u32[]{:S(2)}) copy-start(f32[1,1,64,4096]{3,2,1,0:T(8,128)} %param.12) | copy-start | bytes 3145732
  123.8 6.6 %copy-start.1 = (f32[1,1,64,4096]{3,2,1,0:T(8,128)S(1)}, f32[1,1,64,4096]{3,2,1,0:T(8,128)}, u32[]{:S(2)}) copy-start(f32[1,1,64,4096]{3,2,1,0:T(8,128)} %param.11) | copy-start | bytes 3145732
  139.5 1.0 copy-start.6
  142.0 19.0 %collective-permute-start.9 = (f32[4,128]{1,0:T(4,128)S(1)}, f32[4,128]{1,0:T(4,128)S(1)}, u32[]{:S(2)}, u32[]{:S(2)}) collective-permute-start(f32[4,128]{1,0:T(4,128)S(1)} %bitcast.171), channel_id=1, source_target_pairs={{0,1},{1,0},{2,3},{3,2},{4,5},{5,4},{6,7},{7,6},{8,9},{9,8},{10,11... | collective-permute-start | bytes 6152 | tf_op jit(solution)/shard_map/ppermute | solution.py:20
  152.0 26.0 %collective-permute-start.13 = (bf16[16,4096]{1,0:T(8,128)(2,1)S(1)}, bf16[16,4096]{1,0:T(8,128)(2,1)S(1)}, u32[]{:S(2)}, u32[]{:S(2)}) collective-permute-start(bf16[16,4096]{1,0:T(8,128)(2,1)S(1)} %bitcast.163), channel_id=1, source_target_pairs={{0,256},{64,320},{128,384},{192,448},{256,0},{320,64},{384,128},{4... | collective-permute-start | bytes 393224 | tf_op jit(solution)/shard_map/ppermute | solution.py:20
  161.0 9.4 %collective-permute-start.10 = (f32[4,128]{1,0:T(4,128)S(1)}, f32[4,128]{1,0:T(4,128)S(1)}, u32[]{:S(2)}, u32[]{:S(2)}) collective-permute-start(f32[4,128]{1,0:T(4,128)S(1)} %bitcast_add_fusion.2), channel_id=1, source_target_pairs={{0,2},{1,3},{2,0},{3,1},{4,6},{5,7},{6,4},{7,5},{8,10},{9,11},{10,... | collective-permute-start | bytes 6152 | tf_op jit(solution)/shard_map/ppermute | solution.py:20
  164.2 15.1 %copy-start.14 = (bf16[2,4096]{1,0:T(2,128)(2,1)S(1)}, bf16[2,4096]{1,0:T(2,128)(2,1)}, u32[]{:S(2)}) copy-start(bf16[2,4096]{1,0:T(2,128)(2,1)} %convert_element_type.86) | copy-start | bytes 49156
  164.2 47.5 %all-to-all-start.4 = ((bf16[8,64,512]{2,1,0:T(8,128)(2,1)}), bf16[8,64,512]{2,1,0:T(8,128)(2,1)S(1)}, u32[]{:S(2)}, u32[]{:S(2)}) async-start(bf16[8,64,512]{2,1,0:T(8,128)(2,1)} %bitcast.158), calls=%async_computation.4 | async-start | bytes 1048576 | tf_op jit(solution)/shard_map/all_to_all | solution.py:193
  170.4 18.9 %copy-start.3 = (f32[512,512]{0,1:T(8,128)S(1)}, f32[512,512]{0,1:T(8,128)}, u32[]{:S(2)}) copy-start(f32[512,512]{0,1:T(8,128)} %get-tuple-element.66) | copy-start | bytes 3145732
  170.4 18.9 %collective-permute-start.11 = (f32[4,128]{1,0:T(4,128)S(1)}, f32[4,128]{1,0:T(4,128)S(1)}, u32[]{:S(2)}, u32[]{:S(2)}) collective-permute-start(f32[4,128]{1,0:T(4,128)S(1)} %fusion.42), channel_id=1, source_target_pairs={{0,4},{1,5},{2,6},{3,7},{4,0},{5,1},{6,2},{7,3},{8,12},{9,13},{10,... | collective-permute-start | bytes 6152 | tf_op jit(solution)/shard_map/ppermute | solution.py:20
  179.3 22.0 %collective-permute-start.15 = (bf16[34,4096]{1,0:T(8,128)(2,1)S(1)}, bf16[34,4096]{1,0:T(8,128)(2,1)S(1)}, u32[]{:S(2)}, u32[]{:S(2)}) collective-permute-start(bf16[34,4096]{1,0:T(8,128)(2,1)S(1)} %get-tuple-element.58), channel_id=1, source_target_pairs={{0,128},{64,192},{128,0},{192,64},{256,384},{320,448},{384,256},{4... | collective-permute-start | bytes 835592 | tf_op jit(solution)/shard_map/ppermute | solution.py:20
  181.5 19.9 %collective-permute-start.14 = (bf16[34,4096]{1,0:T(8,128)(2,1)S(1)}, bf16[34,4096]{1,0:T(8,128)(2,1)S(1)}, u32[]{:S(2)}, u32[]{:S(2)}) collective-permute-start(bf16[34,4096]{1,0:T(8,128)(2,1)S(1)} %get-tuple-element.58), channel_id=1, source_target_pairs={{0,64},{64,0},{128,192},{192,128},{256,320},{320,256},{384,448},{4... | collective-permute-start | bytes 835592 | tf_op jit(solution)/shard_map/ppermute | solution.py:20
  185.0 16.3 %collective-permute-start.16 = (bf16[34,4096]{1,0:T(8,128)(2,1)S(1)}, bf16[34,4096]{1,0:T(8,128)(2,1)S(1)}, u32[]{:S(2)}, u32[]{:S(2)}) collective-permute-start(bf16[34,4096]{1,0:T(8,128)(2,1)S(1)} %get-tuple-element.58), channel_id=1, source_target_pairs={{0,192},{64,128},{128,64},{192,0},{256,448},{320,384},{384,320},{4... | collective-permute-start | bytes 835592 | tf_op jit(solution)/shard_map/ppermute | solution.py:20
  190.4 19.3 %collective-permute-start.12 = (bf16[512,512]{0,1:T(8,128)(2,1)}, bf16[512,512]{0,1:T(8,128)(2,1)}, u32[]{:S(2)}, u32[]{:S(2)}) collective-permute-start(bf16[512,512]{0,1:T(8,128)(2,1)} %fusion.7), channel_id=1, source_target_pairs={{8,0},{16,8},{24,16},{32,24},{40,32},{48,40},{56,48},{0,56},{9,1},... | collective-permute-start | bytes 1572872 | tf_op jit(solution)/shard_map/ppermute | solution.py:16
  204.2 1.7 copy-start.10

commit v9 on v8

--- a/solution.py
+++ b/solution.py
@@ -55,6 +55,20 @@
 
 def tied(value, *after):
     return lax.optimization_barrier((value,) + after)[0]
+
+
+def places(spans_ref, section, count):
+    ahead = [jnp.int32(0), jnp.int32(count - spans_ref.shape[1])]
+    found = []
+    for n in range(count):
+        listed = spans_ref[section, 0] == n
+        for j in range(1, spans_ref.shape[1]):
+            listed = listed | (spans_ref[section, j] == n)
+        bit = listed.astype(jnp.int32)
+        slot = jnp.where(listed, ahead[1], ahead[0])
+        found.append((listed, pl.ds(pl.multiple_of(slot * SPAN, SPAN), SPAN)))
+        ahead = [ahead[0] + 1 - bit, ahead[1] + bit]
+    return found
 
 
 def serve_kernel(failed_ref, spans_ref, weight_ref, first_ref, second_ref, out_ref):
@@ -64,16 +78,12 @@
     is_primary = (failed ^ PLANE) == me
     is_second = (failed ^ 1) == me
     part = out_ref.shape[2]
-    for n in range(weight_ref.shape[1] // SPAN):
-        listed = spans_ref[section, 0] == n
-        for j in range(1, spans_ref.shape[1]):
-            listed = listed | (spans_ref[section, j] == n)
+    for n, (listed, place) in enumerate(places(spans_ref, section, weight_ref.shape[1] // SPAN)):
         take = (listed & is_second) | (jnp.logical_not(listed) & is_primary)
-        here = pl.ds(n * SPAN, SPAN)
         for k, ref in enumerate((weight_ref, first_ref, second_ref)):
             for x in range(PLANE):
-                block = ref[x * part : (x + 1) * part, here].astype(SHORT)
-                out_ref[x, k, :, here] = jnp.where(take, block, jnp.zeros_like(block))
+                block = ref[x * part : (x + 1) * part, n * SPAN : (n + 1) * SPAN].astype(SHORT)
+                out_ref[x, k, :, place] = jnp.where(take, block, jnp.zeros_like(block))
 
 
 def serve(failed, spans, weight, first, second):
@@ -87,19 +97,38 @@
     )(failed, spans, weight, first, second)
 
 
-def assemble_kernel(failed_ref, own_ref, fresh0_ref, fresh1_ref, fresh2_ref, fresh3_ref, grads_ref, sent_ref, restored_ref):
+def unpack_kernel(spans_ref, placed_ref, out_ref):
+    section = lax.axis_index("section")
+    for n, (_, place) in enumerate(places(spans_ref, section, out_ref.shape[2] // SPAN)):
+        for k in range(out_ref.shape[0]):
+            out_ref[k, :, n * SPAN : (n + 1) * SPAN] = placed_ref[k, :, place]
+
+
+def unpack(spans, placed):
+    return pl.pallas_call(
+        unpack_kernel,
+        out_shape=jax.ShapeDtypeStruct(placed.shape, placed.dtype),
+        in_specs=[pl.BlockSpec(memory_space=pltpu.SMEM), pl.BlockSpec(memory_space=pltpu.VMEM)],
+        out_specs=pl.BlockSpec(memory_space=pltpu.VMEM),
+        name="unpack",
+    )(spans, placed)
+
+
+def assemble_kernel(failed_ref, spans_ref, own_ref, fresh0_ref, fresh1_ref, fresh2_ref, fresh3_ref, grads_ref, sent_ref, restored_ref):
+    section = lax.axis_index("section")
     me = lax.axis_index("replica")
-    here = failed_ref[lax.axis_index("section"), lax.axis_index("tensor")] == me
-    rows = own_ref.shape[0]
+    here = failed_ref[section, lax.axis_index("tensor")] == me
+    rows, width = own_ref.shape
     groups, _, cols = sent_ref.shape
     part = fresh0_ref.shape[0]
+    apart = cols // SPAN
+    spans = places(spans_ref, section, width // SPAN)
     for k, fresh_ref in enumerate((fresh0_ref, fresh1_ref, fresh2_ref, fresh3_ref)):
         at = pl.ds(pl.multiple_of(((me & 3) ^ k) * part, part), part)
-        for t in range(groups):
-            span = pl.ds(t * cols, cols)
-            block = jnp.where(here, fresh_ref[:, span], own_ref[at, span])
-            restored_ref[at, span] = block
-            sent_ref[t, at, :] = block
+        for n, (_, place) in enumerate(spans):
+            block = jnp.where(here, fresh_ref[:, place], own_ref[at, n * SPAN : (n + 1) * SPAN])
+            restored_ref[at, n * SPAN : (n + 1) * SPAN] = block
+            sent_ref[n // apart, at, (n % apart) * SPAN : (n % apart + 1) * SPAN] = block
     for t in range(groups):
         total = grads_ref[0, t].astype(WIDE)
         for x in range(1, PLANE):
@@ -107,7 +136,7 @@
         sent_ref[t, rows:, :] = total.astype(SHORT)
 
 
-def assemble(failed, own, fresh, grads):
+def assemble(failed, spans, own, fresh, grads):
     rows, width = own.shape
     _, groups, part, cols = grads.shape
     return pl.pallas_call(
@@ -116,10 +145,10 @@
             jax.ShapeDtypeStruct((groups, rows + part, cols), SHORT),
             jax.ShapeDtypeStruct((rows, width), SHORT),
         ),
-        in_specs=[pl.BlockSpec(memory_space=pltpu.SMEM)] + [pl.BlockSpec(memory_space=pltpu.VMEM)] * 6,
+        in_specs=[pl.BlockSpec(memory_space=pltpu.SMEM)] * 2 + [pl.BlockSpec(memory_space=pltpu.VMEM)] * 6,
         out_specs=(pl.BlockSpec(memory_space=pltpu.VMEM),) * 2,
         name="assemble",
-    )(failed, own, *fresh, grads)
+    )(failed, spans, own, *fresh, grads)
 
 
 def adam(first, second, grad):
@@ -140,42 +169,40 @@
     own_second = second_moment[0, 0]
     rows, width = own_weight.shape
     nchunk = width // 128
-    listed = jnp.any(my_spans[:, None] == jnp.arange(nchunk, dtype=jnp.int32)[None, :], axis=0)
-    columns = jnp.repeat(listed, 128)[None, :]
-    primary = jnp.bitwise_xor(failed, PLANE)
-    second = jnp.bitwise_xor(failed, 1)
-    chosen = jnp.where(columns, my_replica == second, my_replica == primary)
     is_failed = my_replica == failed
     part = rows // PLANE
 
     local = activations[0, 0]
     tokens, cols = local.shape
+    squares = jnp.sum(jnp.square(local.astype(WIDE)), axis=1).reshape(-1, 128)
+    squares = from_behind(squares, "section", 1).reshape(1, tokens)
     incoming = from_behind(local, "section", 1)
     x = incoming.astype(WIDE)
 
     mask = serve(failed_replica, resend_spans, own_weight, own_first, own_second)
     served = jnp.sum(exchange_x(mask).astype(WIDE), axis=0).astype(SHORT)
 
-    squares = jnp.sum(x * x, axis=1).reshape(1, -1, 128)
-    squares = lax.all_to_all(jnp.broadcast_to(squares, (8,) + squares.shape[1:]), "tensor", 0, 0, tiled=True)
-    held = tied(key_grads[0, 0].T, mask)
+    high, low = two_halves(squares)
+    extra = jnp.concatenate([high, low, jnp.zeros((6, tokens), SHORT)], axis=0)
+    held = jnp.concatenate([tied(key_grads[0, 0].T, mask), extra], axis=0)
     held = doubled(doubled(held, my_tensor, 0), my_tensor, 1)
     held, served = lax.optimization_barrier((held, served))
-    held = doubled(held, my_tensor, 2)
-    held, squares, served = lax.optimization_barrier((held, squares, served))
-    fresh_weight = served[0] + swap(served[0], "replica", PLANE)
-    fresh_moments = served[1:] + swap(served[1:], "replica", PLANE)
-    kg_all = held.reshape(8 * rows, tokens)
-    inverse_rms = 1.0 / jnp.sqrt(jnp.sum(squares, axis=0).reshape(tokens) / width + 1e-05)
-    fresh_weight = [fresh_weight] + [swap(fresh_weight, "replica", bit) for bit in (1, 2, 3)]
+    cross = width - my_spans.shape[0] * SPAN
+    crossed = served[:, :, :cross] + swap(served[:, :, :cross], "replica", PLANE)
+    fresh = jnp.concatenate([crossed, served[:, :, cross:]], axis=2)
+    fresh_weight = [fresh[0]] + [swap(fresh[0], "replica", bit) for bit in (1, 2, 3)]
+    held = doubled(held, my_tensor, 2).reshape(8, -1, tokens)
+    kg_all = held[:, :rows].reshape(8 * rows, tokens)
+    squares = jnp.sum(held[:, rows].astype(WIDE) + held[:, rows + 1].astype(WIDE), axis=0)
+    inverse_rms = 1.0 / jnp.sqrt(squares / width + 1e-05)
 
     normed = (x * inverse_rms[:, None]).astype(SHORT)
     grad = lax.dot_general(kg_all, normed, (((1,), (0,)), ((), ())), preferred_element_type=WIDE).astype(SHORT)
     grad = grad.reshape(8, PLANE, part, cols).transpose(1, 0, 2, 3)
-    grad, fresh_moments = lax.optimization_barrier((exchange_x(grad), fresh_moments))
-
-    sent, restored_weight = assemble(failed_replica, own_weight, fresh_weight, grad)
-    own_first, own_second, restored_weight = lax.optimization_barrier((own_first, own_second, restored_weight))
+    grad = exchange_x(grad)
+
+    sent, restored_weight = assemble(failed_replica, resend_spans, own_weight, fresh_weight, grad)
+    own_first, own_second, restored_weight, fresh = lax.optimization_barrier((own_first, own_second, restored_weight, fresh))
     got = lax.all_to_all(sent, "tensor", 0, 0, tiled=True)
     weight_cols = got[:, :rows].reshape(8 * rows, cols)
     grad_rows = got[:, rows:].transpose(1, 0, 2).reshape(part, width)
@@ -198,7 +225,7 @@
         mixed = jnp.einsum("jnc,cp->jnp", shaped, probe_matrix, precision=lax.Precision.HIGHEST)
         return mixed.reshape(-1, nchunk * probe_matrix.shape[1])
 
-    fresh = fresh_moments.astype(WIDE)
+    fresh = unpack(resend_spans, fresh[1:]).astype(WIDE)
     fresh_update = adam(fresh[0], fresh[1], mean_rows).astype(SHORT)
     fresh_sums = checksum(fresh.reshape(2 * part, width)).astype(SHORT).reshape(2, width)
     shared = gather_x(jnp.concatenate([mean_rows.astype(SHORT), fresh_update, fresh_sums], axis=0))

time: 214 us -> 206 us (0.963)
  starting transfers between devices: 136 us -> 114 us
  waiting for transfers between devices: 29.5 us -> 39.5 us
  matrix products: 14.7 us -> 17.2 us
  Pallas kernels: 5.97 us -> 8.41 us
    ppermute x15 -> x14, waiting for transfers between devices: 14.1 us -> 36.6 us  [swap(): lax.ppermute(block, axis, [(i, i ^ bit) for i in range(lax.axis_size(axis...]
    all_to_all x1 -> x0, starting transfers between devices: 10.5 us -> none  [shards(): lax.all_to_all(jnp.broadcast_to(squares, (8,) + squares.shape[1:]), 'tens...]
    all_to_all x1 -> x0, waiting for transfers between devices: 9.23 us -> none  [shards(): lax.all_to_all(jnp.broadcast_to(squares, (8,) + squares.shape[1:]), 'tens...]
    ppermute x15 -> x14, starting transfers between devices: 83.1 us -> 74 us  [swap(): lax.ppermute(block, axis, [(i, i ^ bit) for i in range(lax.axis_size(axis...]
    all_to_all x1, starting transfers between devices: 14 us -> 9.49 us  [shards(): got = lax.all_to_all(sent, 'tensor', 0, 0, tiled=True)]
    all_to_all x1, waiting for transfers between devices: 2.94 us -> 0.01 us  [shards(): got = lax.all_to_all(sent, 'tensor', 0, 0, tiled=True)]
    ppermute x2 -> x3, starting transfers between devices: 13.5 us -> 15.6 us  [from_behind(): lax.ppermute(block, axis, [((i - distance) % n, i) for i in range(n)])]
    unnamed x40 -> x42, local copies, waits for them, and re-layouts: 5.99 us -> 7.12 us
  transfers between devices with their start and end apart: 22 -> 21, of which waited for: 6 -> 6; matrix products, arithmetic and copies ran while one was open for 16% -> 17% of each run, Pallas kernels for 0% -> 3%
where the time goes in v9:
time: 206 us; the launch traced here: 205 us
  starting transfers between devices  114 us (55%)
  waiting for transfers between devices  39.5 us (19%)
  matrix products  17.2 us (8%)
  local copies, waits for them, and re-layouts  15.7 us (8%)
  Pallas kernels  8.41 us (4%)
  other arithmetic  7.72 us (4%)
    ppermute x14, starting transfers between devices, swap(): lax.ppermute(block, axis, [(i, i ^ bit) for i in range(lax.axis_size(axis...  74 us
    ppermute x14, waiting for transfers between devices, swap(): lax.ppermute(block, axis, [(i, i ^ bit) for i in range(lax.axis_size(axis...  36.6 us
    ppermute x3, starting transfers between devices, from_behind(): lax.ppermute(block, axis, [((i - distance) % n, i) for i in range(n)])  15.6 us
    dot_general x4, matrix products, checksum(): jnp.einsum('jnc,cp->jnp', shaped, probe_matrix, precision=lax.Precision.H...  13 us
    all_to_all x1, starting transfers between devices, shards(): got = lax.all_to_all(sent, 'tensor', 0, 0, tiled=True)  9.49 us
    all_to_all x2, starting transfers between devices, exchange_x(): lax.all_to_all(block, 'replica', 0, 0, axis_index_groups=groups, tiled=True)  8.76 us
    unnamed x42, local copies, waits for them, and re-layouts  7.12 us
    all_to_all x1, starting transfers between devices, shards(): lax.all_to_all(keys.reshape(8, rows, tokens), 'tensor', 0, 0, tiled=True)  6.23 us
  transfers between devices with their start and end apart: 21, of which 6 were waited for; matrix products, arithmetic and copies ran while one was open for 17% of the time, Pallas kernels for 3%

profile of v9, /device:TPU:1, one launch (start us, length us, event | category | flops | bytes accessed | tf_op | source)
XLA Modules:
  0.0 204.6 jit_solution(2991916638722730590)
XLA Ops:
  0.6 1.3 copy.44
  2.1 2.7 %collective-permute-start = (f32[4,128]{1,0:T(4,128)S(1)}, f32[4,128]{1,0:T(4,128)S(1)}, u32[]{:S(2)}, u32[]{:S(2)}) collective-permute-start(f32[4,128]{1,0:T(4,128)S(1)} %bitcast.168), channel_id=1, source_target_pairs={{56,0},{0,8},{8,16},{16,24},{24,32},{32,40},{40,48},{48,56},{57,1}... | collective-permute-start | bytes 6152 | tf_op jit(solution)/shard_map/ppermute | solution.py:16
  4.8 3.7 %serve.1 = bf16[4,3,16,4096]{3,2,1,0:T(8,128)(2,1)} custom-call(s32[8,8]{1,0:T(8,128)} %failed_ref.3, s32[8,8]{1,0:T(8,128)} %spans_ref.5, bf16[64,4096]{1,0:T(8,128)(2,1)} %bitcast.144, f32[64,4096]{1,0:T(8,128)} %bitcast.127, f32[64,4096]{1,0:T(8,128)} %bitcast.130), custom_call_target="tpu_custom_call" | custom-call | tf_op jit(solution)/shard_map/serve/pallas_call | solution.py:91
  8.4 4.1 %all-to-all-start = ((bf16[4,3,16,4096]{3,2,1,0:T(8,128)(2,1)}), bf16[4,3,16,4096]{3,2,1,0:T(8,128)(2,1)S(1)}, u32[]{:S(2)}, u32[]{:S(2)}) async-start(bf16[4,3,16,4096]{3,2,1,0:T(8,128)(2,1)} %serve.1), calls=%async_computation | async-start | bytes 3145728 | tf_op jit(solution)/shard_map/all_to_all | solution.py:25
  12.8 8.8 %collective-permute-start.1 = (bf16[72,512]{1,0:T(8,128)(2,1)S(1)}, bf16[72,512]{1,0:T(8,128)(2,1)S(1)}, u32[]{:S(2)}, u32[]{:S(2)}) collective-permute-start(bf16[72,512]{1,0:T(8,128)(2,1)S(1)} %maximum_maximum_fusion), channel_id=1, source_target_pairs={{0,4},{1,5},{2,6},{3,7},{4,0},{5,1},{6,2},{7,3},{8,12},{9,13},{10,... | collective-permute-start | bytes 221192 | tf_op jit(solution)/shard_map/ppermute | solution.py:20
  21.6 6.5 %collective-permute-done.1 = bf16[72,512]{1,0:T(8,128)(2,1)S(1)} collective-permute-done((bf16[72,512]{1,0:T(8,128)(2,1)S(1)}, bf16[72,512]{1,0:T(8,128)(2,1)S(1)}, u32[]{:S(2)}, u32[]{:S(2)}) %collective-permute-start.1) | collective-permute-done | bytes 73760 | tf_op jit(solution)/shard_map/ppermute | solution.py:20
  28.2 2.4 %collective-permute-start.2 = (bf16[2,72,512]{2,1,0:T(8,128)(2,1)S(1)}, bf16[2,72,512]{2,1,0:T(8,128)(2,1)S(1)}, u32[]{:S(2)}, u32[]{:S(2)}) collective-permute-start(bf16[2,72,512]{2,1,0:T(8,128)(2,1)S(1)} %pad_maximum_fusion.5), channel_id=1, source_target_pairs={{0,2},{1,3},{2,0},{3,1},{4,6},{5,7},{6,4},{7,5},{8,10},{9,11},{10,... | collective-permute-start | bytes 442376 | tf_op jit(solution)/shard_map/ppermute | solution.py:20
  30.6 8.7 %collective-permute-done.2 = bf16[2,72,512]{2,1,0:T(8,128)(2,1)S(1)} collective-permute-done((bf16[2,72,512]{2,1,0:T(8,128)(2,1)S(1)}, bf16[2,72,512]{2,1,0:T(8,128)(2,1)S(1)}, u32[]{:S(2)}, u32[]{:S(2)}) %collective-permute-start.2) | collective-permute-done | bytes 147488 | tf_op jit(solution)/shard_map/ppermute | solution.py:20
  39.7 1.9 collective-permute-start.7
  41.6 1.2 collective-permute-start.8
  42.8 14.4 %collective-permute-start.3 = (bf16[3,16,3072]{2,1,0:T(8,128)(2,1)S(1)}, bf16[3,16,3072]{2,1,0:T(8,128)(2,1)S(1)}, u32[]{:S(2)}, u32[]{:S(2)}) collective-permute-start(bf16[3,16,3072]{2,1,0:T(8,128)(2,1)S(1)} %slice.46), channel_id=1, source_target_pairs={{0,256},{64,320},{128,384},{192,448},{256,0},{320,64},{384,128},{4... | collective-permute-start | bytes 884744 | tf_op jit(solution)/shard_map/ppermute | solution.py:20
  58.0 0.8 copy.74
  58.8 4.6 %all-to-all-start.1 = ((bf16[4,8,16,512]{3,2,1,0:T(8,128)(2,1)}), bf16[4,8,16,512]{3,2,1,0:T(8,128)(2,1)S(1)}, u32[]{:S(2)}, u32[]{:S(2)}) async-start(bf16[4,8,16,512]{3,2,1,0:T(8,128)(2,1)} %bitcast.126), calls=%async_computation.1 | async-start | bytes 1048576 | tf_op jit(solution)/shard_map/all_to_all | solution.py:25
  63.4 17.4 %collective-permute-done.3 = bf16[3,16,3072]{2,1,0:T(8,128)(2,1)S(1)} collective-permute-done((bf16[3,16,3072]{2,1,0:T(8,128)(2,1)S(1)}, bf16[3,16,3072]{2,1,0:T(8,128)(2,1)S(1)}, u32[]{:S(2)}, u32[]{:S(2)}) %collective-permute-start.3) | collective-permute-done | bytes 294944 | tf_op jit(solution)/shard_map/ppermute | solution.py:20
  80.9 5.2 %collective-permute-start.6 = (bf16[16,4096]{1,0:T(8,128)(2,1)S(1)}, bf16[16,4096]{1,0:T(8,128)(2,1)S(1)}, u32[]{:S(2)}, u32[]{:S(2)}) collective-permute-start(bf16[16,4096]{1,0:T(8,128)(2,1)S(1)} %fusion.25.fresh0_ref), channel_id=1, source_target_pairs={{0,192},{64,128},{128,64},{192,0},{256,448},{320,384},{384,320},{4... | collective-permute-start | bytes 393224 | tf_op jit(solution)/shard_map/ppermute | solution.py:20
  86.1 2.5 %collective-permute-start.5 = (bf16[16,4096]{1,0:T(8,128)(2,1)S(1)}, bf16[16,4096]{1,0:T(8,128)(2,1)S(1)}, u32[]{:S(2)}, u32[]{:S(2)}) collective-permute-start(bf16[16,4096]{1,0:T(8,128)(2,1)S(1)} %fusion.25.fresh0_ref), channel_id=1, source_target_pairs={{0,128},{64,192},{128,0},{192,64},{256,384},{320,448},{384,256},{4... | collective-permute-start | bytes 393224 | tf_op jit(solution)/shard_map/ppermute | solution.py:20
  88.6 1.9 collective-permute-start.4
  90.5 2.8 %collective-permute-done.5.fresh2_ref = bf16[16,4096]{1,0:T(8,128)(2,1)S(1)} collective-permute-done((bf16[16,4096]{1,0:T(8,128)(2,1)S(1)}, bf16[16,4096]{1,0:T(8,128)(2,1)S(1)}, u32[]{:S(2)}, u32[]{:S(2)}) %collective-permute-start.5) | collective-permute-done | bytes 131104 | tf_op jit(solution)/shard_map/ppermute | solution.py:20
  93.3 1.3 collective-permute-done.4.fresh1_ref
  95.2 0.8 copy-done.4
  96.0 2.8 %assemble.1 = (bf16[8,80,512]{2,1,0:T(8,128)(2,1)}, bf16[64,4096]{1,0:T(8,128)(2,1)}) custom-call(s32[8,8]{1,0:T(8,128)} %failed_ref.3, s32[8,8]{1,0:T(8,128)} %spans_ref.5, bf16[64,4096]{1,0:T(8,128)(2,1)} %bitcast.145, bf16[16,4096]{1,0:T(8,128)(2,1)} %copy-done.10, bf16[16,4096]{1,0:T(8,128)(2,1)} %copy-done.15, bf16[16,4096]{1,0:T(8,128)(2,1)} %copy-done.14, ...), custom_call_target="tpu_custom_call" | custom-call | tf_op jit(solution)/shard_map/assemble/pallas_call | solution.py:142
  98.9 9.5 %all-to-all-start.2 = ((bf16[8,80,512]{2,1,0:T(8,128)(2,1)}), bf16[8,80,512]{2,1,0:T(8,128)(2,1)S(1)}, u32[]{:S(2)}, u32[]{:S(2)}) async-start(bf16[8,80,512]{2,1,0:T(8,128)(2,1)} %get-tuple-element.17), calls=%async_computation.2 | async-start | bytes 1310720 | tf_op jit(solution)/shard_map/all_to_all | solution.py:206
  108.4 1.3 dynamic_slice.3
  111.0 1.9 unpack.1
  112.9 1.2 copy.68
  114.1 2.1 %fusion.28 = f32[64,32,8]{1,2,0:T(8,128)S(1)} fusion(bf16[64,32,128]{2,1,0:T(8,128)(2,1)S(1)} %bitcast.143, f32[128,8]{0,1:T(8,128)S(1)} %copy-done), kind=kOutput, calls=%fused_computation.65 | convolution fusion | flops 25165824 | bytes 593920 | tf_op jit(solution)/shard_map/jnc,cp->jnp/dot_general | solution.py:225
  117.2 0.8 convert_element_type.137
  118.0 1.1 convolution_convert_fusion.2
  119.4 0.9 convert_element_type.140
  120.4 4.9 %fusion.30 = f32[64,32,8]{1,2,0:T(8,128)} fusion(f32[64,32,128]{2,1,0:T(8,128)S(1)} %bitcast.136, f32[128,8]{0,1:T(8,128)S(1)} %copy-done), kind=kOutput, calls=%fused_computation.67 | convolution fusion | flops 25165824 | bytes 1118208 | tf_op jit(solution)/shard_map/jnc,cp->jnp/dot_general | solution.py:225
  125.3 1.1 copy.54
  126.7 4.9 %fusion.32 = f32[64,32,8]{1,2,0:T(8,128)} fusion(f32[64,32,128]{2,1,0:T(8,128)S(1)} %bitcast.137, f32[128,8]{0,1:T(8,128)S(1)} %copy-done), kind=kOutput, calls=%fused_computation.69 | convolution fusion | flops 25165824 | bytes 1118208 | tf_op jit(solution)/shard_map/jnc,cp->jnp/dot_general | solution.py:225
  131.5 1.1 copy.53
  133.3 2.5 %fusion.7 = (f32[512]{0:T(512)S(1)}, f32[512,512]{0,1:T(8,128)}) fusion(bf16[512,512]{0,1:T(8,128)(2,1)} %copy-done.7, bf16[8,80,512]{2,1,0:T(8,128)(2,1)S(1)} %all-to-all-done.2, bf16[8,72,512]{2,1,0:T(8,128)(2,1)S(1)} %bitcast.141), kind=kOutput, calls=%fused_computation.19 | convolution fusion | flops 269221376 | bytes 2623488 | tf_op jit(solution)/shard_map/dot_general | solution.py:212
  135.8 9.2 %collective-permute-start.9 = (f32[4,128]{1,0:T(4,128)S(1)}, f32[4,128]{1,0:T(4,128)S(1)}, u32[]{:S(2)}, u32[]{:S(2)}) collective-permute-start(f32[4,128]{1,0:T(4,128)S(1)} %bitcast.165), channel_id=1, source_target_pairs={{0,1},{1,0},{2,3},{3,2},{4,5},{5,4},{6,7},{7,6},{8,9},{9,8},{10,11... | collective-permute-start | bytes 6152 | tf_op jit(solution)/shard_map/ppermute | solution.py:20
  145.1 8.9 %collective-permute-start.13 = (bf16[16,4096]{1,0:T(8,128)(2,1)S(1)}, bf16[16,4096]{1,0:T(8,128)(2,1)}, u32[]{:S(2)}, u32[]{:S(2)}) collective-permute-start(bf16[16,4096]{1,0:T(8,128)(2,1)S(1)} %bitcast.157), channel_id=1, source_target_pairs={{0,256},{64,320},{128,384},{192,448},{256,0},{320,64},{384,128},{4... | collective-permute-start | bytes 393224 | tf_op jit(solution)/shard_map/ppermute | solution.py:20
  154.1 1.9 collective-permute-start.10
  156.0 1.3 convolution_convert_fusion
  157.3 6.2 %all-to-all-start.3 = ((bf16[8,64,512]{2,1,0:T(8,128)(2,1)}), bf16[8,64,512]{2,1,0:T(8,128)(2,1)S(1)}, u32[]{:S(2)}, u32[]{:S(2)}) async-start(bf16[8,64,512]{2,1,0:T(8,128)(2,1)} %bitcast.151), calls=%async_computation.3 | async-start | bytes 1048576 | tf_op jit(solution)/shard_map/all_to_all | solution.py:220
  163.6 7.4 %collective-permute-start.11 = (f32[4,128]{1,0:T(4,128)S(1)}, f32[4,128]{1,0:T(4,128)S(1)}, u32[]{:S(2)}, u32[]{:S(2)}) collective-permute-start(f32[4,128]{1,0:T(4,128)S(1)} %fusion.44), channel_id=1, source_target_pairs={{0,4},{1,5},{2,6},{3,7},{4,0},{5,1},{6,2},{7,3},{8,12},{9,13},{10,... | collective-permute-start | bytes 6152 | tf_op jit(solution)/shard_map/ppermute | solution.py:20
  171.0 1.1 fusion.23
  172.2 4.0 %collective-permute-start.15 = (bf16[34,4096]{1,0:T(8,128)(2,1)S(1)}, bf16[34,4096]{1,0:T(8,128)(2,1)S(1)}, u32[]{:S(2)}, u32[]{:S(2)}) collective-permute-start(bf16[34,4096]{1,0:T(8,128)(2,1)S(1)} %get-tuple-element.52), channel_id=1, source_target_pairs={{0,128},{64,192},{128,0},{192,64},{256,384},{320,448},{384,256},{4... | collective-permute-start | bytes 835592 | tf_op jit(solution)/shard_map/ppermute | solution.py:20
  176.2 2.7 %collective-permute-start.14 = (bf16[34,4096]{1,0:T(8,128)(2,1)S(1)}, bf16[34,4096]{1,0:T(8,128)(2,1)S(1)}, u32[]{:S(2)}, u32[]{:S(2)}) collective-permute-start(bf16[34,4096]{1,0:T(8,128)(2,1)S(1)} %get-tuple-element.52), channel_id=1, source_target_pairs={{0,64},{64,0},{128,192},{192,128},{256,320},{320,256},{384,448},{4... | collective-permute-start | bytes 835592 | tf_op jit(solution)/shard_map/ppermute | solution.py:20
  178.9 2.8 %collective-permute-start.16 = (bf16[34,4096]{1,0:T(8,128)(2,1)S(1)}, bf16[34,4096]{1,0:T(8,128)(2,1)S(1)}, u32[]{:S(2)}, u32[]{:S(2)}) collective-permute-start(bf16[34,4096]{1,0:T(8,128)(2,1)S(1)} %get-tuple-element.52), channel_id=1, source_target_pairs={{0,192},{64,128},{128,64},{192,0},{256,448},{320,384},{384,320},{4... | collective-permute-start | bytes 835592 | tf_op jit(solution)/shard_map/ppermute | solution.py:20
  182.0 11.7 %collective-permute-start.12 = (bf16[512,512]{0,1:T(8,128)(2,1)S(1)}, bf16[512,512]{0,1:T(8,128)(2,1)}, u32[]{:S(2)}, u32[]{:S(2)}) collective-permute-start(bf16[512,512]{0,1:T(8,128)(2,1)S(1)} %fusion.6), channel_id=1, source_target_pairs={{8,0},{16,8},{24,16},{32,24},{40,32},{48,40},{56,48},{0,56},{9,1},... | collective-permute-start | bytes 1572872 | tf_op jit(solution)/shard_map/ppermute | solution.py:16
  196.6 1.5 fusion.11
  198.9 2.9 %collective-permute-done.12 = bf16[512,512]{0,1:T(8,128)(2,1)} collective-permute-done((bf16[512,512]{0,1:T(8,128)(2,1)S(1)}, bf16[512,512]{0,1:T(8,128)(2,1)}, u32[]{:S(2)}, u32[]{:S(2)}) %collective-permute-start.12) | collective-permute-done | bytes 524320 | tf_op jit(solution)/shard_map/ppermute | solution.py:16
  201.8 2.0 %copy.58 = bf16[1,1,512,512]{3,2,1,0:T(8,128)(2,1)} copy(bf16[1,1,512,512]{2,3,1,0:T(8,128)(2,1)} %bitcast.26) | data formatting | bytes 1048576
  (100 shorter events, 10.1 us)
Async XLA Ops:
  0.6 113.5 %copy-start = (f32[128,8]{0,1:T(8,128)S(1)}, f32[128,8]{0,1:T(8,128)}, u32[]{:S(2)}) copy-start(f32[128,8]{0,1:T(8,128)} %param.13) | copy-start | bytes 12292
  2.1 10.6 %collective-permute-start = (f32[4,128]{1,0:T(4,128)S(1)}, f32[4,128]{1,0:T(4,128)S(1)}, u32[]{:S(2)}, u32[]{:S(2)}) collective-permute-start(f32[4,128]{1,0:T(4,128)S(1)} %bitcast.168), channel_id=1, source_target_pairs={{56,0},{0,8},{8,16},{16,24},{24,32},{32,40},{40,48},{48,56},{57,1}... | collective-permute-start | bytes 6152 | tf_op jit(solution)/shard_map/ppermute | solution.py:16
  8.4 4.3 %copy-start.12 = (bf16[1,1,512,64]{2,3,1,0:T(8,128)(2,1)S(1)}, bf16[1,1,512,64]{2,3,1,0:T(8,128)(2,1)}, u32[]{:S(2)}) copy-start(bf16[1,1,512,64]{2,3,1,0:T(8,128)(2,1)} %param.9) | copy-start | bytes 196612
  8.4 30.9 %all-to-all-start = ((bf16[4,3,16,4096]{3,2,1,0:T(8,128)(2,1)}), bf16[4,3,16,4096]{3,2,1,0:T(8,128)(2,1)S(1)}, u32[]{:S(2)}, u32[]{:S(2)}) async-start(bf16[4,3,16,4096]{3,2,1,0:T(8,128)(2,1)} %serve.1), calls=%async_computation | async-start | bytes 3145728 | tf_op jit(solution)/shard_map/all_to_all | solution.py:25
  12.8 15.3 %collective-permute-start.1 = (bf16[72,512]{1,0:T(8,128)(2,1)S(1)}, bf16[72,512]{1,0:T(8,128)(2,1)S(1)}, u32[]{:S(2)}, u32[]{:S(2)}) collective-permute-start(bf16[72,512]{1,0:T(8,128)(2,1)S(1)} %maximum_maximum_fusion), channel_id=1, source_target_pairs={{0,4},{1,5},{2,6},{3,7},{4,0},{5,1},{6,2},{7,3},{8,12},{9,13},{10,... | collective-permute-start | bytes 221192 | tf_op jit(solution)/shard_map/ppermute | solution.py:20
  28.2 11.1 %collective-permute-start.2 = (bf16[2,72,512]{2,1,0:T(8,128)(2,1)S(1)}, bf16[2,72,512]{2,1,0:T(8,128)(2,1)S(1)}, u32[]{:S(2)}, u32[]{:S(2)}) collective-permute-start(bf16[2,72,512]{2,1,0:T(8,128)(2,1)S(1)} %pad_maximum_fusion.5), channel_id=1, source_target_pairs={{0,2},{1,3},{2,0},{3,1},{4,6},{5,7},{6,4},{7,5},{8,10},{9,11},{10,... | collective-permute-start | bytes 442376 | tf_op jit(solution)/shard_map/ppermute | solution.py:20
  39.7 17.5 %collective-permute-start.7 = (bf16[2,2,72,512]{3,2,0,1:T(8,128)(2,1)S(1)}, bf16[2,2,72,512]{3,2,0,1:T(8,128)(2,1)S(1)}, u32[]{:S(2)}, u32[]{:S(2)}) collective-permute-start(bf16[2,2,72,512]{3,2,0,1:T(8,128)(2,1)S(1)} %pad_maximum_fusion.4), channel_id=1, source_target_pairs={{0,1},{1,0},{2,3},{3,2},{4,5},{5,4},{6,7},{7,6},{8,9},{9,8},{10,11... | collective-permute-start | bytes 884744 | tf_op jit(solution)/shard_map/ppermute | solution.py:20
  41.6 15.9 %collective-permute-start.8 = (bf16[512,512]{0,1:T(8,128)(2,1)S(1)}, bf16[512,512]{0,1:T(8,128)(2,1)S(1)}, u32[]{:S(2)}, u32[]{:S(2)}) collective-permute-start(bf16[512,512]{0,1:T(8,128)(2,1)S(1)} %bitcast.142), channel_id=1, source_target_pairs={{56,0},{0,8},{8,16},{16,24},{24,32},{32,40},{40,48},{48,56},{57,1}... | collective-permute-start | bytes 1572872 | tf_op jit(solution)/shard_map/ppermute | solution.py:16
  42.8 38.0 %collective-permute-start.3 = (bf16[3,16,3072]{2,1,0:T(8,128)(2,1)S(1)}, bf16[3,16,3072]{2,1,0:T(8,128)(2,1)S(1)}, u32[]{:S(2)}, u32[]{:S(2)}) collective-permute-start(bf16[3,16,3072]{2,1,0:T(8,128)(2,1)S(1)} %slice.46), channel_id=1, source_target_pairs={{0,256},{64,320},{128,384},{192,448},{256,0},{320,64},{384,128},{4... | collective-permute-start | bytes 884744 | tf_op jit(solution)/shard_map/ppermute | solution.py:20
  57.5 1.3 copy-start.7
  58.8 35.8 %all-to-all-start.1 = ((bf16[4,8,16,512]{3,2,1,0:T(8,128)(2,1)}), bf16[4,8,16,512]{3,2,1,0:T(8,128)(2,1)S(1)}, u32[]{:S(2)}, u32[]{:S(2)}) async-start(bf16[4,8,16,512]{3,2,1,0:T(8,128)(2,1)} %bitcast.126), calls=%async_computation.1 | async-start | bytes 1048576 | tf_op jit(solution)/shard_map/all_to_all | solution.py:25
  80.9 13.7 %copy-start.10 = (bf16[16,4096]{1,0:T(8,128)(2,1)}, bf16[16,4096]{1,0:T(8,128)(2,1)S(1)}, u32[]{:S(2)}) copy-start(bf16[16,4096]{1,0:T(8,128)(2,1)S(1)} %fusion.25.fresh0_ref) | copy-start | bytes 393220
  80.9 9.6 %collective-permute-start.6 = (bf16[16,4096]{1,0:T(8,128)(2,1)S(1)}, bf16[16,4096]{1,0:T(8,128)(2,1)S(1)}, u32[]{:S(2)}, u32[]{:S(2)}) collective-permute-start(bf16[16,4096]{1,0:T(8,128)(2,1)S(1)} %fusion.25.fresh0_ref), channel_id=1, source_target_pairs={{0,192},{64,128},{128,64},{192,0},{256,448},{320,384},{384,320},{4... | collective-permute-start | bytes 393224 | tf_op jit(solution)/shard_map/ppermute | solution.py:20
  86.1 7.2 %collective-permute-start.5 = (bf16[16,4096]{1,0:T(8,128)(2,1)S(1)}, bf16[16,4096]{1,0:T(8,128)(2,1)S(1)}, u32[]{:S(2)}, u32[]{:S(2)}) collective-permute-start(bf16[16,4096]{1,0:T(8,128)(2,1)S(1)} %fusion.25.fresh0_ref), channel_id=1, source_target_pairs={{0,128},{64,192},{128,0},{192,64},{256,384},{320,448},{384,256},{4... | collective-permute-start | bytes 393224 | tf_op jit(solution)/shard_map/ppermute | solution.py:20
  88.6 6.0 %collective-permute-start.4 = (bf16[16,4096]{1,0:T(8,128)(2,1)S(1)}, bf16[16,4096]{1,0:T(8,128)(2,1)S(1)}, u32[]{:S(2)}, u32[]{:S(2)}) collective-permute-start(bf16[16,4096]{1,0:T(8,128)(2,1)S(1)} %fusion.25.fresh0_ref), channel_id=1, source_target_pairs={{0,64},{64,0},{128,192},{192,128},{256,320},{320,256},{384,448},{4... | collective-permute-start | bytes 393224 | tf_op jit(solution)/shard_map/ppermute | solution.py:20
  90.5 4.1 %copy-start.13 = (bf16[16,4096]{1,0:T(8,128)(2,1)}, bf16[16,4096]{1,0:T(8,128)(2,1)S(1)}, u32[]{:S(2)}) copy-start(bf16[16,4096]{1,0:T(8,128)(2,1)S(1)} %collective-permute-done.6.fresh3_ref) | copy-start | bytes 393220
  93.3 1.3 copy-start.14
  94.6 0.6 copy-start.15
  95.2 0.8 copy-start.4
  98.9 34.5 %all-to-all-start.2 = ((bf16[8,80,512]{2,1,0:T(8,128)(2,1)}), bf16[8,80,512]{2,1,0:T(8,128)(2,1)S(1)}, u32[]{:S(2)}, u32[]{:S(2)}) async-start(bf16[8,80,512]{2,1,0:T(8,128)(2,1)} %get-tuple-element.17), calls=%async_computation.2 | async-start | bytes 1310720 | tf_op jit(solution)/shard_map/all_to_all | solution.py:206
  112.9 4.2 %copy-start.3 = (bf16[2,16,4096]{2,1,0:T(8,128)(2,1)S(1)}, bf16[2,16,4096]{2,1,0:T(8,128)(2,1)}, u32[]{:S(2)}) copy-start(bf16[2,16,4096]{2,1,0:T(8,128)(2,1)} %unpack.1) | copy-start | bytes 786436
  116.4 3.8 %copy-start.2 = (f32[1,1,64,4096]{3,2,1,0:T(8,128)S(1)}, f32[1,1,64,4096]{3,2,1,0:T(8,128)}, u32[]{:S(2)}) copy-start(f32[1,1,64,4096]{3,2,1,0:T(8,128)} %param.12) | copy-start | bytes 3145732
  120.4 6.0 %copy-start.1 = (f32[1,1,64,4096]{3,2,1,0:T(8,128)S(1)}, f32[1,1,64,4096]{3,2,1,0:T(8,128)}, u32[]{:S(2)}) copy-start(f32[1,1,64,4096]{3,2,1,0:T(8,128)} %param.11) | copy-start | bytes 3145732
  135.8 20.2 %copy-start.8 = (bf16[512,512]{0,1:T(8,128)(2,1)S(1)}, bf16[512,512]{0,1:T(8,128)(2,1)}, u32[]{:S(2)}) copy-start(bf16[512,512]{0,1:T(8,128)(2,1)} %copy-done.7) | copy-start | bytes 1572868
  135.8 18.2 %collective-permute-start.9 = (f32[4,128]{1,0:T(4,128)S(1)}, f32[4,128]{1,0:T(4,128)S(1)}, u32[]{:S(2)}, u32[]{:S(2)}) collective-permute-start(f32[4,128]{1,0:T(4,128)S(1)} %bitcast.165), channel_id=1, source_target_pairs={{0,1},{1,0},{2,3},{3,2},{4,5},{5,4},{6,7},{7,6},{8,9},{9,8},{10,11... | collective-permute-start | bytes 6152 | tf_op jit(solution)/shard_map/ppermute | solution.py:20
  145.1 25.9 %collective-permute-start.13 = (bf16[16,4096]{1,0:T(8,128)(2,1)S(1)}, bf16[16,4096]{1,0:T(8,128)(2,1)}, u32[]{:S(2)}, u32[]{:S(2)}) collective-permute-start(bf16[16,4096]{1,0:T(8,128)(2,1)S(1)} %bitcast.157), channel_id=1, source_target_pairs={{0,256},{64,320},{128,384},{192,448},{256,0},{320,64},{384,128},{4... | collective-permute-start | bytes 393224 | tf_op jit(solution)/shard_map/ppermute | solution.py:20
  154.1 9.5 %collective-permute-start.10 = (f32[4,128]{1,0:T(4,128)S(1)}, f32[4,128]{1,0:T(4,128)S(1)}, u32[]{:S(2)}, u32[]{:S(2)}) collective-permute-start(f32[4,128]{1,0:T(4,128)S(1)} %bitcast_add_fusion.2), channel_id=1, source_target_pairs={{0,2},{1,3},{2,0},{3,1},{4,6},{5,7},{6,4},{7,5},{8,10},{9,11},{10,... | collective-permute-start | bytes 6152 | tf_op jit(solution)/shard_map/ppermute | solution.py:20
  156.0 15.0 %copy-start.5 = (f32[2,16,4096]{2,1,0:T(8,128)S(1)}, f32[2,16,4096]{2,1,0:T(8,128)}, u32[]{:S(2)}) copy-start(f32[2,16,4096]{2,1,0:T(8,128)} %convert_element_type.137) | copy-start | bytes 1572868
  157.3 14.8 %copy-start.16 = (bf16[2,4096]{1,0:T(2,128)(2,1)S(1)}, bf16[2,4096]{1,0:T(2,128)(2,1)}, u32[]{:S(2)}) copy-start(bf16[2,4096]{1,0:T(2,128)(2,1)} %convert_element_type.140) | copy-start | bytes 49156
  157.3 46.6 %all-to-all-start.3 = ((bf16[8,64,512]{2,1,0:T(8,128)(2,1)}), bf16[8,64,512]{2,1,0:T(8,128)(2,1)S(1)}, u32[]{:S(2)}, u32[]{:S(2)}) async-start(bf16[8,64,512]{2,1,0:T(8,128)(2,1)} %bitcast.151), calls=%async_computation.3 | async-start | bytes 1048576 | tf_op jit(solution)/shard_map/all_to_all | solution.py:220
  163.5 18.2 %copy-start.6 = (f32[512,512]{0,1:T(8,128)S(1)}, f32[512,512]{0,1:T(8,128)}, u32[]{:S(2)}) copy-start(f32[512,512]{0,1:T(8,128)} %get-tuple-element.60) | copy-start | bytes 3145732
  163.5 18.2 %copy-start.9 = (bf16[512,512]{0,1:T(8,128)(2,1)S(1)}, bf16[512,512]{0,1:T(8,128)(2,1)}, u32[]{:S(2)}) copy-start(bf16[512,512]{0,1:T(8,128)(2,1)} %copy-done.7) | copy-start | bytes 1572868
  163.6 18.1 %collective-permute-start.11 = (f32[4,128]{1,0:T(4,128)S(1)}, f32[4,128]{1,0:T(4,128)S(1)}, u32[]{:S(2)}, u32[]{:S(2)}) collective-permute-start(f32[4,128]{1,0:T(4,128)S(1)} %fusion.44), channel_id=1, source_target_pairs={{0,4},{1,5},{2,6},{3,7},{4,0},{5,1},{6,2},{7,3},{8,12},{9,13},{10,... | collective-permute-start | bytes 6152 | tf_op jit(solution)/shard_map/ppermute | solution.py:20
  172.2 21.5 %collective-permute-start.15 = (bf16[34,4096]{1,0:T(8,128)(2,1)S(1)}, bf16[34,4096]{1,0:T(8,128)(2,1)S(1)}, u32[]{:S(2)}, u32[]{:S(2)}) collective-permute-start(bf16[34,4096]{1,0:T(8,128)(2,1)S(1)} %get-tuple-element.52), channel_id=1, source_target_pairs={{0,128},{64,192},{128,0},{192,64},{256,384},{320,448},{384,256},{4... | collective-permute-start | bytes 835592 | tf_op jit(solution)/shard_map/ppermute | solution.py:20
  176.2 17.5 %collective-permute-start.14 = (bf16[34,4096]{1,0:T(8,128)(2,1)S(1)}, bf16[34,4096]{1,0:T(8,128)(2,1)S(1)}, u32[]{:S(2)}, u32[]{:S(2)}) collective-permute-start(bf16[34,4096]{1,0:T(8,128)(2,1)S(1)} %get-tuple-element.52), channel_id=1, source_target_pairs={{0,64},{64,0},{128,192},{192,128},{256,320},{320,256},{384,448},{4... | collective-permute-start | bytes 835592 | tf_op jit(solution)/shard_map/ppermute | solution.py:20
  178.9 14.8 %collective-permute-start.16 = (bf16[34,4096]{1,0:T(8,128)(2,1)S(1)}, bf16[34,4096]{1,0:T(8,128)(2,1)S(1)}, u32[]{:S(2)}, u32[]{:S(2)}) collective-permute-start(bf16[34,4096]{1,0:T(8,128)(2,1)S(1)} %get-tuple-element.52), channel_id=1, source_target_pairs={{0,192},{64,128},{128,64},{192,0},{256,448},{320,384},{384,320},{4... | collective-permute-start | bytes 835592 | tf_op jit(solution)/shard_map/ppermute | solution.py:20
  182.0 19.8 %collective-permute-start.12 = (bf16[512,512]{0,1:T(8,128)(2,1)S(1)}, bf16[512,512]{0,1:T(8,128)(2,1)}, u32[]{:S(2)}, u32[]{:S(2)}) collective-permute-start(bf16[512,512]{0,1:T(8,128)(2,1)S(1)} %fusion.6), channel_id=1, source_target_pairs={{8,0},{16,8},{24,16},{32,24},{40,32},{48,40},{56,48},{0,56},{9,1},... | collective-permute-start | bytes 1572872 | tf_op jit(solution)/shard_map/ppermute | solution.py:16
  196.6 1.7 copy-start.11

commit v10 on v9

--- a/solution.py
+++ b/solution.py
@@ -37,11 +37,20 @@
     return held
 
 
-def doubled(held, mine, axis):
+def doubled(held, mine, axis, part=None):
     bit = 4 >> axis
-    came = swap(held, "tensor", bit)
-    high = (mine & bit) != 0
-    return jnp.stack([jnp.where(high, came, held), jnp.where(high, held, came)], axis=axis)
+    sent = held
+    if part is not None:
+        high, low = two_halves(part)
+        rows = held.reshape(-1, held.shape[-1])
+        sent = jnp.concatenate([rows, high, low, jnp.zeros((6, held.shape[-1]), SHORT)], axis=0)
+    came = swap(sent, "tensor", bit)
+    if part is not None:
+        part = part + came[-8:-7].astype(WIDE) + came[-7:-6].astype(WIDE)
+        came = came[:-8].reshape(held.shape)
+    upper = (mine & bit) != 0
+    held = jnp.stack([jnp.where(upper, came, held), jnp.where(upper, held, came)], axis=axis)
+    return held if part is None else (held, part)
 
 
 def gather_x(block):
@@ -71,28 +80,35 @@
     return found
 
 
-def serve_kernel(failed_ref, spans_ref, weight_ref, first_ref, second_ref, out_ref):
+def serve_kernel(failed_ref, spans_ref, weight_ref, first_ref, second_ref, weight_out_ref, moments_out_ref):
     section = lax.axis_index("section")
     me = lax.axis_index("replica")
     failed = failed_ref[section, lax.axis_index("tensor")]
     is_primary = (failed ^ PLANE) == me
     is_second = (failed ^ 1) == me
-    part = out_ref.shape[2]
+    part = weight_out_ref.shape[1]
     for n, (listed, place) in enumerate(places(spans_ref, section, weight_ref.shape[1] // SPAN)):
         take = (listed & is_second) | (jnp.logical_not(listed) & is_primary)
-        for k, ref in enumerate((weight_ref, first_ref, second_ref)):
-            for x in range(PLANE):
-                block = ref[x * part : (x + 1) * part, n * SPAN : (n + 1) * SPAN].astype(SHORT)
-                out_ref[x, k, :, place] = jnp.where(take, block, jnp.zeros_like(block))
+        here = pl.ds(n * SPAN, SPAN)
+        for x in range(PLANE):
+            at = pl.ds(x * part, part)
+            block = weight_ref[at, here]
+            weight_out_ref[x, :, place] = jnp.where(take, block, jnp.zeros_like(block))
+            for k, ref in enumerate((first_ref, second_ref)):
+                block = ref[at, here].astype(SHORT)
+                moments_out_ref[x, k, :, place] = jnp.where(take, block, jnp.zeros_like(block))
 
 
 def serve(failed, spans, weight, first, second):
     rows, width = weight.shape
     return pl.pallas_call(
         serve_kernel,
-        out_shape=jax.ShapeDtypeStruct((PLANE, 3, rows // PLANE, width), SHORT),
+        out_shape=(
+            jax.ShapeDtypeStruct((PLANE, rows // PLANE, width), SHORT),
+            jax.ShapeDtypeStruct((PLANE, 2, rows // PLANE, width), SHORT),
+        ),
         in_specs=[pl.BlockSpec(memory_space=pltpu.SMEM)] * 2 + [pl.BlockSpec(memory_space=pltpu.VMEM)] * 3,
-        out_specs=pl.BlockSpec(memory_space=pltpu.VMEM),
+        out_specs=(pl.BlockSpec(memory_space=pltpu.VMEM),) * 2,
         name="serve",
     )(failed, spans, weight, first, second)
 
@@ -179,27 +195,36 @@
     incoming = from_behind(local, "section", 1)
     x = incoming.astype(WIDE)
 
-    mask = serve(failed_replica, resend_spans, own_weight, own_first, own_second)
-    served = jnp.sum(exchange_x(mask).astype(WIDE), axis=0).astype(SHORT)
-
-    high, low = two_halves(squares)
-    extra = jnp.concatenate([high, low, jnp.zeros((6, tokens), SHORT)], axis=0)
-    held = jnp.concatenate([tied(key_grads[0, 0].T, mask), extra], axis=0)
-    held = doubled(doubled(held, my_tensor, 0), my_tensor, 1)
-    held, served = lax.optimization_barrier((held, served))
+    def summed(parts):
+        return jnp.sum(parts.astype(WIDE), axis=0).astype(SHORT)
+
     cross = width - my_spans.shape[0] * SPAN
-    crossed = served[:, :, :cross] + swap(served[:, :, :cross], "replica", PLANE)
-    fresh = jnp.concatenate([crossed, served[:, :, cross:]], axis=2)
-    fresh_weight = [fresh[0]] + [swap(fresh[0], "replica", bit) for bit in (1, 2, 3)]
-    held = doubled(held, my_tensor, 2).reshape(8, -1, tokens)
-    kg_all = held[:, :rows].reshape(8 * rows, tokens)
-    squares = jnp.sum(held[:, rows].astype(WIDE) + held[:, rows + 1].astype(WIDE), axis=0)
-    inverse_rms = 1.0 / jnp.sqrt(squares / width + 1e-05)
+
+    def both_planes(served):
+        crossed = served[..., :cross] + swap(served[..., :cross], "replica", PLANE)
+        return jnp.concatenate([crossed, served[..., cross:]], axis=-1)
+
+    mask_weight, mask_moments = serve(failed_replica, resend_spans, own_weight, own_first, own_second)
+    served_weight = summed(exchange_x(mask_weight))
+
+    held = doubled(tied(key_grads[0, 0].T, mask_weight), my_tensor, 0)
+    squares = squares + swap(squares, "tensor", 4)
+    held, served_weight, mask_moments, squares = lax.optimization_barrier((held, served_weight, mask_moments, squares))
+    held, squares = doubled(held, my_tensor, 1, squares)
+    held, served_weight, mask_moments = lax.optimization_barrier((held, served_weight, mask_moments))
+    served_moments = summed(exchange_x(mask_moments))
+    fresh_weight = both_planes(served_weight)
+    fresh_weight = [fresh_weight] + [swap(fresh_weight, "replica", bit) for bit in (1, 2, 3)]
+    held, squares = doubled(held, my_tensor, 2, squares)
+    kg_all = held.reshape(8 * rows, tokens)
+    inverse_rms = 1.0 / jnp.sqrt(squares.reshape(tokens) / width + 1e-05)
 
     normed = (x * inverse_rms[:, None]).astype(SHORT)
     grad = lax.dot_general(kg_all, normed, (((1,), (0,)), ((), ())), preferred_element_type=WIDE).astype(SHORT)
     grad = grad.reshape(8, PLANE, part, cols).transpose(1, 0, 2, 3)
+    grad, served_moments = lax.optimization_barrier((grad, served_moments))
     grad = exchange_x(grad)
+    fresh = both_planes(served_moments)
 
     sent, restored_weight = assemble(failed_replica, resend_spans, own_weight, fresh_weight, grad)
     own_first, own_second, restored_weight, fresh = lax.optimization_barrier((own_first, own_second, restored_weight, fresh))
@@ -225,7 +250,7 @@
         mixed = jnp.einsum("jnc,cp->jnp", shaped, probe_matrix, precision=lax.Precision.HIGHEST)
         return mixed.reshape(-1, nchunk * probe_matrix.shape[1])
 
-    fresh = unpack(resend_spans, fresh[1:]).astype(WIDE)
+    fresh = unpack(resend_spans, fresh).astype(WIDE)
     fresh_update = adam(fresh[0], fresh[1], mean_rows).astype(SHORT)
     fresh_sums = checksum(fresh.reshape(2 * part, width)).astype(SHORT).reshape(2, width)
     shared = gather_x(jnp.concatenate([mean_rows.astype(SHORT), fresh_update, fresh_sums], axis=0))

time: 206 us -> 208 us (level)
  waiting for transfers between devices: 39.5 us -> 44.3 us
  other arithmetic: 7.72 us -> 12.3 us
  local copies, waits for them, and re-layouts: 15.7 us -> 11.9 us
  matrix products: 17.2 us -> 15.1 us
    ppermute x14 -> x16, waiting for transfers between devices: 36.6 us -> 19.7 us  [swap(): lax.ppermute(block, axis, [(i, i ^ bit) for i in range(lax.axis_size(axis...]
    all_to_all x1, waiting for transfers between devices: 0.01 us -> 16 us  [shards(): got = lax.all_to_all(sent, 'tensor', 0, 0, tiled=True)]
    ppermute x3, waiting for transfers between devices: 2.89 us -> 8.64 us  [from_behind(): lax.ppermute(block, axis, [((i - distance) % n, i) for i in range(n)])]
    all_to_all x1, starting transfers between devices: 9.49 us -> 4.36 us  [shards(): got = lax.all_to_all(sent, 'tensor', 0, 0, tiled=True)]
    all_to_all x2 -> x3, starting transfers between devices: 8.76 us -> 12.9 us  [exchange_x(): lax.all_to_all(block, 'replica', 0, 0, axis_index_groups=groups, tiled=True)]
    ppermute x14 -> x16, starting transfers between devices: 74 us -> 74.7 us  [swap(): lax.ppermute(block, axis, [(i, i ^ bit) for i in range(lax.axis_size(axis...]
    unnamed x42 -> x46, local copies, waits for them, and re-layouts: 7.12 us -> 6.56 us
  transfers between devices with their start and end apart: 21 -> 24, of which waited for: 6 -> 8; matrix products, arithmetic and copies ran while one was open for 17% -> 16% of each run, Pallas kernels for 3% -> 2%
where the time goes in v10:
time: 208 us; the launch traced here: 207 us
  starting transfers between devices  113 us (54%)
  waiting for transfers between devices  44.3 us (21%)
  matrix products  15.1 us (7%)
  other arithmetic  12.3 us (6%)
  local copies, waits for them, and re-layouts  11.9 us (6%)
  Pallas kernels  8.44 us (4%)
    ppermute x16, starting transfers between devices, swap(): lax.ppermute(block, axis, [(i, i ^ bit) for i in range(lax.axis_size(axis...  74.7 us
    ppermute x16, waiting for transfers between devices, swap(): lax.ppermute(block, axis, [(i, i ^ bit) for i in range(lax.axis_size(axis...  19.7 us
    ppermute x3, starting transfers between devices, from_behind(): lax.ppermute(block, axis, [((i - distance) % n, i) for i in range(n)])  16.2 us
    all_to_all x1, waiting for transfers between devices, shards(): got = lax.all_to_all(sent, 'tensor', 0, 0, tiled=True)  16 us
    all_to_all x3, starting transfers between devices, exchange_x(): lax.all_to_all(block, 'replica', 0, 0, axis_index_groups=groups, tiled=True)  12.9 us
    dot_general x4, matrix products, checksum(): jnp.einsum('jnc,cp->jnp', shaped, probe_matrix, precision=lax.Precision.H...  11.6 us
    ppermute x3, waiting for transfers between devices, from_behind(): lax.ppermute(block, axis, [((i - distance) % n, i) for i in range(n)])  8.64 us
    unnamed x46, local copies, waits for them, and re-layouts  6.56 us
  transfers between devices with their start and end apart: 24, of which 8 were waited for; matrix products, arithmetic and copies ran while one was open for 16% of the time, Pallas kernels for 2%

profile of v10, /device:TPU:1, one launch (start us, length us, event | category | flops | bytes accessed | tf_op | source)
XLA Modules:
  0.0 206.9 jit_solution(5284051139076605405)
XLA Ops:
  0.7 3.7 %serve.1 = (bf16[4,16,4096]{2,1,0:T(8,128)(2,1)}, bf16[4,2,16,4096]{3,2,1,0:T(8,128)(2,1)}) custom-call(s32[8,8]{1,0:T(8,128)} %failed_ref.3, s32[8,8]{1,0:T(8,128)} %spans_ref.5, bf16[64,4096]{1,0:T(8,128)(2,1)} %bitcast.144, f32[64,4096]{1,0:T(8,128)} %bitcast.131, f32[64,4096]{1,0:T(8,128)} %bitcast.134), custom_call_target="tpu_custom_call" | custom-call | tf_op jit(solution)/shard_map/serve/pallas_call | solution.py:104
  4.4 4.8 %all-to-all-start = ((bf16[4,16,4096]{2,1,0:T(8,128)(2,1)}), bf16[4,16,4096]{2,1,0:T(8,128)(2,1)S(1)}, u32[]{:S(2)}, u32[]{:S(2)}) async-start(bf16[4,16,4096]{2,1,0:T(8,128)(2,1)} %get-tuple-element.23), calls=%async_computation | async-start | bytes 1048576 | tf_op jit(solution)/shard_map/all_to_all | solution.py:25
  9.2 8.8 %collective-permute-start = (bf16[64,512]{1,0:T(8,128)(2,1)S(1)}, bf16[64,512]{1,0:T(8,128)(2,1)S(1)}, u32[]{:S(2)}, u32[]{:S(2)}) collective-permute-start(bf16[64,512]{1,0:T(8,128)(2,1)S(1)} %bitcast.170), channel_id=1, source_target_pairs={{0,4},{1,5},{2,6},{3,7},{4,0},{5,1},{6,2},{7,3},{8,12},{9,13},{10,... | collective-permute-start | bytes 196616 | tf_op jit(solution)/shard_map/ppermute | solution.py:20
  18.4 2.4 %collective-permute-start.1 = (f32[4,128]{1,0:T(4,128)S(1)}, f32[4,128]{1,0:T(4,128)S(1)}, u32[]{:S(2)}, u32[]{:S(2)}) collective-permute-start(f32[4,128]{1,0:T(4,128)S(1)} %bitcast.178), channel_id=1, source_target_pairs={{56,0},{0,8},{8,16},{16,24},{24,32},{32,40},{40,48},{48,56},{57,1}... | collective-permute-start | bytes 6152 | tf_op jit(solution)/shard_map/ppermute | solution.py:16
  21.5 3.7 %collective-permute-start.2 = (f32[1,512]{1,0:T(1,128)S(1)}, f32[1,512]{1,0:T(1,128)S(1)}, u32[]{:S(2)}, u32[]{:S(2)}) collective-permute-start(f32[1,512]{1,0:T(1,128)S(1)} %bitcast.179), channel_id=1, source_target_pairs={{0,4},{1,5},{2,6},{3,7},{4,0},{5,1},{6,2},{7,3},{8,12},{9,13},{10,... | collective-permute-start | bytes 6152 | tf_op jit(solution)/shard_map/ppermute | solution.py:20
  25.2 4.5 %collective-permute-done.2 = f32[1,512]{1,0:T(1,128)S(1)} collective-permute-done((f32[1,512]{1,0:T(1,128)S(1)}, f32[1,512]{1,0:T(1,128)S(1)}, u32[]{:S(2)}, u32[]{:S(2)}) %collective-permute-start.2) | collective-permute-done | bytes 2080 | tf_op jit(solution)/shard_map/ppermute | solution.py:20
  30.0 4.9 %collective-permute-start.3 = (bf16[136,512]{1,0:T(8,128)(2,1)S(1)}, bf16[136,512]{1,0:T(8,128)(2,1)S(1)}, u32[]{:S(2)}, u32[]{:S(2)}) collective-permute-start(bf16[136,512]{1,0:T(8,128)(2,1)S(1)} %pad_maximum_fusion.6), channel_id=1, source_target_pairs={{0,2},{1,3},{2,0},{3,1},{4,6},{5,7},{6,4},{7,5},{8,10},{9,11},{10,... | collective-permute-start | bytes 417800 | tf_op jit(solution)/shard_map/ppermute | solution.py:20
  34.9 3.7 %collective-permute-start.9 = (bf16[512,512]{0,1:T(8,128)(2,1)S(1)}, bf16[512,512]{0,1:T(8,128)(2,1)S(1)}, u32[]{:S(2)}, u32[]{:S(2)}) collective-permute-start(bf16[512,512]{0,1:T(8,128)(2,1)S(1)} %bitcast.146), channel_id=1, source_target_pairs={{56,0},{0,8},{8,16},{16,24},{24,32},{32,40},{40,48},{48,56},{57,1}... | collective-permute-start | bytes 1572872 | tf_op jit(solution)/shard_map/ppermute | solution.py:16
  38.9 4.5 %all-to-all-start.1 = ((bf16[4,2,16,4096]{3,2,1,0:T(8,128)(2,1)}), bf16[4,2,16,4096]{3,2,1,0:T(8,128)(2,1)S(1)}, u32[]{:S(2)}, u32[]{:S(2)}) async-start(bf16[4,2,16,4096]{3,2,1,0:T(8,128)(2,1)} %get-tuple-element.32), calls=%async_computation.1 | async-start | bytes 2097152 | tf_op jit(solution)/shard_map/all_to_all | solution.py:25
  43.5 10.0 %collective-permute-start.4 = (bf16[16,3072]{1,0:T(8,128)(2,1)S(1)}, bf16[16,3072]{1,0:T(8,128)(2,1)S(1)}, u32[]{:S(2)}, u32[]{:S(2)}) collective-permute-start(bf16[16,3072]{1,0:T(8,128)(2,1)S(1)} %slice.54), channel_id=1, source_target_pairs={{0,256},{64,320},{128,384},{192,448},{256,0},{320,64},{384,128},{4... | collective-permute-start | bytes 294920 | tf_op jit(solution)/shard_map/ppermute | solution.py:20
  53.5 1.9 collective-permute-start.8
  55.4 2.2 %collective-permute-done.4 = bf16[16,3072]{1,0:T(8,128)(2,1)S(1)} collective-permute-done((bf16[16,3072]{1,0:T(8,128)(2,1)S(1)}, bf16[16,3072]{1,0:T(8,128)(2,1)S(1)}, u32[]{:S(2)}, u32[]{:S(2)}) %collective-permute-start.4) | collective-permute-done | bytes 98336 | tf_op jit(solution)/shard_map/ppermute | solution.py:20
  57.6 9.3 %collective-permute-done.8 = bf16[264,512]{1,0:T(8,128)(2,1)S(1)} collective-permute-done((bf16[264,512]{1,0:T(8,128)(2,1)S(1)}, bf16[264,512]{1,0:T(8,128)(2,1)S(1)}, u32[]{:S(2)}, u32[]{:S(2)}) %collective-permute-start.8) | collective-permute-done | bytes 270368 | tf_op jit(solution)/shard_map/ppermute | solution.py:20
  67.9 0.8 copy.76
  69.0 3.5 %all-to-all-start.2 = ((bf16[4,8,16,512]{3,2,1,0:T(8,128)(2,1)}), bf16[4,8,16,512]{3,2,1,0:T(8,128)(2,1)S(1)}, u32[]{:S(2)}, u32[]{:S(2)}) async-start(bf16[4,8,16,512]{3,2,1,0:T(8,128)(2,1)} %bitcast.130), calls=%async_computation.2 | async-start | bytes 1048576 | tf_op jit(solution)/shard_map/all_to_all | solution.py:25
  72.5 4.5 %collective-permute-start.7 = (bf16[16,4096]{1,0:T(8,128)(2,1)S(1)}, bf16[16,4096]{1,0:T(8,128)(2,1)S(1)}, u32[]{:S(2)}, u32[]{:S(2)}) collective-permute-start(bf16[16,4096]{1,0:T(8,128)(2,1)S(1)} %pad_maximum_fusion.8.fresh0_ref), channel_id=1, source_target_pairs={{0,192},{64,128},{128,64},{192,0},{256,448},{320,384},{384,320},{4... | collective-permute-start | bytes 393224 | tf_op jit(solution)/shard_map/ppermute | solution.py:20
  77.0 2.5 %collective-permute-start.6 = (bf16[16,4096]{1,0:T(8,128)(2,1)S(1)}, bf16[16,4096]{1,0:T(8,128)(2,1)S(1)}, u32[]{:S(2)}, u32[]{:S(2)}) collective-permute-start(bf16[16,4096]{1,0:T(8,128)(2,1)S(1)} %pad_maximum_fusion.8.fresh0_ref), channel_id=1, source_target_pairs={{0,128},{64,192},{128,0},{192,64},{256,384},{320,448},{384,256},{4... | collective-permute-start | bytes 393224 | tf_op jit(solution)/shard_map/ppermute | solution.py:20
  79.5 2.0 collective-permute-start.5
  81.5 1.3 dynamic_slice.3
  83.5 5.8 %collective-permute-start.15 = (bf16[2,16,3072]{2,1,0:T(8,128)(2,1)S(1)}, bf16[2,16,3072]{2,1,0:T(8,128)(2,1)S(1)}, u32[]{:S(2)}, u32[]{:S(2)}) collective-permute-start(bf16[2,16,3072]{2,1,0:T(8,128)(2,1)S(1)} %slice.63), channel_id=1, source_target_pairs={{0,256},{64,320},{128,384},{192,448},{256,0},{320,64},{384,128},{4... | collective-permute-start | bytes 589832 | tf_op jit(solution)/shard_map/ppermute | solution.py:20
  90.8 2.9 %assemble.1 = (bf16[8,80,512]{2,1,0:T(8,128)(2,1)}, bf16[64,4096]{1,0:T(8,128)(2,1)}) custom-call(s32[8,8]{1,0:T(8,128)} %failed_ref.3, s32[8,8]{1,0:T(8,128)} %spans_ref.5, bf16[64,4096]{1,0:T(8,128)(2,1)} %bitcast.145, bf16[16,4096]{1,0:T(8,128)(2,1)} %copy-done.11, bf16[16,4096]{1,0:T(8,128)(2,1)} %copy-done.16, bf16[16,4096]{1,0:T(8,128)(2,1)} %copy-done.15, ...), custom_call_target="tpu_custom_call" | custom-call | tf_op jit(solution)/shard_map/assemble/pallas_call | solution.py:158
  93.7 4.4 %all-to-all-start.3 = ((bf16[8,80,512]{2,1,0:T(8,128)(2,1)}), bf16[8,80,512]{2,1,0:T(8,128)(2,1)S(1)}, u32[]{:S(2)}, u32[]{:S(2)}) async-start(bf16[8,80,512]{2,1,0:T(8,128)(2,1)} %get-tuple-element.34), calls=%async_computation.3 | async-start | bytes 1310720 | tf_op jit(solution)/shard_map/all_to_all | solution.py:231
  98.0 3.5 %collective-permute-done.15 = bf16[2,16,3072]{2,1,0:T(8,128)(2,1)S(1)} collective-permute-done((bf16[2,16,3072]{2,1,0:T(8,128)(2,1)S(1)}, bf16[2,16,3072]{2,1,0:T(8,128)(2,1)S(1)}, u32[]{:S(2)}, u32[]{:S(2)}) %collective-permute-start.15) | collective-permute-done | bytes 196640 | tf_op jit(solution)/shard_map/ppermute | solution.py:20
  102.2 1.9 unpack.1
  104.3 2.1 %fusion.24 = f32[64,32,8]{1,2,0:T(8,128)S(1)} fusion(bf16[64,32,128]{2,1,0:T(8,128)(2,1)S(1)} %bitcast.147, f32[128,8]{0,1:T(8,128)S(1)} %copy-done), kind=kOutput, calls=%fused_computation.58 | convolution fusion | flops 25165824 | bytes 593920 | tf_op jit(solution)/shard_map/jnc,cp->jnp/dot_general | solution.py:250
  108.2 1.1 convolution_convert_fusion.2
  109.5 0.9 convert_element_type.132
  110.6 4.2 %fusion.26 = f32[64,32,8]{1,2,0:T(8,128)S(1)} fusion(f32[64,32,128]{2,1,0:T(8,128)S(1)} %bitcast.140, f32[128,8]{0,1:T(8,128)S(1)} %copy-done), kind=kOutput, calls=%fused_computation.60 | convolution fusion | flops 25165824 | bytes 1118208 | tf_op jit(solution)/shard_map/jnc,cp->jnp/dot_general | solution.py:250
  115.2 4.2 %fusion.28 = f32[64,32,8]{1,2,0:T(8,128)S(1)} fusion(f32[64,32,128]{2,1,0:T(8,128)S(1)} %bitcast.141, f32[128,8]{0,1:T(8,128)S(1)} %copy-done), kind=kOutput, calls=%fused_computation.62 | convolution fusion | flops 25165824 | bytes 1118208 | tf_op jit(solution)/shard_map/jnc,cp->jnp/dot_general | solution.py:250
  119.6 16.0 %all-to-all-done.3 = bf16[8,80,512]{2,1,0:T(8,128)(2,1)S(1)} async-done(((bf16[8,80,512]{2,1,0:T(8,128)(2,1)}), bf16[8,80,512]{2,1,0:T(8,128)(2,1)S(1)}, u32[]{:S(2)}, u32[]{:S(2)}) %all-to-all-start.3) | async-done | bytes 655392 | tf_op jit(solution)/shard_map/all_to_all | solution.py:231
  136.4 1.8 fusion.7
  138.2 1.9 collective-permute-start.10
  140.1 0.9 slice_bitcast_fusion
  141.0 9.8 %collective-permute-start.14 = (bf16[16,4096]{1,0:T(8,128)(2,1)S(1)}, bf16[16,4096]{1,0:T(8,128)(2,1)S(1)}, u32[]{:S(2)}, u32[]{:S(2)}) collective-permute-start(bf16[16,4096]{1,0:T(8,128)(2,1)S(1)} %bitcast.165), channel_id=1, source_target_pairs={{0,256},{64,320},{128,384},{192,448},{256,0},{320,64},{384,128},{4... | collective-permute-start | bytes 393224 | tf_op jit(solution)/shard_map/ppermute | solution.py:20
  152.0 1.9 collective-permute-start.11
  153.9 1.3 convolution_convert_fusion
  155.2 4.8 %all-to-all-start.4 = ((bf16[8,64,512]{2,1,0:T(8,128)(2,1)}), bf16[8,64,512]{2,1,0:T(8,128)(2,1)}, u32[]{:S(2)}, u32[]{:S(2)}) async-start(bf16[8,64,512]{2,1,0:T(8,128)(2,1)} %bitcast.160), calls=%async_computation.4 | async-start | bytes 1048576 | tf_op jit(solution)/shard_map/all_to_all | solution.py:245
  160.8 7.3 %collective-permute-start.12 = (f32[4,128]{1,0:T(4,128)S(1)}, f32[4,128]{1,0:T(4,128)S(1)}, u32[]{:S(2)}, u32[]{:S(2)}) collective-permute-start(f32[4,128]{1,0:T(4,128)S(1)} %fusion.48), channel_id=1, source_target_pairs={{0,4},{1,5},{2,6},{3,7},{4,0},{5,1},{6,2},{7,3},{8,12},{9,13},{10,... | collective-permute-start | bytes 6152 | tf_op jit(solution)/shard_map/ppermute | solution.py:20
  168.0 1.2 fusion.23
  170.0 4.9 %collective-permute-start.17 = (bf16[34,4096]{1,0:T(8,128)(2,1)S(1)}, bf16[34,4096]{1,0:T(8,128)(2,1)S(1)}, u32[]{:S(2)}, u32[]{:S(2)}) collective-permute-start(bf16[34,4096]{1,0:T(8,128)(2,1)S(1)} %get-tuple-element.70), channel_id=1, source_target_pairs={{0,128},{64,192},{128,0},{192,64},{256,384},{320,448},{384,256},{4... | collective-permute-start | bytes 835592 | tf_op jit(solution)/shard_map/ppermute | solution.py:20
  174.9 2.2 %collective-permute-start.16 = (bf16[34,4096]{1,0:T(8,128)(2,1)S(1)}, bf16[34,4096]{1,0:T(8,128)(2,1)S(1)}, u32[]{:S(2)}, u32[]{:S(2)}) collective-permute-start(bf16[34,4096]{1,0:T(8,128)(2,1)S(1)} %get-tuple-element.70), channel_id=1, source_target_pairs={{0,64},{64,0},{128,192},{192,128},{256,320},{320,256},{384,448},{4... | collective-permute-start | bytes 835592 | tf_op jit(solution)/shard_map/ppermute | solution.py:20
  177.1 2.7 %collective-permute-start.18 = (bf16[34,4096]{1,0:T(8,128)(2,1)S(1)}, bf16[34,4096]{1,0:T(8,128)(2,1)S(1)}, u32[]{:S(2)}, u32[]{:S(2)}) collective-permute-start(bf16[34,4096]{1,0:T(8,128)(2,1)S(1)} %get-tuple-element.70), channel_id=1, source_target_pairs={{0,192},{64,128},{128,64},{192,0},{256,448},{320,384},{384,320},{4... | collective-permute-start | bytes 835592 | tf_op jit(solution)/shard_map/ppermute | solution.py:20
  179.9 1.0 fusion.6
  180.9 10.0 %collective-permute-start.13 = (bf16[512,512]{0,1:T(8,128)(2,1)}, bf16[512,512]{0,1:T(8,128)(2,1)S(1)}, u32[]{:S(2)}, u32[]{:S(2)}) collective-permute-start(bf16[512,512]{0,1:T(8,128)(2,1)} %fusion.6), channel_id=1, source_target_pairs={{8,0},{16,8},{24,16},{32,24},{40,32},{48,40},{56,48},{0,56},{9,1},... | collective-permute-start | bytes 1572872 | tf_op jit(solution)/shard_map/ppermute | solution.py:16
  193.9 1.5 fusion.11
  196.2 7.9 %collective-permute-done.13 = bf16[512,512]{0,1:T(8,128)(2,1)S(1)} collective-permute-done((bf16[512,512]{0,1:T(8,128)(2,1)}, bf16[512,512]{0,1:T(8,128)(2,1)S(1)}, u32[]{:S(2)}, u32[]{:S(2)}) %collective-permute-start.13) | collective-permute-done | bytes 524320 | tf_op jit(solution)/shard_map/ppermute | solution.py:16
  204.1 1.0 copy.60
  205.1 1.8 reduce_sum.57
  (117 shorter events, 15.2 us)
Async XLA Ops:
  0.6 103.6 %copy-start = (f32[128,8]{0,1:T(8,128)S(1)}, f32[128,8]{0,1:T(8,128)}, u32[]{:S(2)}) copy-start(f32[128,8]{0,1:T(8,128)} %param.13) | copy-start | bytes 12292
  0.6 8.6 %copy-start.17 = (bf16[1,1,512,64]{2,3,1,0:T(8,128)(2,1)S(1)}, bf16[1,1,512,64]{2,3,1,0:T(8,128)(2,1)}, u32[]{:S(2)}) copy-start(bf16[1,1,512,64]{2,3,1,0:T(8,128)(2,1)} %param.9) | copy-start | bytes 196612
  0.7 17.4 %copy-start.12 = (bf16[1,1,512,512]{3,2,1,0:T(8,128)(2,1)S(1)}, bf16[1,1,512,512]{3,2,1,0:T(8,128)(2,1)}, u32[]{:S(2)}) copy-start(bf16[1,1,512,512]{3,2,1,0:T(8,128)(2,1)} %param.8) | copy-start | bytes 1572868
  4.4 25.5 %all-to-all-start = ((bf16[4,16,4096]{2,1,0:T(8,128)(2,1)}), bf16[4,16,4096]{2,1,0:T(8,128)(2,1)S(1)}, u32[]{:S(2)}, u32[]{:S(2)}) async-start(bf16[4,16,4096]{2,1,0:T(8,128)(2,1)} %get-tuple-element.23), calls=%async_computation | async-start | bytes 1048576 | tf_op jit(solution)/shard_map/all_to_all | solution.py:25
  9.2 20.6 %collective-permute-start = (bf16[64,512]{1,0:T(8,128)(2,1)S(1)}, bf16[64,512]{1,0:T(8,128)(2,1)S(1)}, u32[]{:S(2)}, u32[]{:S(2)}) collective-permute-start(bf16[64,512]{1,0:T(8,128)(2,1)S(1)} %bitcast.170), channel_id=1, source_target_pairs={{0,4},{1,5},{2,6},{3,7},{4,0},{5,1},{6,2},{7,3},{8,12},{9,13},{10,... | collective-permute-start | bytes 196616 | tf_op jit(solution)/shard_map/ppermute | solution.py:20
  18.4 3.1 %collective-permute-start.1 = (f32[4,128]{1,0:T(4,128)S(1)}, f32[4,128]{1,0:T(4,128)S(1)}, u32[]{:S(2)}, u32[]{:S(2)}) collective-permute-start(f32[4,128]{1,0:T(4,128)S(1)} %bitcast.178), channel_id=1, source_target_pairs={{56,0},{0,8},{8,16},{16,24},{24,32},{32,40},{40,48},{48,56},{57,1}... | collective-permute-start | bytes 6152 | tf_op jit(solution)/shard_map/ppermute | solution.py:16
  21.5 8.2 %collective-permute-start.2 = (f32[1,512]{1,0:T(1,128)S(1)}, f32[1,512]{1,0:T(1,128)S(1)}, u32[]{:S(2)}, u32[]{:S(2)}) collective-permute-start(f32[1,512]{1,0:T(1,128)S(1)} %bitcast.179), channel_id=1, source_target_pairs={{0,4},{1,5},{2,6},{3,7},{4,0},{5,1},{6,2},{7,3},{8,12},{9,13},{10,... | collective-permute-start | bytes 6152 | tf_op jit(solution)/shard_map/ppermute | solution.py:20
  29.9 27.7 %copy-start.10 = (bf16[16,4096]{1,0:T(8,128)(2,1)}, bf16[16,4096]{1,0:T(8,128)(2,1)S(1)}, u32[]{:S(2)}) copy-start(bf16[16,4096]{1,0:T(8,128)(2,1)S(1)} %reduce_sum.54) | copy-start | bytes 393220
  30.0 8.8 %collective-permute-start.3 = (bf16[136,512]{1,0:T(8,128)(2,1)S(1)}, bf16[136,512]{1,0:T(8,128)(2,1)S(1)}, u32[]{:S(2)}, u32[]{:S(2)}) collective-permute-start(bf16[136,512]{1,0:T(8,128)(2,1)S(1)} %pad_maximum_fusion.6), channel_id=1, source_target_pairs={{0,2},{1,3},{2,0},{3,1},{4,6},{5,7},{6,4},{7,5},{8,10},{9,11},{10,... | collective-permute-start | bytes 417800 | tf_op jit(solution)/shard_map/ppermute | solution.py:20
  34.9 32.2 %collective-permute-start.9 = (bf16[512,512]{0,1:T(8,128)(2,1)S(1)}, bf16[512,512]{0,1:T(8,128)(2,1)S(1)}, u32[]{:S(2)}, u32[]{:S(2)}) collective-permute-start(bf16[512,512]{0,1:T(8,128)(2,1)S(1)} %bitcast.146), channel_id=1, source_target_pairs={{56,0},{0,8},{8,16},{16,24},{24,32},{32,40},{40,48},{48,56},{57,1}... | collective-permute-start | bytes 1572872 | tf_op jit(solution)/shard_map/ppermute | solution.py:16
  38.9 29.8 %all-to-all-start.1 = ((bf16[4,2,16,4096]{3,2,1,0:T(8,128)(2,1)}), bf16[4,2,16,4096]{3,2,1,0:T(8,128)(2,1)S(1)}, u32[]{:S(2)}, u32[]{:S(2)}) async-start(bf16[4,2,16,4096]{3,2,1,0:T(8,128)(2,1)} %get-tuple-element.32), calls=%async_computation.1 | async-start | bytes 2097152 | tf_op jit(solution)/shard_map/all_to_all | solution.py:25
  43.5 14.1 %collective-permute-start.4 = (bf16[16,3072]{1,0:T(8,128)(2,1)S(1)}, bf16[16,3072]{1,0:T(8,128)(2,1)S(1)}, u32[]{:S(2)}, u32[]{:S(2)}) collective-permute-start(bf16[16,3072]{1,0:T(8,128)(2,1)S(1)} %slice.54), channel_id=1, source_target_pairs={{0,256},{64,320},{128,384},{192,448},{256,0},{320,64},{384,128},{4... | collective-permute-start | bytes 294920 | tf_op jit(solution)/shard_map/ppermute | solution.py:20
  53.5 13.4 %collective-permute-start.8 = (bf16[264,512]{1,0:T(8,128)(2,1)S(1)}, bf16[264,512]{1,0:T(8,128)(2,1)S(1)}, u32[]{:S(2)}, u32[]{:S(2)}) collective-permute-start(bf16[264,512]{1,0:T(8,128)(2,1)S(1)} %pad_maximum_fusion.3), channel_id=1, source_target_pairs={{0,1},{1,0},{2,3},{3,2},{4,5},{5,4},{6,7},{7,6},{8,9},{9,8},{10,11... | collective-permute-start | bytes 811016 | tf_op jit(solution)/shard_map/ppermute | solution.py:20
  67.1 0.8 copy-start.9
  67.1 1.6 copy-start.6
  68.7 3.7 %slice-start = ((bf16[16,4096]{1,0:T(8,128)(2,1)}), bf16[16,1024]{1,0:T(8,128)(2,1)S(1)}, s32[]{:S(2)}) async-start(bf16[16,4096]{1,0:T(8,128)(2,1)} %copy-done.10), calls=%async_computation.5 | async-start | bytes 65536 | tf_op jit(solution)/shard_map/slice | solution.py:205
  69.0 20.3 %all-to-all-start.2 = ((bf16[4,8,16,512]{3,2,1,0:T(8,128)(2,1)}), bf16[4,8,16,512]{3,2,1,0:T(8,128)(2,1)S(1)}, u32[]{:S(2)}, u32[]{:S(2)}) async-start(bf16[4,8,16,512]{3,2,1,0:T(8,128)(2,1)} %bitcast.130), calls=%async_computation.2 | async-start | bytes 1048576 | tf_op jit(solution)/shard_map/all_to_all | solution.py:25
  72.5 16.8 %copy-start.11 = (bf16[16,4096]{1,0:T(8,128)(2,1)}, bf16[16,4096]{1,0:T(8,128)(2,1)S(1)}, u32[]{:S(2)}) copy-start(bf16[16,4096]{1,0:T(8,128)(2,1)S(1)} %pad_maximum_fusion.8.fresh0_ref) | copy-start | bytes 393220
  72.5 16.8 %collective-permute-start.7 = (bf16[16,4096]{1,0:T(8,128)(2,1)S(1)}, bf16[16,4096]{1,0:T(8,128)(2,1)S(1)}, u32[]{:S(2)}, u32[]{:S(2)}) collective-permute-start(bf16[16,4096]{1,0:T(8,128)(2,1)S(1)} %pad_maximum_fusion.8.fresh0_ref), channel_id=1, source_target_pairs={{0,192},{64,128},{128,64},{192,0},{256,448},{320,384},{384,320},{4... | collective-permute-start | bytes 393224 | tf_op jit(solution)/shard_map/ppermute | solution.py:20
  77.0 12.2 %collective-permute-start.6 = (bf16[16,4096]{1,0:T(8,128)(2,1)S(1)}, bf16[16,4096]{1,0:T(8,128)(2,1)S(1)}, u32[]{:S(2)}, u32[]{:S(2)}) collective-permute-start(bf16[16,4096]{1,0:T(8,128)(2,1)S(1)} %pad_maximum_fusion.8.fresh0_ref), channel_id=1, source_target_pairs={{0,128},{64,192},{128,0},{192,64},{256,384},{320,448},{384,256},{4... | collective-permute-start | bytes 393224 | tf_op jit(solution)/shard_map/ppermute | solution.py:20
  79.5 9.8 %collective-permute-start.5 = (bf16[16,4096]{1,0:T(8,128)(2,1)S(1)}, bf16[16,4096]{1,0:T(8,128)(2,1)S(1)}, u32[]{:S(2)}, u32[]{:S(2)}) collective-permute-start(bf16[16,4096]{1,0:T(8,128)(2,1)S(1)} %pad_maximum_fusion.8.fresh0_ref), channel_id=1, source_target_pairs={{0,64},{64,0},{128,192},{192,128},{256,320},{320,256},{384,448},{4... | collective-permute-start | bytes 393224 | tf_op jit(solution)/shard_map/ppermute | solution.py:20
  83.5 18.0 %collective-permute-start.15 = (bf16[2,16,3072]{2,1,0:T(8,128)(2,1)S(1)}, bf16[2,16,3072]{2,1,0:T(8,128)(2,1)S(1)}, u32[]{:S(2)}, u32[]{:S(2)}) collective-permute-start(bf16[2,16,3072]{2,1,0:T(8,128)(2,1)S(1)} %slice.63), channel_id=1, source_target_pairs={{0,256},{64,320},{128,384},{192,448},{256,0},{320,64},{384,128},{4... | collective-permute-start | bytes 589832 | tf_op jit(solution)/shard_map/ppermute | solution.py:20
  89.3 0.6 copy-start.14
  89.3 0.7 copy-start.15
  89.3 0.7 copy-start.16
  90.0 0.8 copy-start.5
  93.7 10.5 %copy-start.13 = (bf16[64,4096]{1,0:T(8,128)(2,1)S(1)}, bf16[64,4096]{1,0:T(8,128)(2,1)}, u32[]{:S(2)}) copy-start(bf16[64,4096]{1,0:T(8,128)(2,1)} %get-tuple-element.40) | copy-start | bytes 1572868
  93.7 41.9 %all-to-all-start.3 = ((bf16[8,80,512]{2,1,0:T(8,128)(2,1)}), bf16[8,80,512]{2,1,0:T(8,128)(2,1)S(1)}, u32[]{:S(2)}, u32[]{:S(2)}) async-start(bf16[8,80,512]{2,1,0:T(8,128)(2,1)} %get-tuple-element.34), calls=%async_computation.3 | async-start | bytes 1310720 | tf_op jit(solution)/shard_map/all_to_all | solution.py:231
  104.1 3.1 %copy-start.4 = (bf16[2,16,4096]{2,1,0:T(8,128)(2,1)S(1)}, bf16[2,16,4096]{2,1,0:T(8,128)(2,1)}, u32[]{:S(2)}) copy-start(bf16[2,16,4096]{2,1,0:T(8,128)(2,1)} %unpack.1) | copy-start | bytes 786436
  106.6 3.8 %copy-start.2 = (f32[1,1,64,4096]{3,2,1,0:T(8,128)S(1)}, f32[1,1,64,4096]{3,2,1,0:T(8,128)}, u32[]{:S(2)}) copy-start(f32[1,1,64,4096]{3,2,1,0:T(8,128)} %param.12) | copy-start | bytes 3145732
  110.5 4.4 %copy-start.1 = (f32[1,1,64,4096]{3,2,1,0:T(8,128)S(1)}, f32[1,1,64,4096]{3,2,1,0:T(8,128)}, u32[]{:S(2)}) copy-start(f32[1,1,64,4096]{3,2,1,0:T(8,128)} %param.11) | copy-start | bytes 3145732
  135.6 0.8 copy-start.3
  136.4 17.5 %copy-start.7 = (bf16[512,512]{0,1:T(8,128)(2,1)S(1)}, bf16[512,512]{0,1:T(8,128)(2,1)}, u32[]{:S(2)}) copy-start(bf16[512,512]{0,1:T(8,128)(2,1)} %copy-done.6) | copy-start | bytes 1572868
  138.2 12.7 %collective-permute-start.10 = (f32[4,128]{1,0:T(4,128)S(1)}, f32[4,128]{1,0:T(4,128)S(1)}, u32[]{:S(2)}, u32[]{:S(2)}) collective-permute-start(f32[4,128]{1,0:T(4,128)S(1)} %bitcast.177), channel_id=1, source_target_pairs={{0,1},{1,0},{2,3},{3,2},{4,5},{5,4},{6,7},{7,6},{8,9},{9,8},{10,11... | collective-permute-start | bytes 6152 | tf_op jit(solution)/shard_map/ppermute | solution.py:20
  141.0 27.0 %collective-permute-start.14 = (bf16[16,4096]{1,0:T(8,128)(2,1)S(1)}, bf16[16,4096]{1,0:T(8,128)(2,1)S(1)}, u32[]{:S(2)}, u32[]{:S(2)}) collective-permute-start(bf16[16,4096]{1,0:T(8,128)(2,1)S(1)} %bitcast.165), channel_id=1, source_target_pairs={{0,256},{64,320},{128,384},{192,448},{256,0},{320,64},{384,128},{4... | collective-permute-start | bytes 393224 | tf_op jit(solution)/shard_map/ppermute | solution.py:20
  150.8 0.6 copy-start.18
  152.0 8.0 %collective-permute-start.11 = (f32[4,128]{1,0:T(4,128)}, f32[4,128]{1,0:T(4,128)}, u32[]{:S(2)}, u32[]{:S(2)}) collective-permute-start(f32[4,128]{1,0:T(4,128)} %bitcast_add_fusion.2), channel_id=1, source_target_pairs={{0,2},{1,3},{2,0},{3,1},{4,6},{5,7},{6,4},{7,5},{8,10},{9,11},{10,... | collective-permute-start | bytes 6152 | tf_op jit(solution)/shard_map/ppermute | solution.py:20
  155.2 49.9 %all-to-all-start.4 = ((bf16[8,64,512]{2,1,0:T(8,128)(2,1)}), bf16[8,64,512]{2,1,0:T(8,128)(2,1)}, u32[]{:S(2)}, u32[]{:S(2)}) async-start(bf16[8,64,512]{2,1,0:T(8,128)(2,1)} %bitcast.160), calls=%async_computation.4 | async-start | bytes 1048576 | tf_op jit(solution)/shard_map/all_to_all | solution.py:245
  160.0 19.9 %copy-start.8 = (bf16[512,512]{0,1:T(8,128)(2,1)S(1)}, bf16[512,512]{0,1:T(8,128)(2,1)}, u32[]{:S(2)}) copy-start(bf16[512,512]{0,1:T(8,128)(2,1)} %copy-done.6) | copy-start | bytes 1572868
  160.8 19.1 %collective-permute-start.12 = (f32[4,128]{1,0:T(4,128)S(1)}, f32[4,128]{1,0:T(4,128)S(1)}, u32[]{:S(2)}, u32[]{:S(2)}) collective-permute-start(f32[4,128]{1,0:T(4,128)S(1)} %fusion.48), channel_id=1, source_target_pairs={{0,4},{1,5},{2,6},{3,7},{4,0},{5,1},{6,2},{7,3},{8,12},{9,13},{10,... | collective-permute-start | bytes 6152 | tf_op jit(solution)/shard_map/ppermute | solution.py:20
  170.0 20.9 %collective-permute-start.17 = (bf16[34,4096]{1,0:T(8,128)(2,1)S(1)}, bf16[34,4096]{1,0:T(8,128)(2,1)S(1)}, u32[]{:S(2)}, u32[]{:S(2)}) collective-permute-start(bf16[34,4096]{1,0:T(8,128)(2,1)S(1)} %get-tuple-element.70), channel_id=1, source_target_pairs={{0,128},{64,192},{128,0},{192,64},{256,384},{320,448},{384,256},{4... | collective-permute-start | bytes 835592 | tf_op jit(solution)/shard_map/ppermute | solution.py:20
  174.9 16.1 %collective-permute-start.16 = (bf16[34,4096]{1,0:T(8,128)(2,1)S(1)}, bf16[34,4096]{1,0:T(8,128)(2,1)S(1)}, u32[]{:S(2)}, u32[]{:S(2)}) collective-permute-start(bf16[34,4096]{1,0:T(8,128)(2,1)S(1)} %get-tuple-element.70), channel_id=1, source_target_pairs={{0,64},{64,0},{128,192},{192,128},{256,320},{320,256},{384,448},{4... | collective-permute-start | bytes 835592 | tf_op jit(solution)/shard_map/ppermute | solution.py:20
  177.1 13.9 %collective-permute-start.18 = (bf16[34,4096]{1,0:T(8,128)(2,1)S(1)}, bf16[34,4096]{1,0:T(8,128)(2,1)S(1)}, u32[]{:S(2)}, u32[]{:S(2)}) collective-permute-start(bf16[34,4096]{1,0:T(8,128)(2,1)S(1)} %get-tuple-element.70), channel_id=1, source_target_pairs={{0,192},{64,128},{128,64},{192,0},{256,448},{320,384},{384,320},{4... | collective-permute-start | bytes 835592 | tf_op jit(solution)/shard_map/ppermute | solution.py:20
  180.9 23.2 %collective-permute-start.13 = (bf16[512,512]{0,1:T(8,128)(2,1)}, bf16[512,512]{0,1:T(8,128)(2,1)S(1)}, u32[]{:S(2)}, u32[]{:S(2)}) collective-permute-start(bf16[512,512]{0,1:T(8,128)(2,1)} %fusion.6), channel_id=1, source_target_pairs={{8,0},{16,8},{24,16},{32,24},{40,32},{48,40},{56,48},{0,56},{9,1},... | collective-permute-start | bytes 1572872 | tf_op jit(solution)/shard_map/ppermute | solution.py:16

commit v11 on v9

--- a/solution.py
+++ b/solution.py
@@ -130,15 +130,12 @@
             restored_ref[at, n * SPAN : (n + 1) * SPAN] = block
             sent_ref[n // apart, at, (n % apart) * SPAN : (n % apart + 1) * SPAN] = block
     for t in range(groups):
-        total = grads_ref[0, t].astype(WIDE)
-        for x in range(1, PLANE):
-            total = total + grads_ref[x, t].astype(WIDE)
-        sent_ref[t, rows:, :] = total.astype(SHORT)
+        sent_ref[t, rows:, :] = grads_ref[t]
 
 
 def assemble(failed, spans, own, fresh, grads):
     rows, width = own.shape
-    _, groups, part, cols = grads.shape
+    groups, part, cols = grads.shape
     return pl.pallas_call(
         assemble_kernel,
         out_shape=(
@@ -199,14 +196,14 @@
     normed = (x * inverse_rms[:, None]).astype(SHORT)
     grad = lax.dot_general(kg_all, normed, (((1,), (0,)), ((), ())), preferred_element_type=WIDE).astype(SHORT)
     grad = grad.reshape(8, PLANE, part, cols).transpose(1, 0, 2, 3)
-    grad = exchange_x(grad)
+    grad = jnp.sum(exchange_x(grad).astype(WIDE), axis=0).astype(SHORT)
+    grad = ((grad.astype(WIDE) + swap(grad, "replica", PLANE).astype(WIDE)) / copies).astype(SHORT)
 
     sent, restored_weight = assemble(failed_replica, resend_spans, own_weight, fresh_weight, grad)
     own_first, own_second, restored_weight, fresh = lax.optimization_barrier((own_first, own_second, restored_weight, fresh))
     got = lax.all_to_all(sent, "tensor", 0, 0, tiled=True)
     weight_cols = got[:, :rows].reshape(8 * rows, cols)
-    grad_rows = got[:, rows:].transpose(1, 0, 2).reshape(part, width)
-    mean_rows = (grad_rows.astype(WIDE) + swap(grad_rows, "replica", PLANE).astype(WIDE)) / copies
+    mean_rows = got[:, rows:].transpose(1, 0, 2).reshape(part, width)
 
     keys = lax.dot_general(weight_cols, normed, (((1,), (1,)), ((), ())), preferred_element_type=WIDE).astype(SHORT)
     feature = lax.dot_general(kg_all, weight_cols, (((0,), (0,)), ((), ())), preferred_element_type=WIDE)
@@ -226,9 +223,9 @@
         return mixed.reshape(-1, nchunk * probe_matrix.shape[1])
 
     fresh = unpack(resend_spans, fresh[1:]).astype(WIDE)
-    fresh_update = adam(fresh[0], fresh[1], mean_rows).astype(SHORT)
+    fresh_update = adam(fresh[0], fresh[1], mean_rows.astype(WIDE)).astype(SHORT)
     fresh_sums = checksum(fresh.reshape(2 * part, width)).astype(SHORT).reshape(2, width)
-    shared = gather_x(jnp.concatenate([mean_rows.astype(SHORT), fresh_update, fresh_sums], axis=0))
+    shared = gather_x(jnp.concatenate([mean_rows, fresh_update, fresh_sums], axis=0))
     mean_grad = shared[:, :part].reshape(rows, width).astype(WIDE)
     fresh_update = shared[:, part : 2 * part].reshape(rows, width).astype(WIDE)
     fresh_sums = shared[:, 2 * part :].reshape(PLANE, 2, part, -1).transpose(1, 0, 2, 3).reshape(2, rows, -1).astype(WIDE)

time: 206 us -> 211 us (1.024)
  the two profiles are of different devices: /device:TPU:1 before, /device:TPU:8 now
where the time goes in v11:
time: 211 us; the launch traced here: 209 us
  starting transfers between devices  111 us (53%)
  waiting for transfers between devices  43.5 us (21%)
  matrix products  17.3 us (8%)
  local copies, waits for them, and re-layouts  15.7 us (7%)
  other arithmetic  11.9 us (6%)
  Pallas kernels  8.3 us (4%)
    ppermute x14, starting transfers between devices, swap(): lax.ppermute(block, axis, [(i, i ^ bit) for i in range(lax.axis_size(axis...  90.1 us
    ppermute x14, waiting for transfers between devices, swap(): lax.ppermute(block, axis, [(i, i ^ bit) for i in range(lax.axis_size(axis...  23 us
    dot_general x4, matrix products, checksum(): jnp.einsum('jnc,cp->jnp', shaped, probe_matrix, precision=lax.Precision.H...  13 us
    all_to_all x1, waiting for transfers between devices, shards(): lax.all_to_all(keys.reshape(8, rows, tokens), 'tensor', 0, 0, tiled=True)  12.2 us
    all_to_all x2, starting transfers between devices, exchange_x(): lax.all_to_all(block, 'replica', 0, 0, axis_index_groups=groups, tiled=True)  9.3 us
    all_to_all x1, waiting for transfers between devices, shards(): got = lax.all_to_all(sent, 'tensor', 0, 0, tiled=True)  7.68 us
    all_to_all x1, starting transfers between devices, shards(): lax.all_to_all(keys.reshape(8, rows, tokens), 'tensor', 0, 0, tiled=True)  7.44 us
    unnamed x36, local copies, waits for them, and re-layouts  6.34 us
  transfers between devices with their start and end apart: 21, of which 9 were waited for; matrix products, arithmetic and copies ran while one was open for 19% of the time, Pallas kernels for 3%

profile of v11, /device:TPU:8, one launch (start us, length us, event | category | flops | bytes accessed | tf_op | source)
XLA Modules:
  0.0 209.4 jit_solution(6241489274926866919)
XLA Ops:
  0.6 1.3 copy.55
  2.1 3.7 %serve.1 = bf16[4,3,16,4096]{3,2,1,0:T(8,128)(2,1)} custom-call(s32[8,8]{1,0:T(8,128)} %failed_ref.3, s32[8,8]{1,0:T(8,128)} %spans_ref.5, bf16[64,4096]{1,0:T(8,128)(2,1)} %bitcast.132, f32[64,4096]{1,0:T(8,128)} %bitcast.115, f32[64,4096]{1,0:T(8,128)} %bitcast.118), custom_call_target="tpu_custom_call" | custom-call | tf_op jit(solution)/shard_map/serve/pallas_call | solution.py:91
  5.8 4.4 %all-to-all-start = ((bf16[4,3,16,4096]{3,2,1,0:T(8,128)(2,1)}), bf16[4,3,16,4096]{3,2,1,0:T(8,128)(2,1)S(1)}, u32[]{:S(2)}, u32[]{:S(2)}) async-start(bf16[4,3,16,4096]{3,2,1,0:T(8,128)(2,1)} %serve.1), calls=%async_computation | async-start | bytes 3145728 | tf_op jit(solution)/shard_map/all_to_all | solution.py:25
  10.4 9.1 %collective-permute-start.1 = (bf16[72,512]{1,0:T(8,128)(2,1)S(1)}, bf16[72,512]{1,0:T(8,128)(2,1)S(1)}, u32[]{:S(2)}, u32[]{:S(2)}) collective-permute-start(bf16[72,512]{1,0:T(8,128)(2,1)S(1)} %maximum_maximum_fusion), channel_id=1, source_target_pairs={{0,4},{1,5},{2,6},{3,7},{4,0},{5,1},{6,2},{7,3},{8,12},{9,13},{10,... | collective-permute-start | bytes 221192 | tf_op jit(solution)/shard_map/ppermute | solution.py:20
  19.5 2.4 %collective-permute-done.1 = bf16[72,512]{1,0:T(8,128)(2,1)S(1)} collective-permute-done((bf16[72,512]{1,0:T(8,128)(2,1)S(1)}, bf16[72,512]{1,0:T(8,128)(2,1)S(1)}, u32[]{:S(2)}, u32[]{:S(2)}) %collective-permute-start.1) | collective-permute-done | bytes 73760 | tf_op jit(solution)/shard_map/ppermute | solution.py:20
  22.1 7.6 %collective-permute-start.2 = (bf16[2,72,512]{2,1,0:T(8,128)(2,1)S(1)}, bf16[2,72,512]{2,1,0:T(8,128)(2,1)S(1)}, u32[]{:S(2)}, u32[]{:S(2)}) collective-permute-start(bf16[2,72,512]{2,1,0:T(8,128)(2,1)S(1)} %pad_maximum_fusion.5), channel_id=1, source_target_pairs={{0,2},{1,3},{2,0},{3,1},{4,6},{5,7},{6,4},{7,5},{8,10},{9,11},{10,... | collective-permute-start | bytes 442376 | tf_op jit(solution)/shard_map/ppermute | solution.py:20
  29.7 3.4 %collective-permute-done.2 = bf16[2,72,512]{2,1,0:T(8,128)(2,1)S(1)} collective-permute-done((bf16[2,72,512]{2,1,0:T(8,128)(2,1)S(1)}, bf16[2,72,512]{2,1,0:T(8,128)(2,1)S(1)}, u32[]{:S(2)}, u32[]{:S(2)}) %collective-permute-start.2) | collective-permute-done | bytes 147488 | tf_op jit(solution)/shard_map/ppermute | solution.py:20
  33.5 6.5 %collective-permute-start.7 = (bf16[2,2,72,512]{3,2,0,1:T(8,128)(2,1)S(1)}, bf16[2,2,72,512]{3,2,0,1:T(8,128)(2,1)S(1)}, u32[]{:S(2)}, u32[]{:S(2)}) collective-permute-start(bf16[2,2,72,512]{3,2,0,1:T(8,128)(2,1)S(1)} %pad_maximum_fusion.4), channel_id=1, source_target_pairs={{0,1},{1,0},{2,3},{3,2},{4,5},{5,4},{6,7},{7,6},{8,9},{9,8},{10,11... | collective-permute-start | bytes 884744 | tf_op jit(solution)/shard_map/ppermute | solution.py:20
  40.9 14.7 %collective-permute-start.3 = (bf16[3,16,3072]{2,1,0:T(8,128)(2,1)}, bf16[3,16,3072]{2,1,0:T(8,128)(2,1)}, u32[]{:S(2)}, u32[]{:S(2)}) collective-permute-start(bf16[3,16,3072]{2,1,0:T(8,128)(2,1)} %slice.46), channel_id=1, source_target_pairs={{0,256},{64,320},{128,384},{192,448},{256,0},{320,64},{384,128},{4... | collective-permute-start | bytes 884744 | tf_op jit(solution)/shard_map/ppermute | solution.py:20
  56.3 0.8 copy.85
  57.2 4.9 %all-to-all-start.1 = ((bf16[4,8,16,512]{3,2,1,0:T(8,128)(2,1)}), bf16[4,8,16,512]{3,2,1,0:T(8,128)(2,1)S(1)}, u32[]{:S(2)}, u32[]{:S(2)}) async-start(bf16[4,8,16,512]{3,2,1,0:T(8,128)(2,1)} %bitcast.114), calls=%async_computation.1 | async-start | bytes 1048576 | tf_op jit(solution)/shard_map/all_to_all | solution.py:25
  62.1 11.0 %collective-permute-done.3 = bf16[3,16,3072]{2,1,0:T(8,128)(2,1)} collective-permute-done((bf16[3,16,3072]{2,1,0:T(8,128)(2,1)}, bf16[3,16,3072]{2,1,0:T(8,128)(2,1)}, u32[]{:S(2)}, u32[]{:S(2)}) %collective-permute-start.3) | collective-permute-done | bytes 294944 | tf_op jit(solution)/shard_map/ppermute | solution.py:20
  73.1 1.0 slice_add_fusion
  74.2 24.4 %collective-permute-start.9 = (bf16[8,16,512]{2,1,0:T(8,128)(2,1)S(1)}, bf16[8,16,512]{2,1,0:T(8,128)(2,1)S(1)}, u32[]{:S(2)}, u32[]{:S(2)}) collective-permute-start(bf16[8,16,512]{2,1,0:T(8,128)(2,1)S(1)} %reduce_sum.66), channel_id=1, source_target_pairs={{0,256},{64,320},{128,384},{192,448},{256,0},{320,64},{384,128},{4... | collective-permute-start | bytes 393224 | tf_op jit(solution)/shard_map/ppermute | solution.py:20
  98.7 2.8 %collective-permute-start.6 = (bf16[16,4096]{1,0:T(8,128)(2,1)S(1)}, bf16[16,4096]{1,0:T(8,128)(2,1)S(1)}, u32[]{:S(2)}, u32[]{:S(2)}) collective-permute-start(bf16[16,4096]{1,0:T(8,128)(2,1)S(1)} %fusion.24.fresh0_ref), channel_id=1, source_target_pairs={{0,192},{64,128},{128,64},{192,0},{256,448},{320,384},{384,320},{4... | collective-permute-start | bytes 393224 | tf_op jit(solution)/shard_map/ppermute | solution.py:20
  101.4 3.6 %collective-permute-start.5 = (bf16[16,4096]{1,0:T(8,128)(2,1)S(1)}, bf16[16,4096]{1,0:T(8,128)(2,1)S(1)}, u32[]{:S(2)}, u32[]{:S(2)}) collective-permute-start(bf16[16,4096]{1,0:T(8,128)(2,1)S(1)} %fusion.24.fresh0_ref), channel_id=1, source_target_pairs={{0,128},{64,192},{128,0},{192,64},{256,384},{320,448},{384,256},{4... | collective-permute-start | bytes 393224 | tf_op jit(solution)/shard_map/ppermute | solution.py:20
  105.1 3.4 %collective-permute-start.4 = (bf16[16,4096]{1,0:T(8,128)(2,1)S(1)}, bf16[16,4096]{1,0:T(8,128)(2,1)S(1)}, u32[]{:S(2)}, u32[]{:S(2)}) collective-permute-start(bf16[16,4096]{1,0:T(8,128)(2,1)S(1)} %fusion.24.fresh0_ref), channel_id=1, source_target_pairs={{0,64},{64,0},{128,192},{192,128},{256,320},{320,256},{384,448},{4... | collective-permute-start | bytes 393224 | tf_op jit(solution)/shard_map/ppermute | solution.py:20
  109.8 2.1 %collective-permute-done.4.fresh1_ref = bf16[16,4096]{1,0:T(8,128)(2,1)S(1)} collective-permute-done((bf16[16,4096]{1,0:T(8,128)(2,1)S(1)}, bf16[16,4096]{1,0:T(8,128)(2,1)S(1)}, u32[]{:S(2)}, u32[]{:S(2)}) %collective-permute-start.4) | collective-permute-done | bytes 131104 | tf_op jit(solution)/shard_map/ppermute | solution.py:20
  112.6 2.7 %assemble.1 = (bf16[8,80,512]{2,1,0:T(8,128)(2,1)}, bf16[64,4096]{1,0:T(8,128)(2,1)}) custom-call(s32[8,8]{1,0:T(8,128)} %failed_ref.3, s32[8,8]{1,0:T(8,128)} %spans_ref.5, bf16[64,4096]{1,0:T(8,128)(2,1)} %bitcast.133, bf16[16,4096]{1,0:T(8,128)(2,1)} %copy-done.7, bf16[16,4096]{1,0:T(8,128)(2,1)} %copy-done.12, bf16[16,4096]{1,0:T(8,128)(2,1)} %copy-done.11, ...), custom_call_target="tpu_custom_call" | custom-call | tf_op jit(solution)/shard_map/assemble/pallas_call | solution.py:139
  115.3 4.0 %all-to-all-start.2 = ((bf16[8,80,512]{2,1,0:T(8,128)(2,1)}), bf16[8,80,512]{2,1,0:T(8,128)(2,1)S(1)}, u32[]{:S(2)}, u32[]{:S(2)}) async-start(bf16[8,80,512]{2,1,0:T(8,128)(2,1)} %get-tuple-element.17), calls=%async_computation.2 | async-start | bytes 1310720 | tf_op jit(solution)/shard_map/all_to_all | solution.py:204
  119.3 1.3 dynamic_slice.3
  122.0 1.9 unpack.1
  123.9 1.2 copy.79
  125.1 2.1 %fusion.27 = f32[64,32,8]{1,2,0:T(8,128)S(1)} fusion(bf16[64,32,128]{2,1,0:T(8,128)(2,1)S(1)} %bitcast.131, f32[128,8]{0,1:T(8,128)S(1)} %copy-done), kind=kOutput, calls=%fused_computation.66 | convolution fusion | flops 25165824 | bytes 593920 | tf_op jit(solution)/shard_map/jnc,cp->jnp/dot_general | solution.py:222
  128.2 0.8 convert_element_type.142
  129.0 1.1 convolution_convert_fusion.2
  130.3 0.9 convert_element_type.146
  131.4 4.9 %fusion.29 = f32[64,32,8]{1,2,0:T(8,128)} fusion(f32[64,32,128]{2,1,0:T(8,128)S(1)} %bitcast.124, f32[128,8]{0,1:T(8,128)S(1)} %copy-done), kind=kOutput, calls=%fused_computation.68 | convolution fusion | flops 25165824 | bytes 1118208 | tf_op jit(solution)/shard_map/jnc,cp->jnp/dot_general | solution.py:222
  136.3 1.1 copy.65
  137.7 4.9 %fusion.31 = f32[64,32,8]{1,2,0:T(8,128)} fusion(f32[64,32,128]{2,1,0:T(8,128)S(1)} %bitcast.125, f32[128,8]{0,1:T(8,128)S(1)} %copy-done), kind=kOutput, calls=%fused_computation.70 | convolution fusion | flops 25165824 | bytes 1118208 | tf_op jit(solution)/shard_map/jnc,cp->jnp/dot_general | solution.py:222
  142.6 1.1 copy.64
  144.4 7.7 %all-to-all-done.2 = bf16[8,80,512]{2,1,0:T(8,128)(2,1)S(1)} async-done(((bf16[8,80,512]{2,1,0:T(8,128)(2,1)}), bf16[8,80,512]{2,1,0:T(8,128)(2,1)S(1)}, u32[]{:S(2)}, u32[]{:S(2)}) %all-to-all-start.2) | async-done | bytes 655392 | tf_op jit(solution)/shard_map/all_to_all | solution.py:204
  152.1 2.6 %fusion.7 = (f32[512]{0:T(512)S(1)}, f32[512,512]{0,1:T(8,128)}) fusion(bf16[512,512]{0,1:T(8,128)(2,1)} %copy-done.5, bf16[8,80,512]{2,1,0:T(8,128)(2,1)S(1)} %all-to-all-done.2, bf16[8,72,512]{2,1,0:T(8,128)(2,1)S(1)} %bitcast.129), kind=kOutput, calls=%fused_computation.19 | convolution fusion | flops 269221376 | bytes 2623488 | tf_op jit(solution)/shard_map/dot_general | solution.py:209
  154.7 1.9 collective-permute-start.10
  156.8 3.4 %collective-permute-done.10 = f32[4,128]{1,0:T(4,128)S(1)} collective-permute-done((f32[4,128]{1,0:T(4,128)S(1)}, f32[4,128]{1,0:T(4,128)S(1)}, u32[]{:S(2)}, u32[]{:S(2)}) %collective-permute-start.10) | collective-permute-done | bytes 2080 | tf_op jit(solution)/shard_map/ppermute | solution.py:20
  160.2 1.9 collective-permute-start.11
  162.1 4.5 %collective-permute-start.15 = (bf16[34,4096]{1,0:T(8,128)(2,1)S(1)}, bf16[34,4096]{1,0:T(8,128)(2,1)}, u32[]{:S(2)}, u32[]{:S(2)}) collective-permute-start(bf16[34,4096]{1,0:T(8,128)(2,1)S(1)} %get-tuple-element.57), channel_id=1, source_target_pairs={{0,128},{64,192},{128,0},{192,64},{256,384},{320,448},{384,256},{4... | collective-permute-start | bytes 835592 | tf_op jit(solution)/shard_map/ppermute | solution.py:20
  166.6 2.4 %collective-permute-start.14 = (bf16[34,4096]{1,0:T(8,128)(2,1)S(1)}, bf16[34,4096]{1,0:T(8,128)(2,1)}, u32[]{:S(2)}, u32[]{:S(2)}) collective-permute-start(bf16[34,4096]{1,0:T(8,128)(2,1)S(1)} %get-tuple-element.57), channel_id=1, source_target_pairs={{0,64},{64,0},{128,192},{192,128},{256,320},{320,256},{384,448},{4... | collective-permute-start | bytes 835592 | tf_op jit(solution)/shard_map/ppermute | solution.py:20
  169.1 3.1 %collective-permute-start.16 = (bf16[34,4096]{1,0:T(8,128)(2,1)S(1)}, bf16[34,4096]{1,0:T(8,128)(2,1)}, u32[]{:S(2)}, u32[]{:S(2)}) collective-permute-start(bf16[34,4096]{1,0:T(8,128)(2,1)S(1)} %get-tuple-element.57), channel_id=1, source_target_pairs={{0,192},{64,128},{128,64},{192,0},{256,448},{320,384},{384,320},{4... | collective-permute-start | bytes 835592 | tf_op jit(solution)/shard_map/ppermute | solution.py:20
  172.2 4.0 %collective-permute-start.12 = (f32[4,128]{1,0:T(4,128)S(1)}, f32[4,128]{1,0:T(4,128)S(1)}, u32[]{:S(2)}, u32[]{:S(2)}) collective-permute-start(f32[4,128]{1,0:T(4,128)S(1)} %fusion.43), channel_id=1, source_target_pairs={{0,4},{1,5},{2,6},{3,7},{4,0},{5,1},{6,2},{7,3},{8,12},{9,13},{10,... | collective-permute-start | bytes 6152 | tf_op jit(solution)/shard_map/ppermute | solution.py:20
  176.3 1.3 convolution_convert_fusion
  177.6 7.4 %all-to-all-start.3 = ((bf16[8,64,512]{2,1,0:T(8,128)(2,1)}), bf16[8,64,512]{2,1,0:T(8,128)(2,1)S(1)}, u32[]{:S(2)}, u32[]{:S(2)}) async-start(bf16[8,64,512]{2,1,0:T(8,128)(2,1)} %bitcast.141), calls=%async_computation.3 | async-start | bytes 1048576 | tf_op jit(solution)/shard_map/all_to_all | solution.py:217
  185.0 2.4 %fusion.6 = bf16[512,512]{0,1:T(8,128)(2,1)} fusion(bf16[512,512]{0,1:T(8,128)(2,1)} %copy-done.5, f32[512,512]{0,1:T(8,128)} %get-tuple-element.63, f32[512]{0:T(512)S(1)} %add_bitcast_fusion, f32[512]{0:T(512)S(1)} %get-tuple-element.60, f32[512]{0:T(512)S(1)} %get-tuple-element.61), kind=kLoop, calls=%fused_computation.18 | loop fusion | flops 1835008 | bytes 2103296 | tf_op jit(solution)/shard_map/convert_element_type | solution.py:216
  187.4 1.4 pad_maximum_fusion
  189.5 0.8 convert_multiply_fusion.4
  191.5 1.5 fusion.11
  194.4 2.0 copy.69
  196.5 12.2 %all-to-all-done.3 = bf16[8,64,512]{2,1,0:T(8,128)(2,1)S(1)} async-done(((bf16[8,64,512]{2,1,0:T(8,128)(2,1)}), bf16[8,64,512]{2,1,0:T(8,128)(2,1)S(1)}, u32[]{:S(2)}, u32[]{:S(2)}) %all-to-all-start.3) | async-done | bytes 524320 | tf_op jit(solution)/shard_map/all_to_all | solution.py:217
  (96 shorter events, 11.7 us)
Async XLA Ops:
  0.6 124.5 %copy-start = (f32[128,8]{0,1:T(8,128)S(1)}, f32[128,8]{0,1:T(8,128)}, u32[]{:S(2)}) copy-start(f32[128,8]{0,1:T(8,128)} %param.13) | copy-start | bytes 12292
  2.1 8.2 %collective-permute-start = (f32[4,128]{1,0:T(4,128)S(1)}, f32[4,128]{1,0:T(4,128)S(1)}, u32[]{:S(2)}, u32[]{:S(2)}) collective-permute-start(f32[4,128]{1,0:T(4,128)S(1)} %bitcast.153), channel_id=1, source_target_pairs={{56,0},{0,8},{8,16},{16,24},{24,32},{32,40},{40,48},{48,56},{57,1}... | collective-permute-start | bytes 6152 | tf_op jit(solution)/shard_map/ppermute | solution.py:16
  5.8 4.5 %copy-start.9 = (bf16[1,1,512,64]{2,3,1,0:T(8,128)(2,1)S(1)}, bf16[1,1,512,64]{2,3,1,0:T(8,128)(2,1)}, u32[]{:S(2)}) copy-start(bf16[1,1,512,64]{2,3,1,0:T(8,128)(2,1)} %param.9) | copy-start | bytes 196612
  5.8 27.5 %all-to-all-start = ((bf16[4,3,16,4096]{3,2,1,0:T(8,128)(2,1)}), bf16[4,3,16,4096]{3,2,1,0:T(8,128)(2,1)S(1)}, u32[]{:S(2)}, u32[]{:S(2)}) async-start(bf16[4,3,16,4096]{3,2,1,0:T(8,128)(2,1)} %serve.1), calls=%async_computation | async-start | bytes 3145728 | tf_op jit(solution)/shard_map/all_to_all | solution.py:25
  10.4 11.5 %collective-permute-start.1 = (bf16[72,512]{1,0:T(8,128)(2,1)S(1)}, bf16[72,512]{1,0:T(8,128)(2,1)S(1)}, u32[]{:S(2)}, u32[]{:S(2)}) collective-permute-start(bf16[72,512]{1,0:T(8,128)(2,1)S(1)} %maximum_maximum_fusion), channel_id=1, source_target_pairs={{0,4},{1,5},{2,6},{3,7},{4,0},{5,1},{6,2},{7,3},{8,12},{9,13},{10,... | collective-permute-start | bytes 221192 | tf_op jit(solution)/shard_map/ppermute | solution.py:20
  22.1 11.1 %collective-permute-start.2 = (bf16[2,72,512]{2,1,0:T(8,128)(2,1)S(1)}, bf16[2,72,512]{2,1,0:T(8,128)(2,1)S(1)}, u32[]{:S(2)}, u32[]{:S(2)}) collective-permute-start(bf16[2,72,512]{2,1,0:T(8,128)(2,1)S(1)} %pad_maximum_fusion.5), channel_id=1, source_target_pairs={{0,2},{1,3},{2,0},{3,1},{4,6},{5,7},{6,4},{7,5},{8,10},{9,11},{10,... | collective-permute-start | bytes 442376 | tf_op jit(solution)/shard_map/ppermute | solution.py:20
  33.5 22.0 %collective-permute-start.7 = (bf16[2,2,72,512]{3,2,0,1:T(8,128)(2,1)S(1)}, bf16[2,2,72,512]{3,2,0,1:T(8,128)(2,1)S(1)}, u32[]{:S(2)}, u32[]{:S(2)}) collective-permute-start(bf16[2,2,72,512]{3,2,0,1:T(8,128)(2,1)S(1)} %pad_maximum_fusion.4), channel_id=1, source_target_pairs={{0,1},{1,0},{2,3},{3,2},{4,5},{5,4},{6,7},{7,6},{8,9},{9,8},{10,11... | collective-permute-start | bytes 884744 | tf_op jit(solution)/shard_map/ppermute | solution.py:20
  40.1 15.7 %collective-permute-start.8 = (bf16[512,512]{0,1:T(8,128)(2,1)S(1)}, bf16[512,512]{0,1:T(8,128)(2,1)S(1)}, u32[]{:S(2)}, u32[]{:S(2)}) collective-permute-start(bf16[512,512]{0,1:T(8,128)(2,1)S(1)} %bitcast.130), channel_id=1, source_target_pairs={{56,0},{0,8},{8,16},{16,24},{24,32},{32,40},{40,48},{48,56},{57,1}... | collective-permute-start | bytes 1572872 | tf_op jit(solution)/shard_map/ppermute | solution.py:16
  40.9 32.2 %collective-permute-start.3 = (bf16[3,16,3072]{2,1,0:T(8,128)(2,1)}, bf16[3,16,3072]{2,1,0:T(8,128)(2,1)}, u32[]{:S(2)}, u32[]{:S(2)}) collective-permute-start(bf16[3,16,3072]{2,1,0:T(8,128)(2,1)} %slice.46), channel_id=1, source_target_pairs={{0,256},{64,320},{128,384},{192,448},{256,0},{320,64},{384,128},{4... | collective-permute-start | bytes 884744 | tf_op jit(solution)/shard_map/ppermute | solution.py:20
  55.8 1.3 copy-start.5
  57.2 16.9 %all-to-all-start.1 = ((bf16[4,8,16,512]{3,2,1,0:T(8,128)(2,1)}), bf16[4,8,16,512]{3,2,1,0:T(8,128)(2,1)S(1)}, u32[]{:S(2)}, u32[]{:S(2)}) async-start(bf16[4,8,16,512]{3,2,1,0:T(8,128)(2,1)} %bitcast.114), calls=%async_computation.1 | async-start | bytes 1048576 | tf_op jit(solution)/shard_map/all_to_all | solution.py:25
  74.2 34.3 %collective-permute-start.9 = (bf16[8,16,512]{2,1,0:T(8,128)(2,1)S(1)}, bf16[8,16,512]{2,1,0:T(8,128)(2,1)S(1)}, u32[]{:S(2)}, u32[]{:S(2)}) collective-permute-start(bf16[8,16,512]{2,1,0:T(8,128)(2,1)S(1)} %reduce_sum.66), channel_id=1, source_target_pairs={{0,256},{64,320},{128,384},{192,448},{256,0},{320,64},{384,128},{4... | collective-permute-start | bytes 393224 | tf_op jit(solution)/shard_map/ppermute | solution.py:20
  98.7 13.3 %copy-start.7 = (bf16[16,4096]{1,0:T(8,128)(2,1)}, bf16[16,4096]{1,0:T(8,128)(2,1)S(1)}, u32[]{:S(2)}) copy-start(bf16[16,4096]{1,0:T(8,128)(2,1)S(1)} %fusion.24.fresh0_ref) | copy-start | bytes 393220
  98.7 10.6 %collective-permute-start.6 = (bf16[16,4096]{1,0:T(8,128)(2,1)S(1)}, bf16[16,4096]{1,0:T(8,128)(2,1)S(1)}, u32[]{:S(2)}, u32[]{:S(2)}) collective-permute-start(bf16[16,4096]{1,0:T(8,128)(2,1)S(1)} %fusion.24.fresh0_ref), channel_id=1, source_target_pairs={{0,192},{64,128},{128,64},{192,0},{256,448},{320,384},{384,320},{4... | collective-permute-start | bytes 393224 | tf_op jit(solution)/shard_map/ppermute | solution.py:20
  101.4 8.4 %collective-permute-start.5 = (bf16[16,4096]{1,0:T(8,128)(2,1)S(1)}, bf16[16,4096]{1,0:T(8,128)(2,1)S(1)}, u32[]{:S(2)}, u32[]{:S(2)}) collective-permute-start(bf16[16,4096]{1,0:T(8,128)(2,1)S(1)} %fusion.24.fresh0_ref), channel_id=1, source_target_pairs={{0,128},{64,192},{128,0},{192,64},{256,384},{320,448},{384,256},{4... | collective-permute-start | bytes 393224 | tf_op jit(solution)/shard_map/ppermute | solution.py:20
  105.1 6.9 %collective-permute-start.4 = (bf16[16,4096]{1,0:T(8,128)(2,1)S(1)}, bf16[16,4096]{1,0:T(8,128)(2,1)S(1)}, u32[]{:S(2)}, u32[]{:S(2)}) collective-permute-start(bf16[16,4096]{1,0:T(8,128)(2,1)S(1)} %fusion.24.fresh0_ref), channel_id=1, source_target_pairs={{0,64},{64,0},{128,192},{192,128},{256,320},{320,256},{384,448},{4... | collective-permute-start | bytes 393224 | tf_op jit(solution)/shard_map/ppermute | solution.py:20
  109.2 2.7 %copy-start.10 = (bf16[16,4096]{1,0:T(8,128)(2,1)}, bf16[16,4096]{1,0:T(8,128)(2,1)S(1)}, u32[]{:S(2)}) copy-start(bf16[16,4096]{1,0:T(8,128)(2,1)S(1)} %collective-permute-done.6.fresh3_ref) | copy-start | bytes 393220
  109.8 2.2 %copy-start.11 = (bf16[16,4096]{1,0:T(8,128)(2,1)}, bf16[16,4096]{1,0:T(8,128)(2,1)S(1)}, u32[]{:S(2)}) copy-start(bf16[16,4096]{1,0:T(8,128)(2,1)S(1)} %collective-permute-done.5.fresh2_ref) | copy-start | bytes 393220
  112.0 0.6 copy-start.12
  115.3 36.8 %all-to-all-start.2 = ((bf16[8,80,512]{2,1,0:T(8,128)(2,1)}), bf16[8,80,512]{2,1,0:T(8,128)(2,1)S(1)}, u32[]{:S(2)}, u32[]{:S(2)}) async-start(bf16[8,80,512]{2,1,0:T(8,128)(2,1)} %get-tuple-element.17), calls=%async_computation.2 | async-start | bytes 1310720 | tf_op jit(solution)/shard_map/all_to_all | solution.py:204
  123.9 4.2 %copy-start.3 = (bf16[2,16,4096]{2,1,0:T(8,128)(2,1)S(1)}, bf16[2,16,4096]{2,1,0:T(8,128)(2,1)}, u32[]{:S(2)}) copy-start(bf16[2,16,4096]{2,1,0:T(8,128)(2,1)} %unpack.1) | copy-start | bytes 786436
  127.4 3.8 %copy-start.2 = (f32[1,1,64,4096]{3,2,1,0:T(8,128)S(1)}, f32[1,1,64,4096]{3,2,1,0:T(8,128)}, u32[]{:S(2)}) copy-start(f32[1,1,64,4096]{3,2,1,0:T(8,128)} %param.12) | copy-start | bytes 3145732
  131.4 6.1 %copy-start.1 = (f32[1,1,64,4096]{3,2,1,0:T(8,128)S(1)}, f32[1,1,64,4096]{3,2,1,0:T(8,128)}, u32[]{:S(2)}) copy-start(f32[1,1,64,4096]{3,2,1,0:T(8,128)} %param.11) | copy-start | bytes 3145732
  152.1 4.5 %copy-start.4 = (f32[2,16,4096]{2,1,0:T(8,128)S(1)}, f32[2,16,4096]{2,1,0:T(8,128)}, u32[]{:S(2)}) copy-start(f32[2,16,4096]{2,1,0:T(8,128)} %convert_element_type.142) | copy-start | bytes 1572868
  152.1 10.0 %copy-start.13 = (bf16[2,4096]{1,0:T(2,128)(2,1)S(1)}, bf16[2,4096]{1,0:T(2,128)(2,1)}, u32[]{:S(2)}) copy-start(bf16[2,4096]{1,0:T(2,128)(2,1)} %convert_element_type.146) | copy-start | bytes 49156
  154.7 5.5 %collective-permute-start.10 = (f32[4,128]{1,0:T(4,128)S(1)}, f32[4,128]{1,0:T(4,128)S(1)}, u32[]{:S(2)}, u32[]{:S(2)}) collective-permute-start(f32[4,128]{1,0:T(4,128)S(1)} %bitcast.150), channel_id=1, source_target_pairs={{0,1},{1,0},{2,3},{3,2},{4,5},{5,4},{6,7},{7,6},{8,9},{9,8},{10,11... | collective-permute-start | bytes 6152 | tf_op jit(solution)/shard_map/ppermute | solution.py:20
  156.6 19.7 %copy-start.6 = (bf16[512,512]{0,1:T(8,128)(2,1)S(1)}, bf16[512,512]{0,1:T(8,128)(2,1)}, u32[]{:S(2)}) copy-start(bf16[512,512]{0,1:T(8,128)(2,1)} %copy-done.5) | copy-start | bytes 1572868
  160.2 12.1 %collective-permute-start.11 = (f32[4,128]{1,0:T(4,128)S(1)}, f32[4,128]{1,0:T(4,128)S(1)}, u32[]{:S(2)}, u32[]{:S(2)}) collective-permute-start(f32[4,128]{1,0:T(4,128)S(1)} %bitcast_add_fusion.2), channel_id=1, source_target_pairs={{0,2},{1,3},{2,0},{3,1},{4,6},{5,7},{6,4},{7,5},{8,10},{9,11},{10,... | collective-permute-start | bytes 6152 | tf_op jit(solution)/shard_map/ppermute | solution.py:20
  162.1 25.3 %collective-permute-start.15 = (bf16[34,4096]{1,0:T(8,128)(2,1)S(1)}, bf16[34,4096]{1,0:T(8,128)(2,1)}, u32[]{:S(2)}, u32[]{:S(2)}) collective-permute-start(bf16[34,4096]{1,0:T(8,128)(2,1)S(1)} %get-tuple-element.57), channel_id=1, source_target_pairs={{0,128},{64,192},{128,0},{192,64},{256,384},{320,448},{384,256},{4... | collective-permute-start | bytes 835592 | tf_op jit(solution)/shard_map/ppermute | solution.py:20
  166.6 20.8 %collective-permute-start.14 = (bf16[34,4096]{1,0:T(8,128)(2,1)S(1)}, bf16[34,4096]{1,0:T(8,128)(2,1)}, u32[]{:S(2)}, u32[]{:S(2)}) collective-permute-start(bf16[34,4096]{1,0:T(8,128)(2,1)S(1)} %get-tuple-element.57), channel_id=1, source_target_pairs={{0,64},{64,0},{128,192},{192,128},{256,320},{320,256},{384,448},{4... | collective-permute-start | bytes 835592 | tf_op jit(solution)/shard_map/ppermute | solution.py:20
  169.1 18.4 %collective-permute-start.16 = (bf16[34,4096]{1,0:T(8,128)(2,1)S(1)}, bf16[34,4096]{1,0:T(8,128)(2,1)}, u32[]{:S(2)}, u32[]{:S(2)}) collective-permute-start(bf16[34,4096]{1,0:T(8,128)(2,1)S(1)} %get-tuple-element.57), channel_id=1, source_target_pairs={{0,192},{64,128},{128,64},{192,0},{256,448},{320,384},{384,320},{4... | collective-permute-start | bytes 835592 | tf_op jit(solution)/shard_map/ppermute | solution.py:20
  172.2 12.7 %collective-permute-start.12 = (f32[4,128]{1,0:T(4,128)S(1)}, f32[4,128]{1,0:T(4,128)S(1)}, u32[]{:S(2)}, u32[]{:S(2)}) collective-permute-start(f32[4,128]{1,0:T(4,128)S(1)} %fusion.43), channel_id=1, source_target_pairs={{0,4},{1,5},{2,6},{3,7},{4,0},{5,1},{6,2},{7,3},{8,12},{9,13},{10,... | collective-permute-start | bytes 6152 | tf_op jit(solution)/shard_map/ppermute | solution.py:20
  177.6 31.2 %all-to-all-start.3 = ((bf16[8,64,512]{2,1,0:T(8,128)(2,1)}), bf16[8,64,512]{2,1,0:T(8,128)(2,1)S(1)}, u32[]{:S(2)}, u32[]{:S(2)}) async-start(bf16[8,64,512]{2,1,0:T(8,128)(2,1)} %bitcast.141), calls=%async_computation.3 | async-start | bytes 1048576 | tf_op jit(solution)/shard_map/all_to_all | solution.py:217
  187.4 7.0 %collective-permute-start.13 = (bf16[512,512]{0,1:T(8,128)(2,1)}, bf16[512,512]{0,1:T(8,128)(2,1)}, u32[]{:S(2)}, u32[]{:S(2)}) collective-permute-start(bf16[512,512]{0,1:T(8,128)(2,1)} %fusion.6), channel_id=1, source_target_pairs={{8,0},{16,8},{24,16},{32,24},{40,32},{48,40},{56,48},{0,56},{9,1},... | collective-permute-start | bytes 1572872 | tf_op jit(solution)/shard_map/ppermute | solution.py:16
  191.5 1.7 copy-start.8

commit v12 on v11

--- a/solution.py
+++ b/solution.py
@@ -30,13 +30,6 @@
     return high, (value - high.astype(WIDE)).astype(SHORT)
 
 
-def in_order(held, mine, bits):
-    for bit in bits:
-        split = held.reshape((held.shape[0] // (2 * bit), 2, bit) + held.shape[1:])
-        held = jnp.where((mine & bit) != 0, split[:, ::-1], split).reshape(held.shape)
-    return held
-
-
 def doubled(held, mine, axis):
     bit = 4 >> axis
     came = swap(held, "tensor", bit)
@@ -45,12 +38,8 @@
 
 
 def gather_x(block):
-    held = jnp.stack([block] + [swap(block, "replica", bit) for bit in (1, 2, 3)])
-    return in_order(held, lax.axis_index("replica") & 3, (2, 1))
-
-
-def broadcast_x(block):
-    return exchange_x(jnp.broadcast_to(block[None], (PLANE,) + block.shape))
+    groups = [[0, 1, 2, 3], [4, 5, 6, 7]]
+    return lax.all_gather(block, "replica", axis=0, tiled=True, axis_index_groups=groups)
 
 
 def tied(value, *after):
@@ -225,10 +214,9 @@
     fresh = unpack(resend_spans, fresh[1:]).astype(WIDE)
     fresh_update = adam(fresh[0], fresh[1], mean_rows.astype(WIDE)).astype(SHORT)
     fresh_sums = checksum(fresh.reshape(2 * part, width)).astype(SHORT).reshape(2, width)
-    shared = gather_x(jnp.concatenate([mean_rows, fresh_update, fresh_sums], axis=0))
-    mean_grad = shared[:, :part].reshape(rows, width).astype(WIDE)
-    fresh_update = shared[:, part : 2 * part].reshape(rows, width).astype(WIDE)
-    fresh_sums = shared[:, 2 * part :].reshape(PLANE, 2, part, -1).transpose(1, 0, 2, 3).reshape(2, rows, -1).astype(WIDE)
+    mean_grad = gather_x(mean_rows).astype(WIDE)
+    fresh_update = gather_x(fresh_update).astype(WIDE)
+    fresh_sums = gather_x(fresh_sums).reshape(PLANE, 2, part, -1).transpose(1, 0, 2, 3).reshape(2, rows, -1).astype(WIDE)
     update = jnp.where(is_failed, fresh_update, adam(own_first, own_second, mean_grad))
     own_sums = jnp.stack([checksum(own_first), checksum(own_second)])
     checksums = jnp.where(is_failed, fresh_sums, own_sums)

time: 211 us -> 235 us (1.11)
  the two profiles are of different devices: /device:TPU:8 before, /device:TPU:1 now
where the time goes in v12:
time: 235 us; the launch traced here: 234 us
  starting transfers between devices  121 us (51%)
  waiting for transfers between devices  35.3 us (15%)
  blocking collectives  30.5 us (13%)
  matrix products  16.3 us (7%)
  local copies, waits for them, and re-layouts  12.5 us (5%)
  Pallas kernels  8.25 us (4%)
  other arithmetic  7.97 us (3%)
    ppermute x11, starting transfers between devices, swap(): lax.ppermute(block, axis, [(i, i ^ bit) for i in range(lax.axis_size(axis...  72.8 us
    all_gather x3, blocking collectives, gather_x(): lax.all_gather(block, 'replica', axis=0, tiled=True, axis_index_groups=gr...  30.5 us
    ppermute x11, waiting for transfers between devices, swap(): lax.ppermute(block, axis, [(i, i ^ bit) for i in range(lax.axis_size(axis...  26.2 us
    all_to_all x1, starting transfers between devices, shards(): got = lax.all_to_all(sent, 'tensor', 0, 0, tiled=True)  16.8 us
    ppermute x3, starting transfers between devices, from_behind(): lax.ppermute(block, axis, [((i - distance) % n, i) for i in range(n)])  13.1 us
    dot_general x4, matrix products, checksum(): jnp.einsum('jnc,cp->jnp', shaped, probe_matrix, precision=lax.Precision.H...  13 us
    all_to_all x1, starting transfers between devices, shards(): lax.all_to_all(keys.reshape(8, rows, tokens), 'tensor', 0, 0, tiled=True)  9.64 us
    all_to_all x2, starting transfers between devices, exchange_x(): lax.all_to_all(block, 'replica', 0, 0, axis_index_groups=groups, tiled=True)  8.76 us
  transfers between devices with their start and end apart: 18, of which 8 were waited for; matrix products, arithmetic and copies ran while one was open for 13% of the time, Pallas kernels for 2%

profile of v12, /device:TPU:1, one launch (start us, length us, event | category | flops | bytes accessed | tf_op | source)
XLA Modules:
  0.0 233.7 jit_solution(2916563021344765102)
XLA Ops:
  0.6 1.3 copy.53
  2.1 2.7 %collective-permute-start = (f32[4,128]{1,0:T(4,128)S(1)}, f32[4,128]{1,0:T(4,128)S(1)}, u32[]{:S(2)}, u32[]{:S(2)}) collective-permute-start(f32[4,128]{1,0:T(4,128)S(1)} %bitcast.126), channel_id=1, source_target_pairs={{56,0},{0,8},{8,16},{16,24},{24,32},{32,40},{40,48},{48,56},{57,1}... | collective-permute-start | bytes 6152 | tf_op jit(solution)/shard_map/ppermute | solution.py:16
  4.8 3.6 %serve.1 = bf16[4,3,16,4096]{3,2,1,0:T(8,128)(2,1)} custom-call(s32[8,8]{1,0:T(8,128)} %failed_ref.3, s32[8,8]{1,0:T(8,128)} %spans_ref.5, bf16[64,4096]{1,0:T(8,128)(2,1)} %bitcast.105, f32[64,4096]{1,0:T(8,128)} %bitcast.91, f32[64,4096]{1,0:T(8,128)} %bitcast.94), custom_call_target="tpu_custom_call" | custom-call | tf_op jit(solution)/shard_map/serve/pallas_call | solution.py:80
  8.4 4.1 %all-to-all-start = ((bf16[4,3,16,4096]{3,2,1,0:T(8,128)(2,1)}), bf16[4,3,16,4096]{3,2,1,0:T(8,128)(2,1)S(1)}, u32[]{:S(2)}, u32[]{:S(2)}) async-start(bf16[4,3,16,4096]{3,2,1,0:T(8,128)(2,1)} %serve.1), calls=%async_computation | async-start | bytes 3145728 | tf_op jit(solution)/shard_map/all_to_all | solution.py:25
  12.8 8.8 %collective-permute-start.1 = (bf16[72,512]{1,0:T(8,128)(2,1)S(1)}, bf16[72,512]{1,0:T(8,128)(2,1)S(1)}, u32[]{:S(2)}, u32[]{:S(2)}) collective-permute-start(bf16[72,512]{1,0:T(8,128)(2,1)S(1)} %maximum_maximum_fusion), channel_id=1, source_target_pairs={{0,4},{1,5},{2,6},{3,7},{4,0},{5,1},{6,2},{7,3},{8,12},{9,13},{10,... | collective-permute-start | bytes 221192 | tf_op jit(solution)/shard_map/ppermute | solution.py:20
  21.6 6.5 %collective-permute-done.1 = bf16[72,512]{1,0:T(8,128)(2,1)S(1)} collective-permute-done((bf16[72,512]{1,0:T(8,128)(2,1)S(1)}, bf16[72,512]{1,0:T(8,128)(2,1)S(1)}, u32[]{:S(2)}, u32[]{:S(2)}) %collective-permute-start.1) | collective-permute-done | bytes 73760 | tf_op jit(solution)/shard_map/ppermute | solution.py:20
  28.2 2.4 %collective-permute-start.2 = (bf16[2,72,512]{2,1,0:T(8,128)(2,1)S(1)}, bf16[2,72,512]{2,1,0:T(8,128)(2,1)S(1)}, u32[]{:S(2)}, u32[]{:S(2)}) collective-permute-start(bf16[2,72,512]{2,1,0:T(8,128)(2,1)S(1)} %pad_maximum_fusion.3), channel_id=1, source_target_pairs={{0,2},{1,3},{2,0},{3,1},{4,6},{5,7},{6,4},{7,5},{8,10},{9,11},{10,... | collective-permute-start | bytes 442376 | tf_op jit(solution)/shard_map/ppermute | solution.py:20
  30.6 8.7 %collective-permute-done.2 = bf16[2,72,512]{2,1,0:T(8,128)(2,1)S(1)} collective-permute-done((bf16[2,72,512]{2,1,0:T(8,128)(2,1)S(1)}, bf16[2,72,512]{2,1,0:T(8,128)(2,1)S(1)}, u32[]{:S(2)}, u32[]{:S(2)}) %collective-permute-start.2) | collective-permute-done | bytes 147488 | tf_op jit(solution)/shard_map/ppermute | solution.py:20
  39.6 1.9 collective-permute-start.7
  41.6 1.2 collective-permute-start.8
  42.7 1.3 dynamic_slice.3
  44.7 14.4 %collective-permute-start.3 = (bf16[3,16,3072]{2,1,0:T(8,128)(2,1)S(1)}, bf16[3,16,3072]{2,1,0:T(8,128)(2,1)S(1)}, u32[]{:S(2)}, u32[]{:S(2)}) collective-permute-start(bf16[3,16,3072]{2,1,0:T(8,128)(2,1)S(1)} %slice.37), channel_id=1, source_target_pairs={{0,256},{64,320},{128,384},{192,448},{256,0},{320,64},{384,128},{4... | collective-permute-start | bytes 884744 | tf_op jit(solution)/shard_map/ppermute | solution.py:20
  59.9 0.8 copy.73
  60.7 4.6 %all-to-all-start.1 = ((bf16[4,8,16,512]{3,2,1,0:T(8,128)(2,1)}), bf16[4,8,16,512]{3,2,1,0:T(8,128)(2,1)S(1)}, u32[]{:S(2)}, u32[]{:S(2)}) async-start(bf16[4,8,16,512]{3,2,1,0:T(8,128)(2,1)} %bitcast.90), calls=%async_computation.1 | async-start | bytes 1048576 | tf_op jit(solution)/shard_map/all_to_all | solution.py:25
  65.3 7.0 %collective-permute-done.3 = bf16[3,16,3072]{2,1,0:T(8,128)(2,1)S(1)} collective-permute-done((bf16[3,16,3072]{2,1,0:T(8,128)(2,1)S(1)}, bf16[3,16,3072]{2,1,0:T(8,128)(2,1)S(1)}, u32[]{:S(2)}, u32[]{:S(2)}) %collective-permute-start.3) | collective-permute-done | bytes 294944 | tf_op jit(solution)/shard_map/ppermute | solution.py:20
  72.4 2.8 %all-to-all-done.1 = bf16[4,8,16,512]{3,2,1,0:T(8,128)(2,1)S(1)} async-done(((bf16[4,8,16,512]{3,2,1,0:T(8,128)(2,1)}), bf16[4,8,16,512]{3,2,1,0:T(8,128)(2,1)S(1)}, u32[]{:S(2)}, u32[]{:S(2)}) %all-to-all-start.1) | async-done | bytes 524320 | tf_op jit(solution)/shard_map/all_to_all | solution.py:25
  75.2 9.8 %collective-permute-start.9 = (bf16[8,16,512]{2,1,0:T(8,128)(2,1)S(1)}, bf16[8,16,512]{2,1,0:T(8,128)(2,1)S(1)}, u32[]{:S(2)}, u32[]{:S(2)}) collective-permute-start(bf16[8,16,512]{2,1,0:T(8,128)(2,1)S(1)} %reduce_sum.66), channel_id=1, source_target_pairs={{0,256},{64,320},{128,384},{192,448},{256,0},{320,64},{384,128},{4... | collective-permute-start | bytes 393224 | tf_op jit(solution)/shard_map/ppermute | solution.py:20
  85.1 4.9 %collective-permute-start.6 = (bf16[16,4096]{1,0:T(8,128)(2,1)S(1)}, bf16[16,4096]{1,0:T(8,128)(2,1)S(1)}, u32[]{:S(2)}, u32[]{:S(2)}) collective-permute-start(bf16[16,4096]{1,0:T(8,128)(2,1)S(1)} %fusion.26.fresh0_ref), channel_id=1, source_target_pairs={{0,192},{64,128},{128,64},{192,0},{256,448},{320,384},{384,320},{4... | collective-permute-start | bytes 393224 | tf_op jit(solution)/shard_map/ppermute | solution.py:20
  90.0 2.5 %collective-permute-start.5 = (bf16[16,4096]{1,0:T(8,128)(2,1)S(1)}, bf16[16,4096]{1,0:T(8,128)(2,1)S(1)}, u32[]{:S(2)}, u32[]{:S(2)}) collective-permute-start(bf16[16,4096]{1,0:T(8,128)(2,1)S(1)} %fusion.26.fresh0_ref), channel_id=1, source_target_pairs={{0,128},{64,192},{128,0},{192,64},{256,384},{320,448},{384,256},{4... | collective-permute-start | bytes 393224 | tf_op jit(solution)/shard_map/ppermute | solution.py:20
  92.5 1.9 collective-permute-start.4
  95.2 2.1 collective-permute-done.5.fresh2_ref
  97.2 1.0 collective-permute-done.4.fresh1_ref
  98.9 2.7 %assemble.1 = (bf16[8,80,512]{2,1,0:T(8,128)(2,1)}, bf16[64,4096]{1,0:T(8,128)(2,1)}) custom-call(s32[8,8]{1,0:T(8,128)} %failed_ref.3, s32[8,8]{1,0:T(8,128)} %spans_ref.5, bf16[64,4096]{1,0:T(8,128)(2,1)} %bitcast.106, bf16[16,4096]{1,0:T(8,128)(2,1)} %copy-done.9, bf16[16,4096]{1,0:T(8,128)(2,1)} %copy-done.13, bf16[16,4096]{1,0:T(8,128)(2,1)} %copy-done.12, ...), custom_call_target="tpu_custom_call" | custom-call | tf_op jit(solution)/shard_map/assemble/pallas_call | solution.py:128
  101.6 16.8 %all-to-all-start.2 = ((bf16[8,80,512]{2,1,0:T(8,128)(2,1)}), bf16[8,80,512]{2,1,0:T(8,128)(2,1)S(1)}, u32[]{:S(2)}, u32[]{:S(2)}) async-start(bf16[8,80,512]{2,1,0:T(8,128)(2,1)} %get-tuple-element.17), calls=%async_computation.2 | async-start | bytes 1310720 | tf_op jit(solution)/shard_map/all_to_all | solution.py:193
  119.1 1.9 unpack.1
  121.2 2.1 fusion.29
  125.1 1.1 convolution_convert_fusion.2
  126.6 9.5 %all-gather = bf16[4,2,4096]{2,1,0:T(2,128)(2,1)S(1)} all-gather(bf16[1,2,4096]{2,1,0:T(2,128)(2,1)S(1)} %reshape.167), channel_id=1, replica_groups={{0,64,128,192},{256,320,384,448},{1,65,129,193},{257,321,385,449},{2,66..., dimensions={0}, use_global_device_ids=true | all-gather | bytes 81920 | tf_op jit(solution)/shard_map/all_gather | solution.py:42
  137.1 4.9 %fusion.31 = f32[64,32,8]{1,2,0:T(8,128)} fusion(f32[64,32,128]{2,1,0:T(8,128)S(1)} %bitcast.97, f32[128,8]{0,1:T(8,128)S(1)} %copy-done), kind=kOutput, calls=%fused_computation.63 | convolution fusion | flops 25165824 | bytes 1118208 | tf_op jit(solution)/shard_map/jnc,cp->jnp/dot_general | solution.py:211
  142.0 1.1 copy.60
  143.3 4.9 %fusion.33 = f32[64,32,8]{1,2,0:T(8,128)} fusion(f32[64,32,128]{2,1,0:T(8,128)S(1)} %bitcast.98, f32[128,8]{0,1:T(8,128)S(1)} %copy-done), kind=kOutput, calls=%fused_computation.65 | convolution fusion | flops 25165824 | bytes 1118208 | tf_op jit(solution)/shard_map/jnc,cp->jnp/dot_general | solution.py:211
  148.2 1.1 copy.59
  150.0 1.5 maximum_select_fusion
  151.6 1.0 copy-done.6
  152.6 1.2 convolution_convert_fusion
  153.8 9.6 %all-to-all-start.3 = ((bf16[8,64,512]{2,1,0:T(8,128)(2,1)}), bf16[8,64,512]{2,1,0:T(8,128)(2,1)}, u32[]{:S(2)}, u32[]{:S(2)}) async-start(bf16[8,64,512]{2,1,0:T(8,128)(2,1)} %bitcast.113), calls=%async_computation.3 | async-start | bytes 1048576 | tf_op jit(solution)/shard_map/all_to_all | solution.py:206
  163.5 1.6 fusion.13
  165.1 3.5 %collective-permute-start.10 = (f32[4,128]{1,0:T(4,128)S(1)}, f32[4,128]{1,0:T(4,128)S(1)}, u32[]{:S(2)}, u32[]{:S(2)}) collective-permute-start(f32[4,128]{1,0:T(4,128)S(1)} %bitcast.123), channel_id=1, source_target_pairs={{0,1},{1,0},{2,3},{3,2},{4,5},{5,4},{6,7},{7,6},{8,9},{9,8},{10,11... | collective-permute-start | bytes 6152 | tf_op jit(solution)/shard_map/ppermute | solution.py:20
  168.8 1.0 collective-permute-done.10
  169.8 18.7 %collective-permute-start.11 = (f32[4,128]{1,0:T(4,128)S(1)}, f32[4,128]{1,0:T(4,128)S(1)}, u32[]{:S(2)}, u32[]{:S(2)}) collective-permute-start(f32[4,128]{1,0:T(4,128)S(1)} %bitcast_add_fusion), channel_id=1, source_target_pairs={{0,2},{1,3},{2,0},{3,1},{4,6},{5,7},{6,4},{7,5},{8,10},{9,11},{10,... | collective-permute-start | bytes 6152 | tf_op jit(solution)/shard_map/ppermute | solution.py:20
  188.4 11.1 %all_gather.10 = bf16[64,4096]{1,0:T(8,128)(2,1)S(1)} all-gather(bf16[16,4096]{1,0:T(8,128)(2,1)S(1)} %bitcast.108), channel_id=1, replica_groups={{0,64,128,192},{256,320,384,448},{1,65,129,193},{257,321,385,449},{2,66..., dimensions={0}, use_global_device_ids=true | all-gather | bytes 655360 | tf_op jit(solution)/shard_map/all_gather | solution.py:42
  199.6 4.0 %collective-permute-start.12 = (f32[4,128]{1,0:T(4,128)S(1)}, f32[4,128]{1,0:T(4,128)S(1)}, u32[]{:S(2)}, u32[]{:S(2)}) collective-permute-start(f32[4,128]{1,0:T(4,128)S(1)} %fusion.44), channel_id=1, source_target_pairs={{0,4},{1,5},{2,6},{3,7},{4,0},{5,1},{6,2},{7,3},{8,12},{9,13},{10,... | collective-permute-start | bytes 6152 | tf_op jit(solution)/shard_map/ppermute | solution.py:20
  203.6 9.9 %all_gather.9 = bf16[64,4096]{1,0:T(8,128)(2,1)S(1)} all-gather(bf16[16,4096]{1,0:T(8,128)(2,1)S(1)} %fusion.18), channel_id=1, replica_groups={{0,64,128,192},{256,320,384,448},{1,65,129,193},{257,321,385,449},{2,66..., dimensions={0}, use_global_device_ids=true | all-gather | bytes 655360 | tf_op jit(solution)/shard_map/all_gather | solution.py:42
  213.7 9.3 %collective-permute-start.13 = (bf16[512,512]{0,1:T(8,128)(2,1)S(1)}, bf16[512,512]{0,1:T(8,128)(2,1)S(1)}, u32[]{:S(2)}, u32[]{:S(2)}) collective-permute-start(bf16[512,512]{0,1:T(8,128)(2,1)S(1)} %fusion.12), channel_id=1, source_target_pairs={{8,0},{16,8},{24,16},{32,24},{40,32},{48,40},{56,48},{0,56},{9,1},... | collective-permute-start | bytes 1572872 | tf_op jit(solution)/shard_map/ppermute | solution.py:16
  223.0 1.7 fusion.3
  224.6 6.3 %collective-permute-done.13 = bf16[512,512]{0,1:T(8,128)(2,1)S(1)} collective-permute-done((bf16[512,512]{0,1:T(8,128)(2,1)S(1)}, bf16[512,512]{0,1:T(8,128)(2,1)S(1)}, u32[]{:S(2)}, u32[]{:S(2)}) %collective-permute-start.13) | collective-permute-done | bytes 524320 | tf_op jit(solution)/shard_map/ppermute | solution.py:16
  231.0 1.0 copy.64
  232.0 1.8 reduce_sum.67
  (84 shorter events, 8.6 us)
Async XLA Ops:
  0.6 120.5 %copy-start = (f32[128,8]{0,1:T(8,128)S(1)}, f32[128,8]{0,1:T(8,128)}, u32[]{:S(2)}) copy-start(f32[128,8]{0,1:T(8,128)} %param.13) | copy-start | bytes 12292
  2.1 10.6 %collective-permute-start = (f32[4,128]{1,0:T(4,128)S(1)}, f32[4,128]{1,0:T(4,128)S(1)}, u32[]{:S(2)}, u32[]{:S(2)}) collective-permute-start(f32[4,128]{1,0:T(4,128)S(1)} %bitcast.126), channel_id=1, source_target_pairs={{56,0},{0,8},{8,16},{16,24},{24,32},{32,40},{40,48},{48,56},{57,1}... | collective-permute-start | bytes 6152 | tf_op jit(solution)/shard_map/ppermute | solution.py:16
  8.4 4.3 %copy-start.10 = (bf16[1,1,512,64]{2,3,1,0:T(8,128)(2,1)S(1)}, bf16[1,1,512,64]{2,3,1,0:T(8,128)(2,1)}, u32[]{:S(2)}) copy-start(bf16[1,1,512,64]{2,3,1,0:T(8,128)(2,1)} %param.9) | copy-start | bytes 196612
  8.4 30.9 %all-to-all-start = ((bf16[4,3,16,4096]{3,2,1,0:T(8,128)(2,1)}), bf16[4,3,16,4096]{3,2,1,0:T(8,128)(2,1)S(1)}, u32[]{:S(2)}, u32[]{:S(2)}) async-start(bf16[4,3,16,4096]{3,2,1,0:T(8,128)(2,1)} %serve.1), calls=%async_computation | async-start | bytes 3145728 | tf_op jit(solution)/shard_map/all_to_all | solution.py:25
  12.8 15.3 %collective-permute-start.1 = (bf16[72,512]{1,0:T(8,128)(2,1)S(1)}, bf16[72,512]{1,0:T(8,128)(2,1)S(1)}, u32[]{:S(2)}, u32[]{:S(2)}) collective-permute-start(bf16[72,512]{1,0:T(8,128)(2,1)S(1)} %maximum_maximum_fusion), channel_id=1, source_target_pairs={{0,4},{1,5},{2,6},{3,7},{4,0},{5,1},{6,2},{7,3},{8,12},{9,13},{10,... | collective-permute-start | bytes 221192 | tf_op jit(solution)/shard_map/ppermute | solution.py:20
  28.2 11.1 %collective-permute-start.2 = (bf16[2,72,512]{2,1,0:T(8,128)(2,1)S(1)}, bf16[2,72,512]{2,1,0:T(8,128)(2,1)S(1)}, u32[]{:S(2)}, u32[]{:S(2)}) collective-permute-start(bf16[2,72,512]{2,1,0:T(8,128)(2,1)S(1)} %pad_maximum_fusion.3), channel_id=1, source_target_pairs={{0,2},{1,3},{2,0},{3,1},{4,6},{5,7},{6,4},{7,5},{8,10},{9,11},{10,... | collective-permute-start | bytes 442376 | tf_op jit(solution)/shard_map/ppermute | solution.py:20
  39.6 19.5 %collective-permute-start.7 = (bf16[2,2,72,512]{3,2,0,1:T(8,128)(2,1)S(1)}, bf16[2,2,72,512]{3,2,0,1:T(8,128)(2,1)S(1)}, u32[]{:S(2)}, u32[]{:S(2)}) collective-permute-start(bf16[2,2,72,512]{3,2,0,1:T(8,128)(2,1)S(1)} %pad_maximum_fusion.2), channel_id=1, source_target_pairs={{0,1},{1,0},{2,3},{3,2},{4,5},{5,4},{6,7},{7,6},{8,9},{9,8},{10,11... | collective-permute-start | bytes 884744 | tf_op jit(solution)/shard_map/ppermute | solution.py:20
  41.6 17.8 %collective-permute-start.8 = (bf16[512,512]{0,1:T(8,128)(2,1)S(1)}, bf16[512,512]{0,1:T(8,128)(2,1)S(1)}, u32[]{:S(2)}, u32[]{:S(2)}) collective-permute-start(bf16[512,512]{0,1:T(8,128)(2,1)S(1)} %bitcast.103), channel_id=1, source_target_pairs={{56,0},{0,8},{8,16},{16,24},{24,32},{32,40},{40,48},{48,56},{57,1}... | collective-permute-start | bytes 1572872 | tf_op jit(solution)/shard_map/ppermute | solution.py:16
  44.7 27.6 %collective-permute-start.3 = (bf16[3,16,3072]{2,1,0:T(8,128)(2,1)S(1)}, bf16[3,16,3072]{2,1,0:T(8,128)(2,1)S(1)}, u32[]{:S(2)}, u32[]{:S(2)}) collective-permute-start(bf16[3,16,3072]{2,1,0:T(8,128)(2,1)S(1)} %slice.37), channel_id=1, source_target_pairs={{0,256},{64,320},{128,384},{192,448},{256,0},{320,64},{384,128},{4... | collective-permute-start | bytes 884744 | tf_op jit(solution)/shard_map/ppermute | solution.py:20
  59.4 1.3 copy-start.5
  60.7 14.4 %all-to-all-start.1 = ((bf16[4,8,16,512]{3,2,1,0:T(8,128)(2,1)}), bf16[4,8,16,512]{3,2,1,0:T(8,128)(2,1)S(1)}, u32[]{:S(2)}, u32[]{:S(2)}) async-start(bf16[4,8,16,512]{3,2,1,0:T(8,128)(2,1)} %bitcast.90), calls=%async_computation.1 | async-start | bytes 1048576 | tf_op jit(solution)/shard_map/all_to_all | solution.py:25
  75.2 19.3 %collective-permute-start.9 = (bf16[8,16,512]{2,1,0:T(8,128)(2,1)S(1)}, bf16[8,16,512]{2,1,0:T(8,128)(2,1)S(1)}, u32[]{:S(2)}, u32[]{:S(2)}) collective-permute-start(bf16[8,16,512]{2,1,0:T(8,128)(2,1)S(1)} %reduce_sum.66), channel_id=1, source_target_pairs={{0,256},{64,320},{128,384},{192,448},{256,0},{320,64},{384,128},{4... | collective-permute-start | bytes 393224 | tf_op jit(solution)/shard_map/ppermute | solution.py:20
  85.1 13.2 %copy-start.9 = (bf16[16,4096]{1,0:T(8,128)(2,1)}, bf16[16,4096]{1,0:T(8,128)(2,1)S(1)}, u32[]{:S(2)}) copy-start(bf16[16,4096]{1,0:T(8,128)(2,1)S(1)} %fusion.26.fresh0_ref) | copy-start | bytes 393220
  85.1 10.1 %collective-permute-start.6 = (bf16[16,4096]{1,0:T(8,128)(2,1)S(1)}, bf16[16,4096]{1,0:T(8,128)(2,1)S(1)}, u32[]{:S(2)}, u32[]{:S(2)}) collective-permute-start(bf16[16,4096]{1,0:T(8,128)(2,1)S(1)} %fusion.26.fresh0_ref), channel_id=1, source_target_pairs={{0,192},{64,128},{128,64},{192,0},{256,448},{320,384},{384,320},{4... | collective-permute-start | bytes 393224 | tf_op jit(solution)/shard_map/ppermute | solution.py:20
  90.0 7.2 %collective-permute-start.5 = (bf16[16,4096]{1,0:T(8,128)(2,1)S(1)}, bf16[16,4096]{1,0:T(8,128)(2,1)S(1)}, u32[]{:S(2)}, u32[]{:S(2)}) collective-permute-start(bf16[16,4096]{1,0:T(8,128)(2,1)S(1)} %fusion.26.fresh0_ref), channel_id=1, source_target_pairs={{0,128},{64,192},{128,0},{192,64},{256,384},{320,448},{384,256},{4... | collective-permute-start | bytes 393224 | tf_op jit(solution)/shard_map/ppermute | solution.py:20
  92.5 5.7 %collective-permute-start.4 = (bf16[16,4096]{1,0:T(8,128)(2,1)S(1)}, bf16[16,4096]{1,0:T(8,128)(2,1)S(1)}, u32[]{:S(2)}, u32[]{:S(2)}) collective-permute-start(bf16[16,4096]{1,0:T(8,128)(2,1)S(1)} %fusion.26.fresh0_ref), channel_id=1, source_target_pairs={{0,64},{64,0},{128,192},{192,128},{256,320},{320,256},{384,448},{4... | collective-permute-start | bytes 393224 | tf_op jit(solution)/shard_map/ppermute | solution.py:20
  95.2 3.1 %copy-start.11 = (bf16[16,4096]{1,0:T(8,128)(2,1)}, bf16[16,4096]{1,0:T(8,128)(2,1)S(1)}, u32[]{:S(2)}) copy-start(bf16[16,4096]{1,0:T(8,128)(2,1)S(1)} %collective-permute-done.6.fresh3_ref) | copy-start | bytes 393220
  97.2 1.0 copy-start.12
  98.2 0.7 copy-start.13
  101.6 19.5 %copy-start.8 = (bf16[64,4096]{1,0:T(8,128)(2,1)S(1)}, bf16[64,4096]{1,0:T(8,128)(2,1)}, u32[]{:S(2)}) copy-start(bf16[64,4096]{1,0:T(8,128)(2,1)} %get-tuple-element.22) | copy-start | bytes 1572868
  101.6 49.9 %all-to-all-start.2 = ((bf16[8,80,512]{2,1,0:T(8,128)(2,1)}), bf16[8,80,512]{2,1,0:T(8,128)(2,1)S(1)}, u32[]{:S(2)}, u32[]{:S(2)}) async-start(bf16[8,80,512]{2,1,0:T(8,128)(2,1)} %get-tuple-element.17), calls=%async_computation.2 | async-start | bytes 1310720 | tf_op jit(solution)/shard_map/all_to_all | solution.py:193
  121.0 3.1 %copy-start.3 = (bf16[2,16,4096]{2,1,0:T(8,128)(2,1)S(1)}, bf16[2,16,4096]{2,1,0:T(8,128)(2,1)}, u32[]{:S(2)}) copy-start(bf16[2,16,4096]{2,1,0:T(8,128)(2,1)} %unpack.1) | copy-start | bytes 786436
  123.5 13.4 %copy-start.2 = (f32[1,1,64,4096]{3,2,1,0:T(8,128)S(1)}, f32[1,1,64,4096]{3,2,1,0:T(8,128)}, u32[]{:S(2)}) copy-start(f32[1,1,64,4096]{3,2,1,0:T(8,128)} %param.12) | copy-start | bytes 3145732
  136.9 6.2 %copy-start.1 = (f32[1,1,64,4096]{3,2,1,0:T(8,128)S(1)}, f32[1,1,64,4096]{3,2,1,0:T(8,128)}, u32[]{:S(2)}) copy-start(f32[1,1,64,4096]{3,2,1,0:T(8,128)} %param.11) | copy-start | bytes 3145732
  151.5 1.0 copy-start.6
  153.8 78.1 %all-to-all-start.3 = ((bf16[8,64,512]{2,1,0:T(8,128)(2,1)}), bf16[8,64,512]{2,1,0:T(8,128)(2,1)}, u32[]{:S(2)}, u32[]{:S(2)}) async-start(bf16[8,64,512]{2,1,0:T(8,128)(2,1)} %bitcast.113), calls=%async_computation.3 | async-start | bytes 1048576 | tf_op jit(solution)/shard_map/all_to_all | solution.py:206
  163.5 5.1 %copy-start.4 = (f32[2,16,4096]{2,1,0:T(8,128)S(1)}, f32[2,16,4096]{2,1,0:T(8,128)}, u32[]{:S(2)}) copy-start(f32[2,16,4096]{2,1,0:T(8,128)} %convert_element_type.138) | copy-start | bytes 1572868
  165.1 48.4 %copy-start.7 = (bf16[512,512]{0,1:T(8,128)(2,1)S(1)}, bf16[512,512]{0,1:T(8,128)(2,1)}, u32[]{:S(2)}) copy-start(bf16[512,512]{0,1:T(8,128)(2,1)} %copy-done.5) | copy-start | bytes 1572868
  165.1 4.7 %collective-permute-start.10 = (f32[4,128]{1,0:T(4,128)S(1)}, f32[4,128]{1,0:T(4,128)S(1)}, u32[]{:S(2)}, u32[]{:S(2)}) collective-permute-start(f32[4,128]{1,0:T(4,128)S(1)} %bitcast.123), channel_id=1, source_target_pairs={{0,1},{1,0},{2,3},{3,2},{4,5},{5,4},{6,7},{7,6},{8,9},{9,8},{10,11... | collective-permute-start | bytes 6152 | tf_op jit(solution)/shard_map/ppermute | solution.py:20
  169.8 29.8 %collective-permute-start.11 = (f32[4,128]{1,0:T(4,128)S(1)}, f32[4,128]{1,0:T(4,128)S(1)}, u32[]{:S(2)}, u32[]{:S(2)}) collective-permute-start(f32[4,128]{1,0:T(4,128)S(1)} %bitcast_add_fusion), channel_id=1, source_target_pairs={{0,2},{1,3},{2,0},{3,1},{4,6},{5,7},{6,4},{7,5},{8,10},{9,11},{10,... | collective-permute-start | bytes 6152 | tf_op jit(solution)/shard_map/ppermute | solution.py:20
  199.6 13.9 %collective-permute-start.12 = (f32[4,128]{1,0:T(4,128)S(1)}, f32[4,128]{1,0:T(4,128)S(1)}, u32[]{:S(2)}, u32[]{:S(2)}) collective-permute-start(f32[4,128]{1,0:T(4,128)S(1)} %fusion.44), channel_id=1, source_target_pairs={{0,4},{1,5},{2,6},{3,7},{4,0},{5,1},{6,2},{7,3},{8,12},{9,13},{10,... | collective-permute-start | bytes 6152 | tf_op jit(solution)/shard_map/ppermute | solution.py:20
  213.7 17.2 %collective-permute-start.13 = (bf16[512,512]{0,1:T(8,128)(2,1)S(1)}, bf16[512,512]{0,1:T(8,128)(2,1)S(1)}, u32[]{:S(2)}, u32[]{:S(2)}) collective-permute-start(bf16[512,512]{0,1:T(8,128)(2,1)S(1)} %fusion.12), channel_id=1, source_target_pairs={{8,0},{16,8},{24,16},{32,24},{40,32},{48,40},{56,48},{0,56},{9,1},... | collective-permute-start | bytes 1572872 | tf_op jit(solution)/shard_map/ppermute | solution.py:16

commit v13 on v12

--- a/solution.py
+++ b/solution.py
@@ -119,12 +119,15 @@
             restored_ref[at, n * SPAN : (n + 1) * SPAN] = block
             sent_ref[n // apart, at, (n % apart) * SPAN : (n % apart + 1) * SPAN] = block
     for t in range(groups):
-        sent_ref[t, rows:, :] = grads_ref[t]
+        total = grads_ref[0, t].astype(WIDE)
+        for x in range(1, PLANE):
+            total = total + grads_ref[x, t].astype(WIDE)
+        sent_ref[t, rows:, :] = total.astype(SHORT)
 
 
 def assemble(failed, spans, own, fresh, grads):
     rows, width = own.shape
-    groups, part, cols = grads.shape
+    _, groups, part, cols = grads.shape
     return pl.pallas_call(
         assemble_kernel,
         out_shape=(
@@ -185,21 +188,21 @@
     normed = (x * inverse_rms[:, None]).astype(SHORT)
     grad = lax.dot_general(kg_all, normed, (((1,), (0,)), ((), ())), preferred_element_type=WIDE).astype(SHORT)
     grad = grad.reshape(8, PLANE, part, cols).transpose(1, 0, 2, 3)
-    grad = jnp.sum(exchange_x(grad).astype(WIDE), axis=0).astype(SHORT)
-    grad = ((grad.astype(WIDE) + swap(grad, "replica", PLANE).astype(WIDE)) / copies).astype(SHORT)
+    grad = exchange_x(grad)
 
     sent, restored_weight = assemble(failed_replica, resend_spans, own_weight, fresh_weight, grad)
     own_first, own_second, restored_weight, fresh = lax.optimization_barrier((own_first, own_second, restored_weight, fresh))
     got = lax.all_to_all(sent, "tensor", 0, 0, tiled=True)
     weight_cols = got[:, :rows].reshape(8 * rows, cols)
-    mean_rows = got[:, rows:].transpose(1, 0, 2).reshape(part, width)
+    grad_rows = got[:, rows:].transpose(1, 0, 2).reshape(part, width)
+    mean_rows = (grad_rows.astype(WIDE) + swap(grad_rows, "replica", PLANE).astype(WIDE)) / copies
 
     keys = lax.dot_general(weight_cols, normed, (((1,), (1,)), ((), ())), preferred_element_type=WIDE).astype(SHORT)
     feature = lax.dot_general(kg_all, weight_cols, (((0,), (0,)), ((), ())), preferred_element_type=WIDE)
-    product = jnp.sum(feature * x, axis=1).reshape(-1, 128)
-    for bit in (1, 2, 4):
-        product = product + swap(product, "tensor", bit)
-    product = product.reshape(tokens, 1)
+    product = jnp.sum(feature * x, axis=1).reshape(1, -1, 128)
+    product = lax.all_to_all(jnp.broadcast_to(product, (8,) + product.shape[1:]), "tensor", 0, 0, tiled=True)
+    product = jnp.sum(product, axis=0).reshape(tokens, 1)
+    product, keys = lax.optimization_barrier((product, keys))
     scale = inverse_rms[:, None]
     input_grad = scale * feature - scale * scale * scale * x * product / width
     outgoing = from_behind(input_grad.astype(SHORT), "section", -1)
@@ -212,9 +215,9 @@
         return mixed.reshape(-1, nchunk * probe_matrix.shape[1])
 
     fresh = unpack(resend_spans, fresh[1:]).astype(WIDE)
-    fresh_update = adam(fresh[0], fresh[1], mean_rows.astype(WIDE)).astype(SHORT)
+    fresh_update = adam(fresh[0], fresh[1], mean_rows).astype(SHORT)
     fresh_sums = checksum(fresh.reshape(2 * part, width)).astype(SHORT).reshape(2, width)
-    mean_grad = gather_x(mean_rows).astype(WIDE)
+    mean_grad = gather_x(mean_rows.astype(SHORT)).astype(WIDE)
     fresh_update = gather_x(fresh_update).astype(WIDE)
     fresh_sums = gather_x(fresh_sums).reshape(PLANE, 2, part, -1).transpose(1, 0, 2, 3).reshape(2, rows, -1).astype(WIDE)
     update = jnp.where(is_failed, fresh_update, adam(own_first, own_second, mean_grad))

time: 235 us -> 217 us (0.923)
  the two profiles are of different devices: /device:TPU:1 before, /device:TPU:32 now
where the time goes in v13:
time: 217 us; the launch traced here: 216 us
  starting transfers between devices  83.4 us (38%)
  waiting for transfers between devices  42.1 us (19%)
  blocking collectives  38.3 us (18%)
  matrix products  18.3 us (8%)
  local copies, waits for them, and re-layouts  14.8 us (7%)
  other arithmetic  8.47 us (4%)
  Pallas kernels  8.39 us (4%)
    ppermute x8, starting transfers between devices, swap(): lax.ppermute(block, axis, [(i, i ^ bit) for i in range(lax.axis_size(axis...  53.5 us
    all_gather x3, blocking collectives, gather_x(): lax.all_gather(block, 'replica', axis=0, tiled=True, axis_index_groups=gr...  38.3 us
    ppermute x8, waiting for transfers between devices, swap(): lax.ppermute(block, axis, [(i, i ^ bit) for i in range(lax.axis_size(axis...  35.5 us
    dot_general x4, matrix products, checksum(): jnp.einsum('jnc,cp->jnp', shaped, probe_matrix, precision=lax.Precision.H...  13 us
    all_to_all x1, starting transfers between devices, shards(): lax.all_to_all(jnp.broadcast_to(product, (8,) + product.shape[1:]), 'tens...  9.86 us
    all_to_all x2, starting transfers between devices, exchange_x(): lax.all_to_all(block, 'replica', 0, 0, axis_index_groups=groups, tiled=True)  9.31 us
    unnamed x37, local copies, waits for them, and re-layouts  7.1 us
    all_to_all x1, waiting for transfers between devices, shards(): lax.all_to_all(jnp.broadcast_to(product, (8,) + product.shape[1:]), 'tens...  6.65 us
  transfers between devices with their start and end apart: 16, of which 6 were waited for; matrix products, arithmetic and copies ran while one was open for 17% of the time, Pallas kernels for 3%

profile of v13, /device:TPU:32, one launch (start us, length us, event | category | flops | bytes accessed | tf_op | source)
XLA Modules:
  0.0 215.6 jit_solution(14781829598736748138)
XLA Ops:
  0.6 1.3 copy.82
  2.1 3.6 %serve.1 = bf16[4,3,16,4096]{3,2,1,0:T(8,128)(2,1)} custom-call(s32[8,8]{1,0:T(8,128)} %failed_ref.3, s32[8,8]{1,0:T(8,128)} %spans_ref.5, bf16[64,4096]{1,0:T(8,128)(2,1)} %bitcast.114, f32[64,4096]{1,0:T(8,128)} %bitcast.100, f32[64,4096]{1,0:T(8,128)} %bitcast.103), custom_call_target="tpu_custom_call" | custom-call | tf_op jit(solution)/shard_map/serve/pallas_call | solution.py:80
  5.7 4.4 %all-to-all-start = ((bf16[4,3,16,4096]{3,2,1,0:T(8,128)(2,1)}), bf16[4,3,16,4096]{3,2,1,0:T(8,128)(2,1)S(1)}, u32[]{:S(2)}, u32[]{:S(2)}) async-start(bf16[4,3,16,4096]{3,2,1,0:T(8,128)(2,1)} %serve.1), calls=%async_computation | async-start | bytes 3145728 | tf_op jit(solution)/shard_map/all_to_all | solution.py:25
  10.4 9.1 %collective-permute-start.1 = (bf16[72,512]{1,0:T(8,128)(2,1)S(1)}, bf16[72,512]{1,0:T(8,128)(2,1)S(1)}, u32[]{:S(2)}, u32[]{:S(2)}) collective-permute-start(bf16[72,512]{1,0:T(8,128)(2,1)S(1)} %maximum_maximum_fusion), channel_id=1, source_target_pairs={{0,4},{1,5},{2,6},{3,7},{4,0},{5,1},{6,2},{7,3},{8,12},{9,13},{10,... | collective-permute-start | bytes 221192 | tf_op jit(solution)/shard_map/ppermute | solution.py:20
  19.5 3.8 %collective-permute-done.1 = bf16[72,512]{1,0:T(8,128)(2,1)S(1)} collective-permute-done((bf16[72,512]{1,0:T(8,128)(2,1)S(1)}, bf16[72,512]{1,0:T(8,128)(2,1)S(1)}, u32[]{:S(2)}, u32[]{:S(2)}) %collective-permute-start.1) | collective-permute-done | bytes 73760 | tf_op jit(solution)/shard_map/ppermute | solution.py:20
  23.4 7.4 %collective-permute-start.2 = (bf16[2,72,512]{2,1,0:T(8,128)(2,1)S(1)}, bf16[2,72,512]{2,1,0:T(8,128)(2,1)S(1)}, u32[]{:S(2)}, u32[]{:S(2)}) collective-permute-start(bf16[2,72,512]{2,1,0:T(8,128)(2,1)S(1)} %pad_maximum_fusion.3), channel_id=1, source_target_pairs={{0,2},{1,3},{2,0},{3,1},{4,6},{5,7},{6,4},{7,5},{8,10},{9,11},{10,... | collective-permute-start | bytes 442376 | tf_op jit(solution)/shard_map/ppermute | solution.py:20
  30.8 5.1 %collective-permute-done.2 = bf16[2,72,512]{2,1,0:T(8,128)(2,1)S(1)} collective-permute-done((bf16[2,72,512]{2,1,0:T(8,128)(2,1)S(1)}, bf16[2,72,512]{2,1,0:T(8,128)(2,1)S(1)}, u32[]{:S(2)}, u32[]{:S(2)}) %collective-permute-start.2) | collective-permute-done | bytes 147488 | tf_op jit(solution)/shard_map/ppermute | solution.py:20
  36.2 5.1 %collective-permute-start.3 = (bf16[2,2,72,512]{3,2,0,1:T(8,128)(2,1)S(1)}, bf16[2,2,72,512]{3,2,0,1:T(8,128)(2,1)S(1)}, u32[]{:S(2)}, u32[]{:S(2)}) collective-permute-start(bf16[2,2,72,512]{3,2,0,1:T(8,128)(2,1)S(1)} %pad_maximum_fusion.2), channel_id=1, source_target_pairs={{0,1},{1,0},{2,3},{3,2},{4,5},{5,4},{6,7},{7,6},{8,9},{9,8},{10,11... | collective-permute-start | bytes 884744 | tf_op jit(solution)/shard_map/ppermute | solution.py:20
  41.4 13.5 %collective-permute-start.4 = (bf16[3,16,3072]{2,1,0:T(8,128)(2,1)S(1)}, bf16[3,16,3072]{2,1,0:T(8,128)(2,1)S(1)}, u32[]{:S(2)}, u32[]{:S(2)}) collective-permute-start(bf16[3,16,3072]{2,1,0:T(8,128)(2,1)S(1)} %slice.38), channel_id=1, source_target_pairs={{0,256},{64,320},{128,384},{192,448},{256,0},{320,64},{384,128},{4... | collective-permute-start | bytes 884744 | tf_op jit(solution)/shard_map/ppermute | solution.py:20
  55.7 0.8 copy.104
  56.5 4.9 %all-to-all-start.1 = ((bf16[4,8,16,512]{3,2,1,0:T(8,128)(2,1)}), bf16[4,8,16,512]{3,2,1,0:T(8,128)(2,1)S(1)}, u32[]{:S(2)}, u32[]{:S(2)}) async-start(bf16[4,8,16,512]{3,2,1,0:T(8,128)(2,1)} %bitcast.99), calls=%async_computation.1 | async-start | bytes 1048576 | tf_op jit(solution)/shard_map/all_to_all | solution.py:25
  61.4 23.7 %collective-permute-done.4 = bf16[3,16,3072]{2,1,0:T(8,128)(2,1)S(1)} collective-permute-done((bf16[3,16,3072]{2,1,0:T(8,128)(2,1)S(1)}, bf16[3,16,3072]{2,1,0:T(8,128)(2,1)S(1)}, u32[]{:S(2)}, u32[]{:S(2)}) %collective-permute-start.4) | collective-permute-done | bytes 294944 | tf_op jit(solution)/shard_map/ppermute | solution.py:20
  85.1 5.2 %collective-permute-start.7 = (bf16[16,4096]{1,0:T(8,128)(2,1)S(1)}, bf16[16,4096]{1,0:T(8,128)(2,1)S(1)}, u32[]{:S(2)}, u32[]{:S(2)}) collective-permute-start(bf16[16,4096]{1,0:T(8,128)(2,1)S(1)} %fusion.27.fresh0_ref), channel_id=1, source_target_pairs={{0,192},{64,128},{128,64},{192,0},{256,448},{320,384},{384,320},{4... | collective-permute-start | bytes 393224 | tf_op jit(solution)/shard_map/ppermute | solution.py:20
  90.4 2.8 %collective-permute-start.6 = (bf16[16,4096]{1,0:T(8,128)(2,1)S(1)}, bf16[16,4096]{1,0:T(8,128)(2,1)S(1)}, u32[]{:S(2)}, u32[]{:S(2)}) collective-permute-start(bf16[16,4096]{1,0:T(8,128)(2,1)S(1)} %fusion.27.fresh0_ref), channel_id=1, source_target_pairs={{0,128},{64,192},{128,0},{192,64},{256,384},{320,448},{384,256},{4... | collective-permute-start | bytes 393224 | tf_op jit(solution)/shard_map/ppermute | solution.py:20
  93.2 1.9 collective-permute-start.5
  95.1 1.3 dynamic_slice.3
  97.0 2.8 %collective-permute-done.6.fresh2_ref = bf16[16,4096]{1,0:T(8,128)(2,1)S(1)} collective-permute-done((bf16[16,4096]{1,0:T(8,128)(2,1)S(1)}, bf16[16,4096]{1,0:T(8,128)(2,1)S(1)}, u32[]{:S(2)}, u32[]{:S(2)}) %collective-permute-start.6) | collective-permute-done | bytes 131104 | tf_op jit(solution)/shard_map/ppermute | solution.py:20
  100.7 0.8 copy-done.4
  101.5 2.8 %assemble.1 = (bf16[8,80,512]{2,1,0:T(8,128)(2,1)}, bf16[64,4096]{1,0:T(8,128)(2,1)}) custom-call(s32[8,8]{1,0:T(8,128)} %failed_ref.3, s32[8,8]{1,0:T(8,128)} %spans_ref.5, bf16[64,4096]{1,0:T(8,128)(2,1)} %bitcast.115, bf16[16,4096]{1,0:T(8,128)(2,1)} %copy-done.9, bf16[16,4096]{1,0:T(8,128)(2,1)} %copy-done.13, bf16[16,4096]{1,0:T(8,128)(2,1)} %copy-done.12, ...), custom_call_target="tpu_custom_call" | custom-call | tf_op jit(solution)/shard_map/assemble/pallas_call | solution.py:131
  104.3 5.7 %all-to-all-start.2 = ((bf16[8,80,512]{2,1,0:T(8,128)(2,1)}), bf16[8,80,512]{2,1,0:T(8,128)(2,1)S(1)}, u32[]{:S(2)}, u32[]{:S(2)}) async-start(bf16[8,80,512]{2,1,0:T(8,128)(2,1)} %get-tuple-element.19), calls=%async_computation.2 | async-start | bytes 1310720 | tf_op jit(solution)/shard_map/all_to_all | solution.py:195
  110.1 0.7 slice.44.placed_ref
  110.8 1.9 unpack.1
  112.8 2.1 fusion.30
  115.1 0.7 copy.95
  115.8 0.8 convert_element_type.130
  116.7 1.1 convolution_convert_fusion.2
  118.3 11.9 %all-gather = bf16[4,2,4096]{2,1,0:T(2,128)(2,1)S(1)} all-gather(bf16[1,2,4096]{2,1,0:T(2,128)(2,1)S(1)} %reshape.167), channel_id=1, replica_groups={{0,64,128,192},{256,320,384,448},{1,65,129,193},{257,321,385,449},{2,66..., dimensions={0}, use_global_device_ids=true | all-gather | bytes 81920 | tf_op jit(solution)/shard_map/all_gather | solution.py:42
  130.2 0.7 reshape.166
  131.1 4.9 %fusion.32 = f32[64,32,8]{1,2,0:T(8,128)} fusion(f32[64,32,128]{2,1,0:T(8,128)S(1)} %bitcast.106, f32[128,8]{0,1:T(8,128)S(1)} %copy-done), kind=kOutput, calls=%fused_computation.62 | convolution fusion | flops 25165824 | bytes 1118208 | tf_op jit(solution)/shard_map/jnc,cp->jnp/dot_general | solution.py:214
  136.0 1.1 copy.90
  137.4 4.9 %fusion.34 = f32[64,32,8]{1,2,0:T(8,128)} fusion(f32[64,32,128]{2,1,0:T(8,128)S(1)} %bitcast.107, f32[128,8]{0,1:T(8,128)S(1)} %copy-done), kind=kOutput, calls=%fused_computation.64 | convolution fusion | flops 25165824 | bytes 1118208 | tf_op jit(solution)/shard_map/jnc,cp->jnp/dot_general | solution.py:214
  142.2 1.1 copy.89
  143.3 0.7 copy.91
  144.1 1.5 maximum_select_fusion
  145.6 8.5 %collective-permute-start.10 = (bf16[16,4096]{1,0:T(8,128)(2,1)S(1)}, bf16[16,4096]{1,0:T(8,128)(2,1)}, u32[]{:S(2)}, u32[]{:S(2)}) collective-permute-start(bf16[16,4096]{1,0:T(8,128)(2,1)S(1)} %bitcast.127), channel_id=1, source_target_pairs={{0,256},{64,320},{128,384},{192,448},{256,0},{320,64},{384,128},{4... | collective-permute-start | bytes 393224 | tf_op jit(solution)/shard_map/ppermute | solution.py:20
  154.1 2.5 %fusion.9 = (f32[512]{0:T(512)S(1)}, f32[512,512]{0,1:T(8,128)}) fusion(bf16[512,512]{0,1:T(8,128)(2,1)} %copy-done.6, bf16[8,80,512]{2,1,0:T(8,128)(2,1)S(1)} %all-to-all-done.2, bf16[8,72,512]{2,1,0:T(8,128)(2,1)S(1)} %bitcast.111), kind=kOutput, calls=%fused_computation.18 | convolution fusion | flops 269221376 | bytes 2623488 | tf_op jit(solution)/shard_map/dot_general | solution.py:201
  157.2 9.9 %all-to-all-start.3 = ((f32[8,4,128]{2,1,0:T(4,128)}), f32[8,4,128]{2,1,0:T(4,128)S(1)}, u32[]{:S(2)}, u32[]{:S(2)}) async-start(f32[8,4,128]{2,1,0:T(4,128)} %broadcast_in_dim.24), calls=%async_computation.3 | async-start | bytes 32768 | tf_op jit(solution)/shard_map/all_to_all | solution.py:203
  167.1 2.3 %convolution_convert_fusion = bf16[512,512]{1,0:T(8,128)(2,1)} fusion(bf16[512,512]{1,0:T(8,128)(2,1)S(1)} %bitcast.125, bf16[512,512]{0,1:T(8,128)(2,1)} %copy-done.6, f32[512]{0:T(512)S(1)} %get-tuple-element.71), kind=kOutput, calls=%fused_computation.6 | convolution fusion | flops 269484032 | bytes 1574912 | tf_op jit(solution)/shard_map/dot_general | solution.py:200
  169.5 6.6 %all-to-all-done.3 = f32[8,4,128]{2,1,0:T(4,128)S(1)} async-done(((f32[8,4,128]{2,1,0:T(4,128)}), f32[8,4,128]{2,1,0:T(4,128)S(1)}, u32[]{:S(2)}, u32[]{:S(2)}) %all-to-all-start.3) | async-done | bytes 16416 | tf_op jit(solution)/shard_map/all_to_all | solution.py:203
  176.1 5.0 %all-to-all-start.4 = ((bf16[8,64,512]{2,1,0:T(8,128)(2,1)}), bf16[8,64,512]{2,1,0:T(8,128)(2,1)S(1)}, u32[]{:S(2)}, u32[]{:S(2)}) async-start(bf16[8,64,512]{2,1,0:T(8,128)(2,1)} %bitcast.120), calls=%async_computation.4 | async-start | bytes 1048576 | tf_op jit(solution)/shard_map/all_to_all | solution.py:209
  181.2 1.6 fusion.13
  182.8 1.1 fusion.23
  183.9 13.0 %all_gather.9 = bf16[64,4096]{1,0:T(8,128)(2,1)S(1)} all-gather(bf16[16,4096]{1,0:T(8,128)(2,1)S(1)} %get-tuple-element.66), channel_id=1, replica_groups={{0,64,128,192},{256,320,384,448},{1,65,129,193},{257,321,385,449},{2,66..., dimensions={0}, use_global_device_ids=true | all-gather | bytes 655360 | tf_op jit(solution)/shard_map/all_gather | solution.py:42
  196.9 13.4 %all_gather.10 = bf16[64,4096]{1,0:T(8,128)(2,1)S(1)} all-gather(bf16[16,4096]{1,0:T(8,128)(2,1)S(1)} %get-tuple-element.67), channel_id=1, replica_groups={{0,64,128,192},{256,320,384,448},{1,65,129,193},{257,321,385,449},{2,66..., dimensions={0}, use_global_device_ids=true | all-gather | bytes 655360 | tf_op jit(solution)/shard_map/all_gather | solution.py:42
  210.4 1.7 fusion.3
  212.1 0.8 copy-done.7
  212.9 2.0 copy.94
  214.9 0.7 reduce_sum.65
  (77 shorter events, 4.5 us)
Async XLA Ops:
  0.6 112.1 %copy-start = (f32[128,8]{0,1:T(8,128)S(1)}, f32[128,8]{0,1:T(8,128)}, u32[]{:S(2)}) copy-start(f32[128,8]{0,1:T(8,128)} %param.13) | copy-start | bytes 12292
  2.1 8.2 %collective-permute-start = (f32[4,128]{1,0:T(4,128)S(1)}, f32[4,128]{1,0:T(4,128)S(1)}, u32[]{:S(2)}, u32[]{:S(2)}) collective-permute-start(f32[4,128]{1,0:T(4,128)S(1)} %bitcast.135), channel_id=1, source_target_pairs={{56,0},{0,8},{8,16},{16,24},{24,32},{32,40},{40,48},{48,56},{57,1}... | collective-permute-start | bytes 6152 | tf_op jit(solution)/shard_map/ppermute | solution.py:16
  5.7 4.5 %copy-start.10 = (bf16[1,1,512,64]{2,3,1,0:T(8,128)(2,1)S(1)}, bf16[1,1,512,64]{2,3,1,0:T(8,128)(2,1)}, u32[]{:S(2)}) copy-start(bf16[1,1,512,64]{2,3,1,0:T(8,128)(2,1)} %param.9) | copy-start | bytes 196612
  5.7 30.2 %all-to-all-start = ((bf16[4,3,16,4096]{3,2,1,0:T(8,128)(2,1)}), bf16[4,3,16,4096]{3,2,1,0:T(8,128)(2,1)S(1)}, u32[]{:S(2)}, u32[]{:S(2)}) async-start(bf16[4,3,16,4096]{3,2,1,0:T(8,128)(2,1)} %serve.1), calls=%async_computation | async-start | bytes 3145728 | tf_op jit(solution)/shard_map/all_to_all | solution.py:25
  10.4 12.9 %collective-permute-start.1 = (bf16[72,512]{1,0:T(8,128)(2,1)S(1)}, bf16[72,512]{1,0:T(8,128)(2,1)S(1)}, u32[]{:S(2)}, u32[]{:S(2)}) collective-permute-start(bf16[72,512]{1,0:T(8,128)(2,1)S(1)} %maximum_maximum_fusion), channel_id=1, source_target_pairs={{0,4},{1,5},{2,6},{3,7},{4,0},{5,1},{6,2},{7,3},{8,12},{9,13},{10,... | collective-permute-start | bytes 221192 | tf_op jit(solution)/shard_map/ppermute | solution.py:20
  23.4 12.5 %collective-permute-start.2 = (bf16[2,72,512]{2,1,0:T(8,128)(2,1)S(1)}, bf16[2,72,512]{2,1,0:T(8,128)(2,1)S(1)}, u32[]{:S(2)}, u32[]{:S(2)}) collective-permute-start(bf16[2,72,512]{2,1,0:T(8,128)(2,1)S(1)} %pad_maximum_fusion.3), channel_id=1, source_target_pairs={{0,2},{1,3},{2,0},{3,1},{4,6},{5,7},{6,4},{7,5},{8,10},{9,11},{10,... | collective-permute-start | bytes 442376 | tf_op jit(solution)/shard_map/ppermute | solution.py:20
  36.2 18.7 %collective-permute-start.3 = (bf16[2,2,72,512]{3,2,0,1:T(8,128)(2,1)S(1)}, bf16[2,2,72,512]{3,2,0,1:T(8,128)(2,1)S(1)}, u32[]{:S(2)}, u32[]{:S(2)}) collective-permute-start(bf16[2,2,72,512]{3,2,0,1:T(8,128)(2,1)S(1)} %pad_maximum_fusion.2), channel_id=1, source_target_pairs={{0,1},{1,0},{2,3},{3,2},{4,5},{5,4},{6,7},{7,6},{8,9},{9,8},{10,11... | collective-permute-start | bytes 884744 | tf_op jit(solution)/shard_map/ppermute | solution.py:20
  41.3 13.9 %collective-permute-start.8 = (bf16[512,512]{0,1:T(8,128)(2,1)S(1)}, bf16[512,512]{0,1:T(8,128)(2,1)S(1)}, u32[]{:S(2)}, u32[]{:S(2)}) collective-permute-start(bf16[512,512]{0,1:T(8,128)(2,1)S(1)} %bitcast.112), channel_id=1, source_target_pairs={{56,0},{0,8},{8,16},{16,24},{24,32},{32,40},{40,48},{48,56},{57,1}... | collective-permute-start | bytes 1572872 | tf_op jit(solution)/shard_map/ppermute | solution.py:16
  41.4 43.7 %collective-permute-start.4 = (bf16[3,16,3072]{2,1,0:T(8,128)(2,1)S(1)}, bf16[3,16,3072]{2,1,0:T(8,128)(2,1)S(1)}, u32[]{:S(2)}, u32[]{:S(2)}) collective-permute-start(bf16[3,16,3072]{2,1,0:T(8,128)(2,1)S(1)} %slice.38), channel_id=1, source_target_pairs={{0,256},{64,320},{128,384},{192,448},{256,0},{320,64},{384,128},{4... | collective-permute-start | bytes 884744 | tf_op jit(solution)/shard_map/ppermute | solution.py:20
  55.2 1.3 copy-start.6
  56.5 43.5 %all-to-all-start.1 = ((bf16[4,8,16,512]{3,2,1,0:T(8,128)(2,1)}), bf16[4,8,16,512]{3,2,1,0:T(8,128)(2,1)S(1)}, u32[]{:S(2)}, u32[]{:S(2)}) async-start(bf16[4,8,16,512]{3,2,1,0:T(8,128)(2,1)} %bitcast.99), calls=%async_computation.1 | async-start | bytes 1048576 | tf_op jit(solution)/shard_map/all_to_all | solution.py:25
  85.1 14.9 %copy-start.9 = (bf16[16,4096]{1,0:T(8,128)(2,1)}, bf16[16,4096]{1,0:T(8,128)(2,1)S(1)}, u32[]{:S(2)}) copy-start(bf16[16,4096]{1,0:T(8,128)(2,1)S(1)} %fusion.27.fresh0_ref) | copy-start | bytes 393220
  85.1 11.9 %collective-permute-start.7 = (bf16[16,4096]{1,0:T(8,128)(2,1)S(1)}, bf16[16,4096]{1,0:T(8,128)(2,1)S(1)}, u32[]{:S(2)}, u32[]{:S(2)}) collective-permute-start(bf16[16,4096]{1,0:T(8,128)(2,1)S(1)} %fusion.27.fresh0_ref), channel_id=1, source_target_pairs={{0,192},{64,128},{128,64},{192,0},{256,448},{320,384},{384,320},{4... | collective-permute-start | bytes 393224 | tf_op jit(solution)/shard_map/ppermute | solution.py:20
  90.4 9.4 %collective-permute-start.6 = (bf16[16,4096]{1,0:T(8,128)(2,1)S(1)}, bf16[16,4096]{1,0:T(8,128)(2,1)S(1)}, u32[]{:S(2)}, u32[]{:S(2)}) collective-permute-start(bf16[16,4096]{1,0:T(8,128)(2,1)S(1)} %fusion.27.fresh0_ref), channel_id=1, source_target_pairs={{0,128},{64,192},{128,0},{192,64},{256,384},{320,448},{384,256},{4... | collective-permute-start | bytes 393224 | tf_op jit(solution)/shard_map/ppermute | solution.py:20
  93.2 6.9 %collective-permute-start.5 = (bf16[16,4096]{1,0:T(8,128)(2,1)S(1)}, bf16[16,4096]{1,0:T(8,128)(2,1)S(1)}, u32[]{:S(2)}, u32[]{:S(2)}) collective-permute-start(bf16[16,4096]{1,0:T(8,128)(2,1)S(1)} %fusion.27.fresh0_ref), channel_id=1, source_target_pairs={{0,64},{64,0},{128,192},{192,128},{256,320},{320,256},{384,448},{4... | collective-permute-start | bytes 393224 | tf_op jit(solution)/shard_map/ppermute | solution.py:20
  97.0 3.0 %copy-start.11 = (bf16[16,4096]{1,0:T(8,128)(2,1)}, bf16[16,4096]{1,0:T(8,128)(2,1)S(1)}, u32[]{:S(2)}) copy-start(bf16[16,4096]{1,0:T(8,128)(2,1)S(1)} %collective-permute-done.7.fresh3_ref) | copy-start | bytes 393220
  99.8 0.6 copy-start.12
  100.0 0.7 copy-start.13
  100.7 0.8 copy-start.4
  104.3 8.4 %copy-start.8 = (bf16[64,4096]{1,0:T(8,128)(2,1)S(1)}, bf16[64,4096]{1,0:T(8,128)(2,1)}, u32[]{:S(2)}) copy-start(bf16[64,4096]{1,0:T(8,128)(2,1)} %get-tuple-element.26) | copy-start | bytes 1572868
  104.3 41.2 %all-to-all-start.2 = ((bf16[8,80,512]{2,1,0:T(8,128)(2,1)}), bf16[8,80,512]{2,1,0:T(8,128)(2,1)S(1)}, u32[]{:S(2)}, u32[]{:S(2)}) async-start(bf16[8,80,512]{2,1,0:T(8,128)(2,1)} %get-tuple-element.19), calls=%async_computation.2 | async-start | bytes 1310720 | tf_op jit(solution)/shard_map/all_to_all | solution.py:195
  112.7 3.1 %copy-start.3 = (bf16[2,16,4096]{2,1,0:T(8,128)(2,1)S(1)}, bf16[2,16,4096]{2,1,0:T(8,128)(2,1)}, u32[]{:S(2)}) copy-start(bf16[2,16,4096]{2,1,0:T(8,128)(2,1)} %unpack.1) | copy-start | bytes 786436
  115.1 15.8 %copy-start.2 = (f32[1,1,64,4096]{3,2,1,0:T(8,128)S(1)}, f32[1,1,64,4096]{3,2,1,0:T(8,128)}, u32[]{:S(2)}) copy-start(f32[1,1,64,4096]{3,2,1,0:T(8,128)} %param.12) | copy-start | bytes 3145732
  130.9 6.2 %copy-start.1 = (f32[1,1,64,4096]{3,2,1,0:T(8,128)S(1)}, f32[1,1,64,4096]{3,2,1,0:T(8,128)}, u32[]{:S(2)}) copy-start(f32[1,1,64,4096]{3,2,1,0:T(8,128)} %param.11) | copy-start | bytes 3145732
  145.6 37.2 %collective-permute-start.10 = (bf16[16,4096]{1,0:T(8,128)(2,1)S(1)}, bf16[16,4096]{1,0:T(8,128)(2,1)}, u32[]{:S(2)}, u32[]{:S(2)}) collective-permute-start(bf16[16,4096]{1,0:T(8,128)(2,1)S(1)} %bitcast.127), channel_id=1, source_target_pairs={{0,256},{64,320},{128,384},{192,448},{256,0},{320,64},{384,128},{4... | collective-permute-start | bytes 393224 | tf_op jit(solution)/shard_map/ppermute | solution.py:20
  157.2 18.9 %all-to-all-start.3 = ((f32[8,4,128]{2,1,0:T(4,128)}), f32[8,4,128]{2,1,0:T(4,128)S(1)}, u32[]{:S(2)}, u32[]{:S(2)}) async-start(f32[8,4,128]{2,1,0:T(4,128)} %broadcast_in_dim.24), calls=%async_computation.3 | async-start | bytes 32768 | tf_op jit(solution)/shard_map/all_to_all | solution.py:203
  176.1 6.7 %copy-start.5 = (f32[2,16,4096]{2,1,0:T(8,128)S(1)}, f32[2,16,4096]{2,1,0:T(8,128)}, u32[]{:S(2)}) copy-start(f32[2,16,4096]{2,1,0:T(8,128)} %convert_element_type.130) | copy-start | bytes 1572868
  176.1 38.8 %all-to-all-start.4 = ((bf16[8,64,512]{2,1,0:T(8,128)(2,1)}), bf16[8,64,512]{2,1,0:T(8,128)(2,1)S(1)}, u32[]{:S(2)}, u32[]{:S(2)}) async-start(bf16[8,64,512]{2,1,0:T(8,128)(2,1)} %bitcast.120), calls=%async_computation.4 | async-start | bytes 1048576 | tf_op jit(solution)/shard_map/all_to_all | solution.py:209
  182.8 29.3 %collective-permute-start.9 = (bf16[512,512]{0,1:T(8,128)(2,1)S(1)}, bf16[512,512]{0,1:T(8,128)(2,1)S(1)}, u32[]{:S(2)}, u32[]{:S(2)}) collective-permute-start(bf16[512,512]{0,1:T(8,128)(2,1)S(1)} %fusion.13), channel_id=1, source_target_pairs={{8,0},{16,8},{24,16},{32,24},{40,32},{48,40},{56,48},{0,56},{9,1},... | collective-permute-start | bytes 1572872 | tf_op jit(solution)/shard_map/ppermute | solution.py:16
  212.0 0.8 copy-start.7

commit v14 on v10

--- a/solution.py
+++ b/solution.py
@@ -224,10 +224,17 @@
     grad = grad.reshape(8, PLANE, part, cols).transpose(1, 0, 2, 3)
     grad, served_moments = lax.optimization_barrier((grad, served_moments))
     grad = exchange_x(grad)
+
+    sent, restored_weight = assemble(failed_replica, resend_spans, own_weight, fresh_weight, grad)
+    own_first, own_second, restored_weight = lax.optimization_barrier((own_first, own_second, restored_weight))
+    def checksum(source):
+        shaped = source.reshape(-1, nchunk, 128)
+        mixed = jnp.einsum("jnc,cp->jnp", shaped, probe_matrix, precision=lax.Precision.HIGHEST)
+        return mixed.reshape(-1, nchunk * probe_matrix.shape[1])
+
+    weight_checksums = checksum(restored_weight.astype(WIDE))
+    weight_checksums, served_moments = lax.optimization_barrier((weight_checksums, served_moments))
     fresh = both_planes(served_moments)
-
-    sent, restored_weight = assemble(failed_replica, resend_spans, own_weight, fresh_weight, grad)
-    own_first, own_second, restored_weight, fresh = lax.optimization_barrier((own_first, own_second, restored_weight, fresh))
     got = lax.all_to_all(sent, "tensor", 0, 0, tiled=True)
     weight_cols = got[:, :rows].reshape(8 * rows, cols)
     grad_rows = got[:, rows:].transpose(1, 0, 2).reshape(part, width)
@@ -245,11 +252,6 @@
     got = lax.all_to_all(keys.reshape(8, rows, tokens), "tensor", 0, 0, tiled=True)
     key_out = jnp.sum(got.astype(WIDE), axis=0).T.astype(SHORT)
 
-    def checksum(source):
-        shaped = source.reshape(-1, nchunk, 128)
-        mixed = jnp.einsum("jnc,cp->jnp", shaped, probe_matrix, precision=lax.Precision.HIGHEST)
-        return mixed.reshape(-1, nchunk * probe_matrix.shape[1])
-
     fresh = unpack(resend_spans, fresh).astype(WIDE)
     fresh_update = adam(fresh[0], fresh[1], mean_rows).astype(SHORT)
     fresh_sums = checksum(fresh.reshape(2 * part, width)).astype(SHORT).reshape(2, width)
@@ -260,7 +262,6 @@
     update = jnp.where(is_failed, fresh_update, adam(own_first, own_second, mean_grad))
     own_sums = jnp.stack([checksum(own_first), checksum(own_second)])
     checksums = jnp.where(is_failed, fresh_sums, own_sums)
-    weight_checksums = checksum(restored_weight.astype(WIDE))
     return (key_out[None, None], outgoing[None, None], update[None, None], checksums[None, None], weight_checksums[None, None])
 
 

time: 208 us -> 226 us (1.087)
  starting transfers between devices: 113 us -> 139 us
  waiting for transfers between devices: 44.3 us -> 31.8 us
  other arithmetic: 12.3 us -> 15 us
    ppermute x16, starting transfers between devices: 74.7 us -> 95.1 us  [swap(): lax.ppermute(block, axis, [(i, i ^ bit) for i in range(lax.axis_size(axis...]
    all_to_all x1, waiting for transfers between devices: 16 us -> 3.67 us  [shards(): got = lax.all_to_all(sent, 'tensor', 0, 0, tiled=True)]
    all_to_all x1, starting transfers between devices: 4.8 us -> 7.75 us  [shards(): lax.all_to_all(keys.reshape(8, rows, tokens), 'tensor', 0, 0, tiled=True)]
    unnamed x46 -> x44, local copies, waits for them, and re-layouts: 6.56 us -> 7.46 us
  transfers between devices with their start and end apart: 24 -> 24, of which waited for: 8 -> 10; matrix products, arithmetic and copies ran while one was open for 16% -> 16% of each run, Pallas kernels for 2% -> 1%
where the time goes in v14:
time: 226 us; the launch traced here: 225 us
  starting transfers between devices  139 us (62%)
  waiting for transfers between devices  31.8 us (14%)
  matrix products  15.1 us (7%)
  other arithmetic  15 us (7%)
  local copies, waits for them, and re-layouts  14.1 us (6%)
  Pallas kernels  8.44 us (4%)
    ppermute x16, starting transfers between devices, swap(): lax.ppermute(block, axis, [(i, i ^ bit) for i in range(lax.axis_size(axis...  95.1 us
    ppermute x16, waiting for transfers between devices, swap(): lax.ppermute(block, axis, [(i, i ^ bit) for i in range(lax.axis_size(axis...  20.2 us
    ppermute x3, starting transfers between devices, from_behind(): lax.ppermute(block, axis, [((i - distance) % n, i) for i in range(n)])  16.8 us
    all_to_all x3, starting transfers between devices, exchange_x(): lax.all_to_all(block, 'replica', 0, 0, axis_index_groups=groups, tiled=True)  12.9 us
    dot_general x4, matrix products, checksum(): jnp.einsum('jnc,cp->jnp', shaped, probe_matrix, precision=lax.Precision.H...  11.6 us
    ppermute x3, waiting for transfers between devices, from_behind(): lax.ppermute(block, axis, [((i - distance) % n, i) for i in range(n)])  7.89 us
    all_to_all x1, starting transfers between devices, shards(): lax.all_to_all(keys.reshape(8, rows, tokens), 'tensor', 0, 0, tiled=True)  7.75 us
    unnamed x44, local copies, waits for them, and re-layouts  7.46 us
  transfers between devices with their start and end apart: 24, of which 10 were waited for; matrix products, arithmetic and copies ran while one was open for 16% of the time, Pallas kernels for 1%

profile of v14, /device:TPU:1, one launch (start us, length us, event | category | flops | bytes accessed | tf_op | source)
XLA Modules:
  0.0 225.0 jit_solution(7758244680416922654)
XLA Ops:
  0.7 3.7 %serve.1 = (bf16[4,16,4096]{2,1,0:T(8,128)(2,1)}, bf16[4,2,16,4096]{3,2,1,0:T(8,128)(2,1)}) custom-call(s32[8,8]{1,0:T(8,128)} %failed_ref.3, s32[8,8]{1,0:T(8,128)} %spans_ref.5, bf16[64,4096]{1,0:T(8,128)(2,1)} %bitcast.145, f32[64,4096]{1,0:T(8,128)} %bitcast.132, f32[64,4096]{1,0:T(8,128)} %bitcast.135), custom_call_target="tpu_custom_call" | custom-call | tf_op jit(solution)/shard_map/serve/pallas_call | solution.py:104
  4.4 4.8 %all-to-all-start = ((bf16[4,16,4096]{2,1,0:T(8,128)(2,1)}), bf16[4,16,4096]{2,1,0:T(8,128)(2,1)S(1)}, u32[]{:S(2)}, u32[]{:S(2)}) async-start(bf16[4,16,4096]{2,1,0:T(8,128)(2,1)} %get-tuple-element.24), calls=%async_computation | async-start | bytes 1048576 | tf_op jit(solution)/shard_map/all_to_all | solution.py:25
  9.2 8.8 %collective-permute-start = (bf16[64,512]{1,0:T(8,128)(2,1)S(1)}, bf16[64,512]{1,0:T(8,128)(2,1)S(1)}, u32[]{:S(2)}, u32[]{:S(2)}) collective-permute-start(bf16[64,512]{1,0:T(8,128)(2,1)S(1)} %bitcast.171), channel_id=1, source_target_pairs={{0,4},{1,5},{2,6},{3,7},{4,0},{5,1},{6,2},{7,3},{8,12},{9,13},{10,... | collective-permute-start | bytes 196616 | tf_op jit(solution)/shard_map/ppermute | solution.py:20
  18.4 2.4 %collective-permute-start.1 = (f32[4,128]{1,0:T(4,128)S(1)}, f32[4,128]{1,0:T(4,128)S(1)}, u32[]{:S(2)}, u32[]{:S(2)}) collective-permute-start(f32[4,128]{1,0:T(4,128)S(1)} %bitcast.179), channel_id=1, source_target_pairs={{56,0},{0,8},{8,16},{16,24},{24,32},{32,40},{40,48},{48,56},{57,1}... | collective-permute-start | bytes 6152 | tf_op jit(solution)/shard_map/ppermute | solution.py:16
  21.5 3.7 %collective-permute-start.2 = (f32[1,512]{1,0:T(1,128)S(1)}, f32[1,512]{1,0:T(1,128)S(1)}, u32[]{:S(2)}, u32[]{:S(2)}) collective-permute-start(f32[1,512]{1,0:T(1,128)S(1)} %bitcast.180), channel_id=1, source_target_pairs={{0,4},{1,5},{2,6},{3,7},{4,0},{5,1},{6,2},{7,3},{8,12},{9,13},{10,... | collective-permute-start | bytes 6152 | tf_op jit(solution)/shard_map/ppermute | solution.py:20
  25.2 4.5 %collective-permute-done.2 = f32[1,512]{1,0:T(1,128)S(1)} collective-permute-done((f32[1,512]{1,0:T(1,128)S(1)}, f32[1,512]{1,0:T(1,128)S(1)}, u32[]{:S(2)}, u32[]{:S(2)}) %collective-permute-start.2) | collective-permute-done | bytes 2080 | tf_op jit(solution)/shard_map/ppermute | solution.py:20
  30.0 4.9 %collective-permute-start.3 = (bf16[136,512]{1,0:T(8,128)(2,1)S(1)}, bf16[136,512]{1,0:T(8,128)(2,1)S(1)}, u32[]{:S(2)}, u32[]{:S(2)}) collective-permute-start(bf16[136,512]{1,0:T(8,128)(2,1)S(1)} %pad_maximum_fusion.6), channel_id=1, source_target_pairs={{0,2},{1,3},{2,0},{3,1},{4,6},{5,7},{6,4},{7,5},{8,10},{9,11},{10,... | collective-permute-start | bytes 417800 | tf_op jit(solution)/shard_map/ppermute | solution.py:20
  34.9 3.7 %collective-permute-start.9 = (bf16[512,512]{0,1:T(8,128)(2,1)S(1)}, bf16[512,512]{0,1:T(8,128)(2,1)S(1)}, u32[]{:S(2)}, u32[]{:S(2)}) collective-permute-start(bf16[512,512]{0,1:T(8,128)(2,1)S(1)} %bitcast.147), channel_id=1, source_target_pairs={{56,0},{0,8},{8,16},{16,24},{24,32},{32,40},{40,48},{48,56},{57,1}... | collective-permute-start | bytes 1572872 | tf_op jit(solution)/shard_map/ppermute | solution.py:16
  39.0 4.5 %all-to-all-start.1 = ((bf16[4,2,16,4096]{3,2,1,0:T(8,128)(2,1)}), bf16[4,2,16,4096]{3,2,1,0:T(8,128)(2,1)S(1)}, u32[]{:S(2)}, u32[]{:S(2)}) async-start(bf16[4,2,16,4096]{3,2,1,0:T(8,128)(2,1)} %get-tuple-element.33), calls=%async_computation.1 | async-start | bytes 2097152 | tf_op jit(solution)/shard_map/all_to_all | solution.py:25
  43.5 10.0 %collective-permute-start.4 = (bf16[16,3072]{1,0:T(8,128)(2,1)S(1)}, bf16[16,3072]{1,0:T(8,128)(2,1)S(1)}, u32[]{:S(2)}, u32[]{:S(2)}) collective-permute-start(bf16[16,3072]{1,0:T(8,128)(2,1)S(1)} %slice.54), channel_id=1, source_target_pairs={{0,256},{64,320},{128,384},{192,448},{256,0},{320,64},{384,128},{4... | collective-permute-start | bytes 294920 | tf_op jit(solution)/shard_map/ppermute | solution.py:20
  53.5 1.9 collective-permute-start.8
  55.4 2.2 collective-permute-done.4
  57.6 9.3 %collective-permute-done.8 = bf16[264,512]{1,0:T(8,128)(2,1)S(1)} collective-permute-done((bf16[264,512]{1,0:T(8,128)(2,1)S(1)}, bf16[264,512]{1,0:T(8,128)(2,1)S(1)}, u32[]{:S(2)}, u32[]{:S(2)}) %collective-permute-start.8) | collective-permute-done | bytes 270368 | tf_op jit(solution)/shard_map/ppermute | solution.py:20
  69.0 3.5 %all-to-all-start.2 = ((bf16[4,8,16,512]{3,2,1,0:T(8,128)(2,1)}), bf16[4,8,16,512]{3,2,1,0:T(8,128)(2,1)S(1)}, u32[]{:S(2)}, u32[]{:S(2)}) async-start(bf16[4,8,16,512]{3,2,1,0:T(8,128)(2,1)} %bitcast.131), calls=%async_computation.2 | async-start | bytes 1048576 | tf_op jit(solution)/shard_map/all_to_all | solution.py:25
  72.5 4.5 %collective-permute-start.7 = (bf16[16,4096]{1,0:T(8,128)(2,1)S(1)}, bf16[16,4096]{1,0:T(8,128)(2,1)S(1)}, u32[]{:S(2)}, u32[]{:S(2)}) collective-permute-start(bf16[16,4096]{1,0:T(8,128)(2,1)S(1)} %pad_maximum_fusion.8.fresh0_ref), channel_id=1, source_target_pairs={{0,192},{64,128},{128,64},{192,0},{256,448},{320,384},{384,320},{4... | collective-permute-start | bytes 393224 | tf_op jit(solution)/shard_map/ppermute | solution.py:20
  77.1 2.5 %collective-permute-start.6 = (bf16[16,4096]{1,0:T(8,128)(2,1)S(1)}, bf16[16,4096]{1,0:T(8,128)(2,1)S(1)}, u32[]{:S(2)}, u32[]{:S(2)}) collective-permute-start(bf16[16,4096]{1,0:T(8,128)(2,1)S(1)} %pad_maximum_fusion.8.fresh0_ref), channel_id=1, source_target_pairs={{0,128},{64,192},{128,0},{192,64},{256,384},{320,448},{384,256},{4... | collective-permute-start | bytes 393224 | tf_op jit(solution)/shard_map/ppermute | solution.py:20
  79.6 2.0 collective-permute-start.5
  81.5 1.3 dynamic_slice.3
  83.5 1.9 collective-permute-done.6.fresh2_ref
  87.0 2.8 %assemble.1 = (bf16[8,80,512]{2,1,0:T(8,128)(2,1)}, bf16[64,4096]{1,0:T(8,128)(2,1)}) custom-call(s32[8,8]{1,0:T(8,128)} %failed_ref.3, s32[8,8]{1,0:T(8,128)} %spans_ref.5, bf16[64,4096]{1,0:T(8,128)(2,1)} %bitcast.146, bf16[16,4096]{1,0:T(8,128)(2,1)} %copy-done.10, bf16[16,4096]{1,0:T(8,128)(2,1)} %copy-done.15, bf16[16,4096]{1,0:T(8,128)(2,1)} %copy-done.14, ...), custom_call_target="tpu_custom_call" | custom-call | tf_op jit(solution)/shard_map/assemble/pallas_call | solution.py:158
  89.9 6.2 %all-to-all-start.3 = ((bf16[8,80,512]{2,1,0:T(8,128)(2,1)}), bf16[8,80,512]{2,1,0:T(8,128)(2,1)S(1)}, u32[]{:S(2)}, u32[]{:S(2)}) async-start(bf16[8,80,512]{2,1,0:T(8,128)(2,1)} %get-tuple-element.35), calls=%async_computation.3 | async-start | bytes 1310720 | tf_op jit(solution)/shard_map/all_to_all | solution.py:238
  96.2 2.1 fusion.29
  100.5 4.9 %collective-permute-start.15 = (bf16[2,16,3072]{2,1,0:T(8,128)(2,1)}, bf16[2,16,3072]{2,1,0:T(8,128)(2,1)}, u32[]{:S(2)}, u32[]{:S(2)}) collective-permute-start(bf16[2,16,3072]{2,1,0:T(8,128)(2,1)} %slice.63), channel_id=1, source_target_pairs={{0,256},{64,320},{128,384},{192,448},{256,0},{320,64},{384,128},{4... | collective-permute-start | bytes 589832 | tf_op jit(solution)/shard_map/ppermute | solution.py:20
  105.7 4.2 %fusion.24 = f32[64,32,8]{1,2,0:T(8,128)S(1)} fusion(f32[64,32,128]{2,1,0:T(8,128)S(1)} %bitcast.141, f32[128,8]{0,1:T(8,128)S(1)} %copy-done), kind=kOutput, calls=%fused_computation.58 | convolution fusion | flops 25165824 | bytes 1118208 | tf_op jit(solution)/shard_map/jnc,cp->jnp/dot_general | solution.py:232
  110.3 4.2 %fusion.26 = f32[64,32,8]{1,2,0:T(8,128)S(1)} fusion(f32[64,32,128]{2,1,0:T(8,128)S(1)} %bitcast.142, f32[128,8]{0,1:T(8,128)S(1)} %copy-done), kind=kOutput, calls=%fused_computation.60 | convolution fusion | flops 25165824 | bytes 1118208 | tf_op jit(solution)/shard_map/jnc,cp->jnp/dot_general | solution.py:232
  114.7 1.9 collective-permute-done.15
  117.5 1.6 pad_maximum_fusion.5.placed_ref
  119.1 1.9 unpack.1
  121.0 1.8 convert_element_type.129
  123.8 1.1 convolution_convert_fusion.2
  126.0 3.7 %all-to-all-done.3 = bf16[8,80,512]{2,1,0:T(8,128)(2,1)S(1)} async-done(((bf16[8,80,512]{2,1,0:T(8,128)(2,1)}), bf16[8,80,512]{2,1,0:T(8,128)(2,1)S(1)}, u32[]{:S(2)}, u32[]{:S(2)}) %all-to-all-start.3) | async-done | bytes 655392 | tf_op jit(solution)/shard_map/all_to_all | solution.py:238
  130.5 1.8 fusion.7
  132.3 11.4 %collective-permute-start.10 = (f32[4,128]{1,0:T(4,128)S(1)}, f32[4,128]{1,0:T(4,128)S(1)}, u32[]{:S(2)}, u32[]{:S(2)}) collective-permute-start(f32[4,128]{1,0:T(4,128)S(1)} %bitcast.178), channel_id=1, source_target_pairs={{0,1},{1,0},{2,3},{3,2},{4,5},{5,4},{6,7},{7,6},{8,9},{9,8},{10,11... | collective-permute-start | bytes 6152 | tf_op jit(solution)/shard_map/ppermute | solution.py:20
  144.6 3.8 %collective-permute-start.14 = (bf16[16,4096]{1,0:T(8,128)(2,1)S(1)}, bf16[16,4096]{1,0:T(8,128)(2,1)S(1)}, u32[]{:S(2)}, u32[]{:S(2)}) collective-permute-start(bf16[16,4096]{1,0:T(8,128)(2,1)S(1)} %bitcast.166), channel_id=1, source_target_pairs={{0,256},{64,320},{128,384},{192,448},{256,0},{320,64},{384,128},{4... | collective-permute-start | bytes 393224 | tf_op jit(solution)/shard_map/ppermute | solution.py:20
  149.5 20.3 %collective-permute-start.11 = (f32[4,128]{1,0:T(4,128)}, f32[4,128]{1,0:T(4,128)}, u32[]{:S(2)}, u32[]{:S(2)}) collective-permute-start(f32[4,128]{1,0:T(4,128)} %bitcast_add_fusion.2), channel_id=1, source_target_pairs={{0,2},{1,3},{2,0},{3,1},{4,6},{5,7},{6,4},{7,5},{8,10},{9,11},{10,... | collective-permute-start | bytes 6152 | tf_op jit(solution)/shard_map/ppermute | solution.py:20
  169.9 1.3 convolution_convert_fusion
  171.1 7.8 %all-to-all-start.4 = ((bf16[8,64,512]{2,1,0:T(8,128)(2,1)}), bf16[8,64,512]{2,1,0:T(8,128)(2,1)}, u32[]{:S(2)}, u32[]{:S(2)}) async-start(bf16[8,64,512]{2,1,0:T(8,128)(2,1)} %bitcast.161), calls=%async_computation.4 | async-start | bytes 1048576 | tf_op jit(solution)/shard_map/all_to_all | solution.py:252
  179.6 7.3 %collective-permute-start.12 = (f32[4,128]{1,0:T(4,128)S(1)}, f32[4,128]{1,0:T(4,128)S(1)}, u32[]{:S(2)}, u32[]{:S(2)}) collective-permute-start(f32[4,128]{1,0:T(4,128)S(1)} %fusion.48), channel_id=1, source_target_pairs={{0,4},{1,5},{2,6},{3,7},{4,0},{5,1},{6,2},{7,3},{8,12},{9,13},{10,... | collective-permute-start | bytes 6152 | tf_op jit(solution)/shard_map/ppermute | solution.py:20
  186.9 1.2 fusion.23
  188.9 3.5 %collective-permute-start.17 = (bf16[34,4096]{1,0:T(8,128)(2,1)S(1)}, bf16[34,4096]{1,0:T(8,128)(2,1)S(1)}, u32[]{:S(2)}, u32[]{:S(2)}) collective-permute-start(bf16[34,4096]{1,0:T(8,128)(2,1)S(1)} %get-tuple-element.72), channel_id=1, source_target_pairs={{0,128},{64,192},{128,0},{192,64},{256,384},{320,448},{384,256},{4... | collective-permute-start | bytes 835592 | tf_op jit(solution)/shard_map/ppermute | solution.py:20
  192.4 2.2 collective-permute-start.16
  194.6 3.5 %collective-permute-start.18 = (bf16[34,4096]{1,0:T(8,128)(2,1)S(1)}, bf16[34,4096]{1,0:T(8,128)(2,1)S(1)}, u32[]{:S(2)}, u32[]{:S(2)}) collective-permute-start(bf16[34,4096]{1,0:T(8,128)(2,1)S(1)} %get-tuple-element.72), channel_id=1, source_target_pairs={{0,192},{64,128},{128,64},{192,0},{256,448},{320,384},{384,320},{4... | collective-permute-start | bytes 835592 | tf_op jit(solution)/shard_map/ppermute | solution.py:20
  198.2 1.0 fusion.6
  199.2 10.6 %collective-permute-start.13 = (bf16[512,512]{0,1:T(8,128)(2,1)}, bf16[512,512]{0,1:T(8,128)(2,1)S(1)}, u32[]{:S(2)}, u32[]{:S(2)}) collective-permute-start(bf16[512,512]{0,1:T(8,128)(2,1)} %fusion.6), channel_id=1, source_target_pairs={{8,0},{16,8},{24,16},{32,24},{40,32},{48,40},{56,48},{0,56},{9,1},... | collective-permute-start | bytes 1572872 | tf_op jit(solution)/shard_map/ppermute | solution.py:16
  212.8 1.5 fusion.11
  215.1 7.2 %collective-permute-done.13 = bf16[512,512]{0,1:T(8,128)(2,1)S(1)} collective-permute-done((bf16[512,512]{0,1:T(8,128)(2,1)}, bf16[512,512]{0,1:T(8,128)(2,1)S(1)}, u32[]{:S(2)}, u32[]{:S(2)}) %collective-permute-start.13) | collective-permute-done | bytes 524320 | tf_op jit(solution)/shard_map/ppermute | solution.py:16
  222.2 1.0 copy.60
  223.3 1.8 reduce_sum.57
  (115 shorter events, 19.5 us)
Async XLA Ops:
  0.6 95.5 %copy-start = (f32[128,8]{0,1:T(8,128)S(1)}, f32[128,8]{0,1:T(8,128)}, u32[]{:S(2)}) copy-start(f32[128,8]{0,1:T(8,128)} %param.13) | copy-start | bytes 12292
  0.6 8.6 %copy-start.16 = (bf16[1,1,512,64]{2,3,1,0:T(8,128)(2,1)S(1)}, bf16[1,1,512,64]{2,3,1,0:T(8,128)(2,1)}, u32[]{:S(2)}) copy-start(bf16[1,1,512,64]{2,3,1,0:T(8,128)(2,1)} %param.9) | copy-start | bytes 196612
  0.7 17.4 %copy-start.11 = (bf16[1,1,512,512]{3,2,1,0:T(8,128)(2,1)S(1)}, bf16[1,1,512,512]{3,2,1,0:T(8,128)(2,1)}, u32[]{:S(2)}) copy-start(bf16[1,1,512,512]{3,2,1,0:T(8,128)(2,1)} %param.8) | copy-start | bytes 1572868
  4.4 25.5 %all-to-all-start = ((bf16[4,16,4096]{2,1,0:T(8,128)(2,1)}), bf16[4,16,4096]{2,1,0:T(8,128)(2,1)S(1)}, u32[]{:S(2)}, u32[]{:S(2)}) async-start(bf16[4,16,4096]{2,1,0:T(8,128)(2,1)} %get-tuple-element.24), calls=%async_computation | async-start | bytes 1048576 | tf_op jit(solution)/shard_map/all_to_all | solution.py:25
  9.2 20.6 %collective-permute-start = (bf16[64,512]{1,0:T(8,128)(2,1)S(1)}, bf16[64,512]{1,0:T(8,128)(2,1)S(1)}, u32[]{:S(2)}, u32[]{:S(2)}) collective-permute-start(bf16[64,512]{1,0:T(8,128)(2,1)S(1)} %bitcast.171), channel_id=1, source_target_pairs={{0,4},{1,5},{2,6},{3,7},{4,0},{5,1},{6,2},{7,3},{8,12},{9,13},{10,... | collective-permute-start | bytes 196616 | tf_op jit(solution)/shard_map/ppermute | solution.py:20
  18.4 3.2 %collective-permute-start.1 = (f32[4,128]{1,0:T(4,128)S(1)}, f32[4,128]{1,0:T(4,128)S(1)}, u32[]{:S(2)}, u32[]{:S(2)}) collective-permute-start(f32[4,128]{1,0:T(4,128)S(1)} %bitcast.179), channel_id=1, source_target_pairs={{56,0},{0,8},{8,16},{16,24},{24,32},{32,40},{40,48},{48,56},{57,1}... | collective-permute-start | bytes 6152 | tf_op jit(solution)/shard_map/ppermute | solution.py:16
  21.5 8.2 %collective-permute-start.2 = (f32[1,512]{1,0:T(1,128)S(1)}, f32[1,512]{1,0:T(1,128)S(1)}, u32[]{:S(2)}, u32[]{:S(2)}) collective-permute-start(f32[1,512]{1,0:T(1,128)S(1)} %bitcast.180), channel_id=1, source_target_pairs={{0,4},{1,5},{2,6},{3,7},{4,0},{5,1},{6,2},{7,3},{8,12},{9,13},{10,... | collective-permute-start | bytes 6152 | tf_op jit(solution)/shard_map/ppermute | solution.py:20
  29.9 27.7 %copy-start.9 = (bf16[16,4096]{1,0:T(8,128)(2,1)}, bf16[16,4096]{1,0:T(8,128)(2,1)S(1)}, u32[]{:S(2)}) copy-start(bf16[16,4096]{1,0:T(8,128)(2,1)S(1)} %reduce_sum.54) | copy-start | bytes 393220
  30.0 8.8 %collective-permute-start.3 = (bf16[136,512]{1,0:T(8,128)(2,1)S(1)}, bf16[136,512]{1,0:T(8,128)(2,1)S(1)}, u32[]{:S(2)}, u32[]{:S(2)}) collective-permute-start(bf16[136,512]{1,0:T(8,128)(2,1)S(1)} %pad_maximum_fusion.6), channel_id=1, source_target_pairs={{0,2},{1,3},{2,0},{3,1},{4,6},{5,7},{6,4},{7,5},{8,10},{9,11},{10,... | collective-permute-start | bytes 417800 | tf_op jit(solution)/shard_map/ppermute | solution.py:20
  34.9 32.2 %collective-permute-start.9 = (bf16[512,512]{0,1:T(8,128)(2,1)S(1)}, bf16[512,512]{0,1:T(8,128)(2,1)S(1)}, u32[]{:S(2)}, u32[]{:S(2)}) collective-permute-start(bf16[512,512]{0,1:T(8,128)(2,1)S(1)} %bitcast.147), channel_id=1, source_target_pairs={{56,0},{0,8},{8,16},{16,24},{24,32},{32,40},{40,48},{48,56},{57,1}... | collective-permute-start | bytes 1572872 | tf_op jit(solution)/shard_map/ppermute | solution.py:16
  39.0 29.8 %all-to-all-start.1 = ((bf16[4,2,16,4096]{3,2,1,0:T(8,128)(2,1)}), bf16[4,2,16,4096]{3,2,1,0:T(8,128)(2,1)S(1)}, u32[]{:S(2)}, u32[]{:S(2)}) async-start(bf16[4,2,16,4096]{3,2,1,0:T(8,128)(2,1)} %get-tuple-element.33), calls=%async_computation.1 | async-start | bytes 2097152 | tf_op jit(solution)/shard_map/all_to_all | solution.py:25
  43.5 14.1 %collective-permute-start.4 = (bf16[16,3072]{1,0:T(8,128)(2,1)S(1)}, bf16[16,3072]{1,0:T(8,128)(2,1)S(1)}, u32[]{:S(2)}, u32[]{:S(2)}) collective-permute-start(bf16[16,3072]{1,0:T(8,128)(2,1)S(1)} %slice.54), channel_id=1, source_target_pairs={{0,256},{64,320},{128,384},{192,448},{256,0},{320,64},{384,128},{4... | collective-permute-start | bytes 294920 | tf_op jit(solution)/shard_map/ppermute | solution.py:20
  53.5 13.4 %collective-permute-start.8 = (bf16[264,512]{1,0:T(8,128)(2,1)S(1)}, bf16[264,512]{1,0:T(8,128)(2,1)S(1)}, u32[]{:S(2)}, u32[]{:S(2)}) collective-permute-start(bf16[264,512]{1,0:T(8,128)(2,1)S(1)} %pad_maximum_fusion.3), channel_id=1, source_target_pairs={{0,1},{1,0},{2,3},{3,2},{4,5},{5,4},{6,7},{7,6},{8,9},{9,8},{10,11... | collective-permute-start | bytes 811016 | tf_op jit(solution)/shard_map/ppermute | solution.py:20
  67.1 0.8 copy-start.8
  67.1 1.6 copy-start.5
  68.8 3.7 %slice-start = ((bf16[16,4096]{1,0:T(8,128)(2,1)}), bf16[16,1024]{1,0:T(8,128)(2,1)S(1)}, s32[]{:S(2)}) async-start(bf16[16,4096]{1,0:T(8,128)(2,1)} %copy-done.9), calls=%async_computation.5 | async-start | bytes 65536 | tf_op jit(solution)/shard_map/slice | solution.py:205
  69.0 16.6 %all-to-all-start.2 = ((bf16[4,8,16,512]{3,2,1,0:T(8,128)(2,1)}), bf16[4,8,16,512]{3,2,1,0:T(8,128)(2,1)S(1)}, u32[]{:S(2)}, u32[]{:S(2)}) async-start(bf16[4,8,16,512]{3,2,1,0:T(8,128)(2,1)} %bitcast.131), calls=%async_computation.2 | async-start | bytes 1048576 | tf_op jit(solution)/shard_map/all_to_all | solution.py:25
  72.5 13.1 %copy-start.10 = (bf16[16,4096]{1,0:T(8,128)(2,1)}, bf16[16,4096]{1,0:T(8,128)(2,1)S(1)}, u32[]{:S(2)}) copy-start(bf16[16,4096]{1,0:T(8,128)(2,1)S(1)} %pad_maximum_fusion.8.fresh0_ref) | copy-start | bytes 393220
  72.5 10.9 %collective-permute-start.7 = (bf16[16,4096]{1,0:T(8,128)(2,1)S(1)}, bf16[16,4096]{1,0:T(8,128)(2,1)S(1)}, u32[]{:S(2)}, u32[]{:S(2)}) collective-permute-start(bf16[16,4096]{1,0:T(8,128)(2,1)S(1)} %pad_maximum_fusion.8.fresh0_ref), channel_id=1, source_target_pairs={{0,192},{64,128},{128,64},{192,0},{256,448},{320,384},{384,320},{4... | collective-permute-start | bytes 393224 | tf_op jit(solution)/shard_map/ppermute | solution.py:20
  77.1 8.3 %collective-permute-start.6 = (bf16[16,4096]{1,0:T(8,128)(2,1)S(1)}, bf16[16,4096]{1,0:T(8,128)(2,1)S(1)}, u32[]{:S(2)}, u32[]{:S(2)}) collective-permute-start(bf16[16,4096]{1,0:T(8,128)(2,1)S(1)} %pad_maximum_fusion.8.fresh0_ref), channel_id=1, source_target_pairs={{0,128},{64,192},{128,0},{192,64},{256,384},{320,448},{384,256},{4... | collective-permute-start | bytes 393224 | tf_op jit(solution)/shard_map/ppermute | solution.py:20
  79.6 6.0 %collective-permute-start.5 = (bf16[16,4096]{1,0:T(8,128)(2,1)S(1)}, bf16[16,4096]{1,0:T(8,128)(2,1)S(1)}, u32[]{:S(2)}, u32[]{:S(2)}) collective-permute-start(bf16[16,4096]{1,0:T(8,128)(2,1)S(1)} %pad_maximum_fusion.8.fresh0_ref), channel_id=1, source_target_pairs={{0,64},{64,0},{128,192},{192,128},{256,320},{320,256},{384,448},{4... | collective-permute-start | bytes 393224 | tf_op jit(solution)/shard_map/ppermute | solution.py:20
  83.5 2.1 copy-start.13
  85.4 0.7 copy-start.14
  85.6 0.6 copy-start.15
  86.2 0.8 copy-start.4
  89.9 6.2 %copy-start.12 = (bf16[64,4096]{1,0:T(8,128)(2,1)S(1)}, bf16[64,4096]{1,0:T(8,128)(2,1)}, u32[]{:S(2)}) copy-start(bf16[64,4096]{1,0:T(8,128)(2,1)} %get-tuple-element.37) | copy-start | bytes 1572868
  89.9 39.8 %all-to-all-start.3 = ((bf16[8,80,512]{2,1,0:T(8,128)(2,1)}), bf16[8,80,512]{2,1,0:T(8,128)(2,1)S(1)}, u32[]{:S(2)}, u32[]{:S(2)}) async-start(bf16[8,80,512]{2,1,0:T(8,128)(2,1)} %get-tuple-element.35), calls=%async_computation.3 | async-start | bytes 1310720 | tf_op jit(solution)/shard_map/all_to_all | solution.py:238
  96.0 9.4 %copy-start.2 = (f32[1,1,64,4096]{3,2,1,0:T(8,128)S(1)}, f32[1,1,64,4096]{3,2,1,0:T(8,128)}, u32[]{:S(2)}) copy-start(f32[1,1,64,4096]{3,2,1,0:T(8,128)} %param.12) | copy-start | bytes 3145732
  100.5 16.1 %collective-permute-start.15 = (bf16[2,16,3072]{2,1,0:T(8,128)(2,1)}, bf16[2,16,3072]{2,1,0:T(8,128)(2,1)}, u32[]{:S(2)}, u32[]{:S(2)}) collective-permute-start(bf16[2,16,3072]{2,1,0:T(8,128)(2,1)} %slice.63), channel_id=1, source_target_pairs={{0,256},{64,320},{128,384},{192,448},{256,0},{320,64},{384,128},{4... | collective-permute-start | bytes 589832 | tf_op jit(solution)/shard_map/ppermute | solution.py:20
  105.7 4.4 %copy-start.1 = (f32[1,1,64,4096]{3,2,1,0:T(8,128)S(1)}, f32[1,1,64,4096]{3,2,1,0:T(8,128)}, u32[]{:S(2)}) copy-start(f32[1,1,64,4096]{3,2,1,0:T(8,128)} %param.11) | copy-start | bytes 3145732
  129.6 0.8 copy-start.3
  130.5 39.4 %copy-start.6 = (bf16[512,512]{0,1:T(8,128)(2,1)S(1)}, bf16[512,512]{0,1:T(8,128)(2,1)}, u32[]{:S(2)}) copy-start(bf16[512,512]{0,1:T(8,128)(2,1)} %copy-done.5) | copy-start | bytes 1572868
  132.3 16.1 %collective-permute-start.10 = (f32[4,128]{1,0:T(4,128)S(1)}, f32[4,128]{1,0:T(4,128)S(1)}, u32[]{:S(2)}, u32[]{:S(2)}) collective-permute-start(f32[4,128]{1,0:T(4,128)S(1)} %bitcast.178), channel_id=1, source_target_pairs={{0,1},{1,0},{2,3},{3,2},{4,5},{5,4},{6,7},{7,6},{8,9},{9,8},{10,11... | collective-permute-start | bytes 6152 | tf_op jit(solution)/shard_map/ppermute | solution.py:20
  144.6 42.3 %collective-permute-start.14 = (bf16[16,4096]{1,0:T(8,128)(2,1)S(1)}, bf16[16,4096]{1,0:T(8,128)(2,1)S(1)}, u32[]{:S(2)}, u32[]{:S(2)}) collective-permute-start(bf16[16,4096]{1,0:T(8,128)(2,1)S(1)} %bitcast.166), channel_id=1, source_target_pairs={{0,256},{64,320},{128,384},{192,448},{256,0},{320,64},{384,128},{4... | collective-permute-start | bytes 393224 | tf_op jit(solution)/shard_map/ppermute | solution.py:20
  148.3 0.6 copy-start.17
  149.5 29.4 %collective-permute-start.11 = (f32[4,128]{1,0:T(4,128)}, f32[4,128]{1,0:T(4,128)}, u32[]{:S(2)}, u32[]{:S(2)}) collective-permute-start(f32[4,128]{1,0:T(4,128)} %bitcast_add_fusion.2), channel_id=1, source_target_pairs={{0,2},{1,3},{2,0},{3,1},{4,6},{5,7},{6,4},{7,5},{8,10},{9,11},{10,... | collective-permute-start | bytes 6152 | tf_op jit(solution)/shard_map/ppermute | solution.py:20
  171.1 52.1 %all-to-all-start.4 = ((bf16[8,64,512]{2,1,0:T(8,128)(2,1)}), bf16[8,64,512]{2,1,0:T(8,128)(2,1)}, u32[]{:S(2)}, u32[]{:S(2)}) async-start(bf16[8,64,512]{2,1,0:T(8,128)(2,1)} %bitcast.161), calls=%async_computation.4 | async-start | bytes 1048576 | tf_op jit(solution)/shard_map/all_to_all | solution.py:252
  178.9 19.3 %copy-start.7 = (bf16[512,512]{0,1:T(8,128)(2,1)S(1)}, bf16[512,512]{0,1:T(8,128)(2,1)}, u32[]{:S(2)}) copy-start(bf16[512,512]{0,1:T(8,128)(2,1)} %copy-done.5) | copy-start | bytes 1572868
  179.6 18.5 %collective-permute-start.12 = (f32[4,128]{1,0:T(4,128)S(1)}, f32[4,128]{1,0:T(4,128)S(1)}, u32[]{:S(2)}, u32[]{:S(2)}) collective-permute-start(f32[4,128]{1,0:T(4,128)S(1)} %fusion.48), channel_id=1, source_target_pairs={{0,4},{1,5},{2,6},{3,7},{4,0},{5,1},{6,2},{7,3},{8,12},{9,13},{10,... | collective-permute-start | bytes 6152 | tf_op jit(solution)/shard_map/ppermute | solution.py:20
  188.9 20.9 %collective-permute-start.17 = (bf16[34,4096]{1,0:T(8,128)(2,1)S(1)}, bf16[34,4096]{1,0:T(8,128)(2,1)S(1)}, u32[]{:S(2)}, u32[]{:S(2)}) collective-permute-start(bf16[34,4096]{1,0:T(8,128)(2,1)S(1)} %get-tuple-element.72), channel_id=1, source_target_pairs={{0,128},{64,192},{128,0},{192,64},{256,384},{320,448},{384,256},{4... | collective-permute-start | bytes 835592 | tf_op jit(solution)/shard_map/ppermute | solution.py:20
  192.4 17.4 %collective-permute-start.16 = (bf16[34,4096]{1,0:T(8,128)(2,1)S(1)}, bf16[34,4096]{1,0:T(8,128)(2,1)S(1)}, u32[]{:S(2)}, u32[]{:S(2)}) collective-permute-start(bf16[34,4096]{1,0:T(8,128)(2,1)S(1)} %get-tuple-element.72), channel_id=1, source_target_pairs={{0,64},{64,0},{128,192},{192,128},{256,320},{320,256},{384,448},{4... | collective-permute-start | bytes 835592 | tf_op jit(solution)/shard_map/ppermute | solution.py:20
  194.6 15.2 %collective-permute-start.18 = (bf16[34,4096]{1,0:T(8,128)(2,1)S(1)}, bf16[34,4096]{1,0:T(8,128)(2,1)S(1)}, u32[]{:S(2)}, u32[]{:S(2)}) collective-permute-start(bf16[34,4096]{1,0:T(8,128)(2,1)S(1)} %get-tuple-element.72), channel_id=1, source_target_pairs={{0,192},{64,128},{128,64},{192,0},{256,448},{320,384},{384,320},{4... | collective-permute-start | bytes 835592 | tf_op jit(solution)/shard_map/ppermute | solution.py:20
  199.2 23.1 %collective-permute-start.13 = (bf16[512,512]{0,1:T(8,128)(2,1)}, bf16[512,512]{0,1:T(8,128)(2,1)S(1)}, u32[]{:S(2)}, u32[]{:S(2)}) collective-permute-start(bf16[512,512]{0,1:T(8,128)(2,1)} %fusion.6), channel_id=1, source_target_pairs={{8,0},{16,8},{24,16},{32,24},{40,32},{48,40},{56,48},{0,56},{9,1},... | collective-permute-start | bytes 1572872 | tf_op jit(solution)/shard_map/ppermute | solution.py:16

commit v15 on v9

--- a/solution.py
+++ b/solution.py
@@ -37,11 +37,20 @@
     return held
 
 
-def doubled(held, mine, axis):
+def doubled(held, mine, axis, part=None):
     bit = 4 >> axis
-    came = swap(held, "tensor", bit)
-    high = (mine & bit) != 0
-    return jnp.stack([jnp.where(high, came, held), jnp.where(high, held, came)], axis=axis)
+    sent = held
+    if part is not None:
+        high, low = two_halves(part)
+        rows = held.reshape(-1, held.shape[-1])
+        sent = jnp.concatenate([rows, high, low, jnp.zeros((6, held.shape[-1]), SHORT)], axis=0)
+    came = swap(sent, "tensor", bit)
+    if part is not None:
+        part = part + came[-8:-7].astype(WIDE) + came[-7:-6].astype(WIDE)
+        came = came[:-8].reshape(held.shape)
+    upper = (mine & bit) != 0
+    held = jnp.stack([jnp.where(upper, came, held), jnp.where(upper, held, came)], axis=axis)
+    return held if part is None else (held, part)
 
 
 def gather_x(block):
@@ -182,18 +191,16 @@
     mask = serve(failed_replica, resend_spans, own_weight, own_first, own_second)
     served = jnp.sum(exchange_x(mask).astype(WIDE), axis=0).astype(SHORT)
 
-    high, low = two_halves(squares)
-    extra = jnp.concatenate([high, low, jnp.zeros((6, tokens), SHORT)], axis=0)
-    held = jnp.concatenate([tied(key_grads[0, 0].T, mask), extra], axis=0)
-    held = doubled(doubled(held, my_tensor, 0), my_tensor, 1)
+    held = doubled(tied(key_grads[0, 0].T, mask), my_tensor, 0)
+    held, squares = doubled(held, my_tensor, 1, squares)
     held, served = lax.optimization_barrier((held, served))
     cross = width - my_spans.shape[0] * SPAN
     crossed = served[:, :, :cross] + swap(served[:, :, :cross], "replica", PLANE)
     fresh = jnp.concatenate([crossed, served[:, :, cross:]], axis=2)
     fresh_weight = [fresh[0]] + [swap(fresh[0], "replica", bit) for bit in (1, 2, 3)]
-    held = doubled(held, my_tensor, 2).reshape(8, -1, tokens)
-    kg_all = held[:, :rows].reshape(8 * rows, tokens)
-    squares = jnp.sum(held[:, rows].astype(WIDE) + held[:, rows + 1].astype(WIDE), axis=0)
+    held, squares = doubled(held, my_tensor, 2, squares)
+    kg_all = held.reshape(8 * rows, tokens)
+    squares = (squares + swap(squares, "tensor", 4)).reshape(tokens)
     inverse_rms = 1.0 / jnp.sqrt(squares / width + 1e-05)
 
     normed = (x * inverse_rms[:, None]).astype(SHORT)

time: 206 us -> 208 us (level)
  starting transfers between devices: 114 us -> 127 us
  waiting for transfers between devices: 39.5 us -> 29.1 us
  other arithmetic: 7.72 us -> 11.6 us
  local copies, waits for them, and re-layouts: 15.7 us -> 13.3 us
  matrix products: 17.2 us -> 15 us
    ppermute x14 -> x15, waiting for transfers between devices: 36.6 us -> 22.1 us  [swap(): lax.ppermute(block, axis, [(i, i ^ bit) for i in range(lax.axis_size(axis...]
    ppermute x14 -> x15, starting transfers between devices: 74 us -> 82.3 us  [swap(): lax.ppermute(block, axis, [(i, i ^ bit) for i in range(lax.axis_size(axis...]
    all_to_all x1, starting transfers between devices: 9.49 us -> 13.6 us  [shards(): got = lax.all_to_all(sent, 'tensor', 0, 0, tiled=True)]
    all_to_all x1, waiting for transfers between devices: 0.01 us -> 4 us  [shards(): got = lax.all_to_all(sent, 'tensor', 0, 0, tiled=True)]
  transfers between devices with their start and end apart: 21 -> 22, of which waited for: 6 -> 6; matrix products, arithmetic and copies ran while one was open for 17% -> 15% of each run, Pallas kernels for 3% -> 3%
where the time goes in v15:
time: 208 us; the launch traced here: 207 us
  starting transfers between devices  127 us (61%)
  waiting for transfers between devices  29.1 us (14%)
  matrix products  15 us (7%)
  local copies, waits for them, and re-layouts  13.3 us (6%)
  other arithmetic  11.6 us (6%)
  Pallas kernels  8.41 us (4%)
    ppermute x15, starting transfers between devices, swap(): lax.ppermute(block, axis, [(i, i ^ bit) for i in range(lax.axis_size(axis...  82.3 us
    ppermute x15, waiting for transfers between devices, swap(): lax.ppermute(block, axis, [(i, i ^ bit) for i in range(lax.axis_size(axis...  22.1 us
    ppermute x3, starting transfers between devices, from_behind(): lax.ppermute(block, axis, [((i - distance) % n, i) for i in range(n)])  15.5 us
    all_to_all x1, starting transfers between devices, shards(): got = lax.all_to_all(sent, 'tensor', 0, 0, tiled=True)  13.6 us
    dot_general x4, matrix products, checksum(): jnp.einsum('jnc,cp->jnp', shaped, probe_matrix, precision=lax.Precision.H...  11.6 us
    all_to_all x2, starting transfers between devices, exchange_x(): lax.all_to_all(block, 'replica', 0, 0, axis_index_groups=groups, tiled=True)  8.88 us
    unnamed x42, local copies, waits for them, and re-layouts  7.33 us
    all_to_all x1, starting transfers between devices, shards(): lax.all_to_all(keys.reshape(8, rows, tokens), 'tensor', 0, 0, tiled=True)  6.98 us
  transfers between devices with their start and end apart: 22, of which 6 were waited for; matrix products, arithmetic and copies ran while one was open for 15% of the time, Pallas kernels for 3%

profile of v15, /device:TPU:1, one launch (start us, length us, event | category | flops | bytes accessed | tf_op | source)
XLA Modules:
  0.0 206.7 jit_solution(2433102468545125504)
XLA Ops:
  0.6 1.3 copy.43
  2.1 2.7 %collective-permute-start.1 = (f32[4,128]{1,0:T(4,128)S(1)}, f32[4,128]{1,0:T(4,128)S(1)}, u32[]{:S(2)}, u32[]{:S(2)}) collective-permute-start(f32[4,128]{1,0:T(4,128)S(1)} %bitcast.183), channel_id=1, source_target_pairs={{56,0},{0,8},{8,16},{16,24},{24,32},{32,40},{40,48},{48,56},{57,1}... | collective-permute-start | bytes 6152 | tf_op jit(solution)/shard_map/ppermute | solution.py:16
  4.8 3.7 %serve.1 = bf16[4,3,16,4096]{3,2,1,0:T(8,128)(2,1)} custom-call(s32[8,8]{1,0:T(8,128)} %failed_ref.3, s32[8,8]{1,0:T(8,128)} %spans_ref.5, bf16[64,4096]{1,0:T(8,128)(2,1)} %bitcast.152, f32[64,4096]{1,0:T(8,128)} %bitcast.133, f32[64,4096]{1,0:T(8,128)} %bitcast.136), custom_call_target="tpu_custom_call" | custom-call | tf_op jit(solution)/shard_map/serve/pallas_call | solution.py:100
  8.4 4.1 %all-to-all-start = ((bf16[4,3,16,4096]{3,2,1,0:T(8,128)(2,1)}), bf16[4,3,16,4096]{3,2,1,0:T(8,128)(2,1)S(1)}, u32[]{:S(2)}, u32[]{:S(2)}) async-start(bf16[4,3,16,4096]{3,2,1,0:T(8,128)(2,1)} %serve.1), calls=%async_computation | async-start | bytes 3145728 | tf_op jit(solution)/shard_map/all_to_all | solution.py:25
  12.6 8.8 %collective-permute-start = (bf16[64,512]{1,0:T(8,128)(2,1)S(1)}, bf16[64,512]{1,0:T(8,128)(2,1)S(1)}, u32[]{:S(2)}, u32[]{:S(2)}) collective-permute-start(bf16[64,512]{1,0:T(8,128)(2,1)S(1)} %bitcast.172), channel_id=1, source_target_pairs={{0,4},{1,5},{2,6},{3,7},{4,0},{5,1},{6,2},{7,3},{8,12},{9,13},{10,... | collective-permute-start | bytes 196616 | tf_op jit(solution)/shard_map/ppermute | solution.py:20
  21.4 1.6 collective-permute-done
  23.1 6.7 %collective-permute-start.2 = (bf16[136,512]{1,0:T(8,128)(2,1)S(1)}, bf16[136,512]{1,0:T(8,128)(2,1)S(1)}, u32[]{:S(2)}, u32[]{:S(2)}) collective-permute-start(bf16[136,512]{1,0:T(8,128)(2,1)S(1)} %pad_maximum_fusion.6), channel_id=1, source_target_pairs={{0,2},{1,3},{2,0},{3,1},{4,6},{5,7},{6,4},{7,5},{8,10},{9,11},{10,... | collective-permute-start | bytes 417800 | tf_op jit(solution)/shard_map/ppermute | solution.py:20
  29.8 2.7 %collective-permute-done.2 = bf16[136,512]{1,0:T(8,128)(2,1)S(1)} collective-permute-done((bf16[136,512]{1,0:T(8,128)(2,1)S(1)}, bf16[136,512]{1,0:T(8,128)(2,1)S(1)}, u32[]{:S(2)}, u32[]{:S(2)}) %collective-permute-start.2) | collective-permute-done | bytes 139296 | tf_op jit(solution)/shard_map/ppermute | solution.py:20
  33.0 6.8 %collective-permute-start.7 = (bf16[264,512]{1,0:T(8,128)(2,1)S(1)}, bf16[264,512]{1,0:T(8,128)(2,1)S(1)}, u32[]{:S(2)}, u32[]{:S(2)}) collective-permute-start(bf16[264,512]{1,0:T(8,128)(2,1)S(1)} %pad_maximum_fusion.4), channel_id=1, source_target_pairs={{0,1},{1,0},{2,3},{3,2},{4,5},{5,4},{6,7},{7,6},{8,9},{9,8},{10,11... | collective-permute-start | bytes 811016 | tf_op jit(solution)/shard_map/ppermute | solution.py:20
  39.8 2.0 collective-permute-start.8
  41.8 14.4 %collective-permute-start.3 = (bf16[3,16,3072]{2,1,0:T(8,128)(2,1)S(1)}, bf16[3,16,3072]{2,1,0:T(8,128)(2,1)S(1)}, u32[]{:S(2)}, u32[]{:S(2)}) collective-permute-start(bf16[3,16,3072]{2,1,0:T(8,128)(2,1)S(1)} %slice.56), channel_id=1, source_target_pairs={{0,256},{64,320},{128,384},{192,448},{256,0},{320,64},{384,128},{4... | collective-permute-start | bytes 884744 | tf_op jit(solution)/shard_map/ppermute | solution.py:20
  56.2 3.1 %collective-permute-start.9 = (f32[1,512]{1,0:T(1,128)S(1)}, f32[1,512]{1,0:T(1,128)S(1)}, u32[]{:S(2)}, u32[]{:S(2)}) collective-permute-start(f32[1,512]{1,0:T(1,128)S(1)} %fusion.37), channel_id=1, source_target_pairs={{0,4},{1,5},{2,6},{3,7},{4,0},{5,1},{6,2},{7,3},{8,12},{9,13},{10,... | collective-permute-start | bytes 6152 | tf_op jit(solution)/shard_map/ppermute | solution.py:20
  59.4 12.3 %collective-permute-done.9 = f32[1,512]{1,0:T(1,128)S(1)} collective-permute-done((f32[1,512]{1,0:T(1,128)S(1)}, f32[1,512]{1,0:T(1,128)S(1)}, u32[]{:S(2)}, u32[]{:S(2)}) %collective-permute-start.9) | collective-permute-done | bytes 2080 | tf_op jit(solution)/shard_map/ppermute | solution.py:20
  72.3 0.8 copy.73
  73.1 4.7 %all-to-all-start.1 = ((bf16[4,8,16,512]{3,2,1,0:T(8,128)(2,1)}), bf16[4,8,16,512]{3,2,1,0:T(8,128)(2,1)S(1)}, u32[]{:S(2)}, u32[]{:S(2)}) async-start(bf16[4,8,16,512]{3,2,1,0:T(8,128)(2,1)} %bitcast.132), calls=%async_computation.1 | async-start | bytes 1048576 | tf_op jit(solution)/shard_map/all_to_all | solution.py:25
  77.9 4.6 %collective-permute-start.6 = (bf16[16,4096]{1,0:T(8,128)(2,1)S(1)}, bf16[16,4096]{1,0:T(8,128)(2,1)S(1)}, u32[]{:S(2)}, u32[]{:S(2)}) collective-permute-start(bf16[16,4096]{1,0:T(8,128)(2,1)S(1)} %fusion.25.fresh0_ref), channel_id=1, source_target_pairs={{0,192},{64,128},{128,64},{192,0},{256,448},{320,384},{384,320},{4... | collective-permute-start | bytes 393224 | tf_op jit(solution)/shard_map/ppermute | solution.py:20
  82.5 2.5 %collective-permute-start.5 = (bf16[16,4096]{1,0:T(8,128)(2,1)S(1)}, bf16[16,4096]{1,0:T(8,128)(2,1)S(1)}, u32[]{:S(2)}, u32[]{:S(2)}) collective-permute-start(bf16[16,4096]{1,0:T(8,128)(2,1)S(1)} %fusion.25.fresh0_ref), channel_id=1, source_target_pairs={{0,128},{64,192},{128,0},{192,64},{256,384},{320,448},{384,256},{4... | collective-permute-start | bytes 393224 | tf_op jit(solution)/shard_map/ppermute | solution.py:20
  85.0 1.9 collective-permute-start.4
  86.9 5.4 %collective-permute-done.6.fresh3_ref = bf16[16,4096]{1,0:T(8,128)(2,1)S(1)} collective-permute-done((bf16[16,4096]{1,0:T(8,128)(2,1)S(1)}, bf16[16,4096]{1,0:T(8,128)(2,1)S(1)}, u32[]{:S(2)}, u32[]{:S(2)}) %collective-permute-start.6) | collective-permute-done | bytes 131104 | tf_op jit(solution)/shard_map/ppermute | solution.py:20
  93.9 2.8 %assemble.1 = (bf16[8,80,512]{2,1,0:T(8,128)(2,1)}, bf16[64,4096]{1,0:T(8,128)(2,1)}) custom-call(s32[8,8]{1,0:T(8,128)} %failed_ref.3, s32[8,8]{1,0:T(8,128)} %spans_ref.5, bf16[64,4096]{1,0:T(8,128)(2,1)} %bitcast.153, bf16[16,4096]{1,0:T(8,128)(2,1)} %copy-done.11, bf16[16,4096]{1,0:T(8,128)(2,1)} %copy-done.14, bf16[16,4096]{1,0:T(8,128)(2,1)} %copy-done.13, ...), custom_call_target="tpu_custom_call" | custom-call | tf_op jit(solution)/shard_map/assemble/pallas_call | solution.py:151
  96.7 13.6 %all-to-all-start.2 = ((bf16[8,80,512]{2,1,0:T(8,128)(2,1)}), bf16[8,80,512]{2,1,0:T(8,128)(2,1)S(1)}, u32[]{:S(2)}, u32[]{:S(2)}) async-start(bf16[8,80,512]{2,1,0:T(8,128)(2,1)} %get-tuple-element.17), calls=%async_computation.2 | async-start | bytes 1310720 | tf_op jit(solution)/shard_map/all_to_all | solution.py:213
  110.3 1.3 dynamic_slice.3
  113.0 1.9 unpack.1
  115.0 2.1 %fusion.30 = f32[64,32,8]{1,2,0:T(8,128)S(1)} fusion(bf16[64,32,128]{2,1,0:T(8,128)(2,1)S(1)} %bitcast.147, f32[128,8]{0,1:T(8,128)S(1)} %copy-done), kind=kOutput, calls=%fused_computation.66 | convolution fusion | flops 25165824 | bytes 593920 | tf_op jit(solution)/shard_map/jnc,cp->jnp/dot_general | solution.py:232
  118.0 0.8 convert_element_type.155
  118.9 1.1 convolution_convert_fusion.2
  120.2 0.9 convert_element_type.158
  121.3 4.2 %fusion.32 = f32[64,32,8]{1,2,0:T(8,128)S(1)} fusion(f32[64,32,128]{2,1,0:T(8,128)S(1)} %bitcast.142, f32[128,8]{0,1:T(8,128)S(1)} %copy-done), kind=kOutput, calls=%fused_computation.68 | convolution fusion | flops 25165824 | bytes 1118208 | tf_op jit(solution)/shard_map/jnc,cp->jnp/dot_general | solution.py:232
  125.9 4.2 %fusion.34 = f32[64,32,8]{1,2,0:T(8,128)S(1)} fusion(f32[64,32,128]{2,1,0:T(8,128)S(1)} %bitcast.143, f32[128,8]{0,1:T(8,128)S(1)} %copy-done), kind=kOutput, calls=%fused_computation.70 | convolution fusion | flops 25165824 | bytes 1118208 | tf_op jit(solution)/shard_map/jnc,cp->jnp/dot_general | solution.py:232
  130.3 4.0 %all-to-all-done.2 = bf16[8,80,512]{2,1,0:T(8,128)(2,1)S(1)} async-done(((bf16[8,80,512]{2,1,0:T(8,128)(2,1)}), bf16[8,80,512]{2,1,0:T(8,128)(2,1)S(1)}, u32[]{:S(2)}, u32[]{:S(2)}) %all-to-all-start.2) | async-done | bytes 655392 | tf_op jit(solution)/shard_map/all_to_all | solution.py:213
  135.2 1.8 fusion.7
  136.9 10.0 %collective-permute-start.10 = (f32[4,128]{1,0:T(4,128)S(1)}, f32[4,128]{1,0:T(4,128)S(1)}, u32[]{:S(2)}, u32[]{:S(2)}) collective-permute-start(f32[4,128]{1,0:T(4,128)S(1)} %bitcast.182), channel_id=1, source_target_pairs={{0,1},{1,0},{2,3},{3,2},{4,5},{5,4},{6,7},{7,6},{8,9},{9,8},{10,11... | collective-permute-start | bytes 6152 | tf_op jit(solution)/shard_map/ppermute | solution.py:20
  147.0 0.9 slice_bitcast_fusion
  147.9 5.4 %collective-permute-start.14 = (bf16[16,4096]{1,0:T(8,128)(2,1)S(1)}, bf16[16,4096]{1,0:T(8,128)(2,1)S(1)}, u32[]{:S(2)}, u32[]{:S(2)}) collective-permute-start(bf16[16,4096]{1,0:T(8,128)(2,1)S(1)} %bitcast.167), channel_id=1, source_target_pairs={{0,256},{64,320},{128,384},{192,448},{256,0},{320,64},{384,128},{4... | collective-permute-start | bytes 393224 | tf_op jit(solution)/shard_map/ppermute | solution.py:20
  154.5 1.9 collective-permute-start.11
  156.5 1.2 convolution_convert_fusion
  157.7 7.0 %all-to-all-start.3 = ((bf16[8,64,512]{2,1,0:T(8,128)(2,1)}), bf16[8,64,512]{2,1,0:T(8,128)(2,1)}, u32[]{:S(2)}, u32[]{:S(2)}) async-start(bf16[8,64,512]{2,1,0:T(8,128)(2,1)} %bitcast.161), calls=%async_computation.3 | async-start | bytes 1048576 | tf_op jit(solution)/shard_map/all_to_all | solution.py:227
  165.4 7.3 %collective-permute-start.12 = (f32[4,128]{1,0:T(4,128)S(1)}, f32[4,128]{1,0:T(4,128)S(1)}, u32[]{:S(2)}, u32[]{:S(2)}) collective-permute-start(f32[4,128]{1,0:T(4,128)S(1)} %fusion.52), channel_id=1, source_target_pairs={{0,4},{1,5},{2,6},{3,7},{4,0},{5,1},{6,2},{7,3},{8,12},{9,13},{10,... | collective-permute-start | bytes 6152 | tf_op jit(solution)/shard_map/ppermute | solution.py:20
  172.7 1.2 fusion.23
  174.7 4.9 %collective-permute-start.16 = (bf16[34,4096]{1,0:T(8,128)(2,1)S(1)}, bf16[34,4096]{1,0:T(8,128)(2,1)S(1)}, u32[]{:S(2)}, u32[]{:S(2)}) collective-permute-start(bf16[34,4096]{1,0:T(8,128)(2,1)S(1)} %get-tuple-element.52), channel_id=1, source_target_pairs={{0,128},{64,192},{128,0},{192,64},{256,384},{320,448},{384,256},{4... | collective-permute-start | bytes 835592 | tf_op jit(solution)/shard_map/ppermute | solution.py:20
  179.6 2.2 %collective-permute-start.15 = (bf16[34,4096]{1,0:T(8,128)(2,1)S(1)}, bf16[34,4096]{1,0:T(8,128)(2,1)S(1)}, u32[]{:S(2)}, u32[]{:S(2)}) collective-permute-start(bf16[34,4096]{1,0:T(8,128)(2,1)S(1)} %get-tuple-element.52), channel_id=1, source_target_pairs={{0,64},{64,0},{128,192},{192,128},{256,320},{320,256},{384,448},{4... | collective-permute-start | bytes 835592 | tf_op jit(solution)/shard_map/ppermute | solution.py:20
  181.8 2.0 collective-permute-start.17
  183.8 1.0 fusion.6
  184.8 10.9 %collective-permute-start.13 = (bf16[512,512]{0,1:T(8,128)(2,1)}, bf16[512,512]{0,1:T(8,128)(2,1)S(1)}, u32[]{:S(2)}, u32[]{:S(2)}) collective-permute-start(bf16[512,512]{0,1:T(8,128)(2,1)} %fusion.6), channel_id=1, source_target_pairs={{8,0},{16,8},{24,16},{32,24},{40,32},{48,40},{56,48},{0,56},{9,1},... | collective-permute-start | bytes 1572872 | tf_op jit(solution)/shard_map/ppermute | solution.py:16
  198.6 1.5 fusion.11
  200.9 3.0 %collective-permute-done.13 = bf16[512,512]{0,1:T(8,128)(2,1)S(1)} collective-permute-done((bf16[512,512]{0,1:T(8,128)(2,1)}, bf16[512,512]{0,1:T(8,128)(2,1)S(1)}, u32[]{:S(2)}, u32[]{:S(2)}) %collective-permute-start.13) | collective-permute-done | bytes 524320 | tf_op jit(solution)/shard_map/ppermute | solution.py:16
  203.9 1.0 copy.57
  204.9 1.8 reduce_sum.44
  (105 shorter events, 12.9 us)
Async XLA Ops:
  0.6 114.4 %copy-start = (f32[128,8]{0,1:T(8,128)S(1)}, f32[128,8]{0,1:T(8,128)}, u32[]{:S(2)}) copy-start(f32[128,8]{0,1:T(8,128)} %param.13) | copy-start | bytes 12292
  2.1 19.3 %collective-permute-start.1 = (f32[4,128]{1,0:T(4,128)S(1)}, f32[4,128]{1,0:T(4,128)S(1)}, u32[]{:S(2)}, u32[]{:S(2)}) collective-permute-start(f32[4,128]{1,0:T(4,128)S(1)} %bitcast.183), channel_id=1, source_target_pairs={{56,0},{0,8},{8,16},{16,24},{24,32},{32,40},{40,48},{48,56},{57,1}... | collective-permute-start | bytes 6152 | tf_op jit(solution)/shard_map/ppermute | solution.py:16
  8.4 4.1 %copy-start.15 = (bf16[1,1,512,64]{2,3,1,0:T(8,128)(2,1)S(1)}, bf16[1,1,512,64]{2,3,1,0:T(8,128)(2,1)}, u32[]{:S(2)}) copy-start(bf16[1,1,512,64]{2,3,1,0:T(8,128)(2,1)} %param.9) | copy-start | bytes 196612
  8.4 24.2 %all-to-all-start = ((bf16[4,3,16,4096]{3,2,1,0:T(8,128)(2,1)}), bf16[4,3,16,4096]{3,2,1,0:T(8,128)(2,1)S(1)}, u32[]{:S(2)}, u32[]{:S(2)}) async-start(bf16[4,3,16,4096]{3,2,1,0:T(8,128)(2,1)} %serve.1), calls=%async_computation | async-start | bytes 3145728 | tf_op jit(solution)/shard_map/all_to_all | solution.py:25
  12.6 10.5 %collective-permute-start = (bf16[64,512]{1,0:T(8,128)(2,1)S(1)}, bf16[64,512]{1,0:T(8,128)(2,1)S(1)}, u32[]{:S(2)}, u32[]{:S(2)}) collective-permute-start(bf16[64,512]{1,0:T(8,128)(2,1)S(1)} %bitcast.172), channel_id=1, source_target_pairs={{0,4},{1,5},{2,6},{3,7},{4,0},{5,1},{6,2},{7,3},{8,12},{9,13},{10,... | collective-permute-start | bytes 196616 | tf_op jit(solution)/shard_map/ppermute | solution.py:20
  23.1 9.4 %collective-permute-start.2 = (bf16[136,512]{1,0:T(8,128)(2,1)S(1)}, bf16[136,512]{1,0:T(8,128)(2,1)S(1)}, u32[]{:S(2)}, u32[]{:S(2)}) collective-permute-start(bf16[136,512]{1,0:T(8,128)(2,1)S(1)} %pad_maximum_fusion.6), channel_id=1, source_target_pairs={{0,2},{1,3},{2,0},{3,1},{4,6},{5,7},{6,4},{7,5},{8,10},{9,11},{10,... | collective-permute-start | bytes 417800 | tf_op jit(solution)/shard_map/ppermute | solution.py:20
  33.0 23.1 %collective-permute-start.7 = (bf16[264,512]{1,0:T(8,128)(2,1)S(1)}, bf16[264,512]{1,0:T(8,128)(2,1)S(1)}, u32[]{:S(2)}, u32[]{:S(2)}) collective-permute-start(bf16[264,512]{1,0:T(8,128)(2,1)S(1)} %pad_maximum_fusion.4), channel_id=1, source_target_pairs={{0,1},{1,0},{2,3},{3,2},{4,5},{5,4},{6,7},{7,6},{8,9},{9,8},{10,11... | collective-permute-start | bytes 811016 | tf_op jit(solution)/shard_map/ppermute | solution.py:20
  39.8 32.0 %collective-permute-start.8 = (bf16[512,512]{0,1:T(8,128)(2,1)S(1)}, bf16[512,512]{0,1:T(8,128)(2,1)S(1)}, u32[]{:S(2)}, u32[]{:S(2)}) collective-permute-start(bf16[512,512]{0,1:T(8,128)(2,1)S(1)} %bitcast.146), channel_id=1, source_target_pairs={{56,0},{0,8},{8,16},{16,24},{24,32},{32,40},{40,48},{48,56},{57,1}... | collective-permute-start | bytes 1572872 | tf_op jit(solution)/shard_map/ppermute | solution.py:16
  41.8 36.1 %collective-permute-start.3 = (bf16[3,16,3072]{2,1,0:T(8,128)(2,1)S(1)}, bf16[3,16,3072]{2,1,0:T(8,128)(2,1)S(1)}, u32[]{:S(2)}, u32[]{:S(2)}) collective-permute-start(bf16[3,16,3072]{2,1,0:T(8,128)(2,1)S(1)} %slice.56), channel_id=1, source_target_pairs={{0,256},{64,320},{128,384},{192,448},{256,0},{320,64},{384,128},{4... | collective-permute-start | bytes 884744 | tf_op jit(solution)/shard_map/ppermute | solution.py:20
  56.2 15.6 %collective-permute-start.9 = (f32[1,512]{1,0:T(1,128)S(1)}, f32[1,512]{1,0:T(1,128)S(1)}, u32[]{:S(2)}, u32[]{:S(2)}) collective-permute-start(f32[1,512]{1,0:T(1,128)S(1)} %fusion.37), channel_id=1, source_target_pairs={{0,4},{1,5},{2,6},{3,7},{4,0},{5,1},{6,2},{7,3},{8,12},{9,13},{10,... | collective-permute-start | bytes 6152 | tf_op jit(solution)/shard_map/ppermute | solution.py:20
  59.4 13.7 %copy-start.9 = (bf16[2,2,2,64,512]{4,3,2,1,0:T(8,128)(2,1)}, bf16[2,2,2,64,512]{4,3,2,1,0:T(8,128)(2,1)S(1)}, u32[]{:S(2)}) copy-start(bf16[2,2,2,64,512]{4,3,2,1,0:T(8,128)(2,1)S(1)} %pad_maximum_fusion.1) | copy-start | bytes 1572868
  71.8 1.3 copy-start.6
  73.1 19.2 %all-to-all-start.1 = ((bf16[4,8,16,512]{3,2,1,0:T(8,128)(2,1)}), bf16[4,8,16,512]{3,2,1,0:T(8,128)(2,1)S(1)}, u32[]{:S(2)}, u32[]{:S(2)}) async-start(bf16[4,8,16,512]{3,2,1,0:T(8,128)(2,1)} %bitcast.132), calls=%async_computation.1 | async-start | bytes 1048576 | tf_op jit(solution)/shard_map/all_to_all | solution.py:25
  77.9 14.4 %copy-start.11 = (bf16[16,4096]{1,0:T(8,128)(2,1)}, bf16[16,4096]{1,0:T(8,128)(2,1)S(1)}, u32[]{:S(2)}) copy-start(bf16[16,4096]{1,0:T(8,128)(2,1)S(1)} %fusion.25.fresh0_ref) | copy-start | bytes 393220
  77.9 14.4 %collective-permute-start.6 = (bf16[16,4096]{1,0:T(8,128)(2,1)S(1)}, bf16[16,4096]{1,0:T(8,128)(2,1)S(1)}, u32[]{:S(2)}, u32[]{:S(2)}) collective-permute-start(bf16[16,4096]{1,0:T(8,128)(2,1)S(1)} %fusion.25.fresh0_ref), channel_id=1, source_target_pairs={{0,192},{64,128},{128,64},{192,0},{256,448},{320,384},{384,320},{4... | collective-permute-start | bytes 393224 | tf_op jit(solution)/shard_map/ppermute | solution.py:20
  82.5 9.8 %collective-permute-start.5 = (bf16[16,4096]{1,0:T(8,128)(2,1)S(1)}, bf16[16,4096]{1,0:T(8,128)(2,1)S(1)}, u32[]{:S(2)}, u32[]{:S(2)}) collective-permute-start(bf16[16,4096]{1,0:T(8,128)(2,1)S(1)} %fusion.25.fresh0_ref), channel_id=1, source_target_pairs={{0,128},{64,192},{128,0},{192,64},{256,384},{320,448},{384,256},{4... | collective-permute-start | bytes 393224 | tf_op jit(solution)/shard_map/ppermute | solution.py:20
  85.0 7.3 %collective-permute-start.4 = (bf16[16,4096]{1,0:T(8,128)(2,1)S(1)}, bf16[16,4096]{1,0:T(8,128)(2,1)S(1)}, u32[]{:S(2)}, u32[]{:S(2)}) collective-permute-start(bf16[16,4096]{1,0:T(8,128)(2,1)S(1)} %fusion.25.fresh0_ref), channel_id=1, source_target_pairs={{0,64},{64,0},{128,192},{192,128},{256,320},{320,256},{384,448},{4... | collective-permute-start | bytes 393224 | tf_op jit(solution)/shard_map/ppermute | solution.py:20
  92.3 0.7 copy-start.12
  92.3 0.7 copy-start.13
  92.3 0.7 copy-start.14
  93.1 0.8 copy-start.5
  96.7 18.2 %copy-start.10 = (bf16[64,4096]{1,0:T(8,128)(2,1)S(1)}, bf16[64,4096]{1,0:T(8,128)(2,1)}, u32[]{:S(2)}) copy-start(bf16[64,4096]{1,0:T(8,128)(2,1)} %get-tuple-element.22) | copy-start | bytes 1572868
  96.7 37.6 %all-to-all-start.2 = ((bf16[8,80,512]{2,1,0:T(8,128)(2,1)}), bf16[8,80,512]{2,1,0:T(8,128)(2,1)S(1)}, u32[]{:S(2)}, u32[]{:S(2)}) async-start(bf16[8,80,512]{2,1,0:T(8,128)(2,1)} %get-tuple-element.17), calls=%async_computation.2 | async-start | bytes 1310720 | tf_op jit(solution)/shard_map/all_to_all | solution.py:213
  114.9 3.1 %copy-start.4 = (bf16[2,16,4096]{2,1,0:T(8,128)(2,1)S(1)}, bf16[2,16,4096]{2,1,0:T(8,128)(2,1)}, u32[]{:S(2)}) copy-start(bf16[2,16,4096]{2,1,0:T(8,128)(2,1)} %unpack.1) | copy-start | bytes 786436
  117.3 3.8 %copy-start.2 = (f32[1,1,64,4096]{3,2,1,0:T(8,128)S(1)}, f32[1,1,64,4096]{3,2,1,0:T(8,128)}, u32[]{:S(2)}) copy-start(f32[1,1,64,4096]{3,2,1,0:T(8,128)} %param.12) | copy-start | bytes 3145732
  121.3 4.4 %copy-start.1 = (f32[1,1,64,4096]{3,2,1,0:T(8,128)S(1)}, f32[1,1,64,4096]{3,2,1,0:T(8,128)}, u32[]{:S(2)}) copy-start(f32[1,1,64,4096]{3,2,1,0:T(8,128)} %param.11) | copy-start | bytes 3145732
  134.3 0.8 copy-start.3
  135.2 21.3 %copy-start.7 = (bf16[512,512]{0,1:T(8,128)(2,1)S(1)}, bf16[512,512]{0,1:T(8,128)(2,1)}, u32[]{:S(2)}) copy-start(bf16[512,512]{0,1:T(8,128)(2,1)} %copy-done.6) | copy-start | bytes 1572868
  136.9 16.4 %collective-permute-start.10 = (f32[4,128]{1,0:T(4,128)S(1)}, f32[4,128]{1,0:T(4,128)S(1)}, u32[]{:S(2)}, u32[]{:S(2)}) collective-permute-start(f32[4,128]{1,0:T(4,128)S(1)} %bitcast.182), channel_id=1, source_target_pairs={{0,1},{1,0},{2,3},{3,2},{4,5},{5,4},{6,7},{7,6},{8,9},{9,8},{10,11... | collective-permute-start | bytes 6152 | tf_op jit(solution)/shard_map/ppermute | solution.py:20
  147.9 24.8 %collective-permute-start.14 = (bf16[16,4096]{1,0:T(8,128)(2,1)S(1)}, bf16[16,4096]{1,0:T(8,128)(2,1)S(1)}, u32[]{:S(2)}, u32[]{:S(2)}) collective-permute-start(bf16[16,4096]{1,0:T(8,128)(2,1)S(1)} %bitcast.167), channel_id=1, source_target_pairs={{0,256},{64,320},{128,384},{192,448},{256,0},{320,64},{384,128},{4... | collective-permute-start | bytes 393224 | tf_op jit(solution)/shard_map/ppermute | solution.py:20
  153.4 0.6 copy-start.16
  154.5 10.2 %collective-permute-start.11 = (f32[4,128]{1,0:T(4,128)}, f32[4,128]{1,0:T(4,128)}, u32[]{:S(2)}, u32[]{:S(2)}) collective-permute-start(f32[4,128]{1,0:T(4,128)} %bitcast_add_fusion.2), channel_id=1, source_target_pairs={{0,2},{1,3},{2,0},{3,1},{4,6},{5,7},{6,4},{7,5},{8,10},{9,11},{10,... | collective-permute-start | bytes 6152 | tf_op jit(solution)/shard_map/ppermute | solution.py:20
  157.7 47.2 %all-to-all-start.3 = ((bf16[8,64,512]{2,1,0:T(8,128)(2,1)}), bf16[8,64,512]{2,1,0:T(8,128)(2,1)}, u32[]{:S(2)}, u32[]{:S(2)}) async-start(bf16[8,64,512]{2,1,0:T(8,128)(2,1)} %bitcast.161), calls=%async_computation.3 | async-start | bytes 1048576 | tf_op jit(solution)/shard_map/all_to_all | solution.py:227
  164.7 19.1 %copy-start.8 = (bf16[512,512]{0,1:T(8,128)(2,1)S(1)}, bf16[512,512]{0,1:T(8,128)(2,1)}, u32[]{:S(2)}) copy-start(bf16[512,512]{0,1:T(8,128)(2,1)} %copy-done.6) | copy-start | bytes 1572868
  165.4 18.3 %collective-permute-start.12 = (f32[4,128]{1,0:T(4,128)S(1)}, f32[4,128]{1,0:T(4,128)S(1)}, u32[]{:S(2)}, u32[]{:S(2)}) collective-permute-start(f32[4,128]{1,0:T(4,128)S(1)} %fusion.52), channel_id=1, source_target_pairs={{0,4},{1,5},{2,6},{3,7},{4,0},{5,1},{6,2},{7,3},{8,12},{9,13},{10,... | collective-permute-start | bytes 6152 | tf_op jit(solution)/shard_map/ppermute | solution.py:20
  174.7 20.9 %collective-permute-start.16 = (bf16[34,4096]{1,0:T(8,128)(2,1)S(1)}, bf16[34,4096]{1,0:T(8,128)(2,1)S(1)}, u32[]{:S(2)}, u32[]{:S(2)}) collective-permute-start(bf16[34,4096]{1,0:T(8,128)(2,1)S(1)} %get-tuple-element.52), channel_id=1, source_target_pairs={{0,128},{64,192},{128,0},{192,64},{256,384},{320,448},{384,256},{4... | collective-permute-start | bytes 835592 | tf_op jit(solution)/shard_map/ppermute | solution.py:20
  179.6 16.1 %collective-permute-start.15 = (bf16[34,4096]{1,0:T(8,128)(2,1)S(1)}, bf16[34,4096]{1,0:T(8,128)(2,1)S(1)}, u32[]{:S(2)}, u32[]{:S(2)}) collective-permute-start(bf16[34,4096]{1,0:T(8,128)(2,1)S(1)} %get-tuple-element.52), channel_id=1, source_target_pairs={{0,64},{64,0},{128,192},{192,128},{256,320},{320,256},{384,448},{4... | collective-permute-start | bytes 835592 | tf_op jit(solution)/shard_map/ppermute | solution.py:20
  181.8 13.9 %collective-permute-start.17 = (bf16[34,4096]{1,0:T(8,128)(2,1)S(1)}, bf16[34,4096]{1,0:T(8,128)(2,1)S(1)}, u32[]{:S(2)}, u32[]{:S(2)}) collective-permute-start(bf16[34,4096]{1,0:T(8,128)(2,1)S(1)} %get-tuple-element.52), channel_id=1, source_target_pairs={{0,192},{64,128},{128,64},{192,0},{256,448},{320,384},{384,320},{4... | collective-permute-start | bytes 835592 | tf_op jit(solution)/shard_map/ppermute | solution.py:20
  184.8 19.1 %collective-permute-start.13 = (bf16[512,512]{0,1:T(8,128)(2,1)}, bf16[512,512]{0,1:T(8,128)(2,1)S(1)}, u32[]{:S(2)}, u32[]{:S(2)}) collective-permute-start(bf16[512,512]{0,1:T(8,128)(2,1)} %fusion.6), channel_id=1, source_target_pairs={{8,0},{16,8},{24,16},{32,24},{40,32},{48,40},{56,48},{0,56},{9,1},... | collective-permute-start | bytes 1572872 | tf_op jit(solution)/shard_map/ppermute | solution.py:16

commit v16 on v9

--- a/solution.py
+++ b/solution.py
@@ -206,9 +206,10 @@
     got = lax.all_to_all(sent, "tensor", 0, 0, tiled=True)
     weight_cols = got[:, :rows].reshape(8 * rows, cols)
     grad_rows = got[:, rows:].transpose(1, 0, 2).reshape(part, width)
+
+    keys = lax.dot_general(weight_cols, normed, (((1,), (1,)), ((), ())), preferred_element_type=WIDE).astype(SHORT)
+    weight_cols, keys, grad_rows = lax.optimization_barrier((weight_cols, keys, grad_rows))
     mean_rows = (grad_rows.astype(WIDE) + swap(grad_rows, "replica", PLANE).astype(WIDE)) / copies
-
-    keys = lax.dot_general(weight_cols, normed, (((1,), (1,)), ((), ())), preferred_element_type=WIDE).astype(SHORT)
     feature = lax.dot_general(kg_all, weight_cols, (((0,), (0,)), ((), ())), preferred_element_type=WIDE)
     product = jnp.sum(feature * x, axis=1).reshape(-1, 128)
     for bit in (1, 2, 4):

time: 206 us -> 243 us (1.18)
  the two profiles are of different devices: /device:TPU:1 before, /device:TPU:136 now
where the time goes in v16:
time: 243 us; the launch traced here: 241 us
  starting transfers between devices  101 us (42%)
  waiting for transfers between devices  78.9 us (32%)
  local copies, waits for them, and re-layouts  20.2 us (8%)
  matrix products  17 us (7%)
  other arithmetic  13.7 us (6%)
  Pallas kernels  8.43 us (3%)
    ppermute x14, waiting for transfers between devices, swap(): lax.ppermute(block, axis, [(i, i ^ bit) for i in range(lax.axis_size(axis...  66.8 us
    ppermute x14, starting transfers between devices, swap(): lax.ppermute(block, axis, [(i, i ^ bit) for i in range(lax.axis_size(axis...  65.8 us
    all_to_all x1, starting transfers between devices, shards(): got = lax.all_to_all(sent, 'tensor', 0, 0, tiled=True)  18.4 us
    dot_general x4, matrix products, checksum(): jnp.einsum('jnc,cp->jnp', shaped, probe_matrix, precision=lax.Precision.H...  13.6 us
    all_to_all x1, waiting for transfers between devices, shards(): got = lax.all_to_all(sent, 'tensor', 0, 0, tiled=True)  12 us
    all_to_all x2, starting transfers between devices, exchange_x(): lax.all_to_all(block, 'replica', 0, 0, axis_index_groups=groups, tiled=True)  9.31 us
    unnamed x48, local copies, waits for them, and re-layouts  8.57 us
    all_to_all x1, starting transfers between devices, shards(): lax.all_to_all(keys.reshape(8, rows, tokens), 'tensor', 0, 0, tiled=True)  7.46 us
  transfers between devices with their start and end apart: 21, of which 10 were waited for; matrix products, arithmetic and copies ran while one was open for 16% of the time, Pallas kernels for 2%

profile of v16, /device:TPU:136, one launch (start us, length us, event | category | flops | bytes accessed | tf_op | source)
XLA Modules:
  0.0 241.2 jit_solution(8887577894231784391)
XLA Ops:
  0.6 2.1 copy.45
  2.7 1.2 multiply_reduce_fusion
  3.9 3.7 %serve.1 = bf16[4,3,16,4096]{3,2,1,0:T(8,128)(2,1)} custom-call(s32[8,8]{1,0:T(8,128)} %failed_ref.3, s32[8,8]{1,0:T(8,128)} %spans_ref.5, bf16[64,4096]{1,0:T(8,128)(2,1)} %bitcast.150, f32[64,4096]{1,0:T(8,128)} %bitcast.131, f32[64,4096]{1,0:T(8,128)} %bitcast.134), custom_call_target="tpu_custom_call" | custom-call | tf_op jit(solution)/shard_map/serve/pallas_call | solution.py:91
  7.6 4.4 %all-to-all-start = ((bf16[4,3,16,4096]{3,2,1,0:T(8,128)(2,1)}), bf16[4,3,16,4096]{3,2,1,0:T(8,128)(2,1)S(1)}, u32[]{:S(2)}, u32[]{:S(2)}) async-start(bf16[4,3,16,4096]{3,2,1,0:T(8,128)(2,1)} %serve.1), calls=%async_computation | async-start | bytes 3145728 | tf_op jit(solution)/shard_map/all_to_all | solution.py:25
  12.2 1.9 collective-permute-start.1
  14.2 8.8 %collective-permute-done.1 = bf16[72,512]{1,0:T(8,128)(2,1)S(1)} collective-permute-done((bf16[72,512]{1,0:T(8,128)(2,1)S(1)}, bf16[72,512]{1,0:T(8,128)(2,1)S(1)}, u32[]{:S(2)}, u32[]{:S(2)}) %collective-permute-start.1) | collective-permute-done | bytes 73760 | tf_op jit(solution)/shard_map/ppermute | solution.py:20
  23.1 7.7 %collective-permute-start.2 = (bf16[2,72,512]{2,1,0:T(8,128)(2,1)S(1)}, bf16[2,72,512]{2,1,0:T(8,128)(2,1)S(1)}, u32[]{:S(2)}, u32[]{:S(2)}) collective-permute-start(bf16[2,72,512]{2,1,0:T(8,128)(2,1)S(1)} %pad_maximum_fusion.5), channel_id=1, source_target_pairs={{0,2},{1,3},{2,0},{3,1},{4,6},{5,7},{6,4},{7,5},{8,10},{9,11},{10,... | collective-permute-start | bytes 442376 | tf_op jit(solution)/shard_map/ppermute | solution.py:20
  30.8 7.2 %collective-permute-done.2 = bf16[2,72,512]{2,1,0:T(8,128)(2,1)S(1)} collective-permute-done((bf16[2,72,512]{2,1,0:T(8,128)(2,1)S(1)}, bf16[2,72,512]{2,1,0:T(8,128)(2,1)S(1)}, u32[]{:S(2)}, u32[]{:S(2)}) %collective-permute-start.2) | collective-permute-done | bytes 147488 | tf_op jit(solution)/shard_map/ppermute | solution.py:20
  38.4 2.6 %collective-permute-start.7 = (bf16[2,2,72,512]{3,2,1,0:T(8,128)(2,1)S(1)}, bf16[2,2,72,512]{3,2,1,0:T(8,128)(2,1)S(1)}, u32[]{:S(2)}, u32[]{:S(2)}) collective-permute-start(bf16[2,2,72,512]{3,2,1,0:T(8,128)(2,1)S(1)} %pad_maximum_fusion.4), channel_id=1, source_target_pairs={{0,1},{1,0},{2,3},{3,2},{4,5},{5,4},{6,7},{7,6},{8,9},{9,8},{10,11... | collective-permute-start | bytes 884744 | tf_op jit(solution)/shard_map/ppermute | solution.py:20
  41.1 9.8 %collective-permute-start.3 = (bf16[3,16,3072]{2,1,0:T(8,128)(2,1)S(1)}, bf16[3,16,3072]{2,1,0:T(8,128)(2,1)S(1)}, u32[]{:S(2)}, u32[]{:S(2)}) collective-permute-start(bf16[3,16,3072]{2,1,0:T(8,128)(2,1)S(1)} %slice.46), channel_id=1, source_target_pairs={{0,256},{64,320},{128,384},{192,448},{256,0},{320,64},{384,128},{4... | collective-permute-start | bytes 884744 | tf_op jit(solution)/shard_map/ppermute | solution.py:20
  52.5 4.9 %all-to-all-start.1 = ((bf16[4,8,16,512]{3,2,1,0:T(8,128)(2,1)}), bf16[4,8,16,512]{3,2,1,0:T(8,128)(2,1)S(1)}, u32[]{:S(2)}, u32[]{:S(2)}) async-start(bf16[4,8,16,512]{3,2,1,0:T(8,128)(2,1)} %bitcast.130), calls=%async_computation.1 | async-start | bytes 1048576 | tf_op jit(solution)/shard_map/all_to_all | solution.py:25
  57.4 11.2 %collective-permute-done.3 = bf16[3,16,3072]{2,1,0:T(8,128)(2,1)S(1)} collective-permute-done((bf16[3,16,3072]{2,1,0:T(8,128)(2,1)S(1)}, bf16[3,16,3072]{2,1,0:T(8,128)(2,1)S(1)}, u32[]{:S(2)}, u32[]{:S(2)}) %collective-permute-start.3) | collective-permute-done | bytes 294944 | tf_op jit(solution)/shard_map/ppermute | solution.py:20
  68.7 9.5 %collective-permute-start.6 = (bf16[16,4096]{1,0:T(8,128)(2,1)S(1)}, bf16[16,4096]{1,0:T(8,128)(2,1)S(1)}, u32[]{:S(2)}, u32[]{:S(2)}) collective-permute-start(bf16[16,4096]{1,0:T(8,128)(2,1)S(1)} %fusion.25.fresh0_ref), channel_id=1, source_target_pairs={{0,192},{64,128},{128,64},{192,0},{256,448},{320,384},{384,320},{4... | collective-permute-start | bytes 393224 | tf_op jit(solution)/shard_map/ppermute | solution.py:20
  78.2 2.8 %collective-permute-start.5 = (bf16[16,4096]{1,0:T(8,128)(2,1)S(1)}, bf16[16,4096]{1,0:T(8,128)(2,1)S(1)}, u32[]{:S(2)}, u32[]{:S(2)}) collective-permute-start(bf16[16,4096]{1,0:T(8,128)(2,1)S(1)} %fusion.25.fresh0_ref), channel_id=1, source_target_pairs={{0,128},{64,192},{128,0},{192,64},{256,384},{320,448},{384,256},{4... | collective-permute-start | bytes 393224 | tf_op jit(solution)/shard_map/ppermute | solution.py:20
  80.9 1.9 collective-permute-start.4
  82.9 3.6 %collective-permute-done.5.fresh2_ref = bf16[16,4096]{1,0:T(8,128)(2,1)S(1)} collective-permute-done((bf16[16,4096]{1,0:T(8,128)(2,1)S(1)}, bf16[16,4096]{1,0:T(8,128)(2,1)S(1)}, u32[]{:S(2)}, u32[]{:S(2)}) %collective-permute-start.5) | collective-permute-done | bytes 131104 | tf_op jit(solution)/shard_map/ppermute | solution.py:20
  86.5 1.3 collective-permute-done.4.fresh1_ref
  89.2 2.9 %assemble.1 = (bf16[8,80,512]{2,1,0:T(8,128)(2,1)}, bf16[64,4096]{1,0:T(8,128)(2,1)}) custom-call(s32[8,8]{1,0:T(8,128)} %failed_ref.3, s32[8,8]{1,0:T(8,128)} %spans_ref.5, bf16[64,4096]{1,0:T(8,128)(2,1)} %bitcast.151, bf16[16,4096]{1,0:T(8,128)(2,1)} %copy-done.11, bf16[16,4096]{1,0:T(8,128)(2,1)} %copy-done.17, bf16[16,4096]{1,0:T(8,128)(2,1)} %copy-done.16, ...), custom_call_target="tpu_custom_call" | custom-call | tf_op jit(solution)/shard_map/assemble/pallas_call | solution.py:142
  92.1 18.4 %all-to-all-start.2 = ((bf16[8,80,512]{2,1,0:T(8,128)(2,1)}), bf16[8,80,512]{2,1,0:T(8,128)(2,1)S(1)}, u32[]{:S(2)}, u32[]{:S(2)}) async-start(bf16[8,80,512]{2,1,0:T(8,128)(2,1)} %get-tuple-element.20), calls=%async_computation.2 | async-start | bytes 1310720 | tf_op jit(solution)/shard_map/all_to_all | solution.py:206
  110.5 1.3 dynamic_slice.3
  114.3 1.0 copy-done.1
  115.6 4.9 %fusion.30 = f32[64,32,8]{1,2,0:T(8,128)} fusion(f32[64,32,128]{2,1,0:T(8,128)S(1)} %bitcast.141, f32[128,8]{0,1:T(8,128)S(1)} %copy-done), kind=kOutput, calls=%fused_computation.66 | convolution fusion | flops 25165824 | bytes 1118208 | tf_op jit(solution)/shard_map/jnc,cp->jnp/dot_general | solution.py:226
  120.5 4.2 %fusion.32 = f32[64,32,8]{1,2,0:T(8,128)S(1)} fusion(f32[64,32,128]{2,1,0:T(8,128)S(1)} %bitcast.140, f32[128,8]{0,1:T(8,128)S(1)} %copy-done), kind=kOutput, calls=%fused_computation.68 | convolution fusion | flops 25165824 | bytes 1118208 | tf_op jit(solution)/shard_map/jnc,cp->jnp/dot_general | solution.py:226
  124.6 12.0 %all-to-all-done.2 = bf16[8,80,512]{2,1,0:T(8,128)(2,1)S(1)} async-done(((bf16[8,80,512]{2,1,0:T(8,128)(2,1)}), bf16[8,80,512]{2,1,0:T(8,128)(2,1)S(1)}, u32[]{:S(2)}, u32[]{:S(2)}) %all-to-all-start.2) | async-done | bytes 655392 | tf_op jit(solution)/shard_map/all_to_all | solution.py:206
  137.4 1.3 convolution_convert_fusion
  138.6 1.6 fusion.7
  140.3 1.9 collective-permute-start.9
  142.2 2.8 %fusion.28 = f32[64,32,8]{1,2,0:T(8,128)} fusion(bf16[64,32,128]{2,1,0:T(8,128)(2,1)S(1)} %bitcast.145, f32[128,8]{0,1:T(8,128)S(1)} %copy-done), kind=kOutput, calls=%fused_computation.64 | convolution fusion | flops 25165824 | bytes 593920 | tf_op jit(solution)/shard_map/jnc,cp->jnp/dot_general | solution.py:226
  145.8 1.9 unpack.1
  149.3 6.5 %collective-permute-start.10 = (f32[4,128]{1,0:T(4,128)}, f32[4,128]{1,0:T(4,128)}, u32[]{:S(2)}, u32[]{:S(2)}) collective-permute-start(f32[4,128]{1,0:T(4,128)} %bitcast_add_fusion.2), channel_id=1, source_target_pairs={{0,2},{1,3},{2,0},{3,1},{4,6},{5,7},{6,4},{7,5},{8,10},{9,11},{10,... | collective-permute-start | bytes 6152 | tf_op jit(solution)/shard_map/ppermute | solution.py:20
  155.8 1.8 convolution_convert_fusion.2
  157.6 1.8 convert_element_type.137
  159.3 1.1 copy.59
  161.2 1.7 copy.50
  162.8 1.8 convert_element_type.140
  164.6 1.1 copy.56
  166.7 7.5 %all-to-all-start.3 = ((bf16[8,64,512]{2,1,0:T(8,128)(2,1)}), bf16[8,64,512]{2,1,0:T(8,128)(2,1)}, u32[]{:S(2)}, u32[]{:S(2)}) async-start(bf16[8,64,512]{2,1,0:T(8,128)(2,1)} %bitcast.157), calls=%async_computation.3 | async-start | bytes 1048576 | tf_op jit(solution)/shard_map/all_to_all | solution.py:221
  174.2 9.2 %collective-permute-start.13 = (bf16[16,4096]{1,0:T(8,128)(2,1)}, bf16[16,4096]{1,0:T(8,128)(2,1)S(1)}, u32[]{:S(2)}, u32[]{:S(2)}) collective-permute-start(bf16[16,4096]{1,0:T(8,128)(2,1)} %bitcast.162), channel_id=1, source_target_pairs={{0,256},{64,320},{128,384},{192,448},{256,0},{320,64},{384,128},{4... | collective-permute-start | bytes 393224 | tf_op jit(solution)/shard_map/ppermute | solution.py:20
  184.0 1.9 collective-permute-start.11
  186.0 26.1 %collective-permute-done.13 = bf16[16,4096]{1,0:T(8,128)(2,1)S(1)} collective-permute-done((bf16[16,4096]{1,0:T(8,128)(2,1)}, bf16[16,4096]{1,0:T(8,128)(2,1)S(1)}, u32[]{:S(2)}, u32[]{:S(2)}) %collective-permute-start.13) | collective-permute-done | bytes 131104 | tf_op jit(solution)/shard_map/ppermute | solution.py:20
  212.0 1.2 fusion.23
  213.3 4.3 %collective-permute-start.15 = (bf16[34,4096]{1,0:T(8,128)(2,1)S(1)}, bf16[34,4096]{1,0:T(8,128)(2,1)S(1)}, u32[]{:S(2)}, u32[]{:S(2)}) collective-permute-start(bf16[34,4096]{1,0:T(8,128)(2,1)S(1)} %get-tuple-element.58), channel_id=1, source_target_pairs={{0,128},{64,192},{128,0},{192,64},{256,384},{320,448},{384,256},{4... | collective-permute-start | bytes 835592 | tf_op jit(solution)/shard_map/ppermute | solution.py:20
  217.6 3.0 %collective-permute-start.14 = (bf16[34,4096]{1,0:T(8,128)(2,1)S(1)}, bf16[34,4096]{1,0:T(8,128)(2,1)S(1)}, u32[]{:S(2)}, u32[]{:S(2)}) collective-permute-start(bf16[34,4096]{1,0:T(8,128)(2,1)S(1)} %get-tuple-element.58), channel_id=1, source_target_pairs={{0,64},{64,0},{128,192},{192,128},{256,320},{320,256},{384,448},{4... | collective-permute-start | bytes 835592 | tf_op jit(solution)/shard_map/ppermute | solution.py:20
  220.6 2.8 %collective-permute-start.16 = (bf16[34,4096]{1,0:T(8,128)(2,1)S(1)}, bf16[34,4096]{1,0:T(8,128)(2,1)S(1)}, u32[]{:S(2)}, u32[]{:S(2)}) collective-permute-start(bf16[34,4096]{1,0:T(8,128)(2,1)S(1)} %get-tuple-element.58), channel_id=1, source_target_pairs={{0,192},{64,128},{128,64},{192,0},{256,448},{320,384},{384,320},{4... | collective-permute-start | bytes 835592 | tf_op jit(solution)/shard_map/ppermute | solution.py:20
  224.5 2.9 %collective-permute-done.15 = bf16[34,4096]{1,0:T(8,128)(2,1)S(1)} collective-permute-done((bf16[34,4096]{1,0:T(8,128)(2,1)S(1)}, bf16[34,4096]{1,0:T(8,128)(2,1)S(1)}, u32[]{:S(2)}, u32[]{:S(2)}) %collective-permute-start.15) | collective-permute-done | bytes 278560 | tf_op jit(solution)/shard_map/ppermute | solution.py:20
  227.4 5.0 %collective-permute-done.14 = bf16[34,4096]{1,0:T(8,128)(2,1)S(1)} collective-permute-done((bf16[34,4096]{1,0:T(8,128)(2,1)S(1)}, bf16[34,4096]{1,0:T(8,128)(2,1)S(1)}, u32[]{:S(2)}, u32[]{:S(2)}) %collective-permute-start.14) | collective-permute-done | bytes 278560 | tf_op jit(solution)/shard_map/ppermute | solution.py:20
  236.0 1.5 fusion.11
  239.4 1.8 reduce_sum.54
  (105 shorter events, 17.7 us)
Async XLA Ops:
  0.6 114.9 %copy-start = (f32[128,8]{0,1:T(8,128)S(1)}, f32[128,8]{0,1:T(8,128)}, u32[]{:S(2)}) copy-start(f32[128,8]{0,1:T(8,128)} %param.13) | copy-start | bytes 12292
  3.9 8.2 %collective-permute-start = (f32[4,128]{1,0:T(4,128)S(1)}, f32[4,128]{1,0:T(4,128)S(1)}, u32[]{:S(2)}, u32[]{:S(2)}) collective-permute-start(f32[4,128]{1,0:T(4,128)S(1)} %bitcast.173), channel_id=1, source_target_pairs={{56,0},{0,8},{8,16},{16,24},{24,32},{32,40},{40,48},{48,56},{57,1}... | collective-permute-start | bytes 6152 | tf_op jit(solution)/shard_map/ppermute | solution.py:16
  7.6 4.5 %copy-start.14 = (bf16[1,1,512,64]{2,3,1,0:T(8,128)(2,1)S(1)}, bf16[1,1,512,64]{2,3,1,0:T(8,128)(2,1)}, u32[]{:S(2)}) copy-start(bf16[1,1,512,64]{2,3,1,0:T(8,128)(2,1)} %param.9) | copy-start | bytes 196612
  7.6 30.5 %all-to-all-start = ((bf16[4,3,16,4096]{3,2,1,0:T(8,128)(2,1)}), bf16[4,3,16,4096]{3,2,1,0:T(8,128)(2,1)S(1)}, u32[]{:S(2)}, u32[]{:S(2)}) async-start(bf16[4,3,16,4096]{3,2,1,0:T(8,128)(2,1)} %serve.1), calls=%async_computation | async-start | bytes 3145728 | tf_op jit(solution)/shard_map/all_to_all | solution.py:25
  12.2 10.7 %collective-permute-start.1 = (bf16[72,512]{1,0:T(8,128)(2,1)S(1)}, bf16[72,512]{1,0:T(8,128)(2,1)S(1)}, u32[]{:S(2)}, u32[]{:S(2)}) collective-permute-start(bf16[72,512]{1,0:T(8,128)(2,1)S(1)} %maximum_maximum_fusion), channel_id=1, source_target_pairs={{0,4},{1,5},{2,6},{3,7},{4,0},{5,1},{6,2},{7,3},{8,12},{9,13},{10,... | collective-permute-start | bytes 221192 | tf_op jit(solution)/shard_map/ppermute | solution.py:20
  23.1 14.9 %collective-permute-start.2 = (bf16[2,72,512]{2,1,0:T(8,128)(2,1)S(1)}, bf16[2,72,512]{2,1,0:T(8,128)(2,1)S(1)}, u32[]{:S(2)}, u32[]{:S(2)}) collective-permute-start(bf16[2,72,512]{2,1,0:T(8,128)(2,1)S(1)} %pad_maximum_fusion.5), channel_id=1, source_target_pairs={{0,2},{1,3},{2,0},{3,1},{4,6},{5,7},{6,4},{7,5},{8,10},{9,11},{10,... | collective-permute-start | bytes 442376 | tf_op jit(solution)/shard_map/ppermute | solution.py:20
  38.4 12.6 %collective-permute-start.7 = (bf16[2,2,72,512]{3,2,1,0:T(8,128)(2,1)S(1)}, bf16[2,2,72,512]{3,2,1,0:T(8,128)(2,1)S(1)}, u32[]{:S(2)}, u32[]{:S(2)}) collective-permute-start(bf16[2,2,72,512]{3,2,1,0:T(8,128)(2,1)S(1)} %pad_maximum_fusion.4), channel_id=1, source_target_pairs={{0,1},{1,0},{2,3},{3,2},{4,5},{5,4},{6,7},{7,6},{8,9},{9,8},{10,11... | collective-permute-start | bytes 884744 | tf_op jit(solution)/shard_map/ppermute | solution.py:20
  41.0 10.2 %collective-permute-start.8 = (bf16[512,512]{0,1:T(8,128)(2,1)}, bf16[512,512]{0,1:T(8,128)(2,1)S(1)}, u32[]{:S(2)}, u32[]{:S(2)}) collective-permute-start(bf16[512,512]{0,1:T(8,128)(2,1)} %bitcast.5), channel_id=1, source_target_pairs={{56,0},{0,8},{8,16},{16,24},{24,32},{32,40},{40,48},{48,56},{57,1}... | collective-permute-start | bytes 1572872 | tf_op jit(solution)/shard_map/ppermute | solution.py:16
  41.1 27.5 %collective-permute-start.3 = (bf16[3,16,3072]{2,1,0:T(8,128)(2,1)S(1)}, bf16[3,16,3072]{2,1,0:T(8,128)(2,1)S(1)}, u32[]{:S(2)}, u32[]{:S(2)}) collective-permute-start(bf16[3,16,3072]{2,1,0:T(8,128)(2,1)S(1)} %slice.46), channel_id=1, source_target_pairs={{0,256},{64,320},{128,384},{192,448},{256,0},{320,64},{384,128},{4... | collective-permute-start | bytes 884744 | tf_op jit(solution)/shard_map/ppermute | solution.py:20
  51.2 1.4 copy-start.7
  51.2 86.2 %copy-start.4 = (bf16[512,512]{0,1:T(8,128)(2,1)}, bf16[512,512]{0,1:T(8,128)(2,1)S(1)}, u32[]{:S(2)}) copy-start(bf16[512,512]{0,1:T(8,128)(2,1)S(1)} %collective-permute-done.8) | copy-start | bytes 1572868
  52.5 35.3 %all-to-all-start.1 = ((bf16[4,8,16,512]{3,2,1,0:T(8,128)(2,1)}), bf16[4,8,16,512]{3,2,1,0:T(8,128)(2,1)S(1)}, u32[]{:S(2)}, u32[]{:S(2)}) async-start(bf16[4,8,16,512]{3,2,1,0:T(8,128)(2,1)} %bitcast.130), calls=%async_computation.1 | async-start | bytes 1048576 | tf_op jit(solution)/shard_map/all_to_all | solution.py:25
  68.7 19.1 %copy-start.11 = (bf16[16,4096]{1,0:T(8,128)(2,1)}, bf16[16,4096]{1,0:T(8,128)(2,1)S(1)}, u32[]{:S(2)}) copy-start(bf16[16,4096]{1,0:T(8,128)(2,1)S(1)} %fusion.25.fresh0_ref) | copy-start | bytes 393220
  68.7 14.2 %collective-permute-start.6 = (bf16[16,4096]{1,0:T(8,128)(2,1)S(1)}, bf16[16,4096]{1,0:T(8,128)(2,1)S(1)}, u32[]{:S(2)}, u32[]{:S(2)}) collective-permute-start(bf16[16,4096]{1,0:T(8,128)(2,1)S(1)} %fusion.25.fresh0_ref), channel_id=1, source_target_pairs={{0,192},{64,128},{128,64},{192,0},{256,448},{320,384},{384,320},{4... | collective-permute-start | bytes 393224 | tf_op jit(solution)/shard_map/ppermute | solution.py:20
  78.2 8.4 %collective-permute-start.5 = (bf16[16,4096]{1,0:T(8,128)(2,1)S(1)}, bf16[16,4096]{1,0:T(8,128)(2,1)S(1)}, u32[]{:S(2)}, u32[]{:S(2)}) collective-permute-start(bf16[16,4096]{1,0:T(8,128)(2,1)S(1)} %fusion.25.fresh0_ref), channel_id=1, source_target_pairs={{0,128},{64,192},{128,0},{192,64},{256,384},{320,448},{384,256},{4... | collective-permute-start | bytes 393224 | tf_op jit(solution)/shard_map/ppermute | solution.py:20
  80.9 6.9 %collective-permute-start.4 = (bf16[16,4096]{1,0:T(8,128)(2,1)S(1)}, bf16[16,4096]{1,0:T(8,128)(2,1)S(1)}, u32[]{:S(2)}, u32[]{:S(2)}) collective-permute-start(bf16[16,4096]{1,0:T(8,128)(2,1)S(1)} %fusion.25.fresh0_ref), channel_id=1, source_target_pairs={{0,64},{64,0},{128,192},{192,128},{256,320},{320,256},{384,448},{4... | collective-permute-start | bytes 393224 | tf_op jit(solution)/shard_map/ppermute | solution.py:20
  82.9 4.9 %copy-start.15 = (bf16[16,4096]{1,0:T(8,128)(2,1)}, bf16[16,4096]{1,0:T(8,128)(2,1)S(1)}, u32[]{:S(2)}) copy-start(bf16[16,4096]{1,0:T(8,128)(2,1)S(1)} %collective-permute-done.6.fresh3_ref) | copy-start | bytes 393220
  86.5 1.3 copy-start.16
  87.8 0.7 copy-start.17
  88.5 0.8 copy-start.3
  92.1 21.2 %copy-start.10 = (bf16[64,4096]{1,0:T(8,128)(2,1)S(1)}, bf16[64,4096]{1,0:T(8,128)(2,1)}, u32[]{:S(2)}) copy-start(bf16[64,4096]{1,0:T(8,128)(2,1)} %get-tuple-element.28) | copy-start | bytes 1572868
  92.1 22.1 %copy-start.2 = (f32[1,1,64,4096]{3,2,1,0:T(8,128)S(1)}, f32[1,1,64,4096]{3,2,1,0:T(8,128)}, u32[]{:S(2)}) copy-start(f32[1,1,64,4096]{3,2,1,0:T(8,128)} %param.12) | copy-start | bytes 3145732
  92.1 44.5 %all-to-all-start.2 = ((bf16[8,80,512]{2,1,0:T(8,128)(2,1)}), bf16[8,80,512]{2,1,0:T(8,128)(2,1)S(1)}, u32[]{:S(2)}, u32[]{:S(2)}) async-start(bf16[8,80,512]{2,1,0:T(8,128)(2,1)} %get-tuple-element.20), calls=%async_computation.2 | async-start | bytes 1310720 | tf_op jit(solution)/shard_map/all_to_all | solution.py:206
  114.1 1.2 copy-start.1
  137.3 1.3 copy-start.8
  138.6 3.6 %copy-start.6 = (bf16[8,8,32,128]{3,2,1,0:T(8,128)(2,1)S(1)}, bf16[8,8,32,128]{3,2,1,0:T(8,128)(2,1)}, u32[]{:S(2)}) copy-start(bf16[8,8,32,128]{3,2,1,0:T(8,128)(2,1)} %copy.70) | copy-start | bytes 1572868
  138.6 6.4 %copy-start.9 = (bf16[3,16,4096]{2,1,0:T(8,128)(2,1)S(1)}, bf16[3,16,4096]{2,1,0:T(8,128)(2,1)}, u32[]{:S(2)}) copy-start(bf16[3,16,4096]{2,1,0:T(8,128)(2,1)} %pad_maximum_fusion.2) | copy-start | bytes 1179652
  140.3 8.4 %collective-permute-start.9 = (f32[4,128]{1,0:T(4,128)S(1)}, f32[4,128]{1,0:T(4,128)S(1)}, u32[]{:S(2)}, u32[]{:S(2)}) collective-permute-start(f32[4,128]{1,0:T(4,128)S(1)} %bitcast.170), channel_id=1, source_target_pairs={{0,1},{1,0},{2,3},{3,2},{4,5},{5,4},{6,7},{7,6},{8,9},{9,8},{10,11... | collective-permute-start | bytes 6152 | tf_op jit(solution)/shard_map/ppermute | solution.py:20
  148.7 8.9 %copy-start.19 = (f32[4,128]{1,0:T(4,128)}, f32[4,128]{1,0:T(4,128)S(1)}, u32[]{:S(2)}) copy-start(f32[4,128]{1,0:T(4,128)S(1)} %collective-permute-done.9) | copy-start | bytes 6148
  149.3 34.1 %collective-permute-start.10 = (f32[4,128]{1,0:T(4,128)}, f32[4,128]{1,0:T(4,128)}, u32[]{:S(2)}, u32[]{:S(2)}) collective-permute-start(f32[4,128]{1,0:T(4,128)} %bitcast_add_fusion.2), channel_id=1, source_target_pairs={{0,2},{1,3},{2,0},{3,1},{4,6},{5,7},{6,4},{7,5},{8,10},{9,11},{10,... | collective-permute-start | bytes 6152 | tf_op jit(solution)/shard_map/ppermute | solution.py:20
  166.6 45.4 %copy-start.12 = (bf16[8,2,8,512]{3,2,0,1:T(8,128)(2,1)S(1)}, bf16[8,2,8,512]{3,2,0,1:T(8,128)(2,1)}, u32[]{:S(2)}) copy-start(bf16[8,2,8,512]{3,2,0,1:T(8,128)(2,1)} %copy.66) | copy-start | bytes 393220
  166.6 46.6 %copy-start.18 = (bf16[2,4096]{1,0:T(2,128)(2,1)S(1)}, bf16[2,4096]{1,0:T(2,128)(2,1)}, u32[]{:S(2)}) copy-start(bf16[2,4096]{1,0:T(2,128)(2,1)} %convert_element_type.140) | copy-start | bytes 49156
  166.7 72.7 %all-to-all-start.3 = ((bf16[8,64,512]{2,1,0:T(8,128)(2,1)}), bf16[8,64,512]{2,1,0:T(8,128)(2,1)}, u32[]{:S(2)}, u32[]{:S(2)}) async-start(bf16[8,64,512]{2,1,0:T(8,128)(2,1)} %bitcast.157), calls=%async_computation.3 | async-start | bytes 1048576 | tf_op jit(solution)/shard_map/all_to_all | solution.py:221
  174.2 49.3 %copy-start.5 = (bf16[512,512]{0,1:T(8,128)(2,1)S(1)}, bf16[512,512]{0,1:T(8,128)(2,1)}, u32[]{:S(2)}) copy-start(bf16[512,512]{0,1:T(8,128)(2,1)} %copy-done.4) | copy-start | bytes 1572868
  174.2 37.9 %collective-permute-start.13 = (bf16[16,4096]{1,0:T(8,128)(2,1)}, bf16[16,4096]{1,0:T(8,128)(2,1)S(1)}, u32[]{:S(2)}, u32[]{:S(2)}) collective-permute-start(bf16[16,4096]{1,0:T(8,128)(2,1)} %bitcast.162), channel_id=1, source_target_pairs={{0,256},{64,320},{128,384},{192,448},{256,0},{320,64},{384,128},{4... | collective-permute-start | bytes 393224 | tf_op jit(solution)/shard_map/ppermute | solution.py:20
  184.0 39.4 %collective-permute-start.11 = (f32[4,128]{1,0:T(4,128)S(1)}, f32[4,128]{1,0:T(4,128)S(1)}, u32[]{:S(2)}, u32[]{:S(2)}) collective-permute-start(f32[4,128]{1,0:T(4,128)S(1)} %fusion.44), channel_id=1, source_target_pairs={{0,4},{1,5},{2,6},{3,7},{4,0},{5,1},{6,2},{7,3},{8,12},{9,13},{10,... | collective-permute-start | bytes 6152 | tf_op jit(solution)/shard_map/ppermute | solution.py:20
  213.3 14.0 %collective-permute-start.15 = (bf16[34,4096]{1,0:T(8,128)(2,1)S(1)}, bf16[34,4096]{1,0:T(8,128)(2,1)S(1)}, u32[]{:S(2)}, u32[]{:S(2)}) collective-permute-start(bf16[34,4096]{1,0:T(8,128)(2,1)S(1)} %get-tuple-element.58), channel_id=1, source_target_pairs={{0,128},{64,192},{128,0},{192,64},{256,384},{320,448},{384,256},{4... | collective-permute-start | bytes 835592 | tf_op jit(solution)/shard_map/ppermute | solution.py:20
  217.6 14.7 %collective-permute-start.14 = (bf16[34,4096]{1,0:T(8,128)(2,1)S(1)}, bf16[34,4096]{1,0:T(8,128)(2,1)S(1)}, u32[]{:S(2)}, u32[]{:S(2)}) collective-permute-start(bf16[34,4096]{1,0:T(8,128)(2,1)S(1)} %get-tuple-element.58), channel_id=1, source_target_pairs={{0,64},{64,0},{128,192},{192,128},{256,320},{320,256},{384,448},{4... | collective-permute-start | bytes 835592 | tf_op jit(solution)/shard_map/ppermute | solution.py:20
  220.6 12.5 %collective-permute-start.16 = (bf16[34,4096]{1,0:T(8,128)(2,1)S(1)}, bf16[34,4096]{1,0:T(8,128)(2,1)S(1)}, u32[]{:S(2)}, u32[]{:S(2)}) collective-permute-start(bf16[34,4096]{1,0:T(8,128)(2,1)S(1)} %get-tuple-element.58), channel_id=1, source_target_pairs={{0,192},{64,128},{128,64},{192,0},{256,448},{320,384},{384,320},{4... | collective-permute-start | bytes 835592 | tf_op jit(solution)/shard_map/ppermute | solution.py:20
  224.5 13.9 %collective-permute-start.12 = (bf16[512,512]{0,1:T(8,128)(2,1)}, bf16[512,512]{0,1:T(8,128)(2,1)S(1)}, u32[]{:S(2)}, u32[]{:S(2)}) collective-permute-start(bf16[512,512]{0,1:T(8,128)(2,1)} %fusion.6), channel_id=1, source_target_pairs={{8,0},{16,8},{24,16},{32,24},{40,32},{48,40},{56,48},{0,56},{9,1},... | collective-permute-start | bytes 1572872 | tf_op jit(solution)/shard_map/ppermute | solution.py:16
  236.0 1.7 copy-start.13
